TPU v7x, 32 devices: a whole 2x2x4 slice. The times are simulated.
32 devices in a mesh: box: 2 (over x), theta: 4 (over y, core), phi: 4 (over z).
Axes of the slice: x: 2, y: 2, z: 4, core: 2. Of those that a mesh axis runs over, the one named last changes fastest.
Arguments:
- coeffs: bfloat16 [256, 2, 128, 256], P(('box', 'theta', 'phi')), may hold values from -6 to 6
- near_blocks: bfloat16 [256, 12, 2, 128, 128], P(('box', 'theta', 'phi')), may hold values from -0.109375 to 0.109375
- near_ids: int32 [256, 12], P(('box', 'theta', 'phi')), may hold values from 0 to 255, as said below
- near_count: int32 [256], P(('box', 'theta', 'phi')), may hold values from 3 to 12, as said below
- radiation: bfloat16 [256, 2, 128, 128], P(('box', 'theta', 'phi')), may hold values from -0.5 to 0.5
- partners: int32 [32, 16], P('box'), may hold values from 0 to 31, as said below
- vector_ids: int32 [32, 16], P('box'), may hold values from 0 to 315
- pair_count: int32 [32], P('box'), may hold values from 4 to 16, as said below
- translation: bfloat16 [316, 2, 16, 32], P(None, None, 'theta', 'phi'), may hold values from -0.5 to 0.5
Outputs:
- product: float32 [256, 2, 128, 256], P(('box', 'theta', 'phi'))
Inputs may be any that keep to these rules, and one draw needn't show every extreme that they name: `near_ids`: row b lists b itself first, then 12 - 1 further entries; the used ones (before near_count[b]) are distinct other leaf boxes whose index differs from b by at most 8, and some used entry differs by exactly 8. Entries at or after near_count[b] are not used and may repeat b. `near_count`: some leaf box uses all 12 slots. `partners`: row d holds 16 distinct upper boxes other than d whose index differs from d by at most 16; a difference of exactly 16 occurs among used entries. Entries at or after pair_count[d] are not used. `pair_count`: some upper box uses all 16 slots.
All inputs are finite; a program needn't handle non-finite values.
Results may differ from a plain program's by a relative error of at most 0.0055.
Values may be sent and summed in bfloat16 or wider, within the bound.
No kernel may reach another device: no remote copies, remote signals or barrier semaphores. Data moves between devices by JAX's collectives and lax.ppermute only.
A program may use at most 128 MiB of HBM per device.

v0:
```python
import functools
import math

import jax
import jax.numpy as jnp
import ml_dtypes
import numpy as np
from jax import lax
from jax.experimental import pallas as pl
from jax.experimental.pallas import tpu as pltpu
from jax.sharding import PartitionSpec as P

TL = 8
PL = 16
TU = 16
PU = 32

WEIGHT_UP = (-0.0546875, 0.8203125, 0.2734375, -0.0390625)
WEIGHT_DOWN = (-0.0390625, 0.2734375, 0.8203125, -0.0546875)
PHASE_SCALE = 1.3

F32 = jnp.float32
BF16 = jnp.bfloat16
VMEM_LIMIT = 48 * 1024 * 1024
GROUP = 4
NOWHERE = -(2**20)


def lagrange(rows, columns, wrap):
    matrix = np.zeros((rows, columns))
    for row in range(rows):
        weights = WEIGHT_UP if row % 2 else WEIGHT_DOWN
        for order in range(4):
            node = row // 2 + row % 2 - 2 + order
            node = node % columns if wrap else min(max(node, 0), columns - 1)
            matrix[row, node] += weights[order]
    return matrix


def split_weights(matrix):
    high = matrix.astype(ml_dtypes.bfloat16)
    low = (matrix - high.astype(np.float64)).astype(ml_dtypes.bfloat16)
    return high, low


def operators(shares, theta_size, phi_size):
    theta_part = TU // theta_size // shares
    order = np.arange(TU * PU).reshape(theta_size, shares, theta_part, phi_size, PU // phi_size)
    order = order.transpose(1, 0, 3, 2, 4).reshape(-1)
    interp = np.kron(lagrange(TU, TL, False), lagrange(PU, PL, True))
    theta = math.pi * (np.arange(TU) + 0.5) / TU
    azimuth = 2.0 * math.pi * (np.arange(PU) + 0.5) / PU
    up, down = [], []
    for octant in range(4):
        sign_x = 2 * (octant % 2) - 1
        sign_y = 2 * (octant // 2 % 2) - 1
        sign_z = 2 * (octant // 4) - 1
        angle = PHASE_SCALE * (
            sign_x * np.sin(theta)[:, None] * np.cos(azimuth)[None]
            + sign_y * np.sin(theta)[:, None] * np.sin(azimuth)[None]
            + sign_z * np.cos(theta)[:, None]
        ).reshape(-1, 1)
        cos_high, cos_low = split_weights((np.cos(angle) * interp)[order])
        sin_high, sin_low = split_weights((np.sin(angle) * interp)[order])
        up.append(np.concatenate([cos_high, sin_high, cos_low, sin_low], axis=1))
        down.append(
            np.concatenate(
                [
                    np.concatenate([cos_high.T, cos_low.T], axis=1),
                    np.concatenate([sin_high.T, sin_low.T], axis=1),
                ],
                axis=0,
            )
        )
    return np.stack(up), np.stack(down)


def in_hbm(array):
    return pltpu.with_memory_space_constraint(array, pltpu.HBM)


def dot(a, b):
    return jnp.dot(a, b, preferred_element_type=F32)


def up_kernel(x_ref, rad_ref, w_ref, out_ref, acc):
    octant = pl.program_id(0)
    points, basis = rad_ref.shape[2], rad_ref.shape[3]
    rhs = x_ref.shape[3]
    rad_re, rad_im = rad_ref[0, 0], rad_ref[0, 1]
    left = jnp.concatenate(
        [
            jnp.concatenate([rad_re, -rad_im], axis=1),
            jnp.concatenate([rad_im, rad_re], axis=1),
        ],
        axis=0,
    )
    pattern = dot(left, x_ref[0].reshape(2 * basis, rhs)).astype(BF16)
    real, imag = pattern[:points], pattern[points:]
    minus = -imag
    first = octant < 4
    swapped = jnp.concatenate(
        [jnp.where(first, minus, imag), jnp.where(first, real, -real)], axis=1
    )
    straight = jnp.concatenate([real, imag], axis=1)
    right = jnp.concatenate([straight, swapped, straight, swapped], axis=0)

    @pl.when(octant == 0)
    def _():
        acc[...] = dot(w_ref[0], right)

    @pl.when(octant > 0)
    def _():
        acc[...] += dot(w_ref[0], right)

    @pl.when(octant == pl.num_programs(0) - 1)
    def _():
        out_ref[...] = acc[...].astype(BF16).reshape(out_ref.shape)


def upward(coeffs, radiation, weights, groups):
    boxes, _, basis, rhs = coeffs.shape
    points = radiation.shape[2]
    samples = weights.shape[1]
    return pl.pallas_call(
        up_kernel,
        grid=(boxes,),
        in_specs=[
            pl.BlockSpec((1, 2, basis, rhs), lambda o: (o, 0, 0, 0)),
            pl.BlockSpec((1, 2, points, basis), lambda o: (o, 0, 0, 0)),
            pl.BlockSpec((1, samples, 4 * points), lambda o: (jnp.minimum(o, 7 - o), 0, 0)),
        ],
        out_specs=pl.BlockSpec((groups, samples // groups, 2 * rhs), lambda o: (0, 0, 0)),
        out_shape=jax.ShapeDtypeStruct((groups, samples // groups, 2 * rhs), BF16),
        scratch_shapes=[pltpu.VMEM((samples, 2 * rhs), F32)],
        compiler_params=pltpu.CompilerParams(vmem_limit_bytes=VMEM_LIMIT),
        cost_estimate=pl.CostEstimate(
            flops=3 * 10**9, bytes_accessed=5 * 2**20, transcendentals=0
        ),
        name="upward",
    )(in_hbm(coeffs), in_hbm(radiation), in_hbm(weights))


def coupling_kernel(lists_ref, base_ref, table_ref, out_ref):
    rows = lists_ref.shape[0]
    samples = table_ref.shape[1] // 2
    targets = out_ref.shape[0] // (2 * samples)
    columns = out_ref.shape[1]
    slots = rows // targets
    selector = (
        lax.broadcasted_iota(jnp.int32, (rows, table_ref.shape[0]), 1) == lists_ref[:, 1:2]
    )
    chosen = dot(selector.astype(BF16), table_ref[...]).astype(BF16)
    wide = lax.broadcasted_iota(jnp.int32, (rows, columns), 1) // samples
    match = wide + base_ref[0] == lists_ref[:, 0:1]
    spread = lax.broadcasted_iota(jnp.int32, (samples, columns), 0) == (
        lax.broadcasted_iota(jnp.int32, (samples, columns), 1) % samples
    )
    gather = (
        lax.broadcasted_iota(jnp.int32, (targets, rows), 1) // slots
        == lax.broadcasted_iota(jnp.int32, (targets, rows), 0)
    ).astype(BF16)
    tile = spread.astype(BF16)
    for part in range(2):
        lines = dot(chosen[:, part * samples : (part + 1) * samples], tile)
        lines = dot(gather, jnp.where(match, lines, 0.0).astype(BF16))
        for target in range(targets):
            line = jnp.broadcast_to(lines[target : target + 1], spread.shape)
            start = (part * targets + target) * samples
            out_ref[start : start + samples] = jnp.where(spread, line, 0.0).astype(BF16)


def couplings(lists, base, table, targets, names):
    samples = table.shape[1] // 2
    shape = (2 * targets * samples, names * samples)
    vmem = pl.BlockSpec(memory_space=pltpu.VMEM)
    return pl.pallas_call(
        coupling_kernel,
        in_specs=[vmem, pl.BlockSpec(memory_space=pltpu.SMEM), vmem],
        out_specs=vmem,
        out_shape=jax.ShapeDtypeStruct(shape, BF16),
        compiler_params=pltpu.CompilerParams(vmem_limit_bytes=VMEM_LIMIT),
        cost_estimate=pl.CostEstimate(
            flops=2 * 10**8, bytes_accessed=2 * 2**20, transcendentals=0
        ),
        name="coupling",
    )(lists, base, table)


def translate_kernel(coupling_ref, *refs):
    sources, out_ref = refs[:-1], refs[-1]
    targets, samples, width = out_ref.shape
    rhs = width // 2
    total = None
    start = 0
    for source in sources:
        columns = source.shape[0] * samples
        part = dot(coupling_ref[:, start : start + columns], source[...].reshape(columns, width))
        total = part if total is None else total + part
        start += columns
    half = targets * samples
    real = total[:half, :rhs] - total[half:, rhs:]
    imag = total[:half, rhs:] + total[half:, :rhs]
    out_ref[...] = jnp.concatenate([real, imag], axis=1).astype(BF16).reshape(out_ref.shape)


def translate(coupling, sources):
    _, samples, width = sources[0].shape
    targets = coupling.shape[0] // (2 * samples)
    return pl.pallas_call(
        translate_kernel,
        out_shape=jax.ShapeDtypeStruct((targets, samples, width), BF16),
        compiler_params=pltpu.CompilerParams(vmem_limit_bytes=VMEM_LIMIT),
        cost_estimate=pl.CostEstimate(
            flops=10**9, bytes_accessed=2 * 2**20, transcendentals=0
        ),
        name="translate",
    )(coupling, *sources)


def near_kernel(
    ids_ref, count_ref, rank_ref, blocks_ref, low_ref, own_ref, high_ref, out_ref, held, sems
):
    box = pl.program_id(0)
    boxes, _, basis, rhs = own_ref.shape

    @pl.when(box == 0)
    def _():
        copies = [
            pltpu.make_async_copy(ref, held.at[pl.ds(place * boxes, boxes)], sems.at[place])
            for place, ref in enumerate((low_ref, own_ref, high_ref))
        ]
        for copy in copies:
            copy.start()
        for copy in copies:
            copy.wait()

    used = jnp.maximum(count_ref[box], 1)
    first = (rank_ref[0] - 1) * boxes

    def operand(slot, limit):
        real, imag = blocks_ref[0, slot, 0], blocks_ref[0, slot, 1]
        if limit:
            real = jnp.where(slot < used, real, jnp.zeros_like(real))
            imag = jnp.where(slot < used, imag, jnp.zeros_like(imag))
        return jnp.concatenate(
            [
                jnp.concatenate([real, -imag], axis=1),
                jnp.concatenate([imag, real], axis=1),
            ],
            axis=0,
        )

    def source(slot):
        return held[ids_ref[box, slot] - first].reshape(2 * basis, rhs)

    def group(first_slot):
        slots = range(first_slot, first_slot + GROUP)
        left = jnp.concatenate([operand(slot, slot > 0) for slot in slots], axis=1)
        right = jnp.concatenate([source(jnp.minimum(slot, used - 1)) for slot in slots], axis=0)
        return dot(left, right).reshape(2, basis, rhs)

    out_ref[0] = group(0)
    for first_slot in range(GROUP, blocks_ref.shape[1], GROUP):

        @pl.when(used > first_slot)
        def _(first_slot=first_slot):
            out_ref[0] += group(first_slot)


def near_field(ids, counts, rank, blocks, low, own, high):
    boxes, slots, _, basis, _ = blocks.shape
    rhs = own.shape[3]
    anywhere = pl.BlockSpec(memory_space=pl.ANY)
    return pl.pallas_call(
        near_kernel,
        grid_spec=pltpu.PrefetchScalarGridSpec(
            num_scalar_prefetch=3,
            grid=(boxes,),
            in_specs=[
                pl.BlockSpec((1, slots, 2, basis, basis), lambda b, *_: (b, 0, 0, 0, 0)),
                anywhere,
                anywhere,
                anywhere,
            ],
            out_specs=pl.BlockSpec((1, 2, basis, rhs), lambda b, *_: (b, 0, 0, 0)),
            scratch_shapes=[
                pltpu.VMEM((3 * boxes, 2, basis, rhs), BF16),
                pltpu.SemaphoreType.DMA((3,)),
            ],
        ),
        out_shape=jax.ShapeDtypeStruct((boxes, 2, basis, rhs), F32),
        compiler_params=pltpu.CompilerParams(vmem_limit_bytes=VMEM_LIMIT),
        cost_estimate=pl.CostEstimate(
            flops=4 * 10**9, bytes_accessed=12 * 2**20, transcendentals=0
        ),
        name="near",
    )(ids, counts, rank, in_hbm(blocks), low, own, high)


def down_kernel(
    field_ref, w_ref, rad_a_ref, rad_b_ref, near_a_ref, near_b_ref, out_ref, held, sems
):
    step = pl.program_id(0)
    last = pl.num_programs(0) - 1
    boxes = out_ref.shape[0]
    _, _, points, basis = rad_a_ref.shape
    rhs = near_a_ref.shape[3]
    slot = step % 2

    def writes(at, place):
        return [
            pltpu.make_async_copy(held.at[place, 0], out_ref.at[at], sems.at[place, 0]),
            pltpu.make_async_copy(held.at[place, 1], out_ref.at[boxes - 1 - at], sems.at[place, 1]),
        ]

    @pl.when(step >= 2)
    def _():
        for copy in writes(step - 2, slot):
            copy.wait()

    field = field_ref[...].reshape(-1, 2 * rhs)
    mixed = dot(w_ref[0], jnp.concatenate([field, field], axis=0))
    cos_re, cos_im = mixed[:points, :rhs], mixed[:points, rhs:]
    sin_re, sin_im = mixed[points:, :rhs], mixed[points:, rhs:]
    pairs = (
        (rad_a_ref, near_a_ref, cos_re + sin_im, cos_im - sin_re),
        (rad_b_ref, near_b_ref, cos_re - sin_im, cos_im + sin_re),
    )
    for place, (rad_ref, near_ref, real, imag) in enumerate(pairs):
        leaf = jnp.concatenate([real, imag], axis=0).astype(BF16)
        rad_re, rad_im = rad_ref[0, 0], rad_ref[0, 1]
        left = jnp.concatenate(
            [
                jnp.concatenate([rad_re, -rad_im], axis=1),
                jnp.concatenate([rad_im, rad_re], axis=1),
            ],
            axis=0,
        )
        far = lax.dot_general(left, leaf, (((0,), (0,)), ((), ())), preferred_element_type=F32)
        held[slot, place] = near_ref[0] + far.reshape(2, basis, rhs)
    for copy in writes(step, slot):
        copy.start()

    @pl.when(step == last)
    def _():
        for copy in writes(step - 1, 1 - slot) + writes(step, slot):
            copy.wait()


def downward(field, weights, radiation, near):
    boxes, _, basis, rhs = near.shape
    points = radiation.shape[2]
    first = lambda s: (s, 0, 0, 0)
    second = lambda s: (boxes - 1 - s, 0, 0, 0)
    return pl.pallas_call(
        down_kernel,
        grid=(boxes // 2,),
        in_specs=[
            pl.BlockSpec(field.shape, lambda s: (0, 0, 0)),
            pl.BlockSpec((1, *weights.shape[1:]), lambda s: (s, 0, 0)),
            pl.BlockSpec((1, 2, points, basis), first),
            pl.BlockSpec((1, 2, points, basis), second),
            pl.BlockSpec((1, 2, basis, rhs), first),
            pl.BlockSpec((1, 2, basis, rhs), second),
        ],
        out_specs=pl.BlockSpec(memory_space=pl.ANY),
        out_shape=jax.ShapeDtypeStruct(near.shape, F32),
        scratch_shapes=[
            pltpu.VMEM((2, 2, 2, basis, rhs), F32),
            pltpu.SemaphoreType.DMA((2, 2)),
        ],
        compiler_params=pltpu.CompilerParams(vmem_limit_bytes=VMEM_LIMIT),
        cost_estimate=pl.CostEstimate(
            flops=2 * 10**9, bytes_accessed=7 * 2**20, transcendentals=0
        ),
        name="downward",
    )(field, in_hbm(weights), *[in_hbm(radiation)] * 2, *[in_hbm(near)] * 2)


def shift(block, axis, step):
    count = lax.axis_size(axis)
    pairs = [(i, i + step) for i in range(count) if 0 <= i + step < count]
    return lax.ppermute(block, axis, pairs)


def lists_of(partners, vector_ids, pair_count):
    used = jnp.arange(partners.shape[1])[None, :] < pair_count[:, None]
    names = jnp.where(used, partners, NOWHERE)
    return jnp.stack([names, vector_ids], axis=2).reshape(-1, 2)


def far_field(spread, lists, translation, shares):
    operator_total, _, theta_band, phi_band = translation.shape
    rank = lax.axis_index("box")
    if shares == lax.axis_size("box"):
        every = ("box", "theta", "phi")
        for_all = lists
        if shares == 2:
            other = lax.ppermute(lists, "box", [(0, 1), (1, 0)])
            for_all = jnp.where(
                rank == 0, jnp.concatenate([lists, other]), jnp.concatenate([other, lists])
            )
        part = theta_band // shares
        table = lax.dynamic_slice_in_dim(translation, rank * part, part, axis=2)
        table = table.reshape(operator_total, -1)
        sources = spread.shape[0]
        base = jnp.zeros((1,), jnp.int32)
        coupling = couplings(for_all, base, table, sources, sources)
        parents = lax.all_to_all(spread, every, split_axis=0, concat_axis=0, tiled=True)
        incoming = translate(coupling, [parents])
        return lax.all_to_all(incoming, every, split_axis=0, concat_axis=0, tiled=True)
    bands = ("theta", "phi")
    per_group = spread.shape[0]
    table = translation.reshape(operator_total, -1)
    base = ((rank - 1) * per_group).astype(jnp.int32).reshape(1)
    coupling = couplings(lists, base, table, per_group, 3 * per_group)
    parents = lax.all_to_all(spread, bands, split_axis=0, concat_axis=0, tiled=True)
    sources = [shift(parents, "box", 1), parents, shift(parents, "box", -1)]
    incoming = translate(coupling, sources)
    return lax.all_to_all(incoming, bands, split_axis=0, concat_axis=0, tiled=True)


def per_device(
    shares,
    up_weights,
    down_weights,
    coeffs,
    near_blocks,
    near_ids,
    near_count,
    radiation,
    partners,
    vector_ids,
    pair_count,
    translation,
):
    every = ("box", "theta", "phi")
    low = shift(coeffs, every, 1)
    high = shift(coeffs, every, -1)
    groups = shares * lax.axis_size("theta") * lax.axis_size("phi")
    spread = upward(coeffs, radiation, up_weights, groups)
    lists = lists_of(partners, vector_ids, pair_count)
    field = far_field(spread, lists, translation, shares)
    rank = lax.axis_index(every).astype(jnp.int32).reshape(1)
    near = near_field(near_ids, near_count, rank, near_blocks, low, coeffs, high)
    return downward(field, down_weights, radiation, near)


def solution(mesh):
    box_size, theta_size, phi_size = (mesh.shape[axis] for axis in ("box", "theta", "phi"))
    shares = box_size if box_size <= 2 and TU // theta_size % box_size == 0 else 1
    up_weights, down_weights = operators(shares, theta_size, phi_size)
    in_specs = (
        P(),
        P(),
        P(("box", "theta", "phi"), None, None, None),
        P(("box", "theta", "phi"), None, None, None, None),
        P(("box", "theta", "phi"), None),
        P(("box", "theta", "phi")),
        P(("box", "theta", "phi"), None, None, None),
        P("box", None),
        P("box", None),
        P("box"),
        P(None, None, "theta", "phi"),
    )
    out_specs = P(("box", "theta", "phi"), None, None, None)
    mapped = jax.shard_map(
        functools.partial(per_device, shares),
        mesh=mesh,
        in_specs=in_specs,
        out_specs=out_specs,
        check_vma=False,
    )

    def product(*arrays):
        return mapped(jnp.asarray(up_weights), jnp.asarray(down_weights), *arrays)

    return product
```

profile of v0, /device:TPU:8, one launch (start us, length us, event | category | flops | bytes accessed | tf_op | source)
XLA Modules:
  0.0 96.7 jit_solution(5004780293814095753)
XLA Ops:
  0.0 0.0 copy-start
  0.0 0.0 copy-start.7
  0.0 0.0 copy-start.6
  0.0 8.8 %upward.1 = bf16[32,16,512]{2,1,0:T(8,128)(2,1)} custom-call(bf16[8,2,128,256]{3,2,1,0:T(8,128)(2,1)} %own_ref.1, bf16[8,2,128,128]{3,2,1,0:T(8,128)(2,1)} %rad_b_ref.1, bf16[4,512,512]{2,1,0:T(8,128)(2,1)} %constant.29.clone.w_ref), custom_call_target="tpu_custom_call" | custom-call | flops 3000000000 | bytes 5242880 | tf_op jit(solution)/shard_map/upward/pallas_call | solution.py:125
  8.8 6.0 %all-to-all-start = ((bf16[32,16,512]{2,1,0:T(8,128)(2,1)}), bf16[32,16,512]{2,1,0:T(8,128)(2,1)S(1)}, u32[]{:S(2)}, u32[]{:S(2)}) async-start(bf16[32,16,512]{2,1,0:T(8,128)(2,1)} %upward.1), calls=%async_computation | async-start | bytes 1048576 | tf_op jit(solution)/shard_map/all_to_all | solution.py:410
  14.9 0.0 copy-done.2
  14.9 3.4 %collective-permute-start.1 = (bf16[8,2,128,256]{3,2,1,0:T(8,128)(2,1)S(1)}, bf16[8,2,128,256]{3,2,1,0:T(8,128)(2,1)}, u32[]{:S(2)}, u32[]{:S(2)}) collective-permute-start(bf16[8,2,128,256]{3,2,1,0:T(8,128)(2,1)S(1)} %copy-done.2), channel_id=1, source_target_pairs={{0,1},{1,2},{2,3},{3,4},{4,5},{5,6},{6,7},{7,8},{8,9},{9,10},{10,1... | collective-permute-start | bytes 3145736 | tf_op jit(solution)/shard_map/ppermute | solution.py:384
  18.2 3.4 %collective-permute-start.2 = (bf16[8,2,128,256]{3,2,1,0:T(8,128)(2,1)S(1)}, bf16[8,2,128,256]{3,2,1,0:T(8,128)(2,1)}, u32[]{:S(2)}, u32[]{:S(2)}) collective-permute-start(bf16[8,2,128,256]{3,2,1,0:T(8,128)(2,1)S(1)} %copy-done.2), channel_id=1, source_target_pairs={{1,0},{2,1},{3,2},{4,3},{5,4},{6,5},{7,6},{8,7},{9,8},{10,9},{11,1... | collective-permute-start | bytes 3145736 | tf_op jit(solution)/shard_map/ppermute | solution.py:384
  21.7 0.0 copy-done.5
  21.7 0.1 stack.10
  21.8 0.0 copy-done.7
  21.8 0.1 fusion
  21.9 0.1 stack.9
  22.0 0.6 collective-permute-start
  22.5 0.1 copy.18.table_ref
  22.7 3.0 %collective-permute-done = s32[256,2]{0,1:T(2,128)S(1)} collective-permute-done((s32[256,2]{0,1:T(2,128)S(1)}, s32[256,2]{0,1:T(2,128)S(1)}, u32[]{:S(2)}, u32[]{:S(2)}) %collective-permute-start) | collective-permute-done | bytes 2080 | tf_op jit(solution)/shard_map/ppermute | solution.py:400
  25.6 0.1 copy.17
  25.8 0.1 copy.16
  26.0 1.1 %coupling.1.coupling_ref = bf16[1024,512]{1,0:T(8,128)(2,1)S(1)} custom-call(s32[512,2]{1,0:T(8,128)S(1)} %broadcast_select_fusion.lists_ref, s32[1]{0:T(128)} %constant.11.clone.1.base_ref, bf16[316,32]{1,0:T(8,128)(2,1)S(1)} %copy.18.table_ref), custom_call_target="tpu_custom_call" | custom-call | flops 200000000 | bytes 2097152 | tf_op jit(solution)/shard_map/coupling/pallas_call | solution.py:177
  27.1 0.0 copy-start.3
  27.1 0.0 copy-start.4
  27.1 24.0 %all-to-all-done.refs_0_ = bf16[32,16,512]{2,1,0:T(8,128)(2,1)S(1)} async-done(((bf16[32,16,512]{2,1,0:T(8,128)(2,1)}), bf16[32,16,512]{2,1,0:T(8,128)(2,1)S(1)}, u32[]{:S(2)}, u32[]{:S(2)}) %all-to-all-start) | async-done | bytes 524320 | tf_op jit(solution)/shard_map/all_to_all | solution.py:410
  51.1 1.5 %translate.1 = bf16[32,16,512]{2,1,0:T(8,128)(2,1)} custom-call(bf16[1024,512]{1,0:T(8,128)(2,1)S(1)} %coupling.1.coupling_ref, bf16[32,16,512]{2,1,0:T(8,128)(2,1)S(1)} %all-to-all-done.refs_0_), custom_call_target="tpu_custom_call" | custom-call | flops 1000000000 | bytes 2097152 | tf_op jit(solution)/shard_map/translate/pallas_call | solution.py:210
  52.6 3.5 %all-to-all-start.1 = ((bf16[32,16,512]{2,1,0:T(8,128)(2,1)}), bf16[32,16,512]{2,1,0:T(8,128)(2,1)S(1)}, u32[]{:S(2)}, u32[]{:S(2)}) async-start(bf16[32,16,512]{2,1,0:T(8,128)(2,1)} %translate.1), calls=%async_computation.1 | async-start | bytes 1048576 | tf_op jit(solution)/shard_map/all_to_all | solution.py:412
  56.1 9.8 %collective-permute-done.1.low_ref = bf16[8,2,128,256]{3,2,1,0:T(8,128)(2,1)} collective-permute-done((bf16[8,2,128,256]{3,2,1,0:T(8,128)(2,1)S(1)}, bf16[8,2,128,256]{3,2,1,0:T(8,128)(2,1)}, u32[]{:S(2)}, u32[]{:S(2)}) %collective-permute-start.1) | collective-permute-done | bytes 1048608 | tf_op jit(solution)/shard_map/ppermute | solution.py:384
  65.9 13.2 %collective-permute-done.2.high_ref = bf16[8,2,128,256]{3,2,1,0:T(8,128)(2,1)} collective-permute-done((bf16[8,2,128,256]{3,2,1,0:T(8,128)(2,1)S(1)}, bf16[8,2,128,256]{3,2,1,0:T(8,128)(2,1)}, u32[]{:S(2)}, u32[]{:S(2)}) %collective-permute-start.2) | collective-permute-done | bytes 1048608 | tf_op jit(solution)/shard_map/ppermute | solution.py:384
  79.1 0.0 copy-done.3
  79.1 10.7 %near.1.near_a_ref.near_b_ref = f32[8,2,128,256]{3,2,1,0:T(8,128)S(1)} custom-call(s32[8,12]{1,0:T(8,128)S(1)} %copy-done.3, s32[8]{0:T(128)S(1)} %copy-done.4, s32[1]{0:T(128)} %bitcast.1.rank_ref, bf16[8,12,2,128,128]{4,3,2,1,0:T(8,128)(2,1)} %blocks_ref.1, bf16[8,2,128,256]{3,2,1,0:T(8,128)(2,1)} %collective-permute-done.1.low_ref, ...), custom_call_target="tpu_custom_call" | custom-call | flops 4000000000 | bytes 12582912 | tf_op jit(solution)/shard_map/near/pallas_call | solution.py:275
  89.7 0.0 copy-start.1
  89.8 1.3 %copy-done.1 = f32[8,2,128,256]{3,2,1,0:T(8,128)} copy-done((f32[8,2,128,256]{3,2,1,0:T(8,128)}, f32[8,2,128,256]{3,2,1,0:T(8,128)S(1)}, u32[]{:S(2)}) %copy-start.1) | copy-done | bytes 2097176
  91.1 0.0 all-to-all-done.1.field_ref
  91.1 5.6 %downward.1 = f32[8,2,128,256]{3,2,1,0:T(8,128)} custom-call(bf16[32,16,512]{2,1,0:T(8,128)(2,1)S(1)} %all-to-all-done.1.field_ref, bf16[4,256,1024]{2,1,0:T(8,128)(2,1)} %constant.30.clone.w_ref, bf16[8,2,128,128]{3,2,1,0:T(8,128)(2,1)} %rad_b_ref.1, bf16[8,2,128,128]{3,2,1,0:T(8,128)(2,1)} %rad_b_ref.1, f32[8,2,128,256]{3,2,1,0:T(8,128)} %copy-done.1, ...), custom_call_target="tpu_custom_call" | custom-call | flops 2000000000 | bytes 7340032 | tf_op jit(solution)/shard_map/downward/pallas_call | solution.py:356
  (9 shorter events, 0.1 us)
Async XLA Ops:
  0.0 22.5 %copy-start = (bf16[316,2,4,8]{0,3,2,1:T(8,128)(2,1)S(1)}, bf16[316,2,4,8]{0,3,2,1:T(8,128)(2,1)}, u32[]{:S(2)}) copy-start(bf16[316,2,4,8]{0,3,2,1:T(8,128)(2,1)} %param.19) | copy-start | bytes 121348
  0.0 14.9 %copy-start.2 = (bf16[8,2,128,256]{3,2,1,0:T(8,128)(2,1)S(1)}, bf16[8,2,128,256]{3,2,1,0:T(8,128)(2,1)}, u32[]{:S(2)}) copy-start(bf16[8,2,128,256]{3,2,1,0:T(8,128)(2,1)} %own_ref.1) | copy-start | bytes 3145732
  0.0 21.7 %copy-start.5 = (s32[16,16]{1,0:T(8,128)S(1)}, s32[16,16]{1,0:T(8,128)}, u32[]{:S(2)}) copy-start(s32[16,16]{1,0:T(8,128)} %param.17) | copy-start | bytes 3076
  0.0 21.8 %copy-start.7 = (s32[16]{0:T(128)S(1)}, s32[16]{0:T(128)}, u32[]{:S(2)}) copy-start(s32[16]{0:T(128)} %param.18) | copy-start | bytes 196
  0.0 21.8 %copy-start.6 = (s32[16,16]{1,0:T(8,128)S(1)}, s32[16,16]{1,0:T(8,128)}, u32[]{:S(2)}) copy-start(s32[16,16]{1,0:T(8,128)} %param.16) | copy-start | bytes 3076
  8.8 42.3 %all-to-all-start = ((bf16[32,16,512]{2,1,0:T(8,128)(2,1)}), bf16[32,16,512]{2,1,0:T(8,128)(2,1)S(1)}, u32[]{:S(2)}, u32[]{:S(2)}) async-start(bf16[32,16,512]{2,1,0:T(8,128)(2,1)} %upward.1), calls=%async_computation | async-start | bytes 1048576 | tf_op jit(solution)/shard_map/all_to_all | solution.py:410
  14.9 51.0 %collective-permute-start.1 = (bf16[8,2,128,256]{3,2,1,0:T(8,128)(2,1)S(1)}, bf16[8,2,128,256]{3,2,1,0:T(8,128)(2,1)}, u32[]{:S(2)}, u32[]{:S(2)}) collective-permute-start(bf16[8,2,128,256]{3,2,1,0:T(8,128)(2,1)S(1)} %copy-done.2), channel_id=1, source_target_pairs={{0,1},{1,2},{2,3},{3,4},{4,5},{5,6},{6,7},{7,8},{8,9},{9,10},{10,1... | collective-permute-start | bytes 3145736 | tf_op jit(solution)/shard_map/ppermute | solution.py:384
  18.2 60.8 %collective-permute-start.2 = (bf16[8,2,128,256]{3,2,1,0:T(8,128)(2,1)S(1)}, bf16[8,2,128,256]{3,2,1,0:T(8,128)(2,1)}, u32[]{:S(2)}, u32[]{:S(2)}) collective-permute-start(bf16[8,2,128,256]{3,2,1,0:T(8,128)(2,1)S(1)} %copy-done.2), channel_id=1, source_target_pairs={{1,0},{2,1},{3,2},{4,3},{5,4},{6,5},{7,6},{8,7},{9,8},{10,9},{11,1... | collective-permute-start | bytes 3145736 | tf_op jit(solution)/shard_map/ppermute | solution.py:384
  22.0 3.6 %collective-permute-start = (s32[256,2]{0,1:T(2,128)S(1)}, s32[256,2]{0,1:T(2,128)S(1)}, u32[]{:S(2)}, u32[]{:S(2)}) collective-permute-start(s32[256,2]{0,1:T(2,128)S(1)} %pad_add_fusion.1), channel_id=1, source_target_pairs={{0,16},{16,0},{1,17},{17,1},{2,18},{18,2},{3,19},{19,3},{4,20},{20... | collective-permute-start | bytes 6152 | tf_op jit(solution)/shard_map/ppermute | solution.py:400
  27.1 52.0 %copy-start.3 = (s32[8,12]{1,0:T(8,128)S(1)}, s32[8,12]{1,0:T(8,128)}, u32[]{:S(2)}) copy-start(s32[8,12]{1,0:T(8,128)} %ids_ref.1) | copy-start | bytes 1156
  27.1 52.0 %copy-start.4 = (s32[8]{0:T(128)S(1)}, s32[8]{0:T(128)}, u32[]{:S(2)}) copy-start(s32[8]{0:T(128)} %count_ref.1) | copy-start | bytes 100
  52.6 38.5 %all-to-all-start.1 = ((bf16[32,16,512]{2,1,0:T(8,128)(2,1)}), bf16[32,16,512]{2,1,0:T(8,128)(2,1)S(1)}, u32[]{:S(2)}, u32[]{:S(2)}) async-start(bf16[32,16,512]{2,1,0:T(8,128)(2,1)} %translate.1), calls=%async_computation.1 | async-start | bytes 1048576 | tf_op jit(solution)/shard_map/all_to_all | solution.py:412
  89.7 1.3 %copy-start.1 = (f32[8,2,128,256]{3,2,1,0:T(8,128)}, f32[8,2,128,256]{3,2,1,0:T(8,128)S(1)}, u32[]{:S(2)}) copy-start(f32[8,2,128,256]{3,2,1,0:T(8,128)S(1)} %near.1.near_a_ref.near_b_ref) | copy-start | bytes 6291460
where the time goes:
time: 97.7 us; the launch traced here: 96.7 us
  waiting for transfers between devices  49.9 us (51%)
  Pallas kernels  27.6 us (28%)
  starting transfers between devices  16.9 us (17%)
  local copies, waits for them, and re-layouts  1.95 us (2%)
    all_to_all x1, waiting for transfers between devices, far_field(): lax.all_to_all(spread, every, split_axis=0, concat_axis=0, tiled=True)  24 us
    ppermute x2, waiting for transfers between devices, shift(): return lax.ppermute(block, axis, pairs)  23 us
    pallas_call x1, Pallas kernels, near_field(): pl.pallas_call(near_kernel, grid_spec=pltpu.PrefetchScalarGridSpec(num_sc...  10.7 us
    pallas_call x1, Pallas kernels, upward(): pl.pallas_call(up_kernel, grid=(boxes,), in_specs=[pl.BlockSpec((1, 2, ba...  8.77 us
    ppermute x2, starting transfers between devices, shift(): return lax.ppermute(block, axis, pairs)  6.81 us
    all_to_all x1, starting transfers between devices, far_field(): lax.all_to_all(spread, every, split_axis=0, concat_axis=0, tiled=True)  6.04 us
    pallas_call x1, Pallas kernels, downward(): pl.pallas_call(down_kernel, grid=(boxes // 2,), in_specs=[pl.BlockSpec(fi...  5.6 us
    all_to_all x1, starting transfers between devices, far_field(): lax.all_to_all(incoming, every, split_axis=0, concat_axis=0, tiled=True)  3.5 us
  transfers between devices with their start and end apart: 5, of which 4 were waited for; matrix products, arithmetic and copies ran while one was open for 1% of the time, Pallas kernels for 14%

commit v1 on v0

v1 whole, which is shorter than its diff:
```python
import functools
import math

import jax
import jax.numpy as jnp
import ml_dtypes
import numpy as np
from jax import lax
from jax.experimental import pallas as pl
from jax.experimental.pallas import tpu as pltpu
from jax.sharding import PartitionSpec as P

TL = 8
PL = 16
TU = 16
PU = 32

WEIGHT_UP = (-0.0546875, 0.8203125, 0.2734375, -0.0390625)
WEIGHT_DOWN = (-0.0390625, 0.2734375, 0.8203125, -0.0546875)
PHASE_SCALE = 1.3

F32 = jnp.float32
BF16 = jnp.bfloat16
MIB = 2**20
GROUP = 4
NOWHERE = -(2**20)


def lagrange(rows, columns, wrap):
    matrix = np.zeros((rows, columns))
    for row in range(rows):
        weights = WEIGHT_UP if row % 2 else WEIGHT_DOWN
        for order in range(4):
            node = row // 2 + row % 2 - 2 + order
            node = node % columns if wrap else min(max(node, 0), columns - 1)
            matrix[row, node] += weights[order]
    return matrix


def split_weights(matrix):
    high = matrix.astype(ml_dtypes.bfloat16)
    low = (matrix - high.astype(np.float64)).astype(ml_dtypes.bfloat16)
    return high, low


def operators(shares, theta_size, phi_size):
    theta_part = TU // theta_size // shares
    order = np.arange(TU * PU).reshape(theta_size, shares, theta_part, phi_size, PU // phi_size)
    order = order.transpose(1, 0, 3, 2, 4).reshape(-1)
    interp = np.kron(lagrange(TU, TL, False), lagrange(PU, PL, True))
    theta = math.pi * (np.arange(TU) + 0.5) / TU
    azimuth = 2.0 * math.pi * (np.arange(PU) + 0.5) / PU
    up, down = [], []
    for octant in range(4):
        sign_x = 2 * (octant % 2) - 1
        sign_y = 2 * (octant // 2 % 2) - 1
        sign_z = 2 * (octant // 4) - 1
        angle = PHASE_SCALE * (
            sign_x * np.sin(theta)[:, None] * np.cos(azimuth)[None]
            + sign_y * np.sin(theta)[:, None] * np.sin(azimuth)[None]
            + sign_z * np.cos(theta)[:, None]
        ).reshape(-1, 1)
        cos_high, cos_low = split_weights((np.cos(angle) * interp)[order])
        sin_high, sin_low = split_weights((np.sin(angle) * interp)[order])
        up.append(np.concatenate([cos_high, sin_high, cos_low, sin_low], axis=1))
        down.append(
            np.concatenate(
                [
                    np.concatenate([cos_high.T, cos_low.T], axis=1),
                    np.concatenate([sin_high.T, sin_low.T], axis=1),
                ],
                axis=0,
            )
        )
    return np.concatenate(up, axis=1), np.stack(down)


def in_hbm(array):
    return pltpu.with_memory_space_constraint(array, pltpu.HBM)


def dot(a, b):
    return jnp.dot(a, b, preferred_element_type=F32)


def complex_rows(real, imag):
    return jnp.concatenate(
        [
            jnp.concatenate([real, -imag], axis=1),
            jnp.concatenate([imag, real], axis=1),
        ],
        axis=0,
    )


def up_kernel(x_hbm, rad_hbm, w_hbm, out_ref, x_ref, rad_ref, w_ref, right, sems):
    boxes, _, basis, rhs = x_ref.shape
    points = rad_ref.shape[2]
    copies = [
        pltpu.make_async_copy(source, target, sems.at[place])
        for place, (source, target) in enumerate(
            ((x_hbm, x_ref), (rad_hbm, rad_ref), (w_hbm, w_ref))
        )
    ]
    for copy in copies:
        copy.start()
    copies[0].wait()
    copies[1].wait()
    half = boxes // 2
    for octant in range(boxes):
        left = complex_rows(rad_ref[octant, 0], rad_ref[octant, 1])
        pattern = dot(left, x_ref[octant].reshape(2 * basis, rhs)).astype(BF16)
        real, imag = pattern[:points], pattern[points:]
        straight = jnp.concatenate([real, imag], axis=1)
        if octant < half:
            swapped = jnp.concatenate([-imag, real], axis=1)
        else:
            swapped = jnp.concatenate([imag, -real], axis=1)
        place = octant if octant < half else boxes - 1 - octant
        for copy in range(2):
            start = (4 * place + 2 * copy) * points
            right[octant // half, start : start + points] = straight
            right[octant // half, start + points : start + 2 * points] = swapped
    copies[2].wait()
    total = dot(w_ref[...], right[0]) + dot(w_ref[...], right[1])
    out_ref[...] = total.astype(BF16).reshape(out_ref.shape)


def upward(coeffs, radiation, weights, groups):
    boxes, _, basis, rhs = coeffs.shape
    samples, columns = weights.shape
    anywhere = pl.BlockSpec(memory_space=pl.ANY)
    return pl.pallas_call(
        up_kernel,
        in_specs=[anywhere] * 3,
        out_specs=pl.BlockSpec(memory_space=pltpu.VMEM),
        out_shape=jax.ShapeDtypeStruct((groups, samples // groups, 2 * rhs), BF16),
        scratch_shapes=[
            pltpu.VMEM(coeffs.shape, BF16),
            pltpu.VMEM(radiation.shape, BF16),
            pltpu.VMEM(weights.shape, BF16),
            pltpu.VMEM((2, columns, 2 * rhs), BF16),
            pltpu.SemaphoreType.DMA((3,)),
        ],
        compiler_params=pltpu.CompilerParams(vmem_limit_bytes=24 * MIB),
        cost_estimate=pl.CostEstimate(
            flops=2 * 10**9, bytes_accessed=4 * MIB, transcendentals=0
        ),
        name="upward",
    )(in_hbm(coeffs), in_hbm(radiation), in_hbm(weights))


def coupling_kernel(lists_ref, base_ref, table_ref, out_ref):
    rows = lists_ref.shape[0]
    samples = table_ref.shape[1] // 2
    targets = out_ref.shape[0] // (2 * samples)
    columns = out_ref.shape[1]
    slots = rows // targets
    selector = (
        lax.broadcasted_iota(jnp.int32, (rows, table_ref.shape[0]), 1) == lists_ref[:, 1:2]
    )
    chosen = dot(selector.astype(BF16), table_ref[...]).astype(BF16)
    wide = lax.broadcasted_iota(jnp.int32, (rows, columns), 1) // samples
    match = wide + base_ref[0] == lists_ref[:, 0:1]
    spread = lax.broadcasted_iota(jnp.int32, (samples, columns), 0) == (
        lax.broadcasted_iota(jnp.int32, (samples, columns), 1) % samples
    )
    gather = (
        lax.broadcasted_iota(jnp.int32, (targets, rows), 1) // slots
        == lax.broadcasted_iota(jnp.int32, (targets, rows), 0)
    ).astype(BF16)
    tile = spread.astype(BF16)
    for part in range(2):
        lines = dot(chosen[:, part * samples : (part + 1) * samples], tile)
        lines = dot(gather, jnp.where(match, lines, 0.0).astype(BF16))
        for target in range(targets):
            line = jnp.broadcast_to(lines[target : target + 1], spread.shape)
            start = (part * targets + target) * samples
            out_ref[start : start + samples] = jnp.where(spread, line, 0.0).astype(BF16)


def couplings(lists, base, table, targets, names):
    samples = table.shape[1] // 2
    shape = (2 * targets * samples, names * samples)
    vmem = pl.BlockSpec(memory_space=pltpu.VMEM)
    return pl.pallas_call(
        coupling_kernel,
        in_specs=[vmem, pl.BlockSpec(memory_space=pltpu.SMEM), vmem],
        out_specs=vmem,
        out_shape=jax.ShapeDtypeStruct(shape, BF16),
        compiler_params=pltpu.CompilerParams(vmem_limit_bytes=16 * MIB),
        cost_estimate=pl.CostEstimate(
            flops=2 * 10**8, bytes_accessed=2 * 2**20, transcendentals=0
        ),
        name="coupling",
    )(lists, base, table)


def translate_kernel(coupling_ref, *refs):
    sources, out_ref = refs[:-1], refs[-1]
    targets, samples, width = out_ref.shape
    rhs = width // 2
    total = None
    start = 0
    for source in sources:
        columns = source.shape[0] * samples
        part = dot(coupling_ref[:, start : start + columns], source[...].reshape(columns, width))
        total = part if total is None else total + part
        start += columns
    half = targets * samples
    real = total[:half, :rhs] - total[half:, rhs:]
    imag = total[:half, rhs:] + total[half:, :rhs]
    out_ref[...] = jnp.concatenate([real, imag], axis=1).astype(BF16).reshape(out_ref.shape)


def translate(coupling, sources):
    _, samples, width = sources[0].shape
    targets = coupling.shape[0] // (2 * samples)
    return pl.pallas_call(
        translate_kernel,
        out_shape=jax.ShapeDtypeStruct((targets, samples, width), BF16),
        compiler_params=pltpu.CompilerParams(vmem_limit_bytes=16 * MIB),
        cost_estimate=pl.CostEstimate(
            flops=10**9, bytes_accessed=2 * 2**20, transcendentals=0
        ),
        name="translate",
    )(coupling, *sources)


def near_kernel(first, count, begun, *refs):
    ids_ref, used_ref, rank_ref, blocks_hbm = refs[:4]
    sources = refs[4 : 4 + count]
    before_ref = refs[4 + count] if begun else None
    out_ref, blocks, held, listed, sems = refs[4 + count + begun :]
    boxes, slots, _, basis, _ = blocks.shape
    rhs = held.shape[3]
    base = (rank_ref[0] - 1 + first) * boxes
    source_copies = [
        pltpu.make_async_copy(source, held.at[pl.ds(place * boxes, boxes)], sems.at[boxes + place])
        for place, source in enumerate(sources)
    ]
    block_copies = lambda box: pltpu.make_async_copy(blocks_hbm.at[box], blocks.at[box], sems.at[box])
    for copy in source_copies:
        copy.start()
    for box in range(boxes):
        block_copies(box).start()
    for copy in source_copies:
        copy.wait()

    def one_box(box, carry):
        total = jnp.int32(0)
        used = used_ref[box]
        for slot in range(slots):
            place = ids_ref[box, slot] - base
            listed[total] = jnp.int32(slot)
            wanted = (slot < used) & (place >= 0) & (place < count * boxes)
            total += wanted.astype(jnp.int32)
        out_ref[box] = before_ref[box] if begun else jnp.zeros(out_ref.shape[1:], F32)
        block_copies(box).wait()

        def group(index, carry):
            left, right = [], []
            for step in range(GROUP):
                at = index * GROUP + step
                slot = listed[jnp.minimum(at, total - 1)]
                real, imag = blocks[box, slot, 0], blocks[box, slot, 1]
                if step:
                    real = jnp.where(at < total, real, jnp.zeros_like(real))
                    imag = jnp.where(at < total, imag, jnp.zeros_like(imag))
                left.append(complex_rows(real, imag))
                right.append(held[ids_ref[box, slot] - base].reshape(2 * basis, rhs))
            part = dot(jnp.concatenate(left, axis=1), jnp.concatenate(right, axis=0))
            out_ref[box] += part.reshape(2, basis, rhs)
            return carry

        lax.fori_loop(0, (total + GROUP - 1) // GROUP, group, 0)
        return carry

    lax.fori_loop(0, boxes, one_box, 0)


def near_field(ids, used, rank, blocks, sources, first, before=None):
    boxes, slots, _, basis, _ = blocks.shape
    rhs = sources[0].shape[3]
    count = len(sources)
    begun = before is not None
    anywhere = pl.BlockSpec(memory_space=pl.ANY)
    smem = pl.BlockSpec(memory_space=pltpu.SMEM)
    vmem = pl.BlockSpec(memory_space=pltpu.VMEM)
    return pl.pallas_call(
        functools.partial(near_kernel, first, count, begun),
        in_specs=[smem] * 3 + [anywhere] * (1 + count) + [vmem] * begun,
        out_specs=vmem,
        out_shape=jax.ShapeDtypeStruct((boxes, 2, basis, rhs), F32),
        scratch_shapes=[
            pltpu.VMEM(blocks.shape, BF16),
            pltpu.VMEM((count * boxes, 2, basis, rhs), BF16),
            pltpu.SMEM((slots + 1,), jnp.int32),
            pltpu.SemaphoreType.DMA((boxes + count,)),
        ],
        compiler_params=pltpu.CompilerParams(vmem_limit_bytes=24 * MIB),
        cost_estimate=pl.CostEstimate(
            flops=2 * 10**9, bytes_accessed=8 * MIB, transcendentals=0
        ),
        name="near_first" if not begun else "near_last",
    )(ids, used, rank, in_hbm(blocks), *sources, *([before] if begun else []))


def down_kernel(field_ref, w_ref, rad_ref, near_ref, out_hbm, held, sems):
    boxes, _, points, basis = rad_ref.shape
    rhs = near_ref.shape[3]
    field = field_ref[...].reshape(-1, 2 * rhs)
    field = jnp.concatenate([field, field], axis=0)
    copies = []
    for octant in range(boxes // 2):
        mixed = dot(w_ref[octant], field)
        cos_re, cos_im = mixed[:points, :rhs], mixed[:points, rhs:]
        sin_re, sin_im = mixed[points:, :rhs], mixed[points:, rhs:]
        pairs = (
            (octant, cos_re + sin_im, cos_im - sin_re),
            (boxes - 1 - octant, cos_re - sin_im, cos_im + sin_re),
        )
        for box, real, imag in pairs:
            leaf = jnp.concatenate([real, imag], axis=0).astype(BF16)
            left = complex_rows(rad_ref[box, 0], rad_ref[box, 1])
            far = lax.dot_general(
                left, leaf, (((0,), (0,)), ((), ())), preferred_element_type=F32
            )
            held[box] = near_ref[box] + far.reshape(2, basis, rhs)
            copies.append(pltpu.make_async_copy(held.at[box], out_hbm.at[box], sems.at[box]))
            copies[-1].start()
    for copy in copies:
        copy.wait()


def downward(field, weights, radiation, near):
    boxes = near.shape[0]
    vmem = pl.BlockSpec(memory_space=pltpu.VMEM)
    return pl.pallas_call(
        down_kernel,
        in_specs=[vmem] * 4,
        out_specs=pl.BlockSpec(memory_space=pl.ANY),
        out_shape=jax.ShapeDtypeStruct(near.shape, F32),
        scratch_shapes=[
            pltpu.VMEM(near.shape, F32),
            pltpu.SemaphoreType.DMA((boxes,)),
        ],
        compiler_params=pltpu.CompilerParams(vmem_limit_bytes=16 * MIB),
        cost_estimate=pl.CostEstimate(
            flops=2 * 10**9, bytes_accessed=7 * MIB, transcendentals=0
        ),
        name="downward",
    )(field, weights, radiation, near)


def shift(block, axis, step):
    count = lax.axis_size(axis)
    pairs = [(i, i + step) for i in range(count) if 0 <= i + step < count]
    return lax.ppermute(block, axis, pairs)


def lists_of(partners, vector_ids, pair_count):
    used = jnp.arange(partners.shape[1])[None, :] < pair_count[:, None]
    names = jnp.where(used, partners, NOWHERE)
    return jnp.stack([names, vector_ids], axis=2).reshape(-1, 2)


def far_field(spread, lists, translation, shares, near):
    operator_total, _, theta_band, phi_band = translation.shape
    rank = lax.axis_index("box")
    if shares == lax.axis_size("box"):
        every = ("box", "theta", "phi")
        for_all = lists
        if shares == 2:
            other = lax.ppermute(lists, "box", [(0, 1), (1, 0)])
            for_all = jnp.where(
                rank == 0, jnp.concatenate([lists, other]), jnp.concatenate([other, lists])
            )
        part = theta_band // shares
        table = lax.dynamic_slice_in_dim(translation, rank * part, part, axis=2)
        table = table.reshape(operator_total, -1)
        sources = spread.shape[0]
        base = jnp.zeros((1,), jnp.int32)
        coupling = couplings(for_all, base, table, sources, sources)
        parents = lax.all_to_all(spread, every, split_axis=0, concat_axis=0, tiled=True)
        parents, near = lax.optimization_barrier((parents, near))
        incoming = translate(coupling, [parents])
        return lax.all_to_all(incoming, every, split_axis=0, concat_axis=0, tiled=True), near
    bands = ("theta", "phi")
    per_group = spread.shape[0]
    table = translation.reshape(operator_total, -1)
    base = ((rank - 1) * per_group).astype(jnp.int32).reshape(1)
    coupling = couplings(lists, base, table, per_group, 3 * per_group)
    parents = lax.all_to_all(spread, bands, split_axis=0, concat_axis=0, tiled=True)
    parents, near = lax.optimization_barrier((parents, near))
    sources = [shift(parents, "box", 1), parents, shift(parents, "box", -1)]
    incoming = translate(coupling, sources)
    return lax.all_to_all(incoming, bands, split_axis=0, concat_axis=0, tiled=True), near


def per_device(
    shares,
    up_weights,
    down_weights,
    coeffs,
    near_blocks,
    near_ids,
    near_count,
    radiation,
    partners,
    vector_ids,
    pair_count,
    translation,
):
    every = ("box", "theta", "phi")
    low = shift(coeffs, every, 1)
    high = shift(coeffs, every, -1)
    groups = shares * lax.axis_size("theta") * lax.axis_size("phi")
    spread = upward(coeffs, radiation, up_weights, groups)
    lists = lists_of(partners, vector_ids, pair_count)
    rank = lax.axis_index(every).astype(jnp.int32).reshape(1)
    near = near_field(near_ids, near_count, rank, near_blocks, [low, coeffs], 0)
    field, near = far_field(spread, lists, translation, shares, near)
    near = near_field(near_ids, near_count, rank, near_blocks, [high], 2, near)
    return downward(field, down_weights, radiation, near)


def solution(mesh):
    box_size, theta_size, phi_size = (mesh.shape[axis] for axis in ("box", "theta", "phi"))
    shares = box_size if box_size <= 2 and TU // theta_size % box_size == 0 else 1
    up_weights, down_weights = operators(shares, theta_size, phi_size)
    in_specs = (
        P(),
        P(),
        P(("box", "theta", "phi"), None, None, None),
        P(("box", "theta", "phi"), None, None, None, None),
        P(("box", "theta", "phi"), None),
        P(("box", "theta", "phi")),
        P(("box", "theta", "phi"), None, None, None),
        P("box", None),
        P("box", None),
        P("box"),
        P(None, None, "theta", "phi"),
    )
    out_specs = P(("box", "theta", "phi"), None, None, None)
    mapped = jax.shard_map(
        functools.partial(per_device, shares),
        mesh=mesh,
        in_specs=in_specs,
        out_specs=out_specs,
        check_vma=False,
    )

    def product(*arrays):
        return mapped(jnp.asarray(up_weights), jnp.asarray(down_weights), *arrays)

    return product
```

time: 97.7 us -> 94.9 us (0.971)
  the two profiles are of different devices: /device:TPU:8 before, /device:TPU:0 now
where the time goes in v1:
time: 94.9 us; the launch traced here: 93.6 us
  starting transfers between devices  43.3 us (46%)
  Pallas kernels  24.9 us (26%)
  waiting for transfers between devices  14.8 us (16%)
  local copies, waits for them, and re-layouts  10.3 us (11%)
    all_to_all x1, starting transfers between devices, far_field(): lax.all_to_all(incoming, every, split_axis=0, concat_axis=0, tiled=True)  25.6 us
    pallas_call x2, Pallas kernels, near_field(): pl.pallas_call(functools.partial(near_kernel, first, count, begun), in_sp...  12.7 us
    unnamed x32, local copies, waits for them, and re-layouts  9.71 us
    all_to_all x1, waiting for transfers between devices, far_field(): lax.all_to_all(incoming, every, split_axis=0, concat_axis=0, tiled=True)  7.18 us
    ppermute x2, starting transfers between devices, shift(): return lax.ppermute(block, axis, pairs)  6.43 us
    ppermute x1, starting transfers between devices, far_field(): other = lax.ppermute(lists, 'box', [(0, 1), (1, 0)])  6.38 us
    pallas_call x1, Pallas kernels, upward(): pl.pallas_call(up_kernel, in_specs=[anywhere] * 3, out_specs=pl.BlockSpec...  5.22 us
    all_to_all x1, starting transfers between devices, far_field(): lax.all_to_all(spread, every, split_axis=0, concat_axis=0, tiled=True)  4.9 us
  transfers between devices with their start and end apart: 5, of which 4 were waited for; matrix products, arithmetic and copies ran while one was open for 1% of the time, Pallas kernels for 22%

profile of v1, /device:TPU:0, one launch (start us, length us, event | category | flops | bytes accessed | tf_op | source)
XLA Modules:
  0.0 93.6 jit_solution(16593629873631877)
XLA Ops:
  0.0 5.1 %collective-permute-start.1 = (bf16[8,2,128,256]{3,2,1,0:T(8,128)(2,1)}, bf16[8,2,128,256]{3,2,1,0:T(8,128)(2,1)S(1)}, u32[]{:S(2)}, u32[]{:S(2)}) collective-permute-start(bf16[8,2,128,256]{3,2,1,0:T(8,128)(2,1)} %refs_5_.1), channel_id=1, source_target_pairs={{0,1},{1,2},{2,3},{3,4},{4,5},{5,6},{6,7},{7,8},{8,9},{9,10},{10,1... | collective-permute-start | bytes 3145736 | tf_op jit(solution)/shard_map/ppermute | solution.py:359
  5.2 5.2 %upward.1 = bf16[32,16,512]{2,1,0:T(8,128)(2,1)} custom-call(bf16[8,2,128,256]{3,2,1,0:T(8,128)(2,1)} %refs_5_.1, bf16[8,2,128,128]{3,2,1,0:T(8,128)(2,1)} %rad_ref.1, bf16[512,2048]{1,0:T(8,128)(2,1)} %constant.29.clone.w_hbm), custom_call_target="tpu_custom_call" | custom-call | flops 2000000000 | bytes 4194304 | tf_op jit(solution)/shard_map/upward/pallas_call | solution.py:133
  10.4 0.0 copy-start.9
  10.4 4.9 %all-to-all-start = ((bf16[32,16,512]{2,1,0:T(8,128)(2,1)}), bf16[32,16,512]{2,1,0:T(8,128)(2,1)}, u32[]{:S(2)}, u32[]{:S(2)}) async-start(bf16[32,16,512]{2,1,0:T(8,128)(2,1)} %upward.1), calls=%async_computation | async-start | bytes 1048576 | tf_op jit(solution)/shard_map/all_to_all | solution.py:385
  15.3 1.3 %collective-permute-start.2 = (bf16[8,2,128,256]{3,2,1,0:T(8,128)(2,1)S(1)}, bf16[8,2,128,256]{3,2,1,0:T(8,128)(2,1)}, u32[]{:S(2)}, u32[]{:S(2)}) collective-permute-start(bf16[8,2,128,256]{3,2,1,0:T(8,128)(2,1)S(1)} %copy-done.3), channel_id=1, source_target_pairs={{1,0},{2,1},{3,2},{4,3},{5,4},{6,5},{7,6},{8,7},{9,8},{10,9},{11,1... | collective-permute-start | bytes 3145736 | tf_op jit(solution)/shard_map/ppermute | solution.py:359
  16.6 0.1 stack.10
  16.7 0.1 fusion
  16.8 0.1 stack.9
  16.9 6.4 %collective-permute-start = (s32[256,2]{0,1:T(2,128)S(1)}, s32[256,2]{0,1:T(2,128)S(1)}, u32[]{:S(2)}, u32[]{:S(2)}) collective-permute-start(s32[256,2]{0,1:T(2,128)S(1)} %pad_add_fusion.1), channel_id=1, source_target_pairs={{0,16},{16,0},{1,17},{17,1},{2,18},{18,2},{3,19},{19,3},{4,20},{20... | collective-permute-start | bytes 6152 | tf_op jit(solution)/shard_map/ppermute | solution.py:375
  23.3 0.1 copy.18.table_ref
  23.4 1.4 %collective-permute-done = s32[256,2]{0,1:T(2,128)S(1)} collective-permute-done((s32[256,2]{0,1:T(2,128)S(1)}, s32[256,2]{0,1:T(2,128)S(1)}, u32[]{:S(2)}, u32[]{:S(2)}) %collective-permute-start) | collective-permute-done | bytes 2080 | tf_op jit(solution)/shard_map/ppermute | solution.py:375
  24.9 0.1 copy.17
  25.0 0.1 copy.16
  25.2 1.1 %coupling.1.coupling_ref = bf16[1024,512]{1,0:T(8,128)(2,1)S(1)} custom-call(s32[512,2]{1,0:T(8,128)S(1)} %broadcast_select_fusion.lists_ref, s32[1]{0:T(128)} %constant.11.clone.1.base_ref, bf16[316,32]{1,0:T(8,128)(2,1)S(1)} %copy.18.table_ref), custom_call_target="tpu_custom_call" | custom-call | flops 200000000 | bytes 2097152 | tf_op jit(solution)/shard_map/coupling/pallas_call | solution.py:186
  26.3 0.0 copy-start.6
  26.3 1.0 %copy-done.6 = bf16[1024,512]{1,0:T(8,128)(2,1)} copy-done((bf16[1024,512]{1,0:T(8,128)(2,1)}, bf16[1024,512]{1,0:T(8,128)(2,1)S(1)}, u32[]{:S(2)}) %copy-start.6) | copy-done | bytes 1048600
  27.3 1.7 %collective-permute-done.1.refs_4_ = bf16[8,2,128,256]{3,2,1,0:T(8,128)(2,1)S(1)} collective-permute-done((bf16[8,2,128,256]{3,2,1,0:T(8,128)(2,1)}, bf16[8,2,128,256]{3,2,1,0:T(8,128)(2,1)S(1)}, u32[]{:S(2)}, u32[]{:S(2)}) %collective-permute-start.1) | collective-permute-done | bytes 1048608 | tf_op jit(solution)/shard_map/ppermute | solution.py:359
  29.0 1.0 %copy-done.4 = bf16[8,2,128,256]{3,2,1,0:T(8,128)(2,1)} copy-done((bf16[8,2,128,256]{3,2,1,0:T(8,128)(2,1)}, bf16[8,2,128,256]{3,2,1,0:T(8,128)(2,1)S(1)}, u32[]{:S(2)}) %copy-start.4) | copy-done | bytes 1048600
  29.9 1.2 %copy-done.5 = bf16[8,2,128,256]{3,2,1,0:T(8,128)(2,1)S(1)} copy-done((bf16[8,2,128,256]{3,2,1,0:T(8,128)(2,1)S(1)}, bf16[8,2,128,256]{3,2,1,0:T(8,128)(2,1)}, u32[]{:S(2)}) %copy-start.5) | copy-done | bytes 1048600
  31.2 6.9 %near_first.1.refs_5_ = f32[8,2,128,256]{3,2,1,0:T(8,128)S(1)} custom-call(s32[8,12]{1,0:T(8,128)S(1)} %copy-done.9, s32[8]{0:T(128)S(1)} %copy-done.10, s32[1]{0:T(128)} %bitcast.1.refs_2_, bf16[8,12,2,128,128]{4,3,2,1,0:T(8,128)(2,1)} %refs_3_.3, bf16[8,2,128,256]{3,2,1,0:T(8,128)(2,1)S(1)} %copy-done.5, bf16[8,2,128,256]{3,2,1,0:T(8,128)(2,1)S(1)} %copy-done.3), custom_call_target="tpu_custom_call" | custom-call | flops 2000000000 | bytes 8388608 | tf_op jit(solution)/shard_map/near_first/pallas_call | solution.py:290
  38.0 4.5 %all-to-all-done.refs_0_ = bf16[32,16,512]{2,1,0:T(8,128)(2,1)} async-done(((bf16[32,16,512]{2,1,0:T(8,128)(2,1)}), bf16[32,16,512]{2,1,0:T(8,128)(2,1)}, u32[]{:S(2)}, u32[]{:S(2)}) %all-to-all-start) | async-done | bytes 524320 | tf_op jit(solution)/shard_map/all_to_all | solution.py:385
  42.6 1.2 %copy-done.7 = bf16[1024,512]{1,0:T(8,128)(2,1)S(1)} copy-done((bf16[1024,512]{1,0:T(8,128)(2,1)S(1)}, bf16[1024,512]{1,0:T(8,128)(2,1)}, u32[]{:S(2)}) %copy-start.7) | copy-done | bytes 1048600
  43.8 1.7 %translate.1 = bf16[32,16,512]{2,1,0:T(8,128)(2,1)S(1)} custom-call(bf16[1024,512]{1,0:T(8,128)(2,1)S(1)} %copy-done.7, bf16[32,16,512]{2,1,0:T(8,128)(2,1)} %all-to-all-done.refs_0_), custom_call_target="tpu_custom_call" | custom-call | flops 1000000000 | bytes 2097152 | tf_op jit(solution)/shard_map/translate/pallas_call | solution.py:219
  45.5 0.8 copy-done.8
  46.3 25.6 %all-to-all-start.1 = ((bf16[32,16,512]{2,1,0:T(8,128)(2,1)}), bf16[32,16,512]{2,1,0:T(8,128)(2,1)}, u32[]{:S(2)}, u32[]{:S(2)}) async-start(bf16[32,16,512]{2,1,0:T(8,128)(2,1)} %copy-done.8), calls=%async_computation.1 | async-start | bytes 1048576 | tf_op jit(solution)/shard_map/all_to_all | solution.py:388
  71.9 0.0 copy-start.11
  71.9 5.8 %near_last.1.near_ref = f32[8,2,128,256]{3,2,1,0:T(8,128)S(1)} custom-call(s32[8,12]{1,0:T(8,128)S(1)} %copy-done.9, s32[8]{0:T(128)S(1)} %copy-done.10, s32[1]{0:T(128)} %bitcast.1.refs_2_, bf16[8,12,2,128,128]{4,3,2,1,0:T(8,128)(2,1)} %refs_3_.3, bf16[8,2,128,256]{3,2,1,0:T(8,128)(2,1)} %collective-permute-done.2.refs_4_, ...), custom_call_target="tpu_custom_call" | custom-call | flops 2000000000 | bytes 8388608 | tf_op jit(solution)/shard_map/near_last/pallas_call | solution.py:290
  77.8 1.3 %copy-done.1 = f32[8,2,128,256]{3,2,1,0:T(8,128)} copy-done((f32[8,2,128,256]{3,2,1,0:T(8,128)}, f32[8,2,128,256]{3,2,1,0:T(8,128)S(1)}, u32[]{:S(2)}) %copy-start.1) | copy-done | bytes 2097176
  79.1 7.2 %all-to-all-done.1.field_ref = bf16[32,16,512]{2,1,0:T(8,128)(2,1)} async-done(((bf16[32,16,512]{2,1,0:T(8,128)(2,1)}), bf16[32,16,512]{2,1,0:T(8,128)(2,1)}, u32[]{:S(2)}, u32[]{:S(2)}) %all-to-all-start.1) | async-done | bytes 524320 | tf_op jit(solution)/shard_map/all_to_all | solution.py:388
  86.3 1.6 %copy-done.2 = f32[8,2,128,256]{3,2,1,0:T(8,128)S(1)} copy-done((f32[8,2,128,256]{3,2,1,0:T(8,128)S(1)}, f32[8,2,128,256]{3,2,1,0:T(8,128)}, u32[]{:S(2)}) %copy-start.2) | copy-done | bytes 2097176
  87.9 1.6 %copy-done.12 = bf16[4,256,1024]{2,1,0:T(8,128)(2,1)S(1)} copy-done((bf16[4,256,1024]{2,1,0:T(8,128)(2,1)S(1)}, bf16[4,256,1024]{2,1,0:T(8,128)(2,1)}, u32[]{:S(2)}) %copy-start.12) | copy-done | bytes 2097176
  89.5 4.1 %downward.1 = f32[8,2,128,256]{3,2,1,0:T(8,128)} custom-call(bf16[32,16,512]{2,1,0:T(8,128)(2,1)} %all-to-all-done.1.field_ref, bf16[4,256,1024]{2,1,0:T(8,128)(2,1)S(1)} %copy-done.12, bf16[8,2,128,128]{3,2,1,0:T(8,128)(2,1)S(1)} %copy-done.11, f32[8,2,128,256]{3,2,1,0:T(8,128)S(1)} %copy-done.2), custom_call_target="tpu_custom_call" | custom-call | flops 2000000000 | bytes 7340032 | tf_op jit(solution)/shard_map/downward/pallas_call | solution.py:339
  (26 shorter events, 0.1 us)
Async XLA Ops:
  0.0 23.3 %copy-start = (bf16[316,2,4,8]{0,3,2,1:T(8,128)(2,1)S(1)}, bf16[316,2,4,8]{0,3,2,1:T(8,128)(2,1)}, u32[]{:S(2)}) copy-start(bf16[316,2,4,8]{0,3,2,1:T(8,128)(2,1)} %param.19) | copy-start | bytes 121348
  0.0 15.3 %copy-start.3 = (bf16[8,2,128,256]{3,2,1,0:T(8,128)(2,1)S(1)}, bf16[8,2,128,256]{3,2,1,0:T(8,128)(2,1)}, u32[]{:S(2)}) copy-start(bf16[8,2,128,256]{3,2,1,0:T(8,128)(2,1)} %refs_5_.1) | copy-start | bytes 3145732
  0.0 16.6 %copy-start.13 = (s32[16,16]{1,0:T(8,128)S(1)}, s32[16,16]{1,0:T(8,128)}, u32[]{:S(2)}) copy-start(s32[16,16]{1,0:T(8,128)} %param.17) | copy-start | bytes 3076
  0.0 16.7 %copy-start.15 = (s32[16]{0:T(128)S(1)}, s32[16]{0:T(128)}, u32[]{:S(2)}) copy-start(s32[16]{0:T(128)} %param.18) | copy-start | bytes 196
  0.0 16.7 %copy-start.14 = (s32[16,16]{1,0:T(8,128)S(1)}, s32[16,16]{1,0:T(8,128)}, u32[]{:S(2)}) copy-start(s32[16,16]{1,0:T(8,128)} %param.16) | copy-start | bytes 3076
  0.0 28.9 %collective-permute-start.1 = (bf16[8,2,128,256]{3,2,1,0:T(8,128)(2,1)}, bf16[8,2,128,256]{3,2,1,0:T(8,128)(2,1)S(1)}, u32[]{:S(2)}, u32[]{:S(2)}) collective-permute-start(bf16[8,2,128,256]{3,2,1,0:T(8,128)(2,1)} %refs_5_.1), channel_id=1, source_target_pairs={{0,1},{1,2},{2,3},{3,4},{4,5},{5,6},{6,7},{7,8},{8,9},{9,10},{10,1... | collective-permute-start | bytes 3145736 | tf_op jit(solution)/shard_map/ppermute | solution.py:359
  10.4 19.5 %copy-start.9 = (s32[8,12]{1,0:T(8,128)S(1)}, s32[8,12]{1,0:T(8,128)}, u32[]{:S(2)}) copy-start(s32[8,12]{1,0:T(8,128)} %refs_0_.3) | copy-start | bytes 1156
  10.4 19.5 %copy-start.10 = (s32[8]{0:T(128)S(1)}, s32[8]{0:T(128)}, u32[]{:S(2)}) copy-start(s32[8]{0:T(128)} %refs_1_.3) | copy-start | bytes 100
  10.4 32.1 %all-to-all-start = ((bf16[32,16,512]{2,1,0:T(8,128)(2,1)}), bf16[32,16,512]{2,1,0:T(8,128)(2,1)}, u32[]{:S(2)}, u32[]{:S(2)}) async-start(bf16[32,16,512]{2,1,0:T(8,128)(2,1)} %upward.1), calls=%async_computation | async-start | bytes 1048576 | tf_op jit(solution)/shard_map/all_to_all | solution.py:385
  15.3 56.6 %collective-permute-start.2 = (bf16[8,2,128,256]{3,2,1,0:T(8,128)(2,1)S(1)}, bf16[8,2,128,256]{3,2,1,0:T(8,128)(2,1)}, u32[]{:S(2)}, u32[]{:S(2)}) collective-permute-start(bf16[8,2,128,256]{3,2,1,0:T(8,128)(2,1)S(1)} %copy-done.3), channel_id=1, source_target_pairs={{1,0},{2,1},{3,2},{4,3},{5,4},{6,5},{7,6},{8,7},{9,8},{10,9},{11,1... | collective-permute-start | bytes 3145736 | tf_op jit(solution)/shard_map/ppermute | solution.py:359
  16.9 7.9 %collective-permute-start = (s32[256,2]{0,1:T(2,128)S(1)}, s32[256,2]{0,1:T(2,128)S(1)}, u32[]{:S(2)}, u32[]{:S(2)}) collective-permute-start(s32[256,2]{0,1:T(2,128)S(1)} %pad_add_fusion.1), channel_id=1, source_target_pairs={{0,16},{16,0},{1,17},{17,1},{2,18},{18,2},{3,19},{19,3},{4,20},{20... | collective-permute-start | bytes 6152 | tf_op jit(solution)/shard_map/ppermute | solution.py:375
  26.3 1.0 %copy-start.6 = (bf16[1024,512]{1,0:T(8,128)(2,1)}, bf16[1024,512]{1,0:T(8,128)(2,1)S(1)}, u32[]{:S(2)}) copy-start(bf16[1024,512]{1,0:T(8,128)(2,1)S(1)} %coupling.1.coupling_ref) | copy-start | bytes 3145732
  29.0 1.0 %copy-start.4 = (bf16[8,2,128,256]{3,2,1,0:T(8,128)(2,1)}, bf16[8,2,128,256]{3,2,1,0:T(8,128)(2,1)S(1)}, u32[]{:S(2)}) copy-start(bf16[8,2,128,256]{3,2,1,0:T(8,128)(2,1)S(1)} %collective-permute-done.1.refs_4_) | copy-start | bytes 3145732
  29.9 1.2 %copy-start.5 = (bf16[8,2,128,256]{3,2,1,0:T(8,128)(2,1)S(1)}, bf16[8,2,128,256]{3,2,1,0:T(8,128)(2,1)}, u32[]{:S(2)}) copy-start(bf16[8,2,128,256]{3,2,1,0:T(8,128)(2,1)} %copy-done.4) | copy-start | bytes 3145732
  42.6 1.2 %copy-start.7 = (bf16[1024,512]{1,0:T(8,128)(2,1)S(1)}, bf16[1024,512]{1,0:T(8,128)(2,1)}, u32[]{:S(2)}) copy-start(bf16[1024,512]{1,0:T(8,128)(2,1)} %copy-done.6) | copy-start | bytes 3145732
  45.5 0.8 copy-start.8
  46.3 39.9 %all-to-all-start.1 = ((bf16[32,16,512]{2,1,0:T(8,128)(2,1)}), bf16[32,16,512]{2,1,0:T(8,128)(2,1)}, u32[]{:S(2)}, u32[]{:S(2)}) async-start(bf16[32,16,512]{2,1,0:T(8,128)(2,1)} %copy-done.8), calls=%async_computation.1 | async-start | bytes 1048576 | tf_op jit(solution)/shard_map/all_to_all | solution.py:388
  71.9 14.4 %copy-start.11 = (bf16[8,2,128,128]{3,2,1,0:T(8,128)(2,1)S(1)}, bf16[8,2,128,128]{3,2,1,0:T(8,128)(2,1)}, u32[]{:S(2)}) copy-start(bf16[8,2,128,128]{3,2,1,0:T(8,128)(2,1)} %rad_ref.1) | copy-start | bytes 1572868
  77.8 1.3 %copy-start.1 = (f32[8,2,128,256]{3,2,1,0:T(8,128)}, f32[8,2,128,256]{3,2,1,0:T(8,128)S(1)}, u32[]{:S(2)}) copy-start(f32[8,2,128,256]{3,2,1,0:T(8,128)S(1)} %near_last.1.near_ref) | copy-start | bytes 6291460
  86.3 1.6 %copy-start.2 = (f32[8,2,128,256]{3,2,1,0:T(8,128)S(1)}, f32[8,2,128,256]{3,2,1,0:T(8,128)}, u32[]{:S(2)}) copy-start(f32[8,2,128,256]{3,2,1,0:T(8,128)} %copy-done.1) | copy-start | bytes 6291460
  87.9 1.6 %copy-start.12 = (bf16[4,256,1024]{2,1,0:T(8,128)(2,1)S(1)}, bf16[4,256,1024]{2,1,0:T(8,128)(2,1)}, u32[]{:S(2)}) copy-start(bf16[4,256,1024]{2,1,0:T(8,128)(2,1)} %constant.30.clone.w_ref) | copy-start | bytes 6291460

commit v2 on v1

v2 whole, which is shorter than its diff:
```python
import functools
import math

import jax
import jax.numpy as jnp
import ml_dtypes
import numpy as np
from jax import lax
from jax.experimental import pallas as pl
from jax.experimental.pallas import tpu as pltpu
from jax.sharding import PartitionSpec as P

TL = 8
PL = 16
TU = 16
PU = 32

WEIGHT_UP = (-0.0546875, 0.8203125, 0.2734375, -0.0390625)
WEIGHT_DOWN = (-0.0390625, 0.2734375, 0.8203125, -0.0546875)
PHASE_SCALE = 1.3

F32 = jnp.float32
BF16 = jnp.bfloat16
MIB = 2**20
GROUP = 4
NOWHERE = -(2**20)


def lagrange(rows, columns, wrap):
    matrix = np.zeros((rows, columns))
    for row in range(rows):
        weights = WEIGHT_UP if row % 2 else WEIGHT_DOWN
        for order in range(4):
            node = row // 2 + row % 2 - 2 + order
            node = node % columns if wrap else min(max(node, 0), columns - 1)
            matrix[row, node] += weights[order]
    return matrix


def split_weights(matrix):
    high = matrix.astype(ml_dtypes.bfloat16)
    low = (matrix - high.astype(np.float64)).astype(ml_dtypes.bfloat16)
    return high, low


def operators(shares, theta_size, phi_size):
    theta_part = TU // theta_size // shares
    order = np.arange(TU * PU).reshape(theta_size, shares, theta_part, phi_size, PU // phi_size)
    order = order.transpose(1, 0, 3, 2, 4).reshape(-1)
    interp = np.kron(lagrange(TU, TL, False), lagrange(PU, PL, True))
    theta = math.pi * (np.arange(TU) + 0.5) / TU
    azimuth = 2.0 * math.pi * (np.arange(PU) + 0.5) / PU
    up, down = [], []
    for octant in range(4):
        sign_x = 2 * (octant % 2) - 1
        sign_y = 2 * (octant // 2 % 2) - 1
        sign_z = 2 * (octant // 4) - 1
        angle = PHASE_SCALE * (
            sign_x * np.sin(theta)[:, None] * np.cos(azimuth)[None]
            + sign_y * np.sin(theta)[:, None] * np.sin(azimuth)[None]
            + sign_z * np.cos(theta)[:, None]
        ).reshape(-1, 1)
        cos_high, cos_low = split_weights((np.cos(angle) * interp)[order])
        sin_high, sin_low = split_weights((np.sin(angle) * interp)[order])
        high = np.concatenate([cos_high, sin_high], axis=1)
        low = np.concatenate([cos_low, sin_low], axis=1)
        up.append(np.concatenate([high, low], axis=0))
        down.append(np.concatenate([cos_high.T, sin_high.T, cos_low.T, sin_low.T], axis=0))
    return np.concatenate(up, axis=1), np.stack(down)


def dot(a, b):
    return jnp.dot(a, b, preferred_element_type=F32)


def complex_rows(real, imag):
    return jnp.concatenate(
        [
            jnp.concatenate([real, -imag], axis=1),
            jnp.concatenate([imag, real], axis=1),
        ],
        axis=0,
    )


def up_kernel(x_hbm, rad_hbm, w_hbm, out_ref, x_ref, rad_ref, w_ref, right, sems):
    boxes, _, basis, rhs = x_ref.shape
    points = rad_ref.shape[2]
    copies = [
        pltpu.make_async_copy(source, target, sems.at[place])
        for place, (source, target) in enumerate(
            ((x_hbm, x_ref), (rad_hbm, rad_ref), (w_hbm, w_ref))
        )
    ]
    for copy in copies:
        copy.start()
    copies[0].wait()
    copies[1].wait()
    half = boxes // 2
    for octant in range(boxes):
        left = complex_rows(rad_ref[octant, 0], rad_ref[octant, 1])
        pattern = dot(left, x_ref[octant].reshape(2 * basis, rhs)).astype(BF16)
        real, imag = pattern[:points], pattern[points:]
        straight = jnp.concatenate([real, imag], axis=1)
        if octant < half:
            swapped = jnp.concatenate([-imag, real], axis=1)
        else:
            swapped = jnp.concatenate([imag, -real], axis=1)
        place = octant if octant < half else boxes - 1 - octant
        start = 2 * place * points
        right[octant // half, start : start + points] = straight
        right[octant // half, start + points : start + 2 * points] = swapped
    copies[2].wait()
    total = dot(w_ref[...], right[0]) + dot(w_ref[...], right[1])
    samples = total.shape[0] // 2
    total = total[:samples] + total[samples:]
    out_ref[...] = total.astype(BF16).reshape(out_ref.shape)


def upward(coeffs, radiation, weights, groups):
    boxes, _, basis, rhs = coeffs.shape
    rows, columns = weights.shape
    samples = rows // 2
    hbm = pl.BlockSpec(memory_space=pltpu.HBM)
    return pl.pallas_call(
        up_kernel,
        in_specs=[hbm] * 3,
        out_specs=pl.BlockSpec(memory_space=pltpu.VMEM),
        out_shape=jax.ShapeDtypeStruct((groups, samples // groups, 2 * rhs), BF16),
        scratch_shapes=[
            pltpu.VMEM(coeffs.shape, BF16),
            pltpu.VMEM(radiation.shape, BF16),
            pltpu.VMEM(weights.shape, BF16),
            pltpu.VMEM((2, columns, 2 * rhs), BF16),
            pltpu.SemaphoreType.DMA((3,)),
        ],
        compiler_params=pltpu.CompilerParams(vmem_limit_bytes=32 * MIB),
        cost_estimate=pl.CostEstimate(
            flops=2 * 10**9, bytes_accessed=4 * MIB, transcendentals=0
        ),
        name="upward",
    )(coeffs, radiation, weights)


def coupling_kernel(lists_ref, base_ref, table_ref, out_ref):
    rows = lists_ref.shape[0]
    samples = table_ref.shape[1] // 2
    _, targets, columns = out_ref.shape
    slots = rows // targets
    selector = (
        lax.broadcasted_iota(jnp.int32, (rows, table_ref.shape[0]), 1) == lists_ref[:, 1:2]
    )
    chosen = dot(selector.astype(BF16), table_ref[...]).astype(BF16)
    wide = lax.broadcasted_iota(jnp.int32, (rows, columns), 1) // samples
    match = wide + base_ref[0] == lists_ref[:, 0:1]
    spread = lax.broadcasted_iota(jnp.int32, (samples, columns), 0) == (
        lax.broadcasted_iota(jnp.int32, (samples, columns), 1) % samples
    )
    gather = (
        lax.broadcasted_iota(jnp.int32, (targets, rows), 1) // slots
        == lax.broadcasted_iota(jnp.int32, (targets, rows), 0)
    ).astype(BF16)
    tile = spread.astype(BF16)
    for part in range(2):
        lines = dot(chosen[:, part * samples : (part + 1) * samples], tile)
        out_ref[part] = dot(gather, jnp.where(match, lines, 0.0).astype(BF16))


def couplings(lists, base, table, targets, names):
    shape = (2, targets, names * (table.shape[1] // 2))
    vmem = pl.BlockSpec(memory_space=pltpu.VMEM)
    return pl.pallas_call(
        coupling_kernel,
        in_specs=[vmem, pl.BlockSpec(memory_space=pltpu.SMEM), vmem],
        out_specs=vmem,
        out_shape=jax.ShapeDtypeStruct(shape, F32),
        compiler_params=pltpu.CompilerParams(vmem_limit_bytes=16 * MIB),
        cost_estimate=pl.CostEstimate(
            flops=2 * 10**8, bytes_accessed=2 * 2**20, transcendentals=0
        ),
        name="coupling",
    )(lists, base, table)


def translate_kernel(lines_hbm, *refs):
    count = (len(refs) - 5) // 2
    sources, out_hbm = refs[:count], refs[count]
    held, lines, matrix, result, sems = refs[count + 1 :][:count], *refs[2 * count + 1 :]
    targets, samples, width = result.shape
    rhs = width // 2
    copies = [
        pltpu.make_async_copy(source, target, sems.at[place])
        for place, (source, target) in enumerate(zip((lines_hbm, *sources), (lines, *held)))
    ]
    for copy in copies:
        copy.start()
    copies[0].wait()
    columns = matrix.shape[1]
    row = lax.broadcasted_iota(jnp.int32, (samples, columns), 0)
    diagonal = row == lax.broadcasted_iota(jnp.int32, (samples, columns), 1) % samples
    for part in range(2):
        for target in range(targets):
            line = jnp.broadcast_to(lines[part, target : target + 1], diagonal.shape)
            start = (part * targets + target) * samples
            matrix[start : start + samples] = jnp.where(diagonal, line, 0.0).astype(BF16)
    total = None
    start = 0
    for place, source in enumerate(held):
        copies[1 + place].wait()
        stop = start + source.shape[0] * samples
        part = dot(matrix[:, start:stop], source[...].reshape(stop - start, width))
        total = part if total is None else total + part
        start = stop
    half = targets * samples
    real = total[:half, :rhs] - total[half:, rhs:]
    imag = total[:half, rhs:] + total[half:, :rhs]
    result[...] = jnp.concatenate([real, imag], axis=1).astype(BF16).reshape(result.shape)
    pltpu.sync_copy(result, out_hbm)


def translate(lines, sources):
    _, samples, width = sources[0].shape
    _, targets, columns = lines.shape
    shape = (targets, samples, width)
    hbm = pl.BlockSpec(memory_space=pltpu.HBM)
    return pl.pallas_call(
        translate_kernel,
        in_specs=[hbm] * (1 + len(sources)),
        out_specs=hbm,
        out_shape=jax.ShapeDtypeStruct(shape, BF16),
        scratch_shapes=[
            *[pltpu.VMEM(source.shape, BF16) for source in sources],
            pltpu.VMEM(lines.shape, F32),
            pltpu.VMEM((2 * targets * samples, columns), BF16),
            pltpu.VMEM(shape, BF16),
            pltpu.SemaphoreType.DMA((1 + len(sources),)),
        ],
        compiler_params=pltpu.CompilerParams(vmem_limit_bytes=24 * MIB),
        cost_estimate=pl.CostEstimate(
            flops=10**9, bytes_accessed=2 * MIB, transcendentals=0
        ),
        name="translate",
    )(lines, *sources)


def near_kernel(first, count, begun, *refs):
    ids_ref, used_ref, rank_ref, blocks_hbm = refs[:4]
    sources = refs[4 : 4 + count]
    out_hbm, blocks, held, total_ref, listed, sems = refs[4 + count + begun :]
    boxes, slots, _, basis, _ = blocks.shape
    rhs = held.shape[3]
    base = (rank_ref[0] - 1 + first) * boxes
    source_copies = [
        pltpu.make_async_copy(source, held.at[pl.ds(place * boxes, boxes)], sems.at[boxes + place])
        for place, source in enumerate(sources)
    ]

    def block_copy(box):
        return pltpu.make_async_copy(blocks_hbm.at[box], blocks.at[box], sems.at[box])

    def result_copy(box, inward):
        place = boxes + count + box
        if inward:
            return pltpu.make_async_copy(refs[4 + count].at[box], total_ref.at[box], sems.at[place])
        return pltpu.make_async_copy(total_ref.at[box], out_hbm.at[box], sems.at[place])

    for copy in source_copies:
        copy.start()
    for box in range(boxes):
        block_copy(box).start()
        if begun:
            result_copy(box, True).start()
    for copy in source_copies:
        copy.wait()

    def one_box(box, carry):
        total = jnp.int32(0)
        used = used_ref[box]
        for slot in range(slots):
            place = ids_ref[box, slot] - base
            listed[total] = jnp.int32(slot)
            wanted = (slot < used) & (place >= 0) & (place < count * boxes)
            total += wanted.astype(jnp.int32)
        block_copy(box).wait()
        if begun:
            result_copy(box, True).wait()
        else:
            total_ref[box] = jnp.zeros(total_ref.shape[1:], F32)

        def group(index, carry):
            left, right = [], []
            for step in range(GROUP):
                at = index * GROUP + step
                slot = listed[jnp.minimum(at, total - 1)]
                real, imag = blocks[box, slot, 0], blocks[box, slot, 1]
                if step:
                    real = jnp.where(at < total, real, jnp.zeros_like(real))
                    imag = jnp.where(at < total, imag, jnp.zeros_like(imag))
                left.append(complex_rows(real, imag))
                right.append(held[ids_ref[box, slot] - base].reshape(2 * basis, rhs))
            part = dot(jnp.concatenate(left, axis=1), jnp.concatenate(right, axis=0))
            total_ref[box] += part.reshape(2, basis, rhs)
            return carry

        lax.fori_loop(0, (total + GROUP - 1) // GROUP, group, 0)
        result_copy(box, False).start()
        return carry

    lax.fori_loop(0, boxes, one_box, 0)
    for box in range(boxes):
        result_copy(box, False).wait()


def near_field(ids, used, rank, blocks, sources, first, before=None):
    boxes, slots, _, basis, _ = blocks.shape
    rhs = sources[0].shape[3]
    count = len(sources)
    begun = before is not None
    hbm = pl.BlockSpec(memory_space=pltpu.HBM)
    smem = pl.BlockSpec(memory_space=pltpu.SMEM)
    return pl.pallas_call(
        functools.partial(near_kernel, first, count, begun),
        in_specs=[smem] * 3 + [hbm] * (1 + count + begun),
        out_specs=hbm,
        out_shape=jax.ShapeDtypeStruct((boxes, 2, basis, rhs), F32),
        scratch_shapes=[
            pltpu.VMEM(blocks.shape, BF16),
            pltpu.VMEM((count * boxes, 2, basis, rhs), BF16),
            pltpu.VMEM((boxes, 2, basis, rhs), F32),
            pltpu.SMEM((slots + 1,), jnp.int32),
            pltpu.SemaphoreType.DMA((2 * boxes + count,)),
        ],
        compiler_params=pltpu.CompilerParams(vmem_limit_bytes=24 * MIB),
        cost_estimate=pl.CostEstimate(
            flops=10**11 if begun else 2 * 10**9, bytes_accessed=8 * MIB, transcendentals=0
        ),
        name="near_last" if begun else "near_first",
    )(ids, used, rank, blocks, *sources, *([before] if begun else []))


def adjoint_kernel(rad_ref, out_ref):
    for box in range(rad_ref.shape[0]):
        out_ref[box] = complex_rows(rad_ref[box, 0], rad_ref[box, 1]).T


def adjoint(radiation):
    boxes, _, points, basis = radiation.shape
    return pl.pallas_call(
        adjoint_kernel,
        out_shape=jax.ShapeDtypeStruct((boxes, 2 * basis, 2 * points), BF16),
        cost_estimate=pl.CostEstimate(
            flops=10**6, bytes_accessed=2 * MIB, transcendentals=0
        ),
        name="adjoint",
    )(radiation)


def down_kernel(field_hbm, w_hbm, adjoint_hbm, near_hbm, out_hbm, field, w, left, held, sems):
    boxes, width, _ = left.shape
    points = width // 2
    samples = w.shape[2]
    basis, rhs = held.shape[2], held.shape[3]
    half = boxes // 2
    field_copy = pltpu.make_async_copy(field_hbm, field, sems.at[0])
    w_copies, left_copies, near_copies, out_copies = [], [], [], []
    for pair in range(half):
        w_copies.append(pltpu.make_async_copy(w_hbm.at[pair], w.at[pair], sems.at[1 + pair]))
    for box in range(boxes):
        places = [1 + half + turn * boxes + box for turn in range(3)]
        left_copies.append(
            pltpu.make_async_copy(adjoint_hbm.at[box], left.at[box], sems.at[places[0]])
        )
        near_copies.append(
            pltpu.make_async_copy(near_hbm.at[box], held.at[box], sems.at[places[1]])
        )
        out_copies.append(
            pltpu.make_async_copy(held.at[box], out_hbm.at[box], sems.at[places[2]])
        )
    field_copy.start()
    for pair in range(half):
        w_copies[pair].start()
    for pair in range(half):
        for box in (pair, boxes - 1 - pair):
            left_copies[box].start()
            near_copies[box].start()
    field_copy.wait()
    for first in range(0, half, 2):
        for pair in (first, first + 1):
            w_copies[pair].wait()
        rows = w.shape[1]
        mixed = dot(
            w[first : first + 2].reshape(2 * rows, samples), field[...].reshape(samples, 2 * rhs)
        )
        for pair in (first, first + 1):
            part = mixed[(pair - first) * rows : (pair - first + 1) * rows]
            part = part[: rows // 2] + part[rows // 2 :]
            cos_re, cos_im = part[:points, :rhs], part[:points, rhs:]
            sin_re, sin_im = part[points:, :rhs], part[points:, rhs:]
            leaves = (
                (pair, cos_re + sin_im, cos_im - sin_re),
                (boxes - 1 - pair, cos_re - sin_im, cos_im + sin_re),
            )
            for box, real, imag in leaves:
                leaf = jnp.concatenate([real, imag], axis=0).astype(BF16)
                left_copies[box].wait()
                far = dot(left[box], leaf)
                near_copies[box].wait()
                held[box] += far.reshape(2, basis, rhs)
                out_copies[box].start()
    for copy in out_copies:
        copy.wait()


def downward(field, weights, radiation_adjoint, near):
    boxes = near.shape[0]
    hbm = pl.BlockSpec(memory_space=pltpu.HBM)
    return pl.pallas_call(
        down_kernel,
        in_specs=[hbm] * 4,
        out_specs=hbm,
        out_shape=jax.ShapeDtypeStruct(near.shape, F32),
        scratch_shapes=[
            pltpu.VMEM(field.shape, BF16),
            pltpu.VMEM(weights.shape, BF16),
            pltpu.VMEM(radiation_adjoint.shape, BF16),
            pltpu.VMEM(near.shape, F32),
            pltpu.SemaphoreType.DMA((1 + boxes // 2 + 3 * boxes,)),
        ],
        compiler_params=pltpu.CompilerParams(vmem_limit_bytes=32 * MIB),
        cost_estimate=pl.CostEstimate(
            flops=2 * 10**9, bytes_accessed=7 * MIB, transcendentals=0
        ),
        name="downward",
    )(field, weights, radiation_adjoint, near)


def shift(block, axis, step):
    count = lax.axis_size(axis)
    pairs = [(i, i + step) for i in range(count) if 0 <= i + step < count]
    return lax.ppermute(block, axis, pairs)


def lists_of(partners, vector_ids, pair_count):
    used = jnp.arange(partners.shape[1])[None, :] < pair_count[:, None]
    names = jnp.where(used, partners, NOWHERE)
    return jnp.stack([names, vector_ids], axis=2).reshape(-1, 2)


def parent_bands(spread, shares):
    axes = ("box", "theta", "phi") if shares == lax.axis_size("box") else ("theta", "phi")
    return lax.all_to_all(spread, axes, split_axis=0, concat_axis=0, tiled=True)


def translation_lines(lists, translation, shares, per_group):
    operator_total, _, theta_band, phi_band = translation.shape
    rank = lax.axis_index("box")
    if shares < lax.axis_size("box"):
        table = translation.reshape(operator_total, -1)
        base = ((rank - 1) * per_group).astype(jnp.int32).reshape(1)
        return couplings(lists, base, table, per_group, 3 * per_group)
    if shares == 2:
        other = lax.ppermute(lists, "box", [(0, 1), (1, 0)])
        lists = jnp.where(
            rank == 0, jnp.concatenate([lists, other]), jnp.concatenate([other, lists])
        )
    part = theta_band // shares
    table = lax.dynamic_slice_in_dim(translation, rank * part, part, axis=2)
    table = table.reshape(operator_total, -1)
    total = shares * per_group
    return couplings(lists, jnp.zeros((1,), jnp.int32), table, total, total)


def per_device(
    shares,
    up_weights,
    down_weights,
    coeffs,
    near_blocks,
    near_ids,
    near_count,
    radiation,
    partners,
    vector_ids,
    pair_count,
    translation,
):
    every = ("box", "theta", "phi")
    per_group = lax.axis_size("theta") * lax.axis_size("phi")
    rank = lax.axis_index(every).astype(jnp.int32).reshape(1)
    low = shift(coeffs, every, 1)
    spread = upward(coeffs, radiation, up_weights, shares * per_group)
    radiation_adjoint = adjoint(radiation)
    lists = lists_of(partners, vector_ids, pair_count)
    lines = translation_lines(lists, translation, shares, per_group)
    near = near_field(near_ids, near_count, rank, near_blocks, [low, coeffs], 0)
    parents = parent_bands(spread, shares)
    parents, near, late = lax.optimization_barrier((parents, near, coeffs))
    high = shift(late, every, -1)
    sources = [parents]
    if shares < lax.axis_size("box"):
        sources = [shift(parents, "box", 1), parents, shift(parents, "box", -1)]
    incoming = translate(lines, sources)
    field = parent_bands(incoming, shares)
    near = near_field(near_ids, near_count, rank, near_blocks, [high], 2, near)
    return downward(field, down_weights, radiation_adjoint, near)


def solution(mesh):
    box_size, theta_size, phi_size = (mesh.shape[axis] for axis in ("box", "theta", "phi"))
    shares = box_size if box_size <= 2 and TU // theta_size % box_size == 0 else 1
    up_weights, down_weights = operators(shares, theta_size, phi_size)
    in_specs = (
        P(),
        P(),
        P(("box", "theta", "phi"), None, None, None),
        P(("box", "theta", "phi"), None, None, None, None),
        P(("box", "theta", "phi"), None),
        P(("box", "theta", "phi")),
        P(("box", "theta", "phi"), None, None, None),
        P("box", None),
        P("box", None),
        P("box"),
        P(None, None, "theta", "phi"),
    )
    out_specs = P(("box", "theta", "phi"), None, None, None)
    mapped = jax.shard_map(
        functools.partial(per_device, shares),
        mesh=mesh,
        in_specs=in_specs,
        out_specs=out_specs,
        check_vma=False,
    )

    def product(*arrays):
        return mapped(jnp.asarray(up_weights), jnp.asarray(down_weights), *arrays)

    return product
```

time: 94.9 us -> 94.3 us (level)
  the two profiles are of different devices: /device:TPU:0 before, /device:TPU:10 now
where the time goes in v2:
time: 94.3 us; the launch traced here: 92.8 us
  waiting for transfers between devices  28.9 us (31%)
  Pallas kernels  26.9 us (29%)
  local copies, waits for them, and re-layouts  18.2 us (19%)
  starting transfers between devices  17.5 us (19%)
  other arithmetic  1.09 us (1%)
    ppermute x2, waiting for transfers between devices, shift(): return lax.ppermute(block, axis, pairs)  27.7 us
    unnamed x38, local copies, waits for them, and re-layouts  16.9 us
    pallas_call x2, Pallas kernels, near_field(): pl.pallas_call(functools.partial(near_kernel, first, count, begun), in_sp...  11.6 us
    all_to_all x2, starting transfers between devices, parent_bands(): return lax.all_to_all(spread, axes, split_axis=0, concat_axis=0, tiled=True)  8.75 us
    ppermute x2, starting transfers between devices, shift(): return lax.ppermute(block, axis, pairs)  8.66 us
    pallas_call x1, Pallas kernels, downward(): pl.pallas_call(down_kernel, in_specs=[hbm] * 4, out_specs=hbm, out_shape=...  6.05 us
    pallas_call x1, Pallas kernels, upward(): pl.pallas_call(up_kernel, in_specs=[hbm] * 3, out_specs=pl.BlockSpec(memo...  3.84 us
    pallas_call x1, Pallas kernels, adjoint(): pl.pallas_call(adjoint_kernel, out_shape=jax.ShapeDtypeStruct((boxes, 2 *...  2.32 us
  transfers between devices with their start and end apart: 5, of which 4 were waited for; matrix products, arithmetic and copies ran while one was open for 3% of the time, Pallas kernels for 22%

profile of v2, /device:TPU:10, one launch (start us, length us, event | category | flops | bytes accessed | tf_op | source)
XLA Modules:
  0.0 92.8 jit_solution(11738341602682519649)
XLA Ops:
  0.0 3.6 %collective-permute-start.1 = (bf16[8,2,128,256]{3,2,1,0:T(8,128)(2,1)}, bf16[8,2,128,256]{3,2,1,0:T(8,128)(2,1)S(1)}, u32[]{:S(2)}, u32[]{:S(2)}) collective-permute-start(bf16[8,2,128,256]{3,2,1,0:T(8,128)(2,1)} %refs_5_.1), channel_id=1, source_target_pairs={{0,1},{1,2},{2,3},{3,4},{4,5},{5,6},{6,7},{7,8},{8,9},{9,10},{10,1... | collective-permute-start | bytes 3145736 | tf_op jit(solution)/shard_map/ppermute | solution.py:440
  3.6 1.2 %copy-done.7 = bf16[8,2,128,256]{3,2,1,0:T(8,128)(2,1)S(1)} copy-done((bf16[8,2,128,256]{3,2,1,0:T(8,128)(2,1)S(1)}, bf16[8,2,128,256]{3,2,1,0:T(8,128)(2,1)}, u32[]{:S(2)}) %copy-start.7) | copy-done | bytes 1048600
  4.9 1.0 %copy-done.11 = bf16[8,2,128,128]{3,2,1,0:T(8,128)(2,1)S(1)} copy-done((bf16[8,2,128,128]{3,2,1,0:T(8,128)(2,1)S(1)}, bf16[8,2,128,128]{3,2,1,0:T(8,128)(2,1)}, u32[]{:S(2)}) %copy-start.11) | copy-done | bytes 524312
  5.9 1.6 %copy-done.15 = bf16[1024,1024]{1,0:T(8,128)(2,1)S(1)} copy-done((bf16[1024,1024]{1,0:T(8,128)(2,1)S(1)}, bf16[1024,1024]{1,0:T(8,128)(2,1)}, u32[]{:S(2)}) %copy-start.15) | copy-done | bytes 2097176
  7.5 3.8 %upward.1 = bf16[32,16,512]{2,1,0:T(8,128)(2,1)} custom-call(bf16[8,2,128,256]{3,2,1,0:T(8,128)(2,1)S(1)} %copy-done.7, bf16[8,2,128,128]{3,2,1,0:T(8,128)(2,1)S(1)} %copy-done.11, bf16[1024,1024]{1,0:T(8,128)(2,1)S(1)} %copy-done.15), custom_call_target="tpu_custom_call" | custom-call | flops 2000000000 | bytes 4194304 | tf_op jit(solution)/shard_map/upward/pallas_call | solution.py:125
  11.3 5.1 %all-to-all-start = ((bf16[32,16,512]{2,1,0:T(8,128)(2,1)}), bf16[32,16,512]{2,1,0:T(8,128)(2,1)}, u32[]{:S(2)}, u32[]{:S(2)}) async-start(bf16[32,16,512]{2,1,0:T(8,128)(2,1)} %upward.1), calls=%async_computation | async-start | bytes 1048576 | tf_op jit(solution)/shard_map/all_to_all | solution.py:451
  16.4 12.6 %collective-permute-done.1.refs_4_ = bf16[8,2,128,256]{3,2,1,0:T(8,128)(2,1)S(1)} collective-permute-done((bf16[8,2,128,256]{3,2,1,0:T(8,128)(2,1)}, bf16[8,2,128,256]{3,2,1,0:T(8,128)(2,1)S(1)}, u32[]{:S(2)}, u32[]{:S(2)}) %collective-permute-start.1) | collective-permute-done | bytes 1048608 | tf_op jit(solution)/shard_map/ppermute | solution.py:440
  29.0 1.0 %copy-done.9 = bf16[8,2,128,256]{3,2,1,0:T(8,128)(2,1)} copy-done((bf16[8,2,128,256]{3,2,1,0:T(8,128)(2,1)}, bf16[8,2,128,256]{3,2,1,0:T(8,128)(2,1)S(1)}, u32[]{:S(2)}) %copy-start.9) | copy-done | bytes 1048600
  30.0 2.8 %copy-done.1 = bf16[8,12,2,128,128]{4,3,2,1,0:T(8,128)(2,1)S(1)} copy-done((bf16[8,12,2,128,128]{4,3,2,1,0:T(8,128)(2,1)S(1)}, bf16[8,12,2,128,128]{4,3,2,1,0:T(8,128)(2,1)}, u32[]{:S(2)}) %copy-start.1) | copy-done | bytes 6291480
  32.8 1.2 %copy-done.10 = bf16[8,2,128,256]{3,2,1,0:T(8,128)(2,1)S(1)} copy-done((bf16[8,2,128,256]{3,2,1,0:T(8,128)(2,1)S(1)}, bf16[8,2,128,256]{3,2,1,0:T(8,128)(2,1)}, u32[]{:S(2)}) %copy-start.10) | copy-done | bytes 1048600
  34.0 6.8 %near_first.1.refs_5_ = f32[8,2,128,256]{3,2,1,0:T(8,128)S(1)} custom-call(s32[8,12]{1,0:T(8,128)S(1)} %copy-done.13, s32[8]{0:T(128)S(1)} %copy-done.14, s32[1]{0:T(128)} %bitcast.1.refs_2_, bf16[8,12,2,128,128]{4,3,2,1,0:T(8,128)(2,1)S(1)} %copy-done.1, bf16[8,2,128,256]{3,2,1,0:T(8,128)(2,1)S(1)} %copy-done.10, bf16[8,2,128,256]{3,2,1,0:T(8,128)(2,1)S(1)} %copy-done.8), custom_call_target="tpu_custom_call" | custom-call | flops 2000000000 | bytes 8388608 | tf_op jit(solution)/shard_map/near_first/pallas_call | solution.py:321
  40.9 0.2 all-to-all-done.refs_0_
  41.1 5.1 %collective-permute-start.2 = (bf16[8,2,128,256]{3,2,1,0:T(8,128)(2,1)S(1)}, bf16[8,2,128,256]{3,2,1,0:T(8,128)(2,1)}, u32[]{:S(2)}, u32[]{:S(2)}) collective-permute-start(bf16[8,2,128,256]{3,2,1,0:T(8,128)(2,1)S(1)} %copy-done.8), channel_id=1, source_target_pairs={{1,0},{2,1},{3,2},{4,3},{5,4},{6,5},{7,6},{8,7},{9,8},{10,9},{11,1... | collective-permute-start | bytes 3145736 | tf_op jit(solution)/shard_map/ppermute | solution.py:440
  46.2 0.1 stack.9
  46.3 0.1 stack.10
  46.5 0.1 copy.18.table_ref
  46.6 2.3 %adjoint.1.adjoint_hbm = bf16[8,256,256]{2,1,0:T(8,128)(2,1)} custom-call(bf16[8,2,128,128]{3,2,1,0:T(8,128)(2,1)} %rad_ref.1), custom_call_target="tpu_custom_call" | custom-call | flops 1000000 | bytes 2097152 | tf_op jit(solution)/shard_map/adjoint/pallas_call | solution.py:348
  49.0 1.1 %collective-permute-done = s32[256,2]{0,1:T(2,128)S(1)} collective-permute-done((s32[256,2]{0,1:T(2,128)S(1)}, s32[256,2]{0,1:T(2,128)S(1)}, u32[]{:S(2)}, u32[]{:S(2)}) %collective-permute-start) | collective-permute-done | bytes 2080 | tf_op jit(solution)/shard_map/ppermute | solution.py:462
  50.1 0.1 copy.16
  50.2 0.9 copy.17
  51.1 1.0 %broadcast_select_fusion.lists_ref = s32[512,2]{1,0:T(8,128)S(1)} fusion(s32[512,2]{1,0:T(8,128)S(1)} %copy.16, s32[512,2]{1,0:T(8,128)} %copy.17, pred[]{:T(512)S(6)} %eq.3), kind=kLoop, calls=%fused_computation | loop fusion | flops 1024 | bytes 12289 | tf_op jit(solution)/shard_map/jit(_where)/select_n | solution.py:463
  52.1 1.1 %coupling.1.lines_hbm = f32[2,32,512]{2,1,0:T(8,128)S(1)} custom-call(s32[512,2]{1,0:T(8,128)S(1)} %broadcast_select_fusion.lists_ref, s32[1]{0:T(128)} %constant.11.clone.1.base_ref, bf16[316,32]{1,0:T(8,128)(2,1)S(1)} %copy.18.table_ref), custom_call_target="tpu_custom_call" | custom-call | flops 200000000 | bytes 2097152 | tf_op jit(solution)/shard_map/coupling/pallas_call | solution.py:172
  53.1 2.0 %translate.1 = bf16[32,16,512]{2,1,0:T(8,128)(2,1)S(1)} custom-call(f32[2,32,512]{2,1,0:T(8,128)S(1)} %coupling.1.lines_hbm, bf16[32,16,512]{2,1,0:T(8,128)(2,1)} %all-to-all-done.refs_0_), custom_call_target="tpu_custom_call" | custom-call | flops 1000000000 | bytes 2097152 | tf_op jit(solution)/shard_map/translate/pallas_call | solution.py:226
  55.1 0.8 copy-done.12
  55.9 3.7 %all-to-all-start.1 = ((bf16[32,16,512]{2,1,0:T(8,128)(2,1)}), bf16[32,16,512]{2,1,0:T(8,128)(2,1)}, u32[]{:S(2)}, u32[]{:S(2)}) async-start(bf16[32,16,512]{2,1,0:T(8,128)(2,1)} %copy-done.12), calls=%async_computation.1 | async-start | bytes 1048576 | tf_op jit(solution)/shard_map/all_to_all | solution.py:451
  59.6 15.1 %collective-permute-done.2.refs_4_ = bf16[8,2,128,256]{3,2,1,0:T(8,128)(2,1)} collective-permute-done((bf16[8,2,128,256]{3,2,1,0:T(8,128)(2,1)S(1)}, bf16[8,2,128,256]{3,2,1,0:T(8,128)(2,1)}, u32[]{:S(2)}, u32[]{:S(2)}) %collective-permute-start.2) | collective-permute-done | bytes 1048608 | tf_op jit(solution)/shard_map/ppermute | solution.py:440
  74.7 2.8 %copy-done.2 = bf16[8,12,2,128,128]{4,3,2,1,0:T(8,128)(2,1)S(1)} copy-done((bf16[8,12,2,128,128]{4,3,2,1,0:T(8,128)(2,1)S(1)}, bf16[8,12,2,128,128]{4,3,2,1,0:T(8,128)(2,1)}, u32[]{:S(2)}) %copy-start.2) | copy-done | bytes 6291480
  77.4 4.8 %near_last.1.near_hbm = f32[8,2,128,256]{3,2,1,0:T(8,128)S(1)} custom-call(s32[8,12]{1,0:T(8,128)S(1)} %copy-done.13, s32[8]{0:T(128)S(1)} %copy-done.14, s32[1]{0:T(128)} %bitcast.1.refs_2_, bf16[8,12,2,128,128]{4,3,2,1,0:T(8,128)(2,1)S(1)} %copy-done.2, bf16[8,2,128,256]{3,2,1,0:T(8,128)(2,1)} %collective-permute-done.2.refs_4_, ...), custom_call_target="tpu_custom_call" | custom-call | flops 99999997952 | bytes 8388608 | tf_op jit(solution)/shard_map/near_last/pallas_call | solution.py:321
  82.3 1.3 %copy-done.5 = f32[8,2,128,256]{3,2,1,0:T(8,128)} copy-done((f32[8,2,128,256]{3,2,1,0:T(8,128)}, f32[8,2,128,256]{3,2,1,0:T(8,128)S(1)}, u32[]{:S(2)}) %copy-start.5) | copy-done | bytes 2097176
  83.6 1.6 %copy-done.4 = bf16[4,512,512]{2,1,0:T(8,128)(2,1)S(1)} copy-done((bf16[4,512,512]{2,1,0:T(8,128)(2,1)S(1)}, bf16[4,512,512]{2,1,0:T(8,128)(2,1)}, u32[]{:S(2)}) %copy-start.4) | copy-done | bytes 2097176
  85.2 1.6 %copy-done.6 = f32[8,2,128,256]{3,2,1,0:T(8,128)S(1)} copy-done((f32[8,2,128,256]{3,2,1,0:T(8,128)S(1)}, f32[8,2,128,256]{3,2,1,0:T(8,128)}, u32[]{:S(2)}) %copy-start.6) | copy-done | bytes 2097176
  86.8 6.0 %downward.1 = f32[8,2,128,256]{3,2,1,0:T(8,128)} custom-call(bf16[32,16,512]{2,1,0:T(8,128)(2,1)} %all-to-all-done.1.field_hbm, bf16[4,512,512]{2,1,0:T(8,128)(2,1)S(1)} %copy-done.4, bf16[8,256,256]{2,1,0:T(8,128)(2,1)S(1)} %copy-done.3, f32[8,2,128,256]{3,2,1,0:T(8,128)S(1)} %copy-done.6), custom_call_target="tpu_custom_call" | custom-call | flops 2000000000 | bytes 7340032 | tf_op jit(solution)/shard_map/downward/pallas_call | solution.py:417
  (33 shorter events, 0.2 us)
Async XLA Ops:
  0.0 46.5 %copy-start = (bf16[316,2,4,8]{0,3,2,1:T(8,128)(2,1)S(1)}, bf16[316,2,4,8]{0,3,2,1:T(8,128)(2,1)}, u32[]{:S(2)}) copy-start(bf16[316,2,4,8]{0,3,2,1:T(8,128)(2,1)} %param.19) | copy-start | bytes 121348
  0.0 29.0 %collective-permute-start.1 = (bf16[8,2,128,256]{3,2,1,0:T(8,128)(2,1)}, bf16[8,2,128,256]{3,2,1,0:T(8,128)(2,1)S(1)}, u32[]{:S(2)}, u32[]{:S(2)}) collective-permute-start(bf16[8,2,128,256]{3,2,1,0:T(8,128)(2,1)} %refs_5_.1), channel_id=1, source_target_pairs={{0,1},{1,2},{2,3},{3,4},{4,5},{5,6},{6,7},{7,8},{8,9},{9,10},{10,1... | collective-permute-start | bytes 3145736 | tf_op jit(solution)/shard_map/ppermute | solution.py:440
  3.6 1.2 %copy-start.7 = (bf16[8,2,128,256]{3,2,1,0:T(8,128)(2,1)S(1)}, bf16[8,2,128,256]{3,2,1,0:T(8,128)(2,1)}, u32[]{:S(2)}) copy-start(bf16[8,2,128,256]{3,2,1,0:T(8,128)(2,1)} %refs_5_.1) | copy-start | bytes 3145732
  4.9 1.0 %copy-start.11 = (bf16[8,2,128,128]{3,2,1,0:T(8,128)(2,1)S(1)}, bf16[8,2,128,128]{3,2,1,0:T(8,128)(2,1)}, u32[]{:S(2)}) copy-start(bf16[8,2,128,128]{3,2,1,0:T(8,128)(2,1)} %rad_ref.1) | copy-start | bytes 1572868
  5.9 1.6 %copy-start.15 = (bf16[1024,1024]{1,0:T(8,128)(2,1)S(1)}, bf16[1024,1024]{1,0:T(8,128)(2,1)}, u32[]{:S(2)}) copy-start(bf16[1024,1024]{1,0:T(8,128)(2,1)} %constant.29.clone.w_hbm) | copy-start | bytes 6291460
  7.5 22.5 %copy-start.8 = (bf16[8,2,128,256]{3,2,1,0:T(8,128)(2,1)S(1)}, bf16[8,2,128,256]{3,2,1,0:T(8,128)(2,1)}, u32[]{:S(2)}) copy-start(bf16[8,2,128,256]{3,2,1,0:T(8,128)(2,1)} %refs_5_.1) | copy-start | bytes 3145732
  7.5 22.5 %copy-start.13 = (s32[8,12]{1,0:T(8,128)S(1)}, s32[8,12]{1,0:T(8,128)}, u32[]{:S(2)}) copy-start(s32[8,12]{1,0:T(8,128)} %refs_0_.3) | copy-start | bytes 1156
  7.5 22.5 %copy-start.14 = (s32[8]{0:T(128)S(1)}, s32[8]{0:T(128)}, u32[]{:S(2)}) copy-start(s32[8]{0:T(128)} %refs_1_.3) | copy-start | bytes 100
  11.3 29.7 %all-to-all-start = ((bf16[32,16,512]{2,1,0:T(8,128)(2,1)}), bf16[32,16,512]{2,1,0:T(8,128)(2,1)}, u32[]{:S(2)}, u32[]{:S(2)}) async-start(bf16[32,16,512]{2,1,0:T(8,128)(2,1)} %upward.1), calls=%async_computation | async-start | bytes 1048576 | tf_op jit(solution)/shard_map/all_to_all | solution.py:451
  29.0 1.0 %copy-start.9 = (bf16[8,2,128,256]{3,2,1,0:T(8,128)(2,1)}, bf16[8,2,128,256]{3,2,1,0:T(8,128)(2,1)S(1)}, u32[]{:S(2)}) copy-start(bf16[8,2,128,256]{3,2,1,0:T(8,128)(2,1)S(1)} %collective-permute-done.1.refs_4_) | copy-start | bytes 3145732
  30.0 2.8 %copy-start.1 = (bf16[8,12,2,128,128]{4,3,2,1,0:T(8,128)(2,1)S(1)}, bf16[8,12,2,128,128]{4,3,2,1,0:T(8,128)(2,1)}, u32[]{:S(2)}) copy-start(bf16[8,12,2,128,128]{4,3,2,1,0:T(8,128)(2,1)} %refs_3_.3) | copy-start | bytes 18874372
  32.8 1.2 %copy-start.10 = (bf16[8,2,128,256]{3,2,1,0:T(8,128)(2,1)S(1)}, bf16[8,2,128,256]{3,2,1,0:T(8,128)(2,1)}, u32[]{:S(2)}) copy-start(bf16[8,2,128,256]{3,2,1,0:T(8,128)(2,1)} %copy-done.9) | copy-start | bytes 3145732
  34.0 12.1 %copy-start.17 = (s32[16,16]{1,0:T(8,128)S(1)}, s32[16,16]{1,0:T(8,128)}, u32[]{:S(2)}) copy-start(s32[16,16]{1,0:T(8,128)} %param.16) | copy-start | bytes 3076
  34.0 12.1 %copy-start.18 = (s32[16]{0:T(128)S(1)}, s32[16]{0:T(128)}, u32[]{:S(2)}) copy-start(s32[16]{0:T(128)} %param.18) | copy-start | bytes 196
  34.0 12.3 %copy-start.16 = (s32[16,16]{1,0:T(8,128)S(1)}, s32[16,16]{1,0:T(8,128)}, u32[]{:S(2)}) copy-start(s32[16,16]{1,0:T(8,128)} %param.17) | copy-start | bytes 3076
  41.1 33.6 %collective-permute-start.2 = (bf16[8,2,128,256]{3,2,1,0:T(8,128)(2,1)S(1)}, bf16[8,2,128,256]{3,2,1,0:T(8,128)(2,1)}, u32[]{:S(2)}, u32[]{:S(2)}) collective-permute-start(bf16[8,2,128,256]{3,2,1,0:T(8,128)(2,1)S(1)} %copy-done.8), channel_id=1, source_target_pairs={{1,0},{2,1},{3,2},{4,3},{5,4},{6,5},{7,6},{8,7},{9,8},{10,9},{11,1... | collective-permute-start | bytes 3145736 | tf_op jit(solution)/shard_map/ppermute | solution.py:440
  46.4 3.7 %collective-permute-start = (s32[256,2]{0,1:T(2,128)S(1)}, s32[256,2]{0,1:T(2,128)S(1)}, u32[]{:S(2)}, u32[]{:S(2)}) collective-permute-start(s32[256,2]{0,1:T(2,128)S(1)} %pad_add_fusion.1), channel_id=1, source_target_pairs={{0,16},{16,0},{1,17},{17,1},{2,18},{18,2},{3,19},{19,3},{4,20},{20... | collective-permute-start | bytes 6152 | tf_op jit(solution)/shard_map/ppermute | solution.py:462
  55.1 0.8 copy-start.12
  55.9 27.7 %all-to-all-start.1 = ((bf16[32,16,512]{2,1,0:T(8,128)(2,1)}), bf16[32,16,512]{2,1,0:T(8,128)(2,1)}, u32[]{:S(2)}, u32[]{:S(2)}) async-start(bf16[32,16,512]{2,1,0:T(8,128)(2,1)} %copy-done.12), calls=%async_computation.1 | async-start | bytes 1048576 | tf_op jit(solution)/shard_map/all_to_all | solution.py:451
  74.7 2.8 %copy-start.2 = (bf16[8,12,2,128,128]{4,3,2,1,0:T(8,128)(2,1)S(1)}, bf16[8,12,2,128,128]{4,3,2,1,0:T(8,128)(2,1)}, u32[]{:S(2)}) copy-start(bf16[8,12,2,128,128]{4,3,2,1,0:T(8,128)(2,1)} %refs_3_.3) | copy-start | bytes 18874372
  77.4 6.1 %copy-start.3 = (bf16[8,256,256]{2,1,0:T(8,128)(2,1)S(1)}, bf16[8,256,256]{2,1,0:T(8,128)(2,1)}, u32[]{:S(2)}) copy-start(bf16[8,256,256]{2,1,0:T(8,128)(2,1)} %adjoint.1.adjoint_hbm) | copy-start | bytes 3145732
  82.2 1.3 %copy-start.5 = (f32[8,2,128,256]{3,2,1,0:T(8,128)}, f32[8,2,128,256]{3,2,1,0:T(8,128)S(1)}, u32[]{:S(2)}) copy-start(f32[8,2,128,256]{3,2,1,0:T(8,128)S(1)} %near_last.1.near_hbm) | copy-start | bytes 6291460
  83.6 1.6 %copy-start.4 = (bf16[4,512,512]{2,1,0:T(8,128)(2,1)S(1)}, bf16[4,512,512]{2,1,0:T(8,128)(2,1)}, u32[]{:S(2)}) copy-start(bf16[4,512,512]{2,1,0:T(8,128)(2,1)} %constant.30.clone.w_hbm) | copy-start | bytes 6291460
  85.2 1.6 %copy-start.6 = (f32[8,2,128,256]{3,2,1,0:T(8,128)S(1)}, f32[8,2,128,256]{3,2,1,0:T(8,128)}, u32[]{:S(2)}) copy-start(f32[8,2,128,256]{3,2,1,0:T(8,128)} %copy-done.5) | copy-start | bytes 6291460

commit v3 on v2

--- a/solution.py
+++ b/solution.py
@@ -69,6 +69,10 @@
     return np.concatenate(up, axis=1), np.stack(down)
 
 
+def in_hbm(*arrays):
+    return [pltpu.with_memory_space_constraint(array, pltpu.HBM) for array in arrays]
+
+
 def dot(a, b):
     return jnp.dot(a, b, preferred_element_type=F32)
 
@@ -83,7 +87,7 @@
     )
 
 
-def up_kernel(x_hbm, rad_hbm, w_hbm, out_ref, x_ref, rad_ref, w_ref, right, sems):
+def up_kernel(x_hbm, rad_hbm, w_hbm, out_hbm, x_ref, rad_ref, w_ref, right, result, sems):
     boxes, _, basis, rhs = x_ref.shape
     points = rad_ref.shape[2]
     copies = [
@@ -114,7 +118,8 @@
     total = dot(w_ref[...], right[0]) + dot(w_ref[...], right[1])
     samples = total.shape[0] // 2
     total = total[:samples] + total[samples:]
-    out_ref[...] = total.astype(BF16).reshape(out_ref.shape)
+    result[...] = total.astype(BF16).reshape(result.shape)
+    pltpu.sync_copy(result, out_hbm)
 
 
 def upward(coeffs, radiation, weights, groups):
@@ -125,13 +130,14 @@
     return pl.pallas_call(
         up_kernel,
         in_specs=[hbm] * 3,
-        out_specs=pl.BlockSpec(memory_space=pltpu.VMEM),
-        out_shape=jax.ShapeDtypeStruct((groups, samples // groups, 2 * rhs), BF16),
+        out_specs=hbm,
+        out_shape=pltpu.HBM((groups, samples // groups, 2 * rhs), BF16),
         scratch_shapes=[
             pltpu.VMEM(coeffs.shape, BF16),
             pltpu.VMEM(radiation.shape, BF16),
             pltpu.VMEM(weights.shape, BF16),
             pltpu.VMEM((2, columns, 2 * rhs), BF16),
+            pltpu.VMEM((groups, samples // groups, 2 * rhs), BF16),
             pltpu.SemaphoreType.DMA((3,)),
         ],
         compiler_params=pltpu.CompilerParams(vmem_limit_bytes=32 * MIB),
@@ -139,7 +145,7 @@
             flops=2 * 10**9, bytes_accessed=4 * MIB, transcendentals=0
         ),
         name="upward",
-    )(coeffs, radiation, weights)
+    )(*in_hbm(coeffs, radiation, weights))
 
 
 def coupling_kernel(lists_ref, base_ref, table_ref, out_ref):
@@ -227,7 +233,7 @@
         translate_kernel,
         in_specs=[hbm] * (1 + len(sources)),
         out_specs=hbm,
-        out_shape=jax.ShapeDtypeStruct(shape, BF16),
+        out_shape=pltpu.HBM(shape, BF16),
         scratch_shapes=[
             *[pltpu.VMEM(source.shape, BF16) for source in sources],
             pltpu.VMEM(lines.shape, F32),
@@ -240,7 +246,7 @@
             flops=10**9, bytes_accessed=2 * MIB, transcendentals=0
         ),
         name="translate",
-    )(lines, *sources)
+    )(*in_hbm(lines, *sources))
 
 
 def near_kernel(first, count, begun, *refs):
@@ -322,7 +328,7 @@
         functools.partial(near_kernel, first, count, begun),
         in_specs=[smem] * 3 + [hbm] * (1 + count + begun),
         out_specs=hbm,
-        out_shape=jax.ShapeDtypeStruct((boxes, 2, basis, rhs), F32),
+        out_shape=pltpu.HBM((boxes, 2, basis, rhs), F32),
         scratch_shapes=[
             pltpu.VMEM(blocks.shape, BF16),
             pltpu.VMEM((count * boxes, 2, basis, rhs), BF16),
@@ -335,19 +341,23 @@
             flops=10**11 if begun else 2 * 10**9, bytes_accessed=8 * MIB, transcendentals=0
         ),
         name="near_last" if begun else "near_first",
-    )(ids, used, rank, blocks, *sources, *([before] if begun else []))
-
-
-def adjoint_kernel(rad_ref, out_ref):
+    )(ids, used, rank, *in_hbm(blocks, *sources, *([before] if begun else [])))
+
+
+def adjoint_kernel(rad_ref, out_hbm, held):
     for box in range(rad_ref.shape[0]):
-        out_ref[box] = complex_rows(rad_ref[box, 0], rad_ref[box, 1]).T
+        held[box] = complex_rows(rad_ref[box, 0], rad_ref[box, 1]).T
+    pltpu.sync_copy(held, out_hbm)
 
 
 def adjoint(radiation):
     boxes, _, points, basis = radiation.shape
     return pl.pallas_call(
         adjoint_kernel,
-        out_shape=jax.ShapeDtypeStruct((boxes, 2 * basis, 2 * points), BF16),
+        in_specs=[pl.BlockSpec(memory_space=pltpu.VMEM)],
+        out_specs=pl.BlockSpec(memory_space=pltpu.HBM),
+        scratch_shapes=[pltpu.VMEM((boxes, 2 * basis, 2 * points), BF16)],
+        out_shape=pltpu.HBM((boxes, 2 * basis, 2 * points), BF16),
         cost_estimate=pl.CostEstimate(
             flops=10**6, bytes_accessed=2 * MIB, transcendentals=0
         ),
@@ -431,7 +441,7 @@
             flops=2 * 10**9, bytes_accessed=7 * MIB, transcendentals=0
         ),
         name="downward",
-    )(field, weights, radiation_adjoint, near)
+    )(*in_hbm(field, weights, radiation_adjoint, near))
 
 
 def shift(block, axis, step):
@@ -492,10 +502,12 @@
     radiation_adjoint = adjoint(radiation)
     lists = lists_of(partners, vector_ids, pair_count)
     lines = translation_lines(lists, translation, shares, per_group)
+    rank, lines, radiation_adjoint = lax.optimization_barrier((rank, lines, radiation_adjoint))
+    low, late = lax.optimization_barrier((low, coeffs))
+    high = shift(late, every, -1)
     near = near_field(near_ids, near_count, rank, near_blocks, [low, coeffs], 0)
     parents = parent_bands(spread, shares)
-    parents, near, late = lax.optimization_barrier((parents, near, coeffs))
-    high = shift(late, every, -1)
+    parents, near = lax.optimization_barrier((parents, near))
     sources = [parents]
     if shares < lax.axis_size("box"):
         sources = [shift(parents, "box", 1), parents, shift(parents, "box", -1)]

time: 94.3 us -> 93.4 us (level)
  the two profiles are of different devices: /device:TPU:10 before, /device:TPU:0 now
where the time goes in v3:
time: 93.4 us; the launch traced here: 92.3 us
  starting transfers between devices  36.5 us (39%)
  Pallas kernels  30.5 us (33%)
  waiting for transfers between devices  22.1 us (24%)
  local copies, waits for them, and re-layouts  2.88 us (3%)
    all_to_all x2, starting transfers between devices, parent_bands(): return lax.all_to_all(spread, axes, split_axis=0, concat_axis=0, tiled=True)  24.2 us
    ppermute x2, waiting for transfers between devices, shift(): return lax.ppermute(block, axis, pairs)  13.6 us
    pallas_call x2, Pallas kernels, near_field(): pl.pallas_call(functools.partial(near_kernel, first, count, begun), in_sp...  13.5 us
    all_to_all x2, waiting for transfers between devices, parent_bands(): return lax.all_to_all(spread, axes, split_axis=0, concat_axis=0, tiled=True)  8.44 us
    ppermute x2, starting transfers between devices, shift(): return lax.ppermute(block, axis, pairs)  6.42 us
    ppermute x1, starting transfers between devices, translation_lines(): other = lax.ppermute(lists, 'box', [(0, 1), (1, 0)])  5.96 us
    pallas_call x1, Pallas kernels, downward(): pl.pallas_call(down_kernel, in_specs=[hbm] * 4, out_specs=hbm, out_shape=...  5.76 us
    pallas_call x1, Pallas kernels, upward(): pl.pallas_call(up_kernel, in_specs=[hbm] * 3, out_specs=hbm, out_shape=pl...  5.25 us
  transfers between devices with their start and end apart: 5, of which 2 were waited for; matrix products, arithmetic and copies ran while one was open for 1% of the time, Pallas kernels for 27%

profile of v3, /device:TPU:0, one launch (start us, length us, event | category | flops | bytes accessed | tf_op | source)
XLA Modules:
  0.0 92.3 jit_solution(3767394567937709288)
XLA Ops:
  0.0 0.0 copy-start
  0.0 0.0 copy-start.9
  0.0 5.1 %collective-permute-start.1 = (bf16[8,2,128,256]{3,2,1,0:T(8,128)(2,1)}, bf16[8,2,128,256]{3,2,1,0:T(8,128)(2,1)S(1)}, u32[]{:S(2)}, u32[]{:S(2)}) collective-permute-start(bf16[8,2,128,256]{3,2,1,0:T(8,128)(2,1)} %refs_5_.1), channel_id=1, source_target_pairs={{0,1},{1,2},{2,3},{3,4},{4,5},{5,6},{6,7},{7,8},{8,9},{9,10},{10,1... | collective-permute-start | bytes 3145736 | tf_op jit(solution)/shard_map/ppermute | solution.py:450
  5.2 5.3 %upward.1 = bf16[32,16,512]{2,1,0:T(8,128)(2,1)} custom-call(bf16[8,2,128,256]{3,2,1,0:T(8,128)(2,1)} %refs_5_.1, bf16[8,2,128,128]{3,2,1,0:T(8,128)(2,1)} %rad_hbm.1, bf16[1024,1024]{1,0:T(8,128)(2,1)} %constant.29.clone.w_hbm), custom_call_target="tpu_custom_call" | custom-call | flops 2000000000 | bytes 4194304 | tf_op jit(solution)/shard_map/upward/pallas_call | solution.py:130
  10.4 4.8 %all-to-all-start = ((bf16[32,16,512]{2,1,0:T(8,128)(2,1)}), bf16[32,16,512]{2,1,0:T(8,128)(2,1)S(1)}, u32[]{:S(2)}, u32[]{:S(2)}) async-start(bf16[32,16,512]{2,1,0:T(8,128)(2,1)} %upward.1), calls=%async_computation | async-start | bytes 1048576 | tf_op jit(solution)/shard_map/all_to_all | solution.py:461
  15.2 0.0 copy-start.1
  15.2 0.0 copy-start.2
  15.3 0.1 stack.10
  15.3 13.6 %collective-permute-done.1.refs_4_ = bf16[8,2,128,256]{3,2,1,0:T(8,128)(2,1)S(1)} collective-permute-done((bf16[8,2,128,256]{3,2,1,0:T(8,128)(2,1)}, bf16[8,2,128,256]{3,2,1,0:T(8,128)(2,1)S(1)}, u32[]{:S(2)}, u32[]{:S(2)}) %collective-permute-start.1) | collective-permute-done | bytes 1048608 | tf_op jit(solution)/shard_map/ppermute | solution.py:450
  29.0 0.0 copy-done.5
  29.0 1.3 %collective-permute-start.2 = (bf16[8,2,128,256]{3,2,1,0:T(8,128)(2,1)S(1)}, bf16[8,2,128,256]{3,2,1,0:T(8,128)(2,1)}, u32[]{:S(2)}, u32[]{:S(2)}) collective-permute-start(bf16[8,2,128,256]{3,2,1,0:T(8,128)(2,1)S(1)} %copy-done.5), channel_id=1, source_target_pairs={{1,0},{2,1},{3,2},{4,3},{5,4},{6,5},{7,6},{8,7},{9,8},{10,9},{11,1... | collective-permute-start | bytes 3145736 | tf_op jit(solution)/shard_map/ppermute | solution.py:450
  30.3 0.0 copy-done.10
  30.3 0.1 fusion
  30.3 0.1 stack.9
  30.4 6.0 %collective-permute-start = (s32[256,2]{0,1:T(2,128)S(1)}, s32[256,2]{0,1:T(2,128)S(1)}, u32[]{:S(2)}, u32[]{:S(2)}) collective-permute-start(s32[256,2]{0,1:T(2,128)S(1)} %pad_add_fusion.1), channel_id=1, source_target_pairs={{0,16},{16,0},{1,17},{17,1},{2,18},{18,2},{3,19},{19,3},{4,20},{20... | collective-permute-start | bytes 6152 | tf_op jit(solution)/shard_map/ppermute | solution.py:472
  36.4 0.1 copy.18.table_ref
  36.5 2.3 %adjoint.1.adjoint_hbm = bf16[8,256,256]{2,1,0:T(8,128)(2,1)} custom-call(bf16[8,2,128,128]{3,2,1,0:T(8,128)(2,1)} %rad_hbm.1), custom_call_target="tpu_custom_call" | custom-call | flops 1000000 | bytes 2097152 | tf_op jit(solution)/shard_map/adjoint/pallas_call | solution.py:355
  38.8 0.0 collective-permute-done
  38.8 0.1 copy.17
  39.0 0.1 copy.16
  39.2 1.1 %coupling.1.lines_hbm = f32[2,32,512]{2,1,0:T(8,128)S(1)} custom-call(s32[512,2]{1,0:T(8,128)S(1)} %broadcast_select_fusion.lists_ref, s32[1]{0:T(128)} %constant.27.clone.1.base_ref, bf16[316,32]{1,0:T(8,128)(2,1)S(1)} %copy.18.table_ref), custom_call_target="tpu_custom_call" | custom-call | flops 200000000 | bytes 2097152 | tf_op jit(solution)/shard_map/coupling/pallas_call | solution.py:178
  40.3 0.7 copy-done.3
  40.9 7.6 %near_first.1.refs_5_ = f32[8,2,128,256]{3,2,1,0:T(8,128)} custom-call(s32[8,12]{1,0:T(8,128)S(1)} %copy-done.1, s32[8]{0:T(128)S(1)} %copy-done.2, s32[1]{0:T(128)} %bitcast.refs_2_, bf16[8,12,2,128,128]{4,3,2,1,0:T(8,128)(2,1)} %refs_3_.3, bf16[8,2,128,256]{3,2,1,0:T(8,128)(2,1)} %copy-done.6, bf16[8,2,128,256]{3,2,1,0:T(8,128)(2,1)} %refs_5_.1), custom_call_target="tpu_custom_call" | custom-call | flops 2000000000 | bytes 8388608 | tf_op jit(solution)/shard_map/near_first/pallas_call | solution.py:327
  48.5 0.0 all-to-all-done.refs_0_
  48.5 0.8 copy-done.7
  49.3 2.6 %translate.1 = bf16[32,16,512]{2,1,0:T(8,128)(2,1)} custom-call(f32[2,32,512]{2,1,0:T(8,128)} %copy-done.3, bf16[32,16,512]{2,1,0:T(8,128)(2,1)} %copy-done.7), custom_call_target="tpu_custom_call" | custom-call | flops 1000000000 | bytes 2097152 | tf_op jit(solution)/shard_map/translate/pallas_call | solution.py:232
  52.0 19.4 %all-to-all-start.1 = ((bf16[32,16,512]{2,1,0:T(8,128)(2,1)}), bf16[32,16,512]{2,1,0:T(8,128)(2,1)S(1)}, u32[]{:S(2)}, u32[]{:S(2)}) async-start(bf16[32,16,512]{2,1,0:T(8,128)(2,1)} %translate.1), calls=%async_computation.1 | async-start | bytes 1048576 | tf_op jit(solution)/shard_map/all_to_all | solution.py:461
  71.3 0.0 collective-permute-done.2.refs_4_
  71.4 5.9 %near_last.1.near_hbm = f32[8,2,128,256]{3,2,1,0:T(8,128)} custom-call(s32[8,12]{1,0:T(8,128)S(1)} %copy-done.1, s32[8]{0:T(128)S(1)} %copy-done.2, s32[1]{0:T(128)} %bitcast.refs_2_, bf16[8,12,2,128,128]{4,3,2,1,0:T(8,128)(2,1)} %refs_3_.3, bf16[8,2,128,256]{3,2,1,0:T(8,128)(2,1)} %collective-permute-done.2.refs_4_, f32[8,2,128,256]{3,2,1,0:T(8,128)} %near_first.1.refs_5_), custom_call_target="tpu_custom_call" | custom-call | flops 99999997952 | bytes 8388608 | tf_op jit(solution)/shard_map/near_last/pallas_call | solution.py:327
  77.3 8.4 %all-to-all-done.1.field_hbm = bf16[32,16,512]{2,1,0:T(8,128)(2,1)S(1)} async-done(((bf16[32,16,512]{2,1,0:T(8,128)(2,1)}), bf16[32,16,512]{2,1,0:T(8,128)(2,1)S(1)}, u32[]{:S(2)}, u32[]{:S(2)}) %all-to-all-start.1) | async-done | bytes 524320 | tf_op jit(solution)/shard_map/all_to_all | solution.py:461
  85.7 0.8 copy-done.4
  86.5 5.8 %downward.1 = f32[8,2,128,256]{3,2,1,0:T(8,128)} custom-call(bf16[32,16,512]{2,1,0:T(8,128)(2,1)} %copy-done.4, bf16[4,512,512]{2,1,0:T(8,128)(2,1)} %constant.30.clone.w_hbm, bf16[8,256,256]{2,1,0:T(8,128)(2,1)} %adjoint.1.adjoint_hbm, f32[8,2,128,256]{3,2,1,0:T(8,128)} %near_last.1.near_hbm), custom_call_target="tpu_custom_call" | custom-call | flops 2000000000 | bytes 7340032 | tf_op jit(solution)/shard_map/downward/pallas_call | solution.py:427
  (17 shorter events, 0.1 us)
Async XLA Ops:
  0.0 36.4 %copy-start = (bf16[316,2,4,8]{0,3,2,1:T(8,128)(2,1)S(1)}, bf16[316,2,4,8]{0,3,2,1:T(8,128)(2,1)}, u32[]{:S(2)}) copy-start(bf16[316,2,4,8]{0,3,2,1:T(8,128)(2,1)} %param.19) | copy-start | bytes 121348
  0.0 29.0 %copy-start.5 = (bf16[8,2,128,256]{3,2,1,0:T(8,128)(2,1)S(1)}, bf16[8,2,128,256]{3,2,1,0:T(8,128)(2,1)}, u32[]{:S(2)}) copy-start(bf16[8,2,128,256]{3,2,1,0:T(8,128)(2,1)} %refs_5_.1) | copy-start | bytes 3145732
  0.0 15.2 %copy-start.8 = (s32[16,16]{1,0:T(8,128)S(1)}, s32[16,16]{1,0:T(8,128)}, u32[]{:S(2)}) copy-start(s32[16,16]{1,0:T(8,128)} %param.17) | copy-start | bytes 3076
  0.0 30.2 %copy-start.10 = (s32[16]{0:T(128)S(1)}, s32[16]{0:T(128)}, u32[]{:S(2)}) copy-start(s32[16]{0:T(128)} %param.18) | copy-start | bytes 196
  0.0 30.3 %copy-start.9 = (s32[16,16]{1,0:T(8,128)S(1)}, s32[16,16]{1,0:T(8,128)}, u32[]{:S(2)}) copy-start(s32[16,16]{1,0:T(8,128)} %param.16) | copy-start | bytes 3076
  0.0 28.9 %collective-permute-start.1 = (bf16[8,2,128,256]{3,2,1,0:T(8,128)(2,1)}, bf16[8,2,128,256]{3,2,1,0:T(8,128)(2,1)S(1)}, u32[]{:S(2)}, u32[]{:S(2)}) collective-permute-start(bf16[8,2,128,256]{3,2,1,0:T(8,128)(2,1)} %refs_5_.1), channel_id=1, source_target_pairs={{0,1},{1,2},{2,3},{3,4},{4,5},{5,6},{6,7},{7,8},{8,9},{9,10},{10,1... | collective-permute-start | bytes 3145736 | tf_op jit(solution)/shard_map/ppermute | solution.py:450
  10.4 38.1 %all-to-all-start = ((bf16[32,16,512]{2,1,0:T(8,128)(2,1)}), bf16[32,16,512]{2,1,0:T(8,128)(2,1)S(1)}, u32[]{:S(2)}, u32[]{:S(2)}) async-start(bf16[32,16,512]{2,1,0:T(8,128)(2,1)} %upward.1), calls=%async_computation | async-start | bytes 1048576 | tf_op jit(solution)/shard_map/all_to_all | solution.py:461
  15.2 25.7 %copy-start.1 = (s32[8,12]{1,0:T(8,128)S(1)}, s32[8,12]{1,0:T(8,128)}, u32[]{:S(2)}) copy-start(s32[8,12]{1,0:T(8,128)} %refs_0_.3) | copy-start | bytes 1156
  15.2 25.7 %copy-start.2 = (s32[8]{0:T(128)S(1)}, s32[8]{0:T(128)}, u32[]{:S(2)}) copy-start(s32[8]{0:T(128)} %refs_1_.3) | copy-start | bytes 100
  29.0 12.0 %copy-start.6 = (bf16[8,2,128,256]{3,2,1,0:T(8,128)(2,1)}, bf16[8,2,128,256]{3,2,1,0:T(8,128)(2,1)S(1)}, u32[]{:S(2)}) copy-start(bf16[8,2,128,256]{3,2,1,0:T(8,128)(2,1)S(1)} %collective-permute-done.1.refs_4_) | copy-start | bytes 3145732
  29.0 42.4 %collective-permute-start.2 = (bf16[8,2,128,256]{3,2,1,0:T(8,128)(2,1)S(1)}, bf16[8,2,128,256]{3,2,1,0:T(8,128)(2,1)}, u32[]{:S(2)}, u32[]{:S(2)}) collective-permute-start(bf16[8,2,128,256]{3,2,1,0:T(8,128)(2,1)S(1)} %copy-done.5), channel_id=1, source_target_pairs={{1,0},{2,1},{3,2},{4,3},{5,4},{6,5},{7,6},{8,7},{9,8},{10,9},{11,1... | collective-permute-start | bytes 3145736 | tf_op jit(solution)/shard_map/ppermute | solution.py:450
  30.4 8.4 %collective-permute-start = (s32[256,2]{0,1:T(2,128)S(1)}, s32[256,2]{0,1:T(2,128)S(1)}, u32[]{:S(2)}, u32[]{:S(2)}) collective-permute-start(s32[256,2]{0,1:T(2,128)S(1)} %pad_add_fusion.1), channel_id=1, source_target_pairs={{0,16},{16,0},{1,17},{17,1},{2,18},{18,2},{3,19},{19,3},{4,20},{20... | collective-permute-start | bytes 6152 | tf_op jit(solution)/shard_map/ppermute | solution.py:472
  40.3 0.7 copy-start.3
  48.5 0.8 copy-start.7
  52.0 33.8 %all-to-all-start.1 = ((bf16[32,16,512]{2,1,0:T(8,128)(2,1)}), bf16[32,16,512]{2,1,0:T(8,128)(2,1)S(1)}, u32[]{:S(2)}, u32[]{:S(2)}) async-start(bf16[32,16,512]{2,1,0:T(8,128)(2,1)} %translate.1), calls=%async_computation.1 | async-start | bytes 1048576 | tf_op jit(solution)/shard_map/all_to_all | solution.py:461
  85.7 0.8 copy-start.4

commit v4 on v3

--- a/solution.py
+++ b/solution.py
@@ -65,8 +65,8 @@
         high = np.concatenate([cos_high, sin_high], axis=1)
         low = np.concatenate([cos_low, sin_low], axis=1)
         up.append(np.concatenate([high, low], axis=0))
-        down.append(np.concatenate([cos_high.T, sin_high.T, cos_low.T, sin_low.T], axis=0))
-    return np.concatenate(up, axis=1), np.stack(down)
+        down += [cos_high.T, sin_high.T]
+    return np.concatenate(up, axis=1), np.concatenate(down, axis=0)
 
 
 def in_hbm(*arrays):
@@ -229,9 +229,10 @@
     _, targets, columns = lines.shape
     shape = (targets, samples, width)
     hbm = pl.BlockSpec(memory_space=pltpu.HBM)
+    anywhere = pl.BlockSpec(memory_space=pl.ANY)
     return pl.pallas_call(
         translate_kernel,
-        in_specs=[hbm] * (1 + len(sources)),
+        in_specs=[hbm] + [anywhere] * len(sources),
         out_specs=hbm,
         out_shape=pltpu.HBM(shape, BF16),
         scratch_shapes=[
@@ -246,7 +247,7 @@
             flops=10**9, bytes_accessed=2 * MIB, transcendentals=0
         ),
         name="translate",
-    )(*in_hbm(lines, *sources))
+    )(*in_hbm(lines), *sources)
 
 
 def near_kernel(first, count, begun, *refs):
@@ -365,58 +366,40 @@
     )(radiation)
 
 
-def down_kernel(field_hbm, w_hbm, adjoint_hbm, near_hbm, out_hbm, field, w, left, held, sems):
+def down_kernel(field_ref, w_hbm, adjoint_hbm, near_hbm, out_hbm, field, w, left, held, sems):
     boxes, width, _ = left.shape
     points = width // 2
-    samples = w.shape[2]
     basis, rhs = held.shape[2], held.shape[3]
-    half = boxes // 2
-    field_copy = pltpu.make_async_copy(field_hbm, field, sems.at[0])
-    w_copies, left_copies, near_copies, out_copies = [], [], [], []
-    for pair in range(half):
-        w_copies.append(pltpu.make_async_copy(w_hbm.at[pair], w.at[pair], sems.at[1 + pair]))
-    for box in range(boxes):
-        places = [1 + half + turn * boxes + box for turn in range(3)]
-        left_copies.append(
-            pltpu.make_async_copy(adjoint_hbm.at[box], left.at[box], sems.at[places[0]])
+    copies = [
+        pltpu.make_async_copy(source, target, sems.at[boxes + place])
+        for place, (source, target) in enumerate(
+            ((field_ref, field), (w_hbm, w), (adjoint_hbm, left), (near_hbm, held))
         )
-        near_copies.append(
-            pltpu.make_async_copy(near_hbm.at[box], held.at[box], sems.at[places[1]])
+    ]
+    out_copies = [
+        pltpu.make_async_copy(held.at[box], out_hbm.at[box], sems.at[box]) for box in range(boxes)
+    ]
+    for copy in copies:
+        copy.start()
+    for copy in copies[:2]:
+        copy.wait()
+    mixed = dot(w[...], field[...].reshape(w.shape[1], 2 * rhs))
+    for copy in copies[2:]:
+        copy.wait()
+    for octant in range(boxes // 2):
+        start = 2 * octant * points
+        cos_part = mixed[start : start + points]
+        sin_part = mixed[start + points : start + 2 * points]
+        cos_re, cos_im = cos_part[:, :rhs], cos_part[:, rhs:]
+        sin_re, sin_im = sin_part[:, :rhs], sin_part[:, rhs:]
+        leaves = (
+            (octant, cos_re + sin_im, cos_im - sin_re),
+            (boxes - 1 - octant, cos_re - sin_im, cos_im + sin_re),
         )
-        out_copies.append(
-            pltpu.make_async_copy(held.at[box], out_hbm.at[box], sems.at[places[2]])
-        )
-    field_copy.start()
-    for pair in range(half):
-        w_copies[pair].start()
-    for pair in range(half):
-        for box in (pair, boxes - 1 - pair):
-            left_copies[box].start()
-            near_copies[box].start()
-    field_copy.wait()
-    for first in range(0, half, 2):
-        for pair in (first, first + 1):
-            w_copies[pair].wait()
-        rows = w.shape[1]
-        mixed = dot(
-            w[first : first + 2].reshape(2 * rows, samples), field[...].reshape(samples, 2 * rhs)
-        )
-        for pair in (first, first + 1):
-            part = mixed[(pair - first) * rows : (pair - first + 1) * rows]
-            part = part[: rows // 2] + part[rows // 2 :]
-            cos_re, cos_im = part[:points, :rhs], part[:points, rhs:]
-            sin_re, sin_im = part[points:, :rhs], part[points:, rhs:]
-            leaves = (
-                (pair, cos_re + sin_im, cos_im - sin_re),
-                (boxes - 1 - pair, cos_re - sin_im, cos_im + sin_re),
-            )
-            for box, real, imag in leaves:
-                leaf = jnp.concatenate([real, imag], axis=0).astype(BF16)
-                left_copies[box].wait()
-                far = dot(left[box], leaf)
-                near_copies[box].wait()
-                held[box] += far.reshape(2, basis, rhs)
-                out_copies[box].start()
+        for box, real, imag in leaves:
+            leaf = jnp.concatenate([real, imag], axis=0).astype(BF16)
+            held[box] += dot(left[box], leaf).reshape(2, basis, rhs)
+            out_copies[box].start()
     for copy in out_copies:
         copy.wait()
 
@@ -426,7 +409,7 @@
     hbm = pl.BlockSpec(memory_space=pltpu.HBM)
     return pl.pallas_call(
         down_kernel,
-        in_specs=[hbm] * 4,
+        in_specs=[pl.BlockSpec(memory_space=pl.ANY)] + [hbm] * 3,
         out_specs=hbm,
         out_shape=jax.ShapeDtypeStruct(near.shape, F32),
         scratch_shapes=[
@@ -434,14 +417,14 @@
             pltpu.VMEM(weights.shape, BF16),
             pltpu.VMEM(radiation_adjoint.shape, BF16),
             pltpu.VMEM(near.shape, F32),
-            pltpu.SemaphoreType.DMA((1 + boxes // 2 + 3 * boxes,)),
+            pltpu.SemaphoreType.DMA((boxes + 4,)),
         ],
         compiler_params=pltpu.CompilerParams(vmem_limit_bytes=32 * MIB),
         cost_estimate=pl.CostEstimate(
             flops=2 * 10**9, bytes_accessed=7 * MIB, transcendentals=0
         ),
         name="downward",
-    )(*in_hbm(field, weights, radiation_adjoint, near))
+    )(field, *in_hbm(weights, radiation_adjoint, near))
 
 
 def shift(block, axis, step):
@@ -502,17 +485,17 @@
     radiation_adjoint = adjoint(radiation)
     lists = lists_of(partners, vector_ids, pair_count)
     lines = translation_lines(lists, translation, shares, per_group)
-    rank, lines, radiation_adjoint = lax.optimization_barrier((rank, lines, radiation_adjoint))
-    low, late = lax.optimization_barrier((low, coeffs))
+    spread, lines, radiation_adjoint = lax.optimization_barrier((spread, lines, radiation_adjoint))
+    parents = parent_bands(spread, shares)
+    parents, low, late = lax.optimization_barrier((parents, low, coeffs))
     high = shift(late, every, -1)
-    near = near_field(near_ids, near_count, rank, near_blocks, [low, coeffs], 0)
-    parents = parent_bands(spread, shares)
-    parents, near = lax.optimization_barrier((parents, near))
     sources = [parents]
     if shares < lax.axis_size("box"):
         sources = [shift(parents, "box", 1), parents, shift(parents, "box", -1)]
     incoming = translate(lines, sources)
+    incoming, low = lax.optimization_barrier((incoming, low))
     field = parent_bands(incoming, shares)
+    near = near_field(near_ids, near_count, rank, near_blocks, [low, coeffs], 0)
     near = near_field(near_ids, near_count, rank, near_blocks, [high], 2, near)
     return downward(field, down_weights, radiation_adjoint, near)
 

time: 93.4 us -> 87.3 us (0.935)
  blocking collectives: 0 us -> 27.1 us
  starting transfers between devices: 36.5 us -> 12.3 us
  waiting for transfers between devices: 22.1 us -> 15.5 us
  Pallas kernels: 30.5 us -> 28.9 us
    all_to_all x0 -> x1, blocking collectives: none -> 27.1 us  [parent_bands(): return lax.all_to_all(spread, axes, split_axis=0, concat_axis=0, tiled=True)]
    all_to_all x2 -> x1, starting transfers between devices: 24.2 us -> 4.42 us  [parent_bands(): return lax.all_to_all(spread, axes, split_axis=0, concat_axis=0, tiled=True)]
    all_to_all x2 -> x1, waiting for transfers between devices: 8.44 us -> 2.51 us  [parent_bands(): return lax.all_to_all(spread, axes, split_axis=0, concat_axis=0, tiled=True)]
    ppermute x1, starting transfers between devices: 5.96 us -> 3 us  [translation_lines(): other = lax.ppermute(lists, 'box', [(0, 1), (1, 0)])]
    pallas_call x2, Pallas kernels: 8.39 us -> 6.43 us  [the longest x1 3.93 us: downward(): pl.pallas_call(down_kernel, in_specs=[pl.BlockSpec(memory_space=pl.ANY)]...]
    unnamed x22 -> x14, local copies, waits for them, and re-layouts: 2.29 us -> 0.68 us
    ppermute x2, starting transfers between devices: 6.42 us -> 4.83 us  [shift(): return lax.ppermute(block, axis, pairs)]
  transfers between devices with their start and end apart: 5 -> 4, of which waited for: 2 -> 2; matrix products, arithmetic and copies ran while one was open for 1% -> 1% of each run, Pallas kernels for 27% -> 29%
where the time goes in v4:
time: 87.3 us; the launch traced here: 86.8 us
  Pallas kernels  28.9 us (33%)
  blocking collectives  27.1 us (31%)
  waiting for transfers between devices  15.5 us (18%)
  starting transfers between devices  12.3 us (14%)
  local copies, waits for them, and re-layouts  1.98 us (2%)
    all_to_all x1, blocking collectives, parent_bands(): return lax.all_to_all(spread, axes, split_axis=0, concat_axis=0, tiled=True)  27.1 us
    pallas_call x2, Pallas kernels, near_field(): pl.pallas_call(functools.partial(near_kernel, first, count, begun), in_sp...  13.8 us
    ppermute x2, waiting for transfers between devices, shift(): return lax.ppermute(block, axis, pairs)  13 us
    pallas_call x1, Pallas kernels, upward(): pl.pallas_call(up_kernel, in_specs=[hbm] * 3, out_specs=hbm, out_shape=pl...  5.23 us
    ppermute x2, starting transfers between devices, shift(): return lax.ppermute(block, axis, pairs)  4.83 us
    all_to_all x1, starting transfers between devices, parent_bands(): return lax.all_to_all(spread, axes, split_axis=0, concat_axis=0, tiled=True)  4.42 us
    pallas_call x1, Pallas kernels, downward(): pl.pallas_call(down_kernel, in_specs=[pl.BlockSpec(memory_space=pl.ANY)]...  3.93 us
    ppermute x1, starting transfers between devices, translation_lines(): other = lax.ppermute(lists, 'box', [(0, 1), (1, 0)])  3 us
  transfers between devices with their start and end apart: 4, of which 2 were waited for; matrix products, arithmetic and copies ran while one was open for 1% of the time, Pallas kernels for 29%

profile of v4, /device:TPU:0, one launch (start us, length us, event | category | flops | bytes accessed | tf_op | source)
XLA Modules:
  0.0 86.8 jit_solution(9968640585923500555)
XLA Ops:
  0.0 0.0 copy-start
  0.0 0.8 stack.10
  0.8 0.8 fusion
  1.6 0.1 stack.9
  1.7 3.0 %collective-permute-start = (s32[256,2]{0,1:T(2,128)S(1)}, s32[256,2]{0,1:T(2,128)S(1)}, u32[]{:S(2)}, u32[]{:S(2)}) collective-permute-start(s32[256,2]{0,1:T(2,128)S(1)} %pad_add_fusion.1), channel_id=1, source_target_pairs={{0,16},{16,0},{1,17},{17,1},{2,18},{18,2},{3,19},{19,3},{4,20},{20... | collective-permute-start | bytes 6152 | tf_op jit(solution)/shard_map/ppermute | solution.py:455
  4.7 3.5 %collective-permute-start.1 = (bf16[8,2,128,256]{3,2,1,0:T(8,128)(2,1)}, bf16[8,2,128,256]{3,2,1,0:T(8,128)(2,1)S(1)}, u32[]{:S(2)}, u32[]{:S(2)}) collective-permute-start(bf16[8,2,128,256]{3,2,1,0:T(8,128)(2,1)} %refs_5_.1), channel_id=1, source_target_pairs={{0,1},{1,2},{2,3},{3,4},{4,5},{5,6},{6,7},{7,8},{8,9},{9,10},{10,1... | collective-permute-start | bytes 3145736 | tf_op jit(solution)/shard_map/ppermute | solution.py:433
  8.2 5.2 %upward.1 = bf16[32,16,512]{2,1,0:T(8,128)(2,1)} custom-call(bf16[8,2,128,256]{3,2,1,0:T(8,128)(2,1)} %refs_5_.1, bf16[8,2,128,128]{3,2,1,0:T(8,128)(2,1)} %rad_ref.1, bf16[1024,1024]{1,0:T(8,128)(2,1)} %constant.29.clone.w_hbm), custom_call_target="tpu_custom_call" | custom-call | flops 2000000000 | bytes 4194304 | tf_op jit(solution)/shard_map/upward/pallas_call | solution.py:130
  13.4 0.0 copy-done
  13.4 0.0 copy-start.6
  13.5 0.1 copy.18.table_ref
  13.6 2.4 %adjoint.1.adjoint_hbm = bf16[8,256,256]{2,1,0:T(8,128)(2,1)} custom-call(bf16[8,2,128,128]{3,2,1,0:T(8,128)(2,1)} %rad_ref.1), custom_call_target="tpu_custom_call" | custom-call | flops 1000000 | bytes 2097152 | tf_op jit(solution)/shard_map/adjoint/pallas_call | solution.py:356
  16.0 0.0 collective-permute-done
  16.0 0.1 copy.17
  16.2 0.1 copy.16
  16.4 1.1 %coupling.1.lines_hbm = f32[2,32,512]{2,1,0:T(8,128)S(1)} custom-call(s32[512,2]{1,0:T(8,128)S(1)} %broadcast_select_fusion.lists_ref, s32[1]{0:T(128)} %constant.11.clone.1.base_ref, bf16[316,32]{1,0:T(8,128)(2,1)S(1)} %copy.18.table_ref), custom_call_target="tpu_custom_call" | custom-call | flops 200000000 | bytes 2097152 | tf_op jit(solution)/shard_map/coupling/pallas_call | solution.py:178
  17.4 0.7 copy-done.3
  18.1 0.0 copy-done.6
  18.1 27.1 %all_to_all.10.refs_0_ = bf16[32,16,512]{2,1,0:T(8,128)(2,1)S(1)} all-to-all(bf16[32,16,512]{2,1,0:T(8,128)(2,1)S(1)} %copy-done.6), channel_id=1, replica_groups=mesh['box'=2,'theta'=4,'phi'=4] {'box','theta','phi'}, dimensions={0} | all-to-all | bytes 1048576 | tf_op jit(solution)/shard_map/all_to_all | solution.py:444
  45.2 0.0 collective-permute-done.1.refs_4_
  45.2 0.0 copy-done.4
  45.2 1.3 %collective-permute-start.2 = (bf16[8,2,128,256]{3,2,1,0:T(8,128)(2,1)S(1)}, bf16[8,2,128,256]{3,2,1,0:T(8,128)(2,1)}, u32[]{:S(2)}, u32[]{:S(2)}) collective-permute-start(bf16[8,2,128,256]{3,2,1,0:T(8,128)(2,1)S(1)} %copy-done.4), channel_id=1, source_target_pairs={{1,0},{2,1},{3,2},{4,3},{5,4},{6,5},{7,6},{8,7},{9,8},{10,9},{11,1... | collective-permute-start | bytes 3145736 | tf_op jit(solution)/shard_map/ppermute | solution.py:433
  46.5 0.0 copy-start.1
  46.5 0.0 copy-start.2
  46.5 2.5 %translate.1 = bf16[32,16,512]{2,1,0:T(8,128)(2,1)} custom-call(f32[2,32,512]{2,1,0:T(8,128)} %copy-done.3, bf16[32,16,512]{2,1,0:T(8,128)(2,1)S(1)} %all_to_all.10.refs_0_), custom_call_target="tpu_custom_call" | custom-call | flops 1000000000 | bytes 2097152 | tf_op jit(solution)/shard_map/translate/pallas_call | solution.py:233
  49.1 0.0 copy-done.5
  49.1 4.4 %all-to-all-start.1 = ((bf16[32,16,512]{2,1,0:T(8,128)(2,1)}), bf16[32,16,512]{2,1,0:T(8,128)(2,1)S(1)}, u32[]{:S(2)}, u32[]{:S(2)}) async-start(bf16[32,16,512]{2,1,0:T(8,128)(2,1)} %translate.1), calls=%async_computation.1 | async-start | bytes 1048576 | tf_op jit(solution)/shard_map/all_to_all | solution.py:444
  53.5 0.0 copy-done.1
  53.5 7.6 %near_first.1.refs_5_ = f32[8,2,128,256]{3,2,1,0:T(8,128)} custom-call(s32[8,12]{1,0:T(8,128)S(1)} %copy-done.1, s32[8]{0:T(128)S(1)} %copy-done.2, s32[1]{0:T(128)} %bitcast.1.refs_2_, bf16[8,12,2,128,128]{4,3,2,1,0:T(8,128)(2,1)} %refs_3_.3, bf16[8,2,128,256]{3,2,1,0:T(8,128)(2,1)} %copy-done.5, bf16[8,2,128,256]{3,2,1,0:T(8,128)(2,1)} %refs_5_.1), custom_call_target="tpu_custom_call" | custom-call | flops 2000000000 | bytes 8388608 | tf_op jit(solution)/shard_map/near_first/pallas_call | solution.py:328
  61.1 13.0 %collective-permute-done.2.refs_4_ = bf16[8,2,128,256]{3,2,1,0:T(8,128)(2,1)} collective-permute-done((bf16[8,2,128,256]{3,2,1,0:T(8,128)(2,1)S(1)}, bf16[8,2,128,256]{3,2,1,0:T(8,128)(2,1)}, u32[]{:S(2)}, u32[]{:S(2)}) %collective-permute-start.2) | collective-permute-done | bytes 1048608 | tf_op jit(solution)/shard_map/ppermute | solution.py:433
  74.1 6.3 %near_last.1.near_hbm = f32[8,2,128,256]{3,2,1,0:T(8,128)} custom-call(s32[8,12]{1,0:T(8,128)S(1)} %copy-done.1, s32[8]{0:T(128)S(1)} %copy-done.2, s32[1]{0:T(128)} %bitcast.1.refs_2_, bf16[8,12,2,128,128]{4,3,2,1,0:T(8,128)(2,1)} %refs_3_.3, bf16[8,2,128,256]{3,2,1,0:T(8,128)(2,1)} %collective-permute-done.2.refs_4_, f32[8,2,128,256]{3,2,1,0:T(8,128)} %near_first.1.refs_5_), custom_call_target="tpu_custom_call" | custom-call | flops 99999997952 | bytes 8388608 | tf_op jit(solution)/shard_map/near_last/pallas_call | solution.py:328
  80.3 2.5 %all-to-all-done.1.field_ref = bf16[32,16,512]{2,1,0:T(8,128)(2,1)S(1)} async-done(((bf16[32,16,512]{2,1,0:T(8,128)(2,1)}), bf16[32,16,512]{2,1,0:T(8,128)(2,1)S(1)}, u32[]{:S(2)}, u32[]{:S(2)}) %all-to-all-start.1) | async-done | bytes 524320 | tf_op jit(solution)/shard_map/all_to_all | solution.py:444
  82.9 3.9 %downward.1 = f32[8,2,128,256]{3,2,1,0:T(8,128)} custom-call(bf16[32,16,512]{2,1,0:T(8,128)(2,1)S(1)} %all-to-all-done.1.field_ref, bf16[1024,512]{1,0:T(8,128)(2,1)} %constant.30.clone.w_hbm, bf16[8,256,256]{2,1,0:T(8,128)(2,1)} %adjoint.1.adjoint_hbm, f32[8,2,128,256]{3,2,1,0:T(8,128)} %near_last.1.near_hbm), custom_call_target="tpu_custom_call" | custom-call | flops 2000000000 | bytes 7340032 | tf_op jit(solution)/shard_map/downward/pallas_call | solution.py:410
  (8 shorter events, 0.1 us)
Async XLA Ops:
  0.0 13.4 %copy-start = (bf16[316,2,4,8]{0,3,2,1:T(8,128)(2,1)S(1)}, bf16[316,2,4,8]{0,3,2,1:T(8,128)(2,1)}, u32[]{:S(2)}) copy-start(bf16[316,2,4,8]{0,3,2,1:T(8,128)(2,1)} %param.19) | copy-start | bytes 121348
  1.7 14.3 %collective-permute-start = (s32[256,2]{0,1:T(2,128)S(1)}, s32[256,2]{0,1:T(2,128)S(1)}, u32[]{:S(2)}, u32[]{:S(2)}) collective-permute-start(s32[256,2]{0,1:T(2,128)S(1)} %pad_add_fusion.1), channel_id=1, source_target_pairs={{0,16},{16,0},{1,17},{17,1},{2,18},{18,2},{3,19},{19,3},{4,20},{20... | collective-permute-start | bytes 6152 | tf_op jit(solution)/shard_map/ppermute | solution.py:455
  4.7 40.6 %collective-permute-start.1 = (bf16[8,2,128,256]{3,2,1,0:T(8,128)(2,1)}, bf16[8,2,128,256]{3,2,1,0:T(8,128)(2,1)S(1)}, u32[]{:S(2)}, u32[]{:S(2)}) collective-permute-start(bf16[8,2,128,256]{3,2,1,0:T(8,128)(2,1)} %refs_5_.1), channel_id=1, source_target_pairs={{0,1},{1,2},{2,3},{3,4},{4,5},{5,6},{6,7},{7,8},{8,9},{9,10},{10,1... | collective-permute-start | bytes 3145736 | tf_op jit(solution)/shard_map/ppermute | solution.py:433
  13.4 4.6 %copy-start.6 = (bf16[32,16,512]{2,1,0:T(8,128)(2,1)S(1)}, bf16[32,16,512]{2,1,0:T(8,128)(2,1)}, u32[]{:S(2)}) copy-start(bf16[32,16,512]{2,1,0:T(8,128)(2,1)} %upward.1) | copy-start | bytes 1572868
  13.6 31.6 %copy-start.4 = (bf16[8,2,128,256]{3,2,1,0:T(8,128)(2,1)S(1)}, bf16[8,2,128,256]{3,2,1,0:T(8,128)(2,1)}, u32[]{:S(2)}) copy-start(bf16[8,2,128,256]{3,2,1,0:T(8,128)(2,1)} %refs_5_.1) | copy-start | bytes 3145732
  17.4 0.7 copy-start.3
  45.2 3.8 %copy-start.5 = (bf16[8,2,128,256]{3,2,1,0:T(8,128)(2,1)}, bf16[8,2,128,256]{3,2,1,0:T(8,128)(2,1)S(1)}, u32[]{:S(2)}) copy-start(bf16[8,2,128,256]{3,2,1,0:T(8,128)(2,1)S(1)} %collective-permute-done.1.refs_4_) | copy-start | bytes 3145732
  45.2 28.9 %collective-permute-start.2 = (bf16[8,2,128,256]{3,2,1,0:T(8,128)(2,1)S(1)}, bf16[8,2,128,256]{3,2,1,0:T(8,128)(2,1)}, u32[]{:S(2)}, u32[]{:S(2)}) collective-permute-start(bf16[8,2,128,256]{3,2,1,0:T(8,128)(2,1)S(1)} %copy-done.4), channel_id=1, source_target_pairs={{1,0},{2,1},{3,2},{4,3},{5,4},{6,5},{7,6},{8,7},{9,8},{10,9},{11,1... | collective-permute-start | bytes 3145736 | tf_op jit(solution)/shard_map/ppermute | solution.py:433
  46.5 7.0 %copy-start.1 = (s32[8,12]{1,0:T(8,128)S(1)}, s32[8,12]{1,0:T(8,128)}, u32[]{:S(2)}) copy-start(s32[8,12]{1,0:T(8,128)} %refs_0_.3) | copy-start | bytes 1156
  46.5 7.0 %copy-start.2 = (s32[8]{0:T(128)S(1)}, s32[8]{0:T(128)}, u32[]{:S(2)}) copy-start(s32[8]{0:T(128)} %refs_1_.3) | copy-start | bytes 100
  49.1 33.8 %all-to-all-start.1 = ((bf16[32,16,512]{2,1,0:T(8,128)(2,1)}), bf16[32,16,512]{2,1,0:T(8,128)(2,1)S(1)}, u32[]{:S(2)}, u32[]{:S(2)}) async-start(bf16[32,16,512]{2,1,0:T(8,128)(2,1)} %translate.1), calls=%async_computation.1 | async-start | bytes 1048576 | tf_op jit(solution)/shard_map/all_to_all | solution.py:444

commit v5 on v4

--- a/solution.py
+++ b/solution.py
@@ -484,18 +484,19 @@
     spread = upward(coeffs, radiation, up_weights, shares * per_group)
     radiation_adjoint = adjoint(radiation)
     lists = lists_of(partners, vector_ids, pair_count)
+    spread, lists = lax.optimization_barrier((spread, lists))
     lines = translation_lines(lists, translation, shares, per_group)
     spread, lines, radiation_adjoint = lax.optimization_barrier((spread, lines, radiation_adjoint))
     parents = parent_bands(spread, shares)
-    parents, low, late = lax.optimization_barrier((parents, low, coeffs))
+    near = near_field(near_ids, near_count, rank, near_blocks, [low, coeffs], 0)
+    near, late = lax.optimization_barrier((near, coeffs))
     high = shift(late, every, -1)
+    parents, near = lax.optimization_barrier((parents, near))
     sources = [parents]
     if shares < lax.axis_size("box"):
         sources = [shift(parents, "box", 1), parents, shift(parents, "box", -1)]
     incoming = translate(lines, sources)
-    incoming, low = lax.optimization_barrier((incoming, low))
     field = parent_bands(incoming, shares)
-    near = near_field(near_ids, near_count, rank, near_blocks, [low, coeffs], 0)
     near = near_field(near_ids, near_count, rank, near_blocks, [high], 2, near)
     return downward(field, down_weights, radiation_adjoint, near)
 

time: 87.3 us -> 83.6 us (0.958)
  the two profiles are of different devices: /device:TPU:0 before, /device:TPU:17 now
where the time goes in v5:
time: 83.6 us; the launch traced here: 82.9 us
  Pallas kernels  30.6 us (37%)
  waiting for transfers between devices  27.4 us (33%)
  starting transfers between devices  21 us (25%)
  local copies, waits for them, and re-layouts  2.93 us (4%)
    pallas_call x2, Pallas kernels, near_field(): pl.pallas_call(functools.partial(near_kernel, first, count, begun), in_sp...  15.5 us
    all_to_all x2, waiting for transfers between devices, parent_bands(): return lax.all_to_all(spread, axes, split_axis=0, concat_axis=0, tiled=True)  15.1 us
    all_to_all x2, starting transfers between devices, parent_bands(): return lax.all_to_all(spread, axes, split_axis=0, concat_axis=0, tiled=True)  14.5 us
    ppermute x2, waiting for transfers between devices, shift(): return lax.ppermute(block, axis, pairs)  12.3 us
    pallas_call x1, Pallas kernels, upward(): pl.pallas_call(up_kernel, in_specs=[hbm] * 3, out_specs=hbm, out_shape=pl...  5.26 us
    ppermute x2, starting transfers between devices, shift(): return lax.ppermute(block, axis, pairs)  5.25 us
    pallas_call x1, Pallas kernels, downward(): pl.pallas_call(down_kernel, in_specs=[pl.BlockSpec(memory_space=pl.ANY)]...  3.93 us
    pallas_call x1, Pallas kernels, translate(): pl.pallas_call(translate_kernel, in_specs=[hbm] + [anywhere] * len(source...  2.49 us
  transfers between devices with their start and end apart: 5, of which 4 were waited for; matrix products, arithmetic and copies ran while one was open for 3% of the time, Pallas kernels for 32%

profile of v5, /device:TPU:17, one launch (start us, length us, event | category | flops | bytes accessed | tf_op | source)
XLA Modules:
  0.0 82.9 jit_solution(15306567382083091595)
XLA Ops:
  0.0 0.0 copy-start
  0.0 3.3 %collective-permute-start.1 = (bf16[8,2,128,256]{3,2,1,0:T(8,128)(2,1)}, bf16[8,2,128,256]{3,2,1,0:T(8,128)(2,1)S(1)}, u32[]{:S(2)}, u32[]{:S(2)}) collective-permute-start(bf16[8,2,128,256]{3,2,1,0:T(8,128)(2,1)} %refs_5_.1), channel_id=1, source_target_pairs={{0,1},{1,2},{2,3},{3,4},{4,5},{5,6},{6,7},{7,8},{8,9},{9,10},{10,1... | collective-permute-start | bytes 3145736 | tf_op jit(solution)/shard_map/ppermute | solution.py:433
  3.3 0.8 stack.10
  4.1 0.8 fusion
  4.9 0.1 stack.9
  5.0 5.3 %upward.1 = bf16[32,16,512]{2,1,0:T(8,128)(2,1)} custom-call(bf16[8,2,128,256]{3,2,1,0:T(8,128)(2,1)} %refs_5_.1, bf16[8,2,128,128]{3,2,1,0:T(8,128)(2,1)} %rad_ref.1, bf16[1024,1024]{1,0:T(8,128)(2,1)} %constant.29.clone.w_hbm), custom_call_target="tpu_custom_call" | custom-call | flops 2000000000 | bytes 4194304 | tf_op jit(solution)/shard_map/upward/pallas_call | solution.py:130
  10.2 1.3 %collective-permute-start = (s32[256,2]{0,1:T(2,128)S(1)}, s32[256,2]{0,1:T(2,128)S(1)}, u32[]{:S(2)}, u32[]{:S(2)}) collective-permute-start(s32[256,2]{0,1:T(2,128)S(1)} %pad_add_fusion.2), channel_id=1, source_target_pairs={{0,16},{16,0},{1,17},{17,1},{2,18},{18,2},{3,19},{19,3},{4,20},{20... | collective-permute-start | bytes 6152 | tf_op jit(solution)/shard_map/ppermute | solution.py:455
  11.5 0.0 copy-done
  11.5 0.1 copy.18.table_ref
  11.7 0.0 copy-start.1
  11.7 0.0 copy-start.2
  11.7 2.3 %adjoint.1.adjoint_hbm = bf16[8,256,256]{2,1,0:T(8,128)(2,1)} custom-call(bf16[8,2,128,128]{3,2,1,0:T(8,128)(2,1)} %rad_ref.1), custom_call_target="tpu_custom_call" | custom-call | flops 1000000 | bytes 2097152 | tf_op jit(solution)/shard_map/adjoint/pallas_call | solution.py:356
  14.0 0.0 collective-permute-done
  14.0 0.1 copy.17
  14.1 0.1 copy.16
  14.3 1.1 %coupling.1.lines_hbm = f32[2,32,512]{2,1,0:T(8,128)S(1)} custom-call(s32[512,2]{1,0:T(8,128)S(1)} %broadcast_select_fusion.lists_ref, s32[1]{0:T(128)} %constant.11.clone.1.base_ref, bf16[316,32]{1,0:T(8,128)(2,1)S(1)} %copy.18.table_ref), custom_call_target="tpu_custom_call" | custom-call | flops 200000000 | bytes 2097152 | tf_op jit(solution)/shard_map/coupling/pallas_call | solution.py:178
  15.4 0.6 copy-done.3
  16.1 5.5 %all-to-all-start = ((bf16[32,16,512]{2,1,0:T(8,128)(2,1)}), bf16[32,16,512]{2,1,0:T(8,128)(2,1)S(1)}, u32[]{:S(2)}, u32[]{:S(2)}) async-start(bf16[32,16,512]{2,1,0:T(8,128)(2,1)} %upward.1), calls=%async_computation | async-start | bytes 1048576 | tf_op jit(solution)/shard_map/all_to_all | solution.py:444
  21.5 4.7 %collective-permute-done.1.refs_4_ = bf16[8,2,128,256]{3,2,1,0:T(8,128)(2,1)S(1)} collective-permute-done((bf16[8,2,128,256]{3,2,1,0:T(8,128)(2,1)}, bf16[8,2,128,256]{3,2,1,0:T(8,128)(2,1)S(1)}, u32[]{:S(2)}, u32[]{:S(2)}) %collective-permute-start.1) | collective-permute-done | bytes 1048608 | tf_op jit(solution)/shard_map/ppermute | solution.py:433
  26.3 1.0 %copy-done.5 = bf16[8,2,128,256]{3,2,1,0:T(8,128)(2,1)} copy-done((bf16[8,2,128,256]{3,2,1,0:T(8,128)(2,1)}, bf16[8,2,128,256]{3,2,1,0:T(8,128)(2,1)S(1)}, u32[]{:S(2)}) %copy-start.5) | copy-done | bytes 1048600
  27.2 0.0 copy-done.1
  27.2 0.0 copy-done.2
  27.2 9.3 %near_first.1.refs_5_ = f32[8,2,128,256]{3,2,1,0:T(8,128)} custom-call(s32[8,12]{1,0:T(8,128)S(1)} %copy-done.1, s32[8]{0:T(128)S(1)} %copy-done.2, s32[1]{0:T(128)} %bitcast.1.refs_2_, bf16[8,12,2,128,128]{4,3,2,1,0:T(8,128)(2,1)} %refs_3_.3, bf16[8,2,128,256]{3,2,1,0:T(8,128)(2,1)} %copy-done.5, bf16[8,2,128,256]{3,2,1,0:T(8,128)(2,1)} %refs_5_.1), custom_call_target="tpu_custom_call" | custom-call | flops 2000000000 | bytes 8388608 | tf_op jit(solution)/shard_map/near_first/pallas_call | solution.py:328
  36.5 0.0 copy-done.4
  36.5 1.9 %collective-permute-start.2 = (bf16[8,2,128,256]{3,2,1,0:T(8,128)(2,1)S(1)}, bf16[8,2,128,256]{3,2,1,0:T(8,128)(2,1)}, u32[]{:S(2)}, u32[]{:S(2)}) collective-permute-start(bf16[8,2,128,256]{3,2,1,0:T(8,128)(2,1)S(1)} %copy-done.4), channel_id=1, source_target_pairs={{1,0},{2,1},{3,2},{4,3},{5,4},{6,5},{7,6},{8,7},{9,8},{10,9},{11,1... | collective-permute-start | bytes 3145736 | tf_op jit(solution)/shard_map/ppermute | solution.py:433
  38.4 1.4 %all-to-all-done.refs_0_ = bf16[32,16,512]{2,1,0:T(8,128)(2,1)S(1)} async-done(((bf16[32,16,512]{2,1,0:T(8,128)(2,1)}), bf16[32,16,512]{2,1,0:T(8,128)(2,1)S(1)}, u32[]{:S(2)}, u32[]{:S(2)}) %all-to-all-start) | async-done | bytes 524320 | tf_op jit(solution)/shard_map/all_to_all | solution.py:444
  39.9 2.5 %translate.1 = bf16[32,16,512]{2,1,0:T(8,128)(2,1)} custom-call(f32[2,32,512]{2,1,0:T(8,128)} %copy-done.3, bf16[32,16,512]{2,1,0:T(8,128)(2,1)S(1)} %all-to-all-done.refs_0_), custom_call_target="tpu_custom_call" | custom-call | flops 1000000000 | bytes 2097152 | tf_op jit(solution)/shard_map/translate/pallas_call | solution.py:233
  42.4 9.0 %all-to-all-start.1 = ((bf16[32,16,512]{2,1,0:T(8,128)(2,1)}), bf16[32,16,512]{2,1,0:T(8,128)(2,1)S(1)}, u32[]{:S(2)}, u32[]{:S(2)}) async-start(bf16[32,16,512]{2,1,0:T(8,128)(2,1)} %translate.1), calls=%async_computation.1 | async-start | bytes 1048576 | tf_op jit(solution)/shard_map/all_to_all | solution.py:444
  51.4 7.6 %collective-permute-done.2.refs_4_ = bf16[8,2,128,256]{3,2,1,0:T(8,128)(2,1)} collective-permute-done((bf16[8,2,128,256]{3,2,1,0:T(8,128)(2,1)S(1)}, bf16[8,2,128,256]{3,2,1,0:T(8,128)(2,1)}, u32[]{:S(2)}, u32[]{:S(2)}) %collective-permute-start.2) | collective-permute-done | bytes 1048608 | tf_op jit(solution)/shard_map/ppermute | solution.py:433
  59.0 6.3 %near_last.1.near_hbm = f32[8,2,128,256]{3,2,1,0:T(8,128)} custom-call(s32[8,12]{1,0:T(8,128)S(1)} %copy-done.1, s32[8]{0:T(128)S(1)} %copy-done.2, s32[1]{0:T(128)} %bitcast.1.refs_2_, bf16[8,12,2,128,128]{4,3,2,1,0:T(8,128)(2,1)} %refs_3_.3, bf16[8,2,128,256]{3,2,1,0:T(8,128)(2,1)} %collective-permute-done.2.refs_4_, f32[8,2,128,256]{3,2,1,0:T(8,128)} %near_first.1.refs_5_), custom_call_target="tpu_custom_call" | custom-call | flops 99999997952 | bytes 8388608 | tf_op jit(solution)/shard_map/near_last/pallas_call | solution.py:328
  65.3 13.6 %all-to-all-done.1.field_ref = bf16[32,16,512]{2,1,0:T(8,128)(2,1)S(1)} async-done(((bf16[32,16,512]{2,1,0:T(8,128)(2,1)}), bf16[32,16,512]{2,1,0:T(8,128)(2,1)S(1)}, u32[]{:S(2)}, u32[]{:S(2)}) %all-to-all-start.1) | async-done | bytes 524320 | tf_op jit(solution)/shard_map/all_to_all | solution.py:444
  78.9 3.9 %downward.1 = f32[8,2,128,256]{3,2,1,0:T(8,128)} custom-call(bf16[32,16,512]{2,1,0:T(8,128)(2,1)S(1)} %all-to-all-done.1.field_ref, bf16[1024,512]{1,0:T(8,128)(2,1)} %constant.30.clone.w_hbm, bf16[8,256,256]{2,1,0:T(8,128)(2,1)} %adjoint.1.adjoint_hbm, f32[8,2,128,256]{3,2,1,0:T(8,128)} %near_last.1.near_hbm), custom_call_target="tpu_custom_call" | custom-call | flops 2000000000 | bytes 7340032 | tf_op jit(solution)/shard_map/downward/pallas_call | solution.py:410
  (7 shorter events, 0.1 us)
Async XLA Ops:
  0.0 11.5 %copy-start = (bf16[316,2,4,8]{0,3,2,1:T(8,128)(2,1)S(1)}, bf16[316,2,4,8]{0,3,2,1:T(8,128)(2,1)}, u32[]{:S(2)}) copy-start(bf16[316,2,4,8]{0,3,2,1:T(8,128)(2,1)} %param.19) | copy-start | bytes 121348
  0.0 26.3 %collective-permute-start.1 = (bf16[8,2,128,256]{3,2,1,0:T(8,128)(2,1)}, bf16[8,2,128,256]{3,2,1,0:T(8,128)(2,1)S(1)}, u32[]{:S(2)}, u32[]{:S(2)}) collective-permute-start(bf16[8,2,128,256]{3,2,1,0:T(8,128)(2,1)} %refs_5_.1), channel_id=1, source_target_pairs={{0,1},{1,2},{2,3},{3,4},{4,5},{5,6},{6,7},{7,8},{8,9},{9,10},{10,1... | collective-permute-start | bytes 3145736 | tf_op jit(solution)/shard_map/ppermute | solution.py:433
  10.2 3.7 %collective-permute-start = (s32[256,2]{0,1:T(2,128)S(1)}, s32[256,2]{0,1:T(2,128)S(1)}, u32[]{:S(2)}, u32[]{:S(2)}) collective-permute-start(s32[256,2]{0,1:T(2,128)S(1)} %pad_add_fusion.2), channel_id=1, source_target_pairs={{0,16},{16,0},{1,17},{17,1},{2,18},{18,2},{3,19},{19,3},{4,20},{20... | collective-permute-start | bytes 6152 | tf_op jit(solution)/shard_map/ppermute | solution.py:455
  11.7 15.6 %copy-start.1 = (s32[8,12]{1,0:T(8,128)S(1)}, s32[8,12]{1,0:T(8,128)}, u32[]{:S(2)}) copy-start(s32[8,12]{1,0:T(8,128)} %refs_0_.3) | copy-start | bytes 1156
  11.7 15.6 %copy-start.2 = (s32[8]{0:T(128)S(1)}, s32[8]{0:T(128)}, u32[]{:S(2)}) copy-start(s32[8]{0:T(128)} %refs_1_.3) | copy-start | bytes 100
  15.4 0.7 copy-start.3
  16.1 23.8 %all-to-all-start = ((bf16[32,16,512]{2,1,0:T(8,128)(2,1)}), bf16[32,16,512]{2,1,0:T(8,128)(2,1)S(1)}, u32[]{:S(2)}, u32[]{:S(2)}) async-start(bf16[32,16,512]{2,1,0:T(8,128)(2,1)} %upward.1), calls=%async_computation | async-start | bytes 1048576 | tf_op jit(solution)/shard_map/all_to_all | solution.py:444
  26.3 1.0 %copy-start.5 = (bf16[8,2,128,256]{3,2,1,0:T(8,128)(2,1)}, bf16[8,2,128,256]{3,2,1,0:T(8,128)(2,1)S(1)}, u32[]{:S(2)}) copy-start(bf16[8,2,128,256]{3,2,1,0:T(8,128)(2,1)S(1)} %collective-permute-done.1.refs_4_) | copy-start | bytes 3145732
  27.2 9.3 %copy-start.4 = (bf16[8,2,128,256]{3,2,1,0:T(8,128)(2,1)S(1)}, bf16[8,2,128,256]{3,2,1,0:T(8,128)(2,1)}, u32[]{:S(2)}) copy-start(bf16[8,2,128,256]{3,2,1,0:T(8,128)(2,1)} %refs_5_.1) | copy-start | bytes 3145732
  36.5 22.5 %collective-permute-start.2 = (bf16[8,2,128,256]{3,2,1,0:T(8,128)(2,1)S(1)}, bf16[8,2,128,256]{3,2,1,0:T(8,128)(2,1)}, u32[]{:S(2)}, u32[]{:S(2)}) collective-permute-start(bf16[8,2,128,256]{3,2,1,0:T(8,128)(2,1)S(1)} %copy-done.4), channel_id=1, source_target_pairs={{1,0},{2,1},{3,2},{4,3},{5,4},{6,5},{7,6},{8,7},{9,8},{10,9},{11,1... | collective-permute-start | bytes 3145736 | tf_op jit(solution)/shard_map/ppermute | solution.py:433
  42.4 36.6 %all-to-all-start.1 = ((bf16[32,16,512]{2,1,0:T(8,128)(2,1)}), bf16[32,16,512]{2,1,0:T(8,128)(2,1)S(1)}, u32[]{:S(2)}, u32[]{:S(2)}) async-start(bf16[32,16,512]{2,1,0:T(8,128)(2,1)} %translate.1), calls=%async_computation.1 | async-start | bytes 1048576 | tf_op jit(solution)/shard_map/all_to_all | solution.py:444

commit v6 on v5

--- a/solution.py
+++ b/solution.py
@@ -339,9 +339,9 @@
         ],
         compiler_params=pltpu.CompilerParams(vmem_limit_bytes=24 * MIB),
         cost_estimate=pl.CostEstimate(
-            flops=10**11 if begun else 2 * 10**9, bytes_accessed=8 * MIB, transcendentals=0
+            flops=10**11 if first == 2 else 2 * 10**9, bytes_accessed=8 * MIB, transcendentals=0
         ),
-        name="near_last" if begun else "near_first",
+        name=("near_low", "near_own", "near_high")[first],
     )(ids, used, rank, *in_hbm(blocks, *sources, *([before] if begun else [])))
 
 
@@ -488,7 +488,8 @@
     lines = translation_lines(lists, translation, shares, per_group)
     spread, lines, radiation_adjoint = lax.optimization_barrier((spread, lines, radiation_adjoint))
     parents = parent_bands(spread, shares)
-    near = near_field(near_ids, near_count, rank, near_blocks, [low, coeffs], 0)
+    near = near_field(near_ids, near_count, rank, near_blocks, [coeffs], 1)
+    near = near_field(near_ids, near_count, rank, near_blocks, [low], 0, near)
     near, late = lax.optimization_barrier((near, coeffs))
     high = shift(late, every, -1)
     parents, near = lax.optimization_barrier((parents, near))

time: 83.6 us -> 82.9 us (level)
  the two profiles are of different devices: /device:TPU:17 before, /device:TPU:0 now
where the time goes in v6:
time: 82.9 us; the launch traced here: 81.8 us
  Pallas kernels  35.3 us (43%)
  waiting for transfers between devices  27.4 us (33%)
  starting transfers between devices  15.2 us (18%)
  local copies, waits for them, and re-layouts  2.93 us (4%)
    pallas_call x3, Pallas kernels, near_field(): pl.pallas_call(functools.partial(near_kernel, first, count, begun), in_sp...  20.3 us
    ppermute x2, waiting for transfers between devices, shift(): return lax.ppermute(block, axis, pairs)  15.3 us
    all_to_all x2, waiting for transfers between devices, parent_bands(): return lax.all_to_all(spread, axes, split_axis=0, concat_axis=0, tiled=True)  12.2 us
    all_to_all x2, starting transfers between devices, parent_bands(): return lax.all_to_all(spread, axes, split_axis=0, concat_axis=0, tiled=True)  7.3 us
    ppermute x2, starting transfers between devices, shift(): return lax.ppermute(block, axis, pairs)  6.41 us
    pallas_call x1, Pallas kernels, upward(): pl.pallas_call(up_kernel, in_specs=[hbm] * 3, out_specs=hbm, out_shape=pl...  5.26 us
    pallas_call x1, Pallas kernels, downward(): pl.pallas_call(down_kernel, in_specs=[pl.BlockSpec(memory_space=pl.ANY)]...  3.93 us
    pallas_call x1, Pallas kernels, translate(): pl.pallas_call(translate_kernel, in_specs=[hbm] + [anywhere] * len(source...  2.49 us
  transfers between devices with their start and end apart: 5, of which 3 were waited for; matrix products, arithmetic and copies ran while one was open for 3% of the time, Pallas kernels for 38%

profile of v6, /device:TPU:0, one launch (start us, length us, event | category | flops | bytes accessed | tf_op | source)
XLA Modules:
  0.0 81.8 jit_solution(5059657849882376535)
XLA Ops:
  0.0 0.0 copy-start
  0.0 5.1 %collective-permute-start.1 = (bf16[8,2,128,256]{3,2,1,0:T(8,128)(2,1)}, bf16[8,2,128,256]{3,2,1,0:T(8,128)(2,1)S(1)}, u32[]{:S(2)}, u32[]{:S(2)}) collective-permute-start(bf16[8,2,128,256]{3,2,1,0:T(8,128)(2,1)} %refs_4_.1), channel_id=1, source_target_pairs={{0,1},{1,2},{2,3},{3,4},{4,5},{5,6},{6,7},{7,8},{8,9},{9,10},{10,1... | collective-permute-start | bytes 3145736 | tf_op jit(solution)/shard_map/ppermute | solution.py:433
  5.1 0.8 fusion
  5.9 0.8 stack.10
  6.7 0.1 stack.9
  6.8 0.0 copy-start.1
  6.8 0.0 copy-start.2
  6.8 5.3 %upward.1 = bf16[32,16,512]{2,1,0:T(8,128)(2,1)} custom-call(bf16[8,2,128,256]{3,2,1,0:T(8,128)(2,1)} %refs_4_.1, bf16[8,2,128,128]{3,2,1,0:T(8,128)(2,1)} %rad_ref.1, bf16[1024,1024]{1,0:T(8,128)(2,1)} %constant.29.clone.w_hbm), custom_call_target="tpu_custom_call" | custom-call | flops 2000000000 | bytes 4194304 | tf_op jit(solution)/shard_map/upward/pallas_call | solution.py:130
  12.1 1.5 %collective-permute-start = (s32[256,2]{0,1:T(2,128)S(1)}, s32[256,2]{0,1:T(2,128)S(1)}, u32[]{:S(2)}, u32[]{:S(2)}) collective-permute-start(s32[256,2]{0,1:T(2,128)S(1)} %pad_add_fusion.2), channel_id=1, source_target_pairs={{0,16},{16,0},{1,17},{17,1},{2,18},{18,2},{3,19},{19,3},{4,20},{20... | collective-permute-start | bytes 6152 | tf_op jit(solution)/shard_map/ppermute | solution.py:455
  13.5 0.0 copy-done.1
  13.5 8.5 %near_own.1.refs_5_ = f32[8,2,128,256]{3,2,1,0:T(8,128)} custom-call(s32[8,12]{1,0:T(8,128)S(1)} %copy-done.1, s32[8]{0:T(128)S(1)} %copy-done.2, s32[1]{0:T(128)} %bitcast.1.refs_2_, bf16[8,12,2,128,128]{4,3,2,1,0:T(8,128)(2,1)} %refs_3_.5, bf16[8,2,128,256]{3,2,1,0:T(8,128)(2,1)} %refs_4_.1), custom_call_target="tpu_custom_call" | custom-call | flops 2000000000 | bytes 8388608 | tf_op jit(solution)/shard_map/near_own/pallas_call | solution.py:328
  22.1 0.1 copy.18.table_ref
  22.2 2.3 %adjoint.1.adjoint_hbm = bf16[8,256,256]{2,1,0:T(8,128)(2,1)} custom-call(bf16[8,2,128,128]{3,2,1,0:T(8,128)(2,1)} %rad_ref.1), custom_call_target="tpu_custom_call" | custom-call | flops 1000000 | bytes 2097152 | tf_op jit(solution)/shard_map/adjoint/pallas_call | solution.py:356
  24.5 0.0 collective-permute-done
  24.5 0.1 copy.17
  24.6 0.1 copy.16
  24.8 1.1 %coupling.1.lines_hbm = f32[2,32,512]{2,1,0:T(8,128)S(1)} custom-call(s32[512,2]{1,0:T(8,128)S(1)} %broadcast_select_fusion.lists_ref, s32[1]{0:T(128)} %constant.11.clone.1.base_ref, bf16[316,32]{1,0:T(8,128)(2,1)S(1)} %copy.18.table_ref), custom_call_target="tpu_custom_call" | custom-call | flops 200000000 | bytes 2097152 | tf_op jit(solution)/shard_map/coupling/pallas_call | solution.py:178
  25.9 0.6 copy-done.3
  26.6 3.2 %all-to-all-start = ((bf16[32,16,512]{2,1,0:T(8,128)(2,1)}), bf16[32,16,512]{2,1,0:T(8,128)(2,1)S(1)}, u32[]{:S(2)}, u32[]{:S(2)}) async-start(bf16[32,16,512]{2,1,0:T(8,128)(2,1)} %upward.1), calls=%async_computation | async-start | bytes 1048576 | tf_op jit(solution)/shard_map/all_to_all | solution.py:444
  29.8 0.0 copy-start.4
  29.8 0.0 collective-permute-done.1.refs_4_
  29.8 0.0 copy-start.5
  29.8 1.0 %copy-done.5 = bf16[8,2,128,256]{3,2,1,0:T(8,128)(2,1)} copy-done((bf16[8,2,128,256]{3,2,1,0:T(8,128)(2,1)}, bf16[8,2,128,256]{3,2,1,0:T(8,128)(2,1)S(1)}, u32[]{:S(2)}) %copy-start.5) | copy-done | bytes 1048600
  30.8 5.6 %near_low.1.refs_5_ = f32[8,2,128,256]{3,2,1,0:T(8,128)} custom-call(s32[8,12]{1,0:T(8,128)S(1)} %copy-done.1, s32[8]{0:T(128)S(1)} %copy-done.2, s32[1]{0:T(128)} %bitcast.1.refs_2_, bf16[8,12,2,128,128]{4,3,2,1,0:T(8,128)(2,1)} %refs_3_.5, bf16[8,2,128,256]{3,2,1,0:T(8,128)(2,1)} %copy-done.5, f32[8,2,128,256]{3,2,1,0:T(8,128)} %near_own.1.refs_5_), custom_call_target="tpu_custom_call" | custom-call | flops 2000000000 | bytes 8388608 | tf_op jit(solution)/shard_map/near_low/pallas_call | solution.py:328
  36.4 1.3 %collective-permute-start.2 = (bf16[8,2,128,256]{3,2,1,0:T(8,128)(2,1)S(1)}, bf16[8,2,128,256]{3,2,1,0:T(8,128)(2,1)}, u32[]{:S(2)}, u32[]{:S(2)}) collective-permute-start(bf16[8,2,128,256]{3,2,1,0:T(8,128)(2,1)S(1)} %copy-done.4), channel_id=1, source_target_pairs={{1,0},{2,1},{3,2},{4,3},{5,4},{6,5},{7,6},{8,7},{9,8},{10,9},{11,1... | collective-permute-start | bytes 3145736 | tf_op jit(solution)/shard_map/ppermute | solution.py:433
  37.7 6.5 %all-to-all-done.refs_0_ = bf16[32,16,512]{2,1,0:T(8,128)(2,1)S(1)} async-done(((bf16[32,16,512]{2,1,0:T(8,128)(2,1)}), bf16[32,16,512]{2,1,0:T(8,128)(2,1)S(1)}, u32[]{:S(2)}, u32[]{:S(2)}) %all-to-all-start) | async-done | bytes 524320 | tf_op jit(solution)/shard_map/all_to_all | solution.py:444
  44.2 2.5 %translate.1 = bf16[32,16,512]{2,1,0:T(8,128)(2,1)} custom-call(f32[2,32,512]{2,1,0:T(8,128)} %copy-done.3, bf16[32,16,512]{2,1,0:T(8,128)(2,1)S(1)} %all-to-all-done.refs_0_), custom_call_target="tpu_custom_call" | custom-call | flops 1000000000 | bytes 2097152 | tf_op jit(solution)/shard_map/translate/pallas_call | solution.py:233
  46.7 4.1 %all-to-all-start.1 = ((bf16[32,16,512]{2,1,0:T(8,128)(2,1)}), bf16[32,16,512]{2,1,0:T(8,128)(2,1)S(1)}, u32[]{:S(2)}, u32[]{:S(2)}) async-start(bf16[32,16,512]{2,1,0:T(8,128)(2,1)} %translate.1), calls=%async_computation.1 | async-start | bytes 1048576 | tf_op jit(solution)/shard_map/all_to_all | solution.py:444
  50.8 15.3 %collective-permute-done.2.refs_4_ = bf16[8,2,128,256]{3,2,1,0:T(8,128)(2,1)} collective-permute-done((bf16[8,2,128,256]{3,2,1,0:T(8,128)(2,1)S(1)}, bf16[8,2,128,256]{3,2,1,0:T(8,128)(2,1)}, u32[]{:S(2)}, u32[]{:S(2)}) %collective-permute-start.2) | collective-permute-done | bytes 1048608 | tf_op jit(solution)/shard_map/ppermute | solution.py:433
  66.0 6.2 %near_high.1.near_hbm = f32[8,2,128,256]{3,2,1,0:T(8,128)} custom-call(s32[8,12]{1,0:T(8,128)S(1)} %copy-done.1, s32[8]{0:T(128)S(1)} %copy-done.2, s32[1]{0:T(128)} %bitcast.1.refs_2_, bf16[8,12,2,128,128]{4,3,2,1,0:T(8,128)(2,1)} %refs_3_.5, bf16[8,2,128,256]{3,2,1,0:T(8,128)(2,1)} %collective-permute-done.2.refs_4_, f32[8,2,128,256]{3,2,1,0:T(8,128)} %near_low.1.refs_5_), custom_call_target="tpu_custom_call" | custom-call | flops 99999997952 | bytes 8388608 | tf_op jit(solution)/shard_map/near_high/pallas_call | solution.py:328
  72.2 5.7 %all-to-all-done.1.field_ref = bf16[32,16,512]{2,1,0:T(8,128)(2,1)S(1)} async-done(((bf16[32,16,512]{2,1,0:T(8,128)(2,1)}), bf16[32,16,512]{2,1,0:T(8,128)(2,1)S(1)}, u32[]{:S(2)}, u32[]{:S(2)}) %all-to-all-start.1) | async-done | bytes 524320 | tf_op jit(solution)/shard_map/all_to_all | solution.py:444
  77.9 3.9 %downward.1 = f32[8,2,128,256]{3,2,1,0:T(8,128)} custom-call(bf16[32,16,512]{2,1,0:T(8,128)(2,1)S(1)} %all-to-all-done.1.field_ref, bf16[1024,512]{1,0:T(8,128)(2,1)} %constant.30.clone.w_hbm, bf16[8,256,256]{2,1,0:T(8,128)(2,1)} %adjoint.1.adjoint_hbm, f32[8,2,128,256]{3,2,1,0:T(8,128)} %near_high.1.near_hbm), custom_call_target="tpu_custom_call" | custom-call | flops 2000000000 | bytes 7340032 | tf_op jit(solution)/shard_map/downward/pallas_call | solution.py:410
  (8 shorter events, 0.1 us)
Async XLA Ops:
  0.0 22.1 %copy-start = (bf16[316,2,4,8]{0,3,2,1:T(8,128)(2,1)S(1)}, bf16[316,2,4,8]{0,3,2,1:T(8,128)(2,1)}, u32[]{:S(2)}) copy-start(bf16[316,2,4,8]{0,3,2,1:T(8,128)(2,1)} %param.19) | copy-start | bytes 121348
  0.0 29.8 %collective-permute-start.1 = (bf16[8,2,128,256]{3,2,1,0:T(8,128)(2,1)}, bf16[8,2,128,256]{3,2,1,0:T(8,128)(2,1)S(1)}, u32[]{:S(2)}, u32[]{:S(2)}) collective-permute-start(bf16[8,2,128,256]{3,2,1,0:T(8,128)(2,1)} %refs_4_.1), channel_id=1, source_target_pairs={{0,1},{1,2},{2,3},{3,4},{4,5},{5,6},{6,7},{7,8},{8,9},{9,10},{10,1... | collective-permute-start | bytes 3145736 | tf_op jit(solution)/shard_map/ppermute | solution.py:433
  6.8 6.8 %copy-start.1 = (s32[8,12]{1,0:T(8,128)S(1)}, s32[8,12]{1,0:T(8,128)}, u32[]{:S(2)}) copy-start(s32[8,12]{1,0:T(8,128)} %refs_0_.5) | copy-start | bytes 1156
  6.8 6.8 %copy-start.2 = (s32[8]{0:T(128)S(1)}, s32[8]{0:T(128)}, u32[]{:S(2)}) copy-start(s32[8]{0:T(128)} %refs_1_.5) | copy-start | bytes 100
  12.1 12.4 %collective-permute-start = (s32[256,2]{0,1:T(2,128)S(1)}, s32[256,2]{0,1:T(2,128)S(1)}, u32[]{:S(2)}, u32[]{:S(2)}) collective-permute-start(s32[256,2]{0,1:T(2,128)S(1)} %pad_add_fusion.2), channel_id=1, source_target_pairs={{0,16},{16,0},{1,17},{17,1},{2,18},{18,2},{3,19},{19,3},{4,20},{20... | collective-permute-start | bytes 6152 | tf_op jit(solution)/shard_map/ppermute | solution.py:455
  25.9 0.7 copy-start.3
  26.6 17.6 %all-to-all-start = ((bf16[32,16,512]{2,1,0:T(8,128)(2,1)}), bf16[32,16,512]{2,1,0:T(8,128)(2,1)S(1)}, u32[]{:S(2)}, u32[]{:S(2)}) async-start(bf16[32,16,512]{2,1,0:T(8,128)(2,1)} %upward.1), calls=%async_computation | async-start | bytes 1048576 | tf_op jit(solution)/shard_map/all_to_all | solution.py:444
  29.8 6.6 %copy-start.4 = (bf16[8,2,128,256]{3,2,1,0:T(8,128)(2,1)S(1)}, bf16[8,2,128,256]{3,2,1,0:T(8,128)(2,1)}, u32[]{:S(2)}) copy-start(bf16[8,2,128,256]{3,2,1,0:T(8,128)(2,1)} %refs_4_.1) | copy-start | bytes 3145732
  29.8 1.0 %copy-start.5 = (bf16[8,2,128,256]{3,2,1,0:T(8,128)(2,1)}, bf16[8,2,128,256]{3,2,1,0:T(8,128)(2,1)S(1)}, u32[]{:S(2)}) copy-start(bf16[8,2,128,256]{3,2,1,0:T(8,128)(2,1)S(1)} %collective-permute-done.1.refs_4_) | copy-start | bytes 3145732
  36.4 29.6 %collective-permute-start.2 = (bf16[8,2,128,256]{3,2,1,0:T(8,128)(2,1)S(1)}, bf16[8,2,128,256]{3,2,1,0:T(8,128)(2,1)}, u32[]{:S(2)}, u32[]{:S(2)}) collective-permute-start(bf16[8,2,128,256]{3,2,1,0:T(8,128)(2,1)S(1)} %copy-done.4), channel_id=1, source_target_pairs={{1,0},{2,1},{3,2},{4,3},{5,4},{6,5},{7,6},{8,7},{9,8},{10,9},{11,1... | collective-permute-start | bytes 3145736 | tf_op jit(solution)/shard_map/ppermute | solution.py:433
  46.7 31.2 %all-to-all-start.1 = ((bf16[32,16,512]{2,1,0:T(8,128)(2,1)}), bf16[32,16,512]{2,1,0:T(8,128)(2,1)S(1)}, u32[]{:S(2)}, u32[]{:S(2)}) async-start(bf16[32,16,512]{2,1,0:T(8,128)(2,1)} %translate.1), calls=%async_computation.1 | async-start | bytes 1048576 | tf_op jit(solution)/shard_map/all_to_all | solution.py:444

commit v7 on v6

--- a/solution.py
+++ b/solution.py
@@ -77,18 +77,16 @@
     return jnp.dot(a, b, preferred_element_type=F32)
 
 
-def complex_rows(real, imag):
-    return jnp.concatenate(
-        [
-            jnp.concatenate([real, -imag], axis=1),
-            jnp.concatenate([imag, real], axis=1),
-        ],
-        axis=0,
-    )
+def side_by_side(real, imag):
+    return jnp.concatenate([real, imag], axis=1)
+
+
+def complex_columns(real, imag):
+    return jnp.concatenate([side_by_side(real, imag), side_by_side(-imag, real)], axis=0)
 
 
 def up_kernel(x_hbm, rad_hbm, w_hbm, out_hbm, x_ref, rad_ref, w_ref, right, result, sems):
-    boxes, _, basis, rhs = x_ref.shape
+    boxes, _, _, rhs = x_ref.shape
     points = rad_ref.shape[2]
     copies = [
         pltpu.make_async_copy(source, target, sems.at[place])
@@ -102,14 +100,13 @@
     copies[1].wait()
     half = boxes // 2
     for octant in range(boxes):
-        left = complex_rows(rad_ref[octant, 0], rad_ref[octant, 1])
-        pattern = dot(left, x_ref[octant].reshape(2 * basis, rhs)).astype(BF16)
-        real, imag = pattern[:points], pattern[points:]
-        straight = jnp.concatenate([real, imag], axis=1)
+        left = side_by_side(rad_ref[octant, 0], rad_ref[octant, 1])
+        straight = dot(left, complex_columns(x_ref[octant, 0], x_ref[octant, 1])).astype(BF16)
+        real, imag = straight[:, :rhs], straight[:, rhs:]
         if octant < half:
-            swapped = jnp.concatenate([-imag, real], axis=1)
+            swapped = side_by_side(-imag, real)
         else:
-            swapped = jnp.concatenate([imag, -real], axis=1)
+            swapped = side_by_side(imag, -real)
         place = octant if octant < half else boxes - 1 - octant
         start = 2 * place * points
         right[octant // half, start : start + points] = straight
@@ -253,7 +250,7 @@
 def near_kernel(first, count, begun, *refs):
     ids_ref, used_ref, rank_ref, blocks_hbm = refs[:4]
     sources = refs[4 : 4 + count]
-    out_hbm, blocks, held, total_ref, listed, sems = refs[4 + count + begun :]
+    out_hbm, blocks, held, wide, total_ref, listed, sems = refs[4 + count + begun :]
     boxes, slots, _, basis, _ = blocks.shape
     rhs = held.shape[3]
     base = (rank_ref[0] - 1 + first) * boxes
@@ -279,6 +276,12 @@
             result_copy(box, True).start()
     for copy in source_copies:
         copy.wait()
+
+    def widen(place, carry):
+        wide[place] = complex_columns(held[place, 0], held[place, 1])
+        return carry
+
+    lax.fori_loop(0, count * boxes, widen, 0)
 
     def one_box(box, carry):
         total = jnp.int32(0)
@@ -303,10 +306,11 @@
                 if step:
                     real = jnp.where(at < total, real, jnp.zeros_like(real))
                     imag = jnp.where(at < total, imag, jnp.zeros_like(imag))
-                left.append(complex_rows(real, imag))
-                right.append(held[ids_ref[box, slot] - base].reshape(2 * basis, rhs))
+                left.append(side_by_side(real, imag))
+                right.append(wide[ids_ref[box, slot] - base])
             part = dot(jnp.concatenate(left, axis=1), jnp.concatenate(right, axis=0))
-            total_ref[box] += part.reshape(2, basis, rhs)
+            total_ref[box, 0] += part[:, :rhs]
+            total_ref[box, 1] += part[:, rhs:]
             return carry
 
         lax.fori_loop(0, (total + GROUP - 1) // GROUP, group, 0)
@@ -333,6 +337,7 @@
         scratch_shapes=[
             pltpu.VMEM(blocks.shape, BF16),
             pltpu.VMEM((count * boxes, 2, basis, rhs), BF16),
+            pltpu.VMEM((count * boxes, 2 * basis, 2 * rhs), BF16),
             pltpu.VMEM((boxes, 2, basis, rhs), F32),
             pltpu.SMEM((slots + 1,), jnp.int32),
             pltpu.SemaphoreType.DMA((2 * boxes + count,)),
@@ -347,7 +352,7 @@
 
 def adjoint_kernel(rad_ref, out_hbm, held):
     for box in range(rad_ref.shape[0]):
-        held[box] = complex_rows(rad_ref[box, 0], rad_ref[box, 1]).T
+        held[box] = side_by_side(rad_ref[box, 0].T, rad_ref[box, 1].T)
     pltpu.sync_copy(held, out_hbm)
 
 
@@ -357,8 +362,8 @@
         adjoint_kernel,
         in_specs=[pl.BlockSpec(memory_space=pltpu.VMEM)],
         out_specs=pl.BlockSpec(memory_space=pltpu.HBM),
-        scratch_shapes=[pltpu.VMEM((boxes, 2 * basis, 2 * points), BF16)],
-        out_shape=pltpu.HBM((boxes, 2 * basis, 2 * points), BF16),
+        scratch_shapes=[pltpu.VMEM((boxes, basis, 2 * points), BF16)],
+        out_shape=pltpu.HBM((boxes, basis, 2 * points), BF16),
         cost_estimate=pl.CostEstimate(
             flops=10**6, bytes_accessed=2 * MIB, transcendentals=0
         ),
@@ -367,9 +372,9 @@
 
 
 def down_kernel(field_ref, w_hbm, adjoint_hbm, near_hbm, out_hbm, field, w, left, held, sems):
-    boxes, width, _ = left.shape
+    boxes, _, width = left.shape
     points = width // 2
-    basis, rhs = held.shape[2], held.shape[3]
+    rhs = held.shape[3]
     copies = [
         pltpu.make_async_copy(source, target, sems.at[boxes + place])
         for place, (source, target) in enumerate(
@@ -397,8 +402,11 @@
             (boxes - 1 - octant, cos_re - sin_im, cos_im + sin_re),
         )
         for box, real, imag in leaves:
-            leaf = jnp.concatenate([real, imag], axis=0).astype(BF16)
-            held[box] += dot(left[box], leaf).reshape(2, basis, rhs)
+            real, imag = real.astype(BF16), imag.astype(BF16)
+            right = jnp.concatenate([side_by_side(real, imag), side_by_side(imag, -real)], axis=0)
+            far = dot(left[box], right)
+            held[box, 0] += far[:, :rhs]
+            held[box, 1] += far[:, rhs:]
             out_copies[box].start()
     for copy in out_copies:
         copy.wait()
@@ -488,8 +496,7 @@
     lines = translation_lines(lists, translation, shares, per_group)
     spread, lines, radiation_adjoint = lax.optimization_barrier((spread, lines, radiation_adjoint))
     parents = parent_bands(spread, shares)
-    near = near_field(near_ids, near_count, rank, near_blocks, [coeffs], 1)
-    near = near_field(near_ids, near_count, rank, near_blocks, [low], 0, near)
+    near = near_field(near_ids, near_count, rank, near_blocks, [low], 0)
     near, late = lax.optimization_barrier((near, coeffs))
     high = shift(late, every, -1)
     parents, near = lax.optimization_barrier((parents, near))
@@ -497,7 +504,9 @@
     if shares < lax.axis_size("box"):
         sources = [shift(parents, "box", 1), parents, shift(parents, "box", -1)]
     incoming = translate(lines, sources)
+    incoming, near = lax.optimization_barrier((incoming, near))
     field = parent_bands(incoming, shares)
+    near = near_field(near_ids, near_count, rank, near_blocks, [coeffs], 1, near)
     near = near_field(near_ids, near_count, rank, near_blocks, [high], 2, near)
     return downward(field, down_weights, radiation_adjoint, near)
 

time: 82.9 us -> 81.2 us (0.979)
  the two profiles are of different devices: /device:TPU:0 before, /device:TPU:12 now
where the time goes in v7:
time: 81.2 us; the launch traced here: 80.7 us
  Pallas kernels  34.5 us (42%)
  waiting for transfers between devices  22.5 us (28%)
  starting transfers between devices  19.8 us (24%)
  local copies, waits for them, and re-layouts  2.92 us (4%)
  other arithmetic  0.82 us (1%)
    ppermute x2, waiting for transfers between devices, shift(): return lax.ppermute(block, axis, pairs)  22.3 us
    pallas_call x3, Pallas kernels, near_field(): pl.pallas_call(functools.partial(near_kernel, first, count, begun), in_sp...  19.8 us
    all_to_all x2, starting transfers between devices, parent_bands(): return lax.all_to_all(spread, axes, split_axis=0, concat_axis=0, tiled=True)  10.9 us
    ppermute x2, starting transfers between devices, shift(): return lax.ppermute(block, axis, pairs)  7.29 us
    pallas_call x1, Pallas kernels, upward(): pl.pallas_call(up_kernel, in_specs=[hbm] * 3, out_specs=hbm, out_shape=pl...  5.26 us
    pallas_call x1, Pallas kernels, downward(): pl.pallas_call(down_kernel, in_specs=[pl.BlockSpec(memory_space=pl.ANY)]...  3.75 us
    pallas_call x1, Pallas kernels, translate(): pl.pallas_call(translate_kernel, in_specs=[hbm] + [anywhere] * len(source...  2.49 us
    pallas_call x1, Pallas kernels, adjoint(): pl.pallas_call(adjoint_kernel, in_specs=[pl.BlockSpec(memory_space=pltpu....  2.08 us
  transfers between devices with their start and end apart: 5, of which 3 were waited for; matrix products, arithmetic and copies ran while one was open for 3% of the time, Pallas kernels for 38%

profile of v7, /device:TPU:12, one launch (start us, length us, event | category | flops | bytes accessed | tf_op | source)
XLA Modules:
  0.0 80.7 jit_solution(2513552002318526191)
XLA Ops:
  0.0 0.0 copy-start
  0.0 3.6 %collective-permute-start.1 = (bf16[8,2,128,256]{3,2,1,0:T(8,128)(2,1)}, bf16[8,2,128,256]{3,2,1,0:T(8,128)(2,1)S(1)}, u32[]{:S(2)}, u32[]{:S(2)}) collective-permute-start(bf16[8,2,128,256]{3,2,1,0:T(8,128)(2,1)} %refs_4_.1), channel_id=1, source_target_pairs={{0,1},{1,2},{2,3},{3,4},{4,5},{5,6},{6,7},{7,8},{8,9},{9,10},{10,1... | collective-permute-start | bytes 3145736 | tf_op jit(solution)/shard_map/ppermute | solution.py:441
  3.6 0.8 stack.10
  4.4 0.8 fusion
  5.2 0.1 stack.9
  5.3 5.3 %upward.1 = bf16[32,16,512]{2,1,0:T(8,128)(2,1)} custom-call(bf16[8,2,128,256]{3,2,1,0:T(8,128)(2,1)} %refs_4_.1, bf16[8,2,128,128]{3,2,1,0:T(8,128)(2,1)} %rad_ref.1, bf16[1024,1024]{1,0:T(8,128)(2,1)} %constant.29.clone.w_hbm), custom_call_target="tpu_custom_call" | custom-call | flops 2000000000 | bytes 4194304 | tf_op jit(solution)/shard_map/upward/pallas_call | solution.py:127
  10.5 1.6 %collective-permute-start = (s32[256,2]{0,1:T(2,128)S(1)}, s32[256,2]{0,1:T(2,128)S(1)}, u32[]{:S(2)}, u32[]{:S(2)}) collective-permute-start(s32[256,2]{0,1:T(2,128)S(1)} %pad_add_fusion.2), channel_id=1, source_target_pairs={{0,16},{16,0},{1,17},{17,1},{2,18},{18,2},{3,19},{19,3},{4,20},{20... | collective-permute-start | bytes 6152 | tf_op jit(solution)/shard_map/ppermute | solution.py:463
  12.1 0.0 copy-done
  12.1 0.1 copy.18.table_ref
  12.2 0.0 copy-start.2
  12.2 2.1 %adjoint.1.adjoint_hbm = bf16[8,128,256]{2,1,0:T(8,128)(2,1)} custom-call(bf16[8,2,128,128]{3,2,1,0:T(8,128)(2,1)} %rad_ref.1), custom_call_target="tpu_custom_call" | custom-call | flops 1000000 | bytes 2097152 | tf_op jit(solution)/shard_map/adjoint/pallas_call | solution.py:361
  14.3 0.0 collective-permute-done
  14.3 0.1 copy.17
  14.5 0.1 copy.16
  14.7 1.1 %coupling.1.lines_hbm = f32[2,32,512]{2,1,0:T(8,128)S(1)} custom-call(s32[512,2]{1,0:T(8,128)S(1)} %broadcast_select_fusion.lists_ref, s32[1]{0:T(128)} %constant.11.clone.1.base_ref, bf16[316,32]{1,0:T(8,128)(2,1)S(1)} %copy.18.table_ref), custom_call_target="tpu_custom_call" | custom-call | flops 200000000 | bytes 2097152 | tf_op jit(solution)/shard_map/coupling/pallas_call | solution.py:175
  15.8 0.6 copy-done.3
  16.4 4.8 %all-to-all-start = ((bf16[32,16,512]{2,1,0:T(8,128)(2,1)}), bf16[32,16,512]{2,1,0:T(8,128)(2,1)S(1)}, u32[]{:S(2)}, u32[]{:S(2)}) async-start(bf16[32,16,512]{2,1,0:T(8,128)(2,1)} %upward.1), calls=%async_computation | async-start | bytes 1048576 | tf_op jit(solution)/shard_map/all_to_all | solution.py:452
  21.3 7.8 %collective-permute-done.1.refs_4_ = bf16[8,2,128,256]{3,2,1,0:T(8,128)(2,1)S(1)} collective-permute-done((bf16[8,2,128,256]{3,2,1,0:T(8,128)(2,1)}, bf16[8,2,128,256]{3,2,1,0:T(8,128)(2,1)S(1)}, u32[]{:S(2)}, u32[]{:S(2)}) %collective-permute-start.1) | collective-permute-done | bytes 1048608 | tf_op jit(solution)/shard_map/ppermute | solution.py:441
  29.0 1.0 %copy-done.4 = bf16[8,2,128,256]{3,2,1,0:T(8,128)(2,1)} copy-done((bf16[8,2,128,256]{3,2,1,0:T(8,128)(2,1)}, bf16[8,2,128,256]{3,2,1,0:T(8,128)(2,1)S(1)}, u32[]{:S(2)}) %copy-start.4) | copy-done | bytes 1048600
  30.0 0.0 copy-done.1
  30.0 0.0 copy-done.2
  30.0 6.0 %near_low.1.refs_5_ = f32[8,2,128,256]{3,2,1,0:T(8,128)} custom-call(s32[8,12]{1,0:T(8,128)S(1)} %copy-done.1, s32[8]{0:T(128)S(1)} %copy-done.2, s32[1]{0:T(128)} %bitcast.1.refs_2_, bf16[8,12,2,128,128]{4,3,2,1,0:T(8,128)(2,1)} %refs_3_.5, bf16[8,2,128,256]{3,2,1,0:T(8,128)(2,1)} %copy-done.4), custom_call_target="tpu_custom_call" | custom-call | flops 2000000000 | bytes 8388608 | tf_op jit(solution)/shard_map/near_low/pallas_call | solution.py:332
  36.0 0.0 copy-done.5
  36.1 3.7 %collective-permute-start.2 = (bf16[8,2,128,256]{3,2,1,0:T(8,128)(2,1)S(1)}, bf16[8,2,128,256]{3,2,1,0:T(8,128)(2,1)}, u32[]{:S(2)}, u32[]{:S(2)}) collective-permute-start(bf16[8,2,128,256]{3,2,1,0:T(8,128)(2,1)S(1)} %copy-done.5), channel_id=1, source_target_pairs={{1,0},{2,1},{3,2},{4,3},{5,4},{6,5},{7,6},{8,7},{9,8},{10,9},{11,1... | collective-permute-start | bytes 3145736 | tf_op jit(solution)/shard_map/ppermute | solution.py:441
  39.7 0.2 all-to-all-done.refs_0_
  40.0 2.5 %translate.1 = bf16[32,16,512]{2,1,0:T(8,128)(2,1)} custom-call(f32[2,32,512]{2,1,0:T(8,128)} %copy-done.3, bf16[32,16,512]{2,1,0:T(8,128)(2,1)S(1)} %all-to-all-done.refs_0_), custom_call_target="tpu_custom_call" | custom-call | flops 1000000000 | bytes 2097152 | tf_op jit(solution)/shard_map/translate/pallas_call | solution.py:230
  42.5 6.1 %all-to-all-start.1 = ((bf16[32,16,512]{2,1,0:T(8,128)(2,1)}), bf16[32,16,512]{2,1,0:T(8,128)(2,1)S(1)}, u32[]{:S(2)}, u32[]{:S(2)}) async-start(bf16[32,16,512]{2,1,0:T(8,128)(2,1)} %translate.1), calls=%async_computation.1 | async-start | bytes 1048576 | tf_op jit(solution)/shard_map/all_to_all | solution.py:452
  48.6 7.2 %near_own.1.refs_5_ = f32[8,2,128,256]{3,2,1,0:T(8,128)} custom-call(s32[8,12]{1,0:T(8,128)S(1)} %copy-done.1, s32[8]{0:T(128)S(1)} %copy-done.2, s32[1]{0:T(128)} %bitcast.1.refs_2_, bf16[8,12,2,128,128]{4,3,2,1,0:T(8,128)(2,1)} %refs_3_.5, bf16[8,2,128,256]{3,2,1,0:T(8,128)(2,1)} %refs_4_.1, f32[8,2,128,256]{3,2,1,0:T(8,128)} %near_low.1.refs_5_), custom_call_target="tpu_custom_call" | custom-call | flops 2000000000 | bytes 8388608 | tf_op jit(solution)/shard_map/near_own/pallas_call | solution.py:332
  55.8 14.5 %collective-permute-done.2.refs_4_ = bf16[8,2,128,256]{3,2,1,0:T(8,128)(2,1)} collective-permute-done((bf16[8,2,128,256]{3,2,1,0:T(8,128)(2,1)S(1)}, bf16[8,2,128,256]{3,2,1,0:T(8,128)(2,1)}, u32[]{:S(2)}, u32[]{:S(2)}) %collective-permute-start.2) | collective-permute-done | bytes 1048608 | tf_op jit(solution)/shard_map/ppermute | solution.py:441
  70.4 6.5 %near_high.1.near_hbm = f32[8,2,128,256]{3,2,1,0:T(8,128)} custom-call(s32[8,12]{1,0:T(8,128)S(1)} %copy-done.1, s32[8]{0:T(128)S(1)} %copy-done.2, s32[1]{0:T(128)} %bitcast.1.refs_2_, bf16[8,12,2,128,128]{4,3,2,1,0:T(8,128)(2,1)} %refs_3_.5, bf16[8,2,128,256]{3,2,1,0:T(8,128)(2,1)} %collective-permute-done.2.refs_4_, f32[8,2,128,256]{3,2,1,0:T(8,128)} %near_own.1.refs_5_), custom_call_target="tpu_custom_call" | custom-call | flops 99999997952 | bytes 8388608 | tf_op jit(solution)/shard_map/near_high/pallas_call | solution.py:332
  76.9 0.0 all-to-all-done.1.field_ref
  76.9 3.8 %downward.1 = f32[8,2,128,256]{3,2,1,0:T(8,128)} custom-call(bf16[32,16,512]{2,1,0:T(8,128)(2,1)S(1)} %all-to-all-done.1.field_ref, bf16[1024,512]{1,0:T(8,128)(2,1)} %constant.30.clone.w_hbm, bf16[8,128,256]{2,1,0:T(8,128)(2,1)} %adjoint.1.adjoint_hbm, f32[8,2,128,256]{3,2,1,0:T(8,128)} %near_high.1.near_hbm), custom_call_target="tpu_custom_call" | custom-call | flops 2000000000 | bytes 7340032 | tf_op jit(solution)/shard_map/downward/pallas_call | solution.py:418
  (8 shorter events, 0.1 us)
Async XLA Ops:
  0.0 12.1 %copy-start = (bf16[316,2,4,8]{0,3,2,1:T(8,128)(2,1)S(1)}, bf16[316,2,4,8]{0,3,2,1:T(8,128)(2,1)}, u32[]{:S(2)}) copy-start(bf16[316,2,4,8]{0,3,2,1:T(8,128)(2,1)} %param.19) | copy-start | bytes 121348
  0.0 29.0 %collective-permute-start.1 = (bf16[8,2,128,256]{3,2,1,0:T(8,128)(2,1)}, bf16[8,2,128,256]{3,2,1,0:T(8,128)(2,1)S(1)}, u32[]{:S(2)}, u32[]{:S(2)}) collective-permute-start(bf16[8,2,128,256]{3,2,1,0:T(8,128)(2,1)} %refs_4_.1), channel_id=1, source_target_pairs={{0,1},{1,2},{2,3},{3,4},{4,5},{5,6},{6,7},{7,8},{8,9},{9,10},{10,1... | collective-permute-start | bytes 3145736 | tf_op jit(solution)/shard_map/ppermute | solution.py:441
  10.5 3.8 %collective-permute-start = (s32[256,2]{0,1:T(2,128)S(1)}, s32[256,2]{0,1:T(2,128)S(1)}, u32[]{:S(2)}, u32[]{:S(2)}) collective-permute-start(s32[256,2]{0,1:T(2,128)S(1)} %pad_add_fusion.2), channel_id=1, source_target_pairs={{0,16},{16,0},{1,17},{17,1},{2,18},{18,2},{3,19},{19,3},{4,20},{20... | collective-permute-start | bytes 6152 | tf_op jit(solution)/shard_map/ppermute | solution.py:463
  12.2 17.8 %copy-start.1 = (s32[8,12]{1,0:T(8,128)S(1)}, s32[8,12]{1,0:T(8,128)}, u32[]{:S(2)}) copy-start(s32[8,12]{1,0:T(8,128)} %refs_0_.5) | copy-start | bytes 1156
  12.2 17.8 %copy-start.2 = (s32[8]{0:T(128)S(1)}, s32[8]{0:T(128)}, u32[]{:S(2)}) copy-start(s32[8]{0:T(128)} %refs_1_.5) | copy-start | bytes 100
  15.8 0.7 copy-start.3
  16.4 23.6 %all-to-all-start = ((bf16[32,16,512]{2,1,0:T(8,128)(2,1)}), bf16[32,16,512]{2,1,0:T(8,128)(2,1)S(1)}, u32[]{:S(2)}, u32[]{:S(2)}) async-start(bf16[32,16,512]{2,1,0:T(8,128)(2,1)} %upward.1), calls=%async_computation | async-start | bytes 1048576 | tf_op jit(solution)/shard_map/all_to_all | solution.py:452
  29.0 1.0 %copy-start.4 = (bf16[8,2,128,256]{3,2,1,0:T(8,128)(2,1)}, bf16[8,2,128,256]{3,2,1,0:T(8,128)(2,1)S(1)}, u32[]{:S(2)}) copy-start(bf16[8,2,128,256]{3,2,1,0:T(8,128)(2,1)S(1)} %collective-permute-done.1.refs_4_) | copy-start | bytes 3145732
  30.0 6.0 %copy-start.5 = (bf16[8,2,128,256]{3,2,1,0:T(8,128)(2,1)S(1)}, bf16[8,2,128,256]{3,2,1,0:T(8,128)(2,1)}, u32[]{:S(2)}) copy-start(bf16[8,2,128,256]{3,2,1,0:T(8,128)(2,1)} %refs_4_.1) | copy-start | bytes 3145732
  36.1 34.3 %collective-permute-start.2 = (bf16[8,2,128,256]{3,2,1,0:T(8,128)(2,1)S(1)}, bf16[8,2,128,256]{3,2,1,0:T(8,128)(2,1)}, u32[]{:S(2)}, u32[]{:S(2)}) collective-permute-start(bf16[8,2,128,256]{3,2,1,0:T(8,128)(2,1)S(1)} %copy-done.5), channel_id=1, source_target_pairs={{1,0},{2,1},{3,2},{4,3},{5,4},{6,5},{7,6},{8,7},{9,8},{10,9},{11,1... | collective-permute-start | bytes 3145736 | tf_op jit(solution)/shard_map/ppermute | solution.py:441
  42.5 34.4 %all-to-all-start.1 = ((bf16[32,16,512]{2,1,0:T(8,128)(2,1)}), bf16[32,16,512]{2,1,0:T(8,128)(2,1)S(1)}, u32[]{:S(2)}, u32[]{:S(2)}) async-start(bf16[32,16,512]{2,1,0:T(8,128)(2,1)} %translate.1), calls=%async_computation.1 | async-start | bytes 1048576 | tf_op jit(solution)/shard_map/all_to_all | solution.py:452

commit v8 on v7

--- a/solution.py
+++ b/solution.py
@@ -371,25 +371,32 @@
     )(radiation)
 
 
-def down_kernel(field_ref, w_hbm, adjoint_hbm, near_hbm, out_hbm, field, w, left, held, sems):
+def down_kernel(phi_ref, w_hbm, adjoint_hbm, near_hbm, *refs):
+    bands_ref, received = refs[0], refs[1:-6]
+    out_hbm, field, w, left, held, sems = refs[-6:]
     boxes, _, width = left.shape
     points = width // 2
     rhs = held.shape[3]
+    phi = phi_ref[0]
+    phi_size = field.shape[1]
+    pairs = [(w_hbm, w), (bands_ref.at[:, phi], field.at[:, phi])]
+    for distance, piece in enumerate(received, 1):
+        pairs.append((piece, field.at[:, lax.rem(phi + phi_size - distance, phi_size)]))
+    first = len(pairs)
+    pairs += [(adjoint_hbm, left), (near_hbm, held)]
     copies = [
         pltpu.make_async_copy(source, target, sems.at[boxes + place])
-        for place, (source, target) in enumerate(
-            ((field_ref, field), (w_hbm, w), (adjoint_hbm, left), (near_hbm, held))
-        )
+        for place, (source, target) in enumerate(pairs)
     ]
     out_copies = [
         pltpu.make_async_copy(held.at[box], out_hbm.at[box], sems.at[box]) for box in range(boxes)
     ]
     for copy in copies:
         copy.start()
-    for copy in copies[:2]:
+    for copy in copies[:first]:
         copy.wait()
     mixed = dot(w[...], field[...].reshape(w.shape[1], 2 * rhs))
-    for copy in copies[2:]:
+    for copy in copies[first:]:
         copy.wait()
     for octant in range(boxes // 2):
         start = 2 * octant * points
@@ -412,27 +419,30 @@
         copy.wait()
 
 
-def downward(field, weights, radiation_adjoint, near):
+def downward(phi, bands, received, weights, radiation_adjoint, near):
     boxes = near.shape[0]
+    anywhere = pl.BlockSpec(memory_space=pl.ANY)
     hbm = pl.BlockSpec(memory_space=pltpu.HBM)
     return pl.pallas_call(
         down_kernel,
-        in_specs=[pl.BlockSpec(memory_space=pl.ANY)] + [hbm] * 3,
+        in_specs=[pl.BlockSpec(memory_space=pltpu.SMEM)]
+        + [hbm] * 3
+        + [anywhere] * (1 + len(received)),
         out_specs=hbm,
         out_shape=jax.ShapeDtypeStruct(near.shape, F32),
         scratch_shapes=[
-            pltpu.VMEM(field.shape, BF16),
+            pltpu.VMEM(bands.shape, BF16),
             pltpu.VMEM(weights.shape, BF16),
             pltpu.VMEM(radiation_adjoint.shape, BF16),
             pltpu.VMEM(near.shape, F32),
-            pltpu.SemaphoreType.DMA((boxes + 4,)),
+            pltpu.SemaphoreType.DMA((boxes + 4 + len(received),)),
         ],
         compiler_params=pltpu.CompilerParams(vmem_limit_bytes=32 * MIB),
         cost_estimate=pl.CostEstimate(
             flops=2 * 10**9, bytes_accessed=7 * MIB, transcendentals=0
         ),
         name="downward",
-    )(field, *in_hbm(weights, radiation_adjoint, near))
+    )(phi, *in_hbm(weights, radiation_adjoint, near), bands, *received)
 
 
 def shift(block, axis, step):
@@ -450,6 +460,20 @@
 def parent_bands(spread, shares):
     axes = ("box", "theta", "phi") if shares == lax.axis_size("box") else ("theta", "phi")
     return lax.all_to_all(spread, axes, split_axis=0, concat_axis=0, tiled=True)
+
+
+def staged_bands(incoming, shares):
+    axes = ("box", "theta") if shares == lax.axis_size("box") else ("theta",)
+    phi_size = lax.axis_size("phi")
+    phi = lax.axis_index("phi")
+    bands = incoming.reshape(-1, phi_size, *incoming.shape[1:])
+    bands = lax.all_to_all(bands, axes, split_axis=0, concat_axis=0, tiled=True)
+    received = []
+    for distance in range(1, phi_size):
+        piece = lax.dynamic_index_in_dim(bands, (phi + distance) % phi_size, 1, keepdims=False)
+        ring = [(place, (place + distance) % phi_size) for place in range(phi_size)]
+        received.append(lax.ppermute(piece, "phi", ring))
+    return phi.astype(jnp.int32).reshape(1), bands, received
 
 
 def translation_lines(lists, translation, shares, per_group):
@@ -505,10 +529,10 @@
         sources = [shift(parents, "box", 1), parents, shift(parents, "box", -1)]
     incoming = translate(lines, sources)
     incoming, near = lax.optimization_barrier((incoming, near))
-    field = parent_bands(incoming, shares)
+    phi, bands, received = staged_bands(incoming, shares)
     near = near_field(near_ids, near_count, rank, near_blocks, [coeffs], 1, near)
     near = near_field(near_ids, near_count, rank, near_blocks, [high], 2, near)
-    return downward(field, down_weights, radiation_adjoint, near)
+    return downward(phi, bands, received, down_weights, radiation_adjoint, near)
 
 
 def solution(mesh):

time: 81.2 us -> 79.9 us (0.984)
  waiting for transfers between devices: 22.5 us -> 15.2 us
  starting transfers between devices: 19.8 us -> 26.2 us
    ppermute x0 -> x3, starting transfers between devices: none -> 8.53 us  [staged_bands(): received.append(lax.ppermute(piece, 'phi', ring))]
    ppermute x2, waiting for transfers between devices: 22.3 us -> 14 us  [shift(): return lax.ppermute(block, axis, pairs)]
    all_to_all x2 -> x1, starting transfers between devices: 10.9 us -> 4.84 us  [parent_bands(): return lax.all_to_all(spread, axes, split_axis=0, concat_axis=0, tiled=True)]
    all_to_all x0 -> x1, starting transfers between devices: none -> 4.27 us  [staged_bands(): bands = lax.all_to_all(bands, axes, split_axis=0, concat_axis=0, tiled=True)]
    all_to_all x0 -> x1, waiting for transfers between devices: none -> 1.04 us  [staged_bands(): bands = lax.all_to_all(bands, axes, split_axis=0, concat_axis=0, tiled=True)]
  transfers between devices with their start and end apart: 5 -> 8, of which waited for: 3 -> 4; matrix products, arithmetic and copies ran while one was open for 3% -> 3% of each run, Pallas kernels for 38% -> 38%
where the time goes in v8:
time: 79.9 us; the launch traced here: 79.5 us
  Pallas kernels  34.2 us (43%)
  starting transfers between devices  26.2 us (33%)
  waiting for transfers between devices  15.2 us (19%)
  local copies, waits for them, and re-layouts  2.97 us (4%)
  other arithmetic  0.82 us (1%)
    pallas_call x3, Pallas kernels, near_field(): pl.pallas_call(functools.partial(near_kernel, first, count, begun), in_sp...  19.5 us
    ppermute x2, waiting for transfers between devices, shift(): return lax.ppermute(block, axis, pairs)  14 us
    ppermute x3, starting transfers between devices, staged_bands(): received.append(lax.ppermute(piece, 'phi', ring))  8.53 us
    ppermute x2, starting transfers between devices, shift(): return lax.ppermute(block, axis, pairs)  6.96 us
    pallas_call x1, Pallas kernels, upward(): pl.pallas_call(up_kernel, in_specs=[hbm] * 3, out_specs=hbm, out_shape=pl...  5.25 us
    all_to_all x1, starting transfers between devices, parent_bands(): return lax.all_to_all(spread, axes, split_axis=0, concat_axis=0, tiled=True)  4.84 us
    all_to_all x1, starting transfers between devices, staged_bands(): bands = lax.all_to_all(bands, axes, split_axis=0, concat_axis=0, tiled=True)  4.27 us
    pallas_call x1, Pallas kernels, downward(): pl.pallas_call(down_kernel, in_specs=[pl.BlockSpec(memory_space=pltpu.SME...  3.77 us
  transfers between devices with their start and end apart: 8, of which 4 were waited for; matrix products, arithmetic and copies ran while one was open for 3% of the time, Pallas kernels for 38%

profile of v8, /device:TPU:12, one launch (start us, length us, event | category | flops | bytes accessed | tf_op | source)
XLA Modules:
  0.0 79.5 jit_solution(4373184638824793733)
XLA Ops:
  0.0 3.6 %collective-permute-start.1 = (bf16[8,2,128,256]{3,2,1,0:T(8,128)(2,1)}, bf16[8,2,128,256]{3,2,1,0:T(8,128)(2,1)S(1)}, u32[]{:S(2)}, u32[]{:S(2)}) collective-permute-start(bf16[8,2,128,256]{3,2,1,0:T(8,128)(2,1)} %refs_4_.1), channel_id=1, source_target_pairs={{0,1},{1,2},{2,3},{3,4},{4,5},{5,6},{6,7},{7,8},{8,9},{9,10},{10,1... | collective-permute-start | bytes 3145736 | tf_op jit(solution)/shard_map/ppermute | solution.py:451
  3.6 0.8 stack.10
  4.4 0.8 fusion
  5.2 0.1 stack.9
  5.2 5.3 %upward.1 = bf16[32,16,512]{2,1,0:T(8,128)(2,1)} custom-call(bf16[8,2,128,256]{3,2,1,0:T(8,128)(2,1)} %refs_4_.1, bf16[8,2,128,128]{3,2,1,0:T(8,128)(2,1)} %rad_ref.1, bf16[1024,1024]{1,0:T(8,128)(2,1)} %constant.58.clone.w_hbm), custom_call_target="tpu_custom_call" | custom-call | flops 2000000000 | bytes 4194304 | tf_op jit(solution)/shard_map/upward/pallas_call | solution.py:127
  10.5 1.6 %collective-permute-start = (s32[256,2]{0,1:T(2,128)S(1)}, s32[256,2]{0,1:T(2,128)S(1)}, u32[]{:S(2)}, u32[]{:S(2)}) collective-permute-start(s32[256,2]{0,1:T(2,128)S(1)} %pad_add_fusion.2), channel_id=1, source_target_pairs={{0,16},{16,0},{1,17},{17,1},{2,18},{18,2},{3,19},{19,3},{4,20},{20... | collective-permute-start | bytes 6152 | tf_op jit(solution)/shard_map/ppermute | solution.py:487
  12.1 0.1 copy.18.table_ref
  12.2 0.0 copy-start.2
  12.2 2.1 %adjoint.1.adjoint_hbm = bf16[8,128,256]{2,1,0:T(8,128)(2,1)} custom-call(bf16[8,2,128,128]{3,2,1,0:T(8,128)(2,1)} %rad_ref.1), custom_call_target="tpu_custom_call" | custom-call | flops 1000000 | bytes 2097152 | tf_op jit(solution)/shard_map/adjoint/pallas_call | solution.py:361
  14.3 0.0 collective-permute-done
  14.3 0.1 copy.16
  14.5 0.1 copy.17
  14.7 1.1 %coupling.1.lines_hbm = f32[2,32,512]{2,1,0:T(8,128)S(1)} custom-call(s32[512,2]{1,0:T(8,128)S(1)} %broadcast_select_fusion.lists_ref, s32[1]{0:T(128)} %constant.51.clone.1.base_ref, bf16[316,32]{1,0:T(8,128)(2,1)S(1)} %copy.18.table_ref), custom_call_target="tpu_custom_call" | custom-call | flops 200000000 | bytes 2097152 | tf_op jit(solution)/shard_map/coupling/pallas_call | solution.py:175
  15.7 0.7 copy-done.3
  16.4 4.8 %all-to-all-start = ((bf16[32,16,512]{2,1,0:T(8,128)(2,1)}), bf16[32,16,512]{2,1,0:T(8,128)(2,1)S(1)}, u32[]{:S(2)}, u32[]{:S(2)}) async-start(bf16[32,16,512]{2,1,0:T(8,128)(2,1)} %upward.1), calls=%async_computation | async-start | bytes 1048576 | tf_op jit(solution)/shard_map/all_to_all | solution.py:462
  21.3 7.8 %collective-permute-done.1.refs_4_ = bf16[8,2,128,256]{3,2,1,0:T(8,128)(2,1)S(1)} collective-permute-done((bf16[8,2,128,256]{3,2,1,0:T(8,128)(2,1)}, bf16[8,2,128,256]{3,2,1,0:T(8,128)(2,1)S(1)}, u32[]{:S(2)}, u32[]{:S(2)}) %collective-permute-start.1) | collective-permute-done | bytes 1048608 | tf_op jit(solution)/shard_map/ppermute | solution.py:451
  29.0 1.0 %copy-done.4 = bf16[8,2,128,256]{3,2,1,0:T(8,128)(2,1)} copy-done((bf16[8,2,128,256]{3,2,1,0:T(8,128)(2,1)}, bf16[8,2,128,256]{3,2,1,0:T(8,128)(2,1)S(1)}, u32[]{:S(2)}) %copy-start.4) | copy-done | bytes 1048600
  30.0 6.4 %near_low.1.refs_5_ = f32[8,2,128,256]{3,2,1,0:T(8,128)} custom-call(s32[8,12]{1,0:T(8,128)S(1)} %copy-done.1, s32[8]{0:T(128)S(1)} %copy-done.2, s32[1]{0:T(128)} %bitcast.2.refs_2_, bf16[8,12,2,128,128]{4,3,2,1,0:T(8,128)(2,1)} %refs_3_.5, bf16[8,2,128,256]{3,2,1,0:T(8,128)(2,1)} %copy-done.4), custom_call_target="tpu_custom_call" | custom-call | flops 2000000000 | bytes 8388608 | tf_op jit(solution)/shard_map/near_low/pallas_call | solution.py:332
  36.4 3.4 %collective-permute-start.2 = (bf16[8,2,128,256]{3,2,1,0:T(8,128)(2,1)S(1)}, bf16[8,2,128,256]{3,2,1,0:T(8,128)(2,1)}, u32[]{:S(2)}, u32[]{:S(2)}) collective-permute-start(bf16[8,2,128,256]{3,2,1,0:T(8,128)(2,1)S(1)} %copy-done.5), channel_id=1, source_target_pairs={{1,0},{2,1},{3,2},{4,3},{5,4},{6,5},{7,6},{8,7},{9,8},{10,9},{11,1... | collective-permute-start | bytes 3145736 | tf_op jit(solution)/shard_map/ppermute | solution.py:451
  39.8 0.2 all-to-all-done.refs_0_
  40.0 2.5 %translate.1 = bf16[32,16,512]{2,1,0:T(8,128)(2,1)} custom-call(f32[2,32,512]{2,1,0:T(8,128)} %copy-done.3, bf16[32,16,512]{2,1,0:T(8,128)(2,1)S(1)} %all-to-all-done.refs_0_), custom_call_target="tpu_custom_call" | custom-call | flops 1000000000 | bytes 2097152 | tf_op jit(solution)/shard_map/translate/pallas_call | solution.py:230
  42.5 4.3 %all-to-all-start.1 = ((bf16[8,4,16,512]{3,2,1,0:T(8,128)(2,1)}), bf16[8,4,16,512]{3,2,1,0:T(8,128)(2,1)S(1)}, u32[]{:S(2)}, u32[]{:S(2)}) async-start(bf16[8,4,16,512]{3,2,1,0:T(8,128)(2,1)} %bitcast.10), calls=%async_computation.1 | async-start | bytes 1048576 | tf_op jit(solution)/shard_map/all_to_all | solution.py:470
  46.7 7.2 %near_own.1.refs_5_ = f32[8,2,128,256]{3,2,1,0:T(8,128)} custom-call(s32[8,12]{1,0:T(8,128)S(1)} %copy-done.1, s32[8]{0:T(128)S(1)} %copy-done.2, s32[1]{0:T(128)} %bitcast.2.refs_2_, bf16[8,12,2,128,128]{4,3,2,1,0:T(8,128)(2,1)} %refs_3_.5, bf16[8,2,128,256]{3,2,1,0:T(8,128)(2,1)} %refs_4_.1, f32[8,2,128,256]{3,2,1,0:T(8,128)} %near_low.1.refs_5_), custom_call_target="tpu_custom_call" | custom-call | flops 2000000000 | bytes 8388608 | tf_op jit(solution)/shard_map/near_own/pallas_call | solution.py:332
  54.0 1.0 %all-to-all-done.1.refs_0_ = bf16[8,4,16,512]{3,2,1,0:T(8,128)(2,1)S(1)} async-done(((bf16[8,4,16,512]{3,2,1,0:T(8,128)(2,1)}), bf16[8,4,16,512]{3,2,1,0:T(8,128)(2,1)S(1)}, u32[]{:S(2)}, u32[]{:S(2)}) %all-to-all-start.1) | async-done | bytes 524320 | tf_op jit(solution)/shard_map/all_to_all | solution.py:470
  55.0 0.7 collective-permute-start.3
  55.7 5.9 %collective-permute-start.4 = (bf16[8,16,512]{2,1,0:T(8,128)(2,1)S(1)}, bf16[8,16,512]{2,1,0:T(8,128)(2,1)S(1)}, u32[]{:S(2)}, u32[]{:S(2)}) collective-permute-start(bf16[8,16,512]{2,1,0:T(8,128)(2,1)S(1)} %get-tuple-element.28), channel_id=1, source_target_pairs={{0,2},{1,3},{2,0},{3,1},{4,6},{5,7},{6,4},{7,5},{8,10},{9,11},{10,... | collective-permute-start | bytes 393224 | tf_op jit(solution)/shard_map/ppermute | solution.py:475
  61.6 1.9 %collective-permute-start.5 = (bf16[8,16,512]{2,1,0:T(8,128)(2,1)S(1)}, bf16[8,16,512]{2,1,0:T(8,128)(2,1)S(1)}, u32[]{:S(2)}, u32[]{:S(2)}) collective-permute-start(bf16[8,16,512]{2,1,0:T(8,128)(2,1)S(1)} %get-tuple-element.27), channel_id=1, source_target_pairs={{0,3},{1,0},{2,1},{3,2},{4,7},{5,4},{6,5},{7,6},{8,11},{9,8},{10,9... | collective-permute-start | bytes 393224 | tf_op jit(solution)/shard_map/ppermute | solution.py:475
  63.6 6.2 %collective-permute-done.2.refs_4_ = bf16[8,2,128,256]{3,2,1,0:T(8,128)(2,1)} collective-permute-done((bf16[8,2,128,256]{3,2,1,0:T(8,128)(2,1)S(1)}, bf16[8,2,128,256]{3,2,1,0:T(8,128)(2,1)}, u32[]{:S(2)}, u32[]{:S(2)}) %collective-permute-start.2) | collective-permute-done | bytes 1048608 | tf_op jit(solution)/shard_map/ppermute | solution.py:451
  69.8 5.9 %near_high.1.near_hbm = f32[8,2,128,256]{3,2,1,0:T(8,128)} custom-call(s32[8,12]{1,0:T(8,128)S(1)} %copy-done.1, s32[8]{0:T(128)S(1)} %copy-done.2, s32[1]{0:T(128)} %bitcast.2.refs_2_, bf16[8,12,2,128,128]{4,3,2,1,0:T(8,128)(2,1)} %refs_3_.5, bf16[8,2,128,256]{3,2,1,0:T(8,128)(2,1)} %collective-permute-done.2.refs_4_, f32[8,2,128,256]{3,2,1,0:T(8,128)} %near_own.1.refs_5_), custom_call_target="tpu_custom_call" | custom-call | flops 99999997952 | bytes 8388608 | tf_op jit(solution)/shard_map/near_high/pallas_call | solution.py:332
  75.7 0.0 collective-permute-done.3.refs_1_
  75.7 0.0 collective-permute-done.5.refs_3_
  75.7 3.8 %downward.1 = f32[8,2,128,256]{3,2,1,0:T(8,128)} custom-call(s32[1]{0:T(128)} %bitcast.phi_ref, bf16[1024,512]{1,0:T(8,128)(2,1)} %constant.59.clone.w_hbm, bf16[8,128,256]{2,1,0:T(8,128)(2,1)} %adjoint.1.adjoint_hbm, f32[8,2,128,256]{3,2,1,0:T(8,128)} %near_high.1.near_hbm, bf16[8,4,16,512]{3,2,1,0:T(8,128)(2,1)S(1)} %all-to-all-done.1.refs_0_, ...), custom_call_target="tpu_custom_call" | custom-call | flops 2000000000 | bytes 7340032 | tf_op jit(solution)/shard_map/downward/pallas_call | solution.py:426
  (15 shorter events, 0.1 us)
Async XLA Ops:
  0.0 12.1 %copy-start = (bf16[316,2,4,8]{0,3,2,1:T(8,128)(2,1)S(1)}, bf16[316,2,4,8]{0,3,2,1:T(8,128)(2,1)}, u32[]{:S(2)}) copy-start(bf16[316,2,4,8]{0,3,2,1:T(8,128)(2,1)} %param.19) | copy-start | bytes 121348
  0.0 29.0 %collective-permute-start.1 = (bf16[8,2,128,256]{3,2,1,0:T(8,128)(2,1)}, bf16[8,2,128,256]{3,2,1,0:T(8,128)(2,1)S(1)}, u32[]{:S(2)}, u32[]{:S(2)}) collective-permute-start(bf16[8,2,128,256]{3,2,1,0:T(8,128)(2,1)} %refs_4_.1), channel_id=1, source_target_pairs={{0,1},{1,2},{2,3},{3,4},{4,5},{5,6},{6,7},{7,8},{8,9},{9,10},{10,1... | collective-permute-start | bytes 3145736 | tf_op jit(solution)/shard_map/ppermute | solution.py:451
  10.5 3.8 %collective-permute-start = (s32[256,2]{0,1:T(2,128)S(1)}, s32[256,2]{0,1:T(2,128)S(1)}, u32[]{:S(2)}, u32[]{:S(2)}) collective-permute-start(s32[256,2]{0,1:T(2,128)S(1)} %pad_add_fusion.2), channel_id=1, source_target_pairs={{0,16},{16,0},{1,17},{17,1},{2,18},{18,2},{3,19},{19,3},{4,20},{20... | collective-permute-start | bytes 6152 | tf_op jit(solution)/shard_map/ppermute | solution.py:487
  12.2 17.8 %copy-start.1 = (s32[8,12]{1,0:T(8,128)S(1)}, s32[8,12]{1,0:T(8,128)}, u32[]{:S(2)}) copy-start(s32[8,12]{1,0:T(8,128)} %refs_0_.5) | copy-start | bytes 1156
  12.2 17.8 %copy-start.2 = (s32[8]{0:T(128)S(1)}, s32[8]{0:T(128)}, u32[]{:S(2)}) copy-start(s32[8]{0:T(128)} %refs_1_.5) | copy-start | bytes 100
  15.7 0.7 copy-start.3
  16.4 23.6 %all-to-all-start = ((bf16[32,16,512]{2,1,0:T(8,128)(2,1)}), bf16[32,16,512]{2,1,0:T(8,128)(2,1)S(1)}, u32[]{:S(2)}, u32[]{:S(2)}) async-start(bf16[32,16,512]{2,1,0:T(8,128)(2,1)} %upward.1), calls=%async_computation | async-start | bytes 1048576 | tf_op jit(solution)/shard_map/all_to_all | solution.py:462
  29.0 1.0 %copy-start.4 = (bf16[8,2,128,256]{3,2,1,0:T(8,128)(2,1)}, bf16[8,2,128,256]{3,2,1,0:T(8,128)(2,1)S(1)}, u32[]{:S(2)}) copy-start(bf16[8,2,128,256]{3,2,1,0:T(8,128)(2,1)S(1)} %collective-permute-done.1.refs_4_) | copy-start | bytes 3145732
  30.0 6.4 %copy-start.5 = (bf16[8,2,128,256]{3,2,1,0:T(8,128)(2,1)S(1)}, bf16[8,2,128,256]{3,2,1,0:T(8,128)(2,1)}, u32[]{:S(2)}) copy-start(bf16[8,2,128,256]{3,2,1,0:T(8,128)(2,1)} %refs_4_.1) | copy-start | bytes 3145732
  36.4 33.4 %collective-permute-start.2 = (bf16[8,2,128,256]{3,2,1,0:T(8,128)(2,1)S(1)}, bf16[8,2,128,256]{3,2,1,0:T(8,128)(2,1)}, u32[]{:S(2)}, u32[]{:S(2)}) collective-permute-start(bf16[8,2,128,256]{3,2,1,0:T(8,128)(2,1)S(1)} %copy-done.5), channel_id=1, source_target_pairs={{1,0},{2,1},{3,2},{4,3},{5,4},{6,5},{7,6},{8,7},{9,8},{10,9},{11,1... | collective-permute-start | bytes 3145736 | tf_op jit(solution)/shard_map/ppermute | solution.py:451
  42.5 12.6 %all-to-all-start.1 = ((bf16[8,4,16,512]{3,2,1,0:T(8,128)(2,1)}), bf16[8,4,16,512]{3,2,1,0:T(8,128)(2,1)S(1)}, u32[]{:S(2)}, u32[]{:S(2)}) async-start(bf16[8,4,16,512]{3,2,1,0:T(8,128)(2,1)} %bitcast.10), calls=%async_computation.1 | async-start | bytes 1048576 | tf_op jit(solution)/shard_map/all_to_all | solution.py:470
  55.0 20.7 %collective-permute-start.3 = (bf16[8,16,512]{2,1,0:T(8,128)(2,1)S(1)}, bf16[8,16,512]{2,1,0:T(8,128)(2,1)S(1)}, u32[]{:S(2)}, u32[]{:S(2)}) collective-permute-start(bf16[8,16,512]{2,1,0:T(8,128)(2,1)S(1)} %get-tuple-element.29), channel_id=1, source_target_pairs={{0,1},{1,2},{2,3},{3,0},{4,5},{5,6},{6,7},{7,4},{8,9},{9,10},{10,1... | collective-permute-start | bytes 393224 | tf_op jit(solution)/shard_map/ppermute | solution.py:475
  55.7 20.0 %collective-permute-start.4 = (bf16[8,16,512]{2,1,0:T(8,128)(2,1)S(1)}, bf16[8,16,512]{2,1,0:T(8,128)(2,1)S(1)}, u32[]{:S(2)}, u32[]{:S(2)}) collective-permute-start(bf16[8,16,512]{2,1,0:T(8,128)(2,1)S(1)} %get-tuple-element.28), channel_id=1, source_target_pairs={{0,2},{1,3},{2,0},{3,1},{4,6},{5,7},{6,4},{7,5},{8,10},{9,11},{10,... | collective-permute-start | bytes 393224 | tf_op jit(solution)/shard_map/ppermute | solution.py:475
  61.6 14.1 %collective-permute-start.5 = (bf16[8,16,512]{2,1,0:T(8,128)(2,1)S(1)}, bf16[8,16,512]{2,1,0:T(8,128)(2,1)S(1)}, u32[]{:S(2)}, u32[]{:S(2)}) collective-permute-start(bf16[8,16,512]{2,1,0:T(8,128)(2,1)S(1)} %get-tuple-element.27), channel_id=1, source_target_pairs={{0,3},{1,0},{2,1},{3,2},{4,7},{5,4},{6,5},{7,6},{8,11},{9,8},{10,9... | collective-permute-start | bytes 393224 | tf_op jit(solution)/shard_map/ppermute | solution.py:475

commit v9 on v8

--- a/solution.py
+++ b/solution.py
@@ -247,107 +247,133 @@
     )(*in_hbm(lines), *sources)
 
 
-def near_kernel(first, count, begun, *refs):
-    ids_ref, used_ref, rank_ref, blocks_hbm = refs[:4]
-    sources = refs[4 : 4 + count]
-    out_hbm, blocks, held, wide, total_ref, listed, sems = refs[4 + count + begun :]
-    boxes, slots, _, basis, _ = blocks.shape
-    rhs = held.shape[3]
+def near_kernel(first, begun, kept, *refs):
+    refs = list(refs)
+    ids_ref, used_ref, rank_ref, blocks_hbm, source_hbm = refs[:5]
+    before_hbm = refs[5] if begun else None
+    kept_hbm = refs[5 + begun : 5 + begun + kept]
+    out_ref = refs[5 + begun + kept]
+    kept_refs = refs[6 + begun + kept : 6 + begun + 2 * kept]
+    blocks, held, wide, total_ref, listed, sems = refs[6 + begun + 2 * kept :]
+    boxes, _, basis, rhs = held.shape
+    slots = blocks_hbm.shape[1]
+    most = boxes * slots
     base = (rank_ref[0] - 1 + first) * boxes
-    source_copies = [
-        pltpu.make_async_copy(source, held.at[pl.ds(place * boxes, boxes)], sems.at[boxes + place])
-        for place, source in enumerate(sources)
-    ]
-
-    def block_copy(box):
-        return pltpu.make_async_copy(blocks_hbm.at[box], blocks.at[box], sems.at[box])
-
-    def result_copy(box, inward):
-        place = boxes + count + box
-        if inward:
-            return pltpu.make_async_copy(refs[4 + count].at[box], total_ref.at[box], sems.at[place])
-        return pltpu.make_async_copy(total_ref.at[box], out_hbm.at[box], sems.at[place])
-
-    for copy in source_copies:
+    others = [pltpu.make_async_copy(source_hbm, held, sems.at[most])]
+    if begun:
+        others.append(pltpu.make_async_copy(before_hbm, total_ref, sems.at[most + 1]))
+    for place in range(kept):
+        others.append(
+            pltpu.make_async_copy(kept_hbm[place], kept_refs[place], sems.at[most + 2 + place])
+        )
+    for copy in others:
         copy.start()
+
+    def block_copy(box, slot, place):
+        return pltpu.make_async_copy(blocks_hbm.at[box, slot], blocks.at[place], sems.at[place])
+
+    starts = [jnp.int32(0)]
     for box in range(boxes):
-        block_copy(box).start()
+        place = starts[box]
+        for slot in range(slots):
+            source = ids_ref[box, slot] - base
+            wanted = (slot < used_ref[box]) & (source >= 0) & (source < boxes)
+
+            @pl.when(wanted)
+            def _(box=box, slot=slot, place=place, source=source):
+                listed[place] = source
+                block_copy(box, slot, place).start()
+
+            place += wanted.astype(jnp.int32)
+        starts.append(place)
+    others[0].wait()
+    for place in range(boxes):
+        wide[place] = complex_columns(held[place, 0], held[place, 1])
+
+    def landed(place, carry):
+        block_copy(0, 0, place).wait()
+        return carry
+
+    lax.fori_loop(0, starts[boxes], landed, 0)
+    for copy in others[1:]:
+        copy.wait()
+
+    def group(box, index):
+        left, right = [], []
+        for step in range(GROUP):
+            place = starts[box] + index * GROUP + step
+            valid = place < starts[box + 1]
+            place = jnp.where(valid, place, 0)
+            real, imag = blocks[place, 0], blocks[place, 1]
+            real = jnp.where(valid, real, jnp.zeros_like(real))
+            imag = jnp.where(valid, imag, jnp.zeros_like(imag))
+            left.append(side_by_side(real, imag))
+            right.append(wide[jnp.where(valid, listed[place], 0)])
+        return dot(jnp.concatenate(left, axis=1), jnp.concatenate(right, axis=0))
+
+    for box in range(boxes):
+        part = group(box, 0)
         if begun:
-            result_copy(box, True).start()
-    for copy in source_copies:
-        copy.wait()
-
-    def widen(place, carry):
-        wide[place] = complex_columns(held[place, 0], held[place, 1])
-        return carry
-
-    lax.fori_loop(0, count * boxes, widen, 0)
-
-    def one_box(box, carry):
-        total = jnp.int32(0)
-        used = used_ref[box]
-        for slot in range(slots):
-            place = ids_ref[box, slot] - base
-            listed[total] = jnp.int32(slot)
-            wanted = (slot < used) & (place >= 0) & (place < count * boxes)
-            total += wanted.astype(jnp.int32)
-        block_copy(box).wait()
-        if begun:
-            result_copy(box, True).wait()
+            total_ref[box, 0] += part[:, :rhs]
+            total_ref[box, 1] += part[:, rhs:]
         else:
-            total_ref[box] = jnp.zeros(total_ref.shape[1:], F32)
-
-        def group(index, carry):
-            left, right = [], []
-            for step in range(GROUP):
-                at = index * GROUP + step
-                slot = listed[jnp.minimum(at, total - 1)]
-                real, imag = blocks[box, slot, 0], blocks[box, slot, 1]
-                if step:
-                    real = jnp.where(at < total, real, jnp.zeros_like(real))
-                    imag = jnp.where(at < total, imag, jnp.zeros_like(imag))
-                left.append(side_by_side(real, imag))
-                right.append(wide[ids_ref[box, slot] - base])
-            part = dot(jnp.concatenate(left, axis=1), jnp.concatenate(right, axis=0))
+            total_ref[box, 0] = part[:, :rhs]
+            total_ref[box, 1] = part[:, rhs:]
+    for box in range(boxes):
+
+        def more(index, carry, box=box):
+            part = group(box, index)
             total_ref[box, 0] += part[:, :rhs]
             total_ref[box, 1] += part[:, rhs:]
             return carry
 
-        lax.fori_loop(0, (total + GROUP - 1) // GROUP, group, 0)
-        result_copy(box, False).start()
-        return carry
-
-    lax.fori_loop(0, boxes, one_box, 0)
-    for box in range(boxes):
-        result_copy(box, False).wait()
-
-
-def near_field(ids, used, rank, blocks, sources, first, before=None):
+        lax.fori_loop(1, (starts[box + 1] - starts[box] + GROUP - 1) // GROUP, more, 0)
+    if not kept:
+        pltpu.sync_copy(total_ref, out_ref)
+
+
+def near_field(ids, used, rank, blocks, source, first, before=None, keep=()):
     boxes, slots, _, basis, _ = blocks.shape
-    rhs = sources[0].shape[3]
-    count = len(sources)
-    begun = before is not None
+    rhs = source.shape[3]
+    begun, kept = before is not None, len(keep)
     hbm = pl.BlockSpec(memory_space=pltpu.HBM)
     smem = pl.BlockSpec(memory_space=pltpu.SMEM)
+    vmem = pl.BlockSpec(memory_space=pltpu.VMEM)
+    shape = (boxes, 2, basis, rhs)
+    scratch = [
+        pltpu.VMEM((boxes * slots, *blocks.shape[2:]), BF16),
+        pltpu.VMEM(source.shape, BF16),
+        pltpu.VMEM((boxes, 2 * basis, 2 * rhs), BF16),
+        pltpu.VMEM(shape, F32),
+        pltpu.SMEM((boxes * slots,), jnp.int32),
+        pltpu.SemaphoreType.DMA((boxes * slots + 2 + kept,)),
+    ]
+    kernel = functools.partial(near_kernel, first, begun, kept)
+    if kept:
+        del scratch[3]
+        inner = kernel
+
+        def kernel(*refs):
+            place = 5 + begun + kept
+            inner(*refs[:-2], refs[place], *refs[-2:])
+
     return pl.pallas_call(
-        functools.partial(near_kernel, first, count, begun),
-        in_specs=[smem] * 3 + [hbm] * (1 + count + begun),
-        out_specs=hbm,
-        out_shape=pltpu.HBM((boxes, 2, basis, rhs), F32),
-        scratch_shapes=[
-            pltpu.VMEM(blocks.shape, BF16),
-            pltpu.VMEM((count * boxes, 2, basis, rhs), BF16),
-            pltpu.VMEM((count * boxes, 2 * basis, 2 * rhs), BF16),
-            pltpu.VMEM((boxes, 2, basis, rhs), F32),
-            pltpu.SMEM((slots + 1,), jnp.int32),
-            pltpu.SemaphoreType.DMA((2 * boxes + count,)),
-        ],
-        compiler_params=pltpu.CompilerParams(vmem_limit_bytes=24 * MIB),
+        kernel,
+        in_specs=[smem] * 3 + [hbm] * (2 + begun + kept),
+        out_specs=[vmem] * (1 + kept) if kept else hbm,
+        out_shape=[
+            pltpu.VMEM(shape, F32),
+            *[pltpu.VMEM(array.shape, array.dtype) for array in keep],
+        ]
+        if kept
+        else pltpu.HBM(shape, F32),
+        scratch_shapes=scratch,
+        compiler_params=pltpu.CompilerParams(vmem_limit_bytes=32 * MIB),
         cost_estimate=pl.CostEstimate(
             flops=10**11 if first == 2 else 2 * 10**9, bytes_accessed=8 * MIB, transcendentals=0
         ),
         name=("near_low", "near_own", "near_high")[first],
-    )(ids, used, rank, *in_hbm(blocks, *sources, *([before] if begun else [])))
+    )(ids, used, rank, *in_hbm(blocks, source, *([before] if begun else []), *keep))
 
 
 def adjoint_kernel(rad_ref, out_hbm, held):
@@ -371,19 +397,17 @@
     )(radiation)
 
 
-def down_kernel(phi_ref, w_hbm, adjoint_hbm, near_hbm, *refs):
-    bands_ref, received = refs[0], refs[1:-6]
-    out_hbm, field, w, left, held, sems = refs[-6:]
-    boxes, _, width = left.shape
+def down_kernel(phi_ref, near_ref, w_ref, adjoint_ref, *refs):
+    bands_ref, received = refs[0], refs[1:-4]
+    out_hbm, field, held, sems = refs[-4:]
+    boxes, _, width = adjoint_ref.shape
     points = width // 2
     rhs = held.shape[3]
     phi = phi_ref[0]
     phi_size = field.shape[1]
-    pairs = [(w_hbm, w), (bands_ref.at[:, phi], field.at[:, phi])]
+    pairs = [(bands_ref.at[:, phi], field.at[:, phi])]
     for distance, piece in enumerate(received, 1):
         pairs.append((piece, field.at[:, lax.rem(phi + phi_size - distance, phi_size)]))
-    first = len(pairs)
-    pairs += [(adjoint_hbm, left), (near_hbm, held)]
     copies = [
         pltpu.make_async_copy(source, target, sems.at[boxes + place])
         for place, (source, target) in enumerate(pairs)
@@ -393,11 +417,9 @@
     ]
     for copy in copies:
         copy.start()
-    for copy in copies[:first]:
+    for copy in copies:
         copy.wait()
-    mixed = dot(w[...], field[...].reshape(w.shape[1], 2 * rhs))
-    for copy in copies[first:]:
-        copy.wait()
+    mixed = dot(w_ref[...], field[...].reshape(w_ref.shape[1], 2 * rhs))
     for octant in range(boxes // 2):
         start = 2 * octant * points
         cos_part = mixed[start : start + points]
@@ -411,38 +433,39 @@
         for box, real, imag in leaves:
             real, imag = real.astype(BF16), imag.astype(BF16)
             right = jnp.concatenate([side_by_side(real, imag), side_by_side(imag, -real)], axis=0)
-            far = dot(left[box], right)
-            held[box, 0] += far[:, :rhs]
-            held[box, 1] += far[:, rhs:]
+            far = dot(adjoint_ref[box], right)
+            held[box, 0] = near_ref[box, 0] + far[:, :rhs]
+            held[box, 1] = near_ref[box, 1] + far[:, rhs:]
             out_copies[box].start()
     for copy in out_copies:
         copy.wait()
 
 
-def downward(phi, bands, received, weights, radiation_adjoint, near):
+def downward(phi, bands, received, near, weights, radiation_adjoint):
     boxes = near.shape[0]
     anywhere = pl.BlockSpec(memory_space=pl.ANY)
-    hbm = pl.BlockSpec(memory_space=pltpu.HBM)
+    ready = [
+        pltpu.with_memory_space_constraint(array, pltpu.VMEM)
+        for array in (near, weights, radiation_adjoint)
+    ]
     return pl.pallas_call(
         down_kernel,
         in_specs=[pl.BlockSpec(memory_space=pltpu.SMEM)]
-        + [hbm] * 3
+        + [pl.BlockSpec(memory_space=pltpu.VMEM)] * 3
         + [anywhere] * (1 + len(received)),
-        out_specs=hbm,
+        out_specs=pl.BlockSpec(memory_space=pltpu.HBM),
         out_shape=jax.ShapeDtypeStruct(near.shape, F32),
         scratch_shapes=[
             pltpu.VMEM(bands.shape, BF16),
-            pltpu.VMEM(weights.shape, BF16),
-            pltpu.VMEM(radiation_adjoint.shape, BF16),
             pltpu.VMEM(near.shape, F32),
-            pltpu.SemaphoreType.DMA((boxes + 4 + len(received),)),
+            pltpu.SemaphoreType.DMA((boxes + 1 + len(received),)),
         ],
         compiler_params=pltpu.CompilerParams(vmem_limit_bytes=32 * MIB),
         cost_estimate=pl.CostEstimate(
             flops=2 * 10**9, bytes_accessed=7 * MIB, transcendentals=0
         ),
         name="downward",
-    )(phi, *in_hbm(weights, radiation_adjoint, near), bands, *received)
+    )(phi, *ready, bands, *received)
 
 
 def shift(block, axis, step):
@@ -520,7 +543,8 @@
     lines = translation_lines(lists, translation, shares, per_group)
     spread, lines, radiation_adjoint = lax.optimization_barrier((spread, lines, radiation_adjoint))
     parents = parent_bands(spread, shares)
-    near = near_field(near_ids, near_count, rank, near_blocks, [low], 0)
+    slots = (near_ids, near_count, rank, near_blocks)
+    near = near_field(*slots, low, 0)
     near, late = lax.optimization_barrier((near, coeffs))
     high = shift(late, every, -1)
     parents, near = lax.optimization_barrier((parents, near))
@@ -530,9 +554,9 @@
     incoming = translate(lines, sources)
     incoming, near = lax.optimization_barrier((incoming, near))
     phi, bands, received = staged_bands(incoming, shares)
-    near = near_field(near_ids, near_count, rank, near_blocks, [coeffs], 1, near)
-    near = near_field(near_ids, near_count, rank, near_blocks, [high], 2, near)
-    return downward(phi, bands, received, down_weights, radiation_adjoint, near)
+    near = near_field(*slots, coeffs, 1, near)
+    ready = near_field(*slots, high, 2, near, keep=(down_weights, radiation_adjoint))
+    return downward(phi, bands, received, *ready)
 
 
 def solution(mesh):

time: 79.9 us -> 78.9 us (0.987)
  the two profiles are of different devices: /device:TPU:12 before, /device:TPU:0 now
where the time goes in v9:
time: 78.9 us; the launch traced here: 77.5 us
  Pallas kernels  33.3 us (42%)
  starting transfers between devices  25.2 us (32%)
  waiting for transfers between devices  13.8 us (17%)
  local copies, waits for them, and re-layouts  3.94 us (5%)
  other arithmetic  0.81 us (1%)
    pallas_call x3, Pallas kernels, near_field(): pl.pallas_call(kernel, in_specs=[smem] * 3 + [hbm] * (2 + begun + kept),...  20.2 us
    ppermute x3, starting transfers between devices, staged_bands(): received.append(lax.ppermute(piece, 'phi', ring))  8.01 us
    ppermute x2, starting transfers between devices, shift(): return lax.ppermute(block, axis, pairs)  6.41 us
    ppermute x2, waiting for transfers between devices, shift(): return lax.ppermute(block, axis, pairs)  6.36 us
    all_to_all x1, waiting for transfers between devices, parent_bands(): return lax.all_to_all(spread, axes, split_axis=0, concat_axis=0, tiled=True)  5.66 us
    pallas_call x1, Pallas kernels, upward(): pl.pallas_call(up_kernel, in_specs=[hbm] * 3, out_specs=hbm, out_shape=pl...  5.25 us
    all_to_all x1, starting transfers between devices, parent_bands(): return lax.all_to_all(spread, axes, split_axis=0, concat_axis=0, tiled=True)  4.74 us
    all_to_all x1, starting transfers between devices, staged_bands(): bands = lax.all_to_all(bands, axes, split_axis=0, concat_axis=0, tiled=True)  4.56 us
  transfers between devices with their start and end apart: 8, of which 3 were waited for; matrix products, arithmetic and copies ran while one was open for 3% of the time, Pallas kernels for 40%

profile of v9, /device:TPU:0, one launch (start us, length us, event | category | flops | bytes accessed | tf_op | source)
XLA Modules:
  0.0 77.5 jit_solution(1669961172405968472)
XLA Ops:
  0.0 5.1 %collective-permute-start = (bf16[8,2,128,256]{3,2,1,0:T(8,128)(2,1)}, bf16[8,2,128,256]{3,2,1,0:T(8,128)(2,1)S(1)}, u32[]{:S(2)}, u32[]{:S(2)}) collective-permute-start(bf16[8,2,128,256]{3,2,1,0:T(8,128)(2,1)} %refs_4_.1), channel_id=1, source_target_pairs={{0,1},{1,2},{2,3},{3,4},{4,5},{5,6},{6,7},{7,8},{8,9},{9,10},{10,1... | collective-permute-start | bytes 3145736 | tf_op jit(solution)/shard_map/ppermute | solution.py:474
  5.1 0.8 fusion
  5.9 0.1 stack.9
  6.0 0.8 %stack.10 = s32[256,1]{0,1:T(1,128)S(1)} reshape(s32[16,16]{1,0:T(8,128)} %param.17) | data formatting | bytes 2048 | tf_op jit(solution)/shard_map/stack | solution.py:480
  6.8 5.2 %upward.1 = bf16[32,16,512]{2,1,0:T(8,128)(2,1)} custom-call(bf16[8,2,128,256]{3,2,1,0:T(8,128)(2,1)} %refs_4_.1, bf16[8,2,128,128]{3,2,1,0:T(8,128)(2,1)} %rad_ref.1, bf16[1024,1024]{1,0:T(8,128)(2,1)} %constant.58.clone.w_hbm), custom_call_target="tpu_custom_call" | custom-call | flops 2000000000 | bytes 4194304 | tf_op jit(solution)/shard_map/upward/pallas_call | solution.py:127
  12.0 1.5 %collective-permute-start.2 = (s32[256,2]{0,1:T(2,128)S(1)}, s32[256,2]{0,1:T(2,128)S(1)}, u32[]{:S(2)}, u32[]{:S(2)}) collective-permute-start(s32[256,2]{0,1:T(2,128)S(1)} %pad_add_fusion.2), channel_id=1, source_target_pairs={{0,16},{16,0},{1,17},{17,1},{2,18},{18,2},{3,19},{19,3},{4,20},{20... | collective-permute-start | bytes 6152 | tf_op jit(solution)/shard_map/ppermute | solution.py:510
  13.5 0.1 copy.18.table_ref
  13.7 0.0 copy-start.2
  13.7 2.0 %adjoint.1.refs_7_ = bf16[8,128,256]{2,1,0:T(8,128)(2,1)} custom-call(bf16[8,2,128,128]{3,2,1,0:T(8,128)(2,1)} %rad_ref.1), custom_call_target="tpu_custom_call" | custom-call | flops 1000000 | bytes 2097152 | tf_op jit(solution)/shard_map/adjoint/pallas_call | solution.py:387
  15.7 0.0 collective-permute-done.2
  15.7 0.1 copy.16
  15.9 0.1 copy.17
  16.1 1.1 %coupling.1.lines_hbm = f32[2,32,512]{2,1,0:T(8,128)S(1)} custom-call(s32[512,2]{1,0:T(8,128)S(1)} %broadcast_select_fusion.lists_ref, s32[1]{0:T(128)} %constant.54.clone.1.base_ref, bf16[316,32]{1,0:T(8,128)(2,1)S(1)} %copy.18.table_ref), custom_call_target="tpu_custom_call" | custom-call | flops 200000000 | bytes 2097152 | tf_op jit(solution)/shard_map/coupling/pallas_call | solution.py:175
  17.2 0.7 copy-done.3
  17.8 4.7 %all-to-all-start = ((bf16[32,16,512]{2,1,0:T(8,128)(2,1)}), bf16[32,16,512]{2,1,0:T(8,128)(2,1)S(1)}, u32[]{:S(2)}, u32[]{:S(2)}) async-start(bf16[32,16,512]{2,1,0:T(8,128)(2,1)} %upward.1), calls=%async_computation | async-start | bytes 1048576 | tf_op jit(solution)/shard_map/all_to_all | solution.py:485
  22.6 6.4 %collective-permute-done.refs_4_ = bf16[8,2,128,256]{3,2,1,0:T(8,128)(2,1)S(1)} collective-permute-done((bf16[8,2,128,256]{3,2,1,0:T(8,128)(2,1)}, bf16[8,2,128,256]{3,2,1,0:T(8,128)(2,1)S(1)}, u32[]{:S(2)}, u32[]{:S(2)}) %collective-permute-start) | collective-permute-done | bytes 1048608 | tf_op jit(solution)/shard_map/ppermute | solution.py:474
  28.9 1.0 %copy-done.4 = bf16[8,2,128,256]{3,2,1,0:T(8,128)(2,1)} copy-done((bf16[8,2,128,256]{3,2,1,0:T(8,128)(2,1)}, bf16[8,2,128,256]{3,2,1,0:T(8,128)(2,1)S(1)}, u32[]{:S(2)}) %copy-start.4) | copy-done | bytes 1048600
  29.9 5.5 %near_low.1.refs_5_ = f32[8,2,128,256]{3,2,1,0:T(8,128)} custom-call(s32[8,12]{1,0:T(8,128)S(1)} %copy-done.1, s32[8]{0:T(128)S(1)} %copy-done.2, s32[1]{0:T(128)} %bitcast.1.refs_2_, bf16[8,12,2,128,128]{4,3,2,1,0:T(8,128)(2,1)} %refs_3_.5, bf16[8,2,128,256]{3,2,1,0:T(8,128)(2,1)} %copy-done.4), custom_call_target="tpu_custom_call" | custom-call | flops 2000000000 | bytes 8388608 | tf_op jit(solution)/shard_map/near_low/pallas_call | solution.py:360
  35.4 1.3 %collective-permute-start.1 = (bf16[8,2,128,256]{3,2,1,0:T(8,128)(2,1)S(1)}, bf16[8,2,128,256]{3,2,1,0:T(8,128)(2,1)S(1)}, u32[]{:S(2)}, u32[]{:S(2)}) collective-permute-start(bf16[8,2,128,256]{3,2,1,0:T(8,128)(2,1)S(1)} %copy-done.5), channel_id=1, source_target_pairs={{1,0},{2,1},{3,2},{4,3},{5,4},{6,5},{7,6},{8,7},{9,8},{10,9},{11,1... | collective-permute-start | bytes 3145736 | tf_op jit(solution)/shard_map/ppermute | solution.py:474
  36.7 5.7 %all-to-all-done.refs_0_ = bf16[32,16,512]{2,1,0:T(8,128)(2,1)S(1)} async-done(((bf16[32,16,512]{2,1,0:T(8,128)(2,1)}), bf16[32,16,512]{2,1,0:T(8,128)(2,1)S(1)}, u32[]{:S(2)}, u32[]{:S(2)}) %all-to-all-start) | async-done | bytes 524320 | tf_op jit(solution)/shard_map/all_to_all | solution.py:485
  42.4 2.5 %translate.1 = bf16[32,16,512]{2,1,0:T(8,128)(2,1)} custom-call(f32[2,32,512]{2,1,0:T(8,128)} %copy-done.3, bf16[32,16,512]{2,1,0:T(8,128)(2,1)S(1)} %all-to-all-done.refs_0_), custom_call_target="tpu_custom_call" | custom-call | flops 1000000000 | bytes 2097152 | tf_op jit(solution)/shard_map/translate/pallas_call | solution.py:230
  44.9 4.6 %all-to-all-start.1 = ((bf16[8,4,16,512]{3,2,1,0:T(8,128)(2,1)}), bf16[8,4,16,512]{3,2,1,0:T(8,128)(2,1)S(1)}, u32[]{:S(2)}, u32[]{:S(2)}) async-start(bf16[8,4,16,512]{3,2,1,0:T(8,128)(2,1)} %bitcast.10), calls=%async_computation.1 | async-start | bytes 1048576 | tf_op jit(solution)/shard_map/all_to_all | solution.py:493
  49.4 9.1 %near_own.1.refs_5_ = f32[8,2,128,256]{3,2,1,0:T(8,128)} custom-call(s32[8,12]{1,0:T(8,128)S(1)} %copy-done.1, s32[8]{0:T(128)S(1)} %copy-done.2, s32[1]{0:T(128)} %bitcast.1.refs_2_, bf16[8,12,2,128,128]{4,3,2,1,0:T(8,128)(2,1)} %refs_3_.5, bf16[8,2,128,256]{3,2,1,0:T(8,128)(2,1)} %refs_4_.1, f32[8,2,128,256]{3,2,1,0:T(8,128)} %near_low.1.refs_5_), custom_call_target="tpu_custom_call" | custom-call | flops 2000000000 | bytes 8388608 | tf_op jit(solution)/shard_map/near_own/pallas_call | solution.py:360
  58.7 0.1 collective-permute-start.3
  58.7 7.9 %collective-permute-start.4 = (bf16[8,16,512]{2,1,0:T(8,128)(2,1)S(1)}, bf16[8,16,512]{2,1,0:T(8,128)(2,1)S(1)}, u32[]{:S(2)}, u32[]{:S(2)}) collective-permute-start(bf16[8,16,512]{2,1,0:T(8,128)(2,1)S(1)} %get-tuple-element.34), channel_id=1, source_target_pairs={{0,2},{1,3},{2,0},{3,1},{4,6},{5,7},{6,4},{7,5},{8,10},{9,11},{10,... | collective-permute-start | bytes 393224 | tf_op jit(solution)/shard_map/ppermute | solution.py:498
  66.7 0.0 collective-permute-start.5
  66.7 1.0 %copy-done.6 = bf16[8,2,128,256]{3,2,1,0:T(8,128)(2,1)} copy-done((bf16[8,2,128,256]{3,2,1,0:T(8,128)(2,1)}, bf16[8,2,128,256]{3,2,1,0:T(8,128)(2,1)S(1)}, u32[]{:S(2)}) %copy-start.6) | copy-done | bytes 1048600
  67.7 5.6 %near_high.1 = (f32[8,2,128,256]{3,2,1,0:T(8,128)S(1)}, bf16[1024,512]{1,0:T(8,128)(2,1)S(1)}, bf16[8,128,256]{2,1,0:T(8,128)(2,1)S(1)}) custom-call(s32[8,12]{1,0:T(8,128)S(1)} %copy-done.1, s32[8]{0:T(128)S(1)} %copy-done.2, s32[1]{0:T(128)} %bitcast.1.refs_2_, bf16[8,12,2,128,128]{4,3,2,1,0:T(8,128)(2,1)} %refs_3_.5, bf16[8,2,128,256]{3,2,1,0:T(8,128)(2,1)} %copy-done.6, ...), custom_call_target="tpu_custom_call" | custom-call | flops 99999997952 | bytes 8388608 | tf_op jit(solution)/shard_map/near_high/pallas_call | solution.py:360
  73.2 0.0 collective-permute-done.3.refs_1_
  73.2 1.8 %collective-permute-done.4.refs_2_ = bf16[8,16,512]{2,1,0:T(8,128)(2,1)S(1)} collective-permute-done((bf16[8,16,512]{2,1,0:T(8,128)(2,1)S(1)}, bf16[8,16,512]{2,1,0:T(8,128)(2,1)S(1)}, u32[]{:S(2)}, u32[]{:S(2)}) %collective-permute-start.4) | collective-permute-done | bytes 131104 | tf_op jit(solution)/shard_map/ppermute | solution.py:498
  75.0 0.0 collective-permute-done.5.refs_3_
  75.1 2.2 %downward.1 = f32[8,2,128,256]{3,2,1,0:T(8,128)} custom-call(s32[1]{0:T(128)} %bitcast.phi_ref, f32[8,2,128,256]{3,2,1,0:T(8,128)S(1)} %get-tuple-element.29.near_ref, bf16[1024,512]{1,0:T(8,128)(2,1)S(1)} %get-tuple-element.30.w_ref, bf16[8,128,256]{2,1,0:T(8,128)(2,1)S(1)} %get-tuple-element.31.adjoint_ref, ...), custom_call_target="tpu_custom_call" | custom-call | flops 2000000000 | bytes 7340032 | tf_op jit(solution)/shard_map/downward/pallas_call | solution.py:451
  (17 shorter events, 0.1 us)
Async XLA Ops:
  0.0 13.5 %copy-start = (bf16[316,2,4,8]{0,3,2,1:T(8,128)(2,1)S(1)}, bf16[316,2,4,8]{0,3,2,1:T(8,128)(2,1)}, u32[]{:S(2)}) copy-start(bf16[316,2,4,8]{0,3,2,1:T(8,128)(2,1)} %param.19) | copy-start | bytes 121348
  0.0 28.9 %collective-permute-start = (bf16[8,2,128,256]{3,2,1,0:T(8,128)(2,1)}, bf16[8,2,128,256]{3,2,1,0:T(8,128)(2,1)S(1)}, u32[]{:S(2)}, u32[]{:S(2)}) collective-permute-start(bf16[8,2,128,256]{3,2,1,0:T(8,128)(2,1)} %refs_4_.1), channel_id=1, source_target_pairs={{0,1},{1,2},{2,3},{3,4},{4,5},{5,6},{6,7},{7,8},{8,9},{9,10},{10,1... | collective-permute-start | bytes 3145736 | tf_op jit(solution)/shard_map/ppermute | solution.py:474
  12.0 3.7 %collective-permute-start.2 = (s32[256,2]{0,1:T(2,128)S(1)}, s32[256,2]{0,1:T(2,128)S(1)}, u32[]{:S(2)}, u32[]{:S(2)}) collective-permute-start(s32[256,2]{0,1:T(2,128)S(1)} %pad_add_fusion.2), channel_id=1, source_target_pairs={{0,16},{16,0},{1,17},{17,1},{2,18},{18,2},{3,19},{19,3},{4,20},{20... | collective-permute-start | bytes 6152 | tf_op jit(solution)/shard_map/ppermute | solution.py:510
  13.7 16.2 %copy-start.1 = (s32[8,12]{1,0:T(8,128)S(1)}, s32[8,12]{1,0:T(8,128)}, u32[]{:S(2)}) copy-start(s32[8,12]{1,0:T(8,128)} %refs_0_.5) | copy-start | bytes 1156
  13.7 16.2 %copy-start.2 = (s32[8]{0:T(128)S(1)}, s32[8]{0:T(128)}, u32[]{:S(2)}) copy-start(s32[8]{0:T(128)} %refs_1_.5) | copy-start | bytes 100
  17.2 0.7 copy-start.3
  17.8 24.6 %all-to-all-start = ((bf16[32,16,512]{2,1,0:T(8,128)(2,1)}), bf16[32,16,512]{2,1,0:T(8,128)(2,1)S(1)}, u32[]{:S(2)}, u32[]{:S(2)}) async-start(bf16[32,16,512]{2,1,0:T(8,128)(2,1)} %upward.1), calls=%async_computation | async-start | bytes 1048576 | tf_op jit(solution)/shard_map/all_to_all | solution.py:485
  28.9 1.0 %copy-start.4 = (bf16[8,2,128,256]{3,2,1,0:T(8,128)(2,1)}, bf16[8,2,128,256]{3,2,1,0:T(8,128)(2,1)S(1)}, u32[]{:S(2)}) copy-start(bf16[8,2,128,256]{3,2,1,0:T(8,128)(2,1)S(1)} %collective-permute-done.refs_4_) | copy-start | bytes 3145732
  29.9 5.5 %copy-start.5 = (bf16[8,2,128,256]{3,2,1,0:T(8,128)(2,1)S(1)}, bf16[8,2,128,256]{3,2,1,0:T(8,128)(2,1)}, u32[]{:S(2)}) copy-start(bf16[8,2,128,256]{3,2,1,0:T(8,128)(2,1)} %refs_4_.1) | copy-start | bytes 3145732
  35.4 31.2 %collective-permute-start.1 = (bf16[8,2,128,256]{3,2,1,0:T(8,128)(2,1)S(1)}, bf16[8,2,128,256]{3,2,1,0:T(8,128)(2,1)S(1)}, u32[]{:S(2)}, u32[]{:S(2)}) collective-permute-start(bf16[8,2,128,256]{3,2,1,0:T(8,128)(2,1)S(1)} %copy-done.5), channel_id=1, source_target_pairs={{1,0},{2,1},{3,2},{4,3},{5,4},{6,5},{7,6},{8,7},{9,8},{10,9},{11,1... | collective-permute-start | bytes 3145736 | tf_op jit(solution)/shard_map/ppermute | solution.py:474
  44.9 13.7 %all-to-all-start.1 = ((bf16[8,4,16,512]{3,2,1,0:T(8,128)(2,1)}), bf16[8,4,16,512]{3,2,1,0:T(8,128)(2,1)S(1)}, u32[]{:S(2)}, u32[]{:S(2)}) async-start(bf16[8,4,16,512]{3,2,1,0:T(8,128)(2,1)} %bitcast.10), calls=%async_computation.1 | async-start | bytes 1048576 | tf_op jit(solution)/shard_map/all_to_all | solution.py:493
  58.7 14.6 %collective-permute-start.3 = (bf16[8,16,512]{2,1,0:T(8,128)(2,1)S(1)}, bf16[8,16,512]{2,1,0:T(8,128)(2,1)S(1)}, u32[]{:S(2)}, u32[]{:S(2)}) collective-permute-start(bf16[8,16,512]{2,1,0:T(8,128)(2,1)S(1)} %get-tuple-element.35), channel_id=1, source_target_pairs={{0,1},{1,2},{2,3},{3,0},{4,5},{5,6},{6,7},{7,4},{8,9},{9,10},{10,1... | collective-permute-start | bytes 393224 | tf_op jit(solution)/shard_map/ppermute | solution.py:498
  58.7 16.3 %collective-permute-start.4 = (bf16[8,16,512]{2,1,0:T(8,128)(2,1)S(1)}, bf16[8,16,512]{2,1,0:T(8,128)(2,1)S(1)}, u32[]{:S(2)}, u32[]{:S(2)}) collective-permute-start(bf16[8,16,512]{2,1,0:T(8,128)(2,1)S(1)} %get-tuple-element.34), channel_id=1, source_target_pairs={{0,2},{1,3},{2,0},{3,1},{4,6},{5,7},{6,4},{7,5},{8,10},{9,11},{10,... | collective-permute-start | bytes 393224 | tf_op jit(solution)/shard_map/ppermute | solution.py:498
  66.7 8.4 %collective-permute-start.5 = (bf16[8,16,512]{2,1,0:T(8,128)(2,1)S(1)}, bf16[8,16,512]{2,1,0:T(8,128)(2,1)S(1)}, u32[]{:S(2)}, u32[]{:S(2)}) collective-permute-start(bf16[8,16,512]{2,1,0:T(8,128)(2,1)S(1)} %get-tuple-element.33), channel_id=1, source_target_pairs={{0,3},{1,0},{2,1},{3,2},{4,7},{5,4},{6,5},{7,6},{8,11},{9,8},{10,9... | collective-permute-start | bytes 393224 | tf_op jit(solution)/shard_map/ppermute | solution.py:498
  66.7 1.0 %copy-start.6 = (bf16[8,2,128,256]{3,2,1,0:T(8,128)(2,1)}, bf16[8,2,128,256]{3,2,1,0:T(8,128)(2,1)S(1)}, u32[]{:S(2)}) copy-start(bf16[8,2,128,256]{3,2,1,0:T(8,128)(2,1)S(1)} %collective-permute-done.1.refs_4_) | copy-start | bytes 3145732

commit v10 on v9

--- a/solution.py
+++ b/solution.py
@@ -259,14 +259,23 @@
     slots = blocks_hbm.shape[1]
     most = boxes * slots
     base = (rank_ref[0] - 1 + first) * boxes
-    others = [pltpu.make_async_copy(source_hbm, held, sems.at[most])]
-    if begun:
-        others.append(pltpu.make_async_copy(before_hbm, total_ref, sems.at[most + 1]))
-    for place in range(kept):
-        others.append(
-            pltpu.make_async_copy(kept_hbm[place], kept_refs[place], sems.at[most + 2 + place])
-        )
-    for copy in others:
+
+    def by_box(source, target, turn):
+        return [
+            pltpu.make_async_copy(
+                source.at[box], target.at[box], sems.at[most + turn * boxes + box]
+            )
+            for box in range(boxes)
+        ]
+
+    source_copies = by_box(source_hbm, held, 0)
+    before_copies = by_box(before_hbm, total_ref, 1) if begun else []
+    out_copies = [] if kept else by_box(total_ref, out_ref, 2)
+    kept_copies = [
+        pltpu.make_async_copy(kept_hbm[place], kept_refs[place], sems.at[most + 3 * boxes + place])
+        for place in range(kept)
+    ]
+    for copy in source_copies:
         copy.start()
 
     def block_copy(box, slot, place):
@@ -286,7 +295,10 @@
 
             place += wanted.astype(jnp.int32)
         starts.append(place)
-    others[0].wait()
+    for copy in before_copies + kept_copies:
+        copy.start()
+    for copy in source_copies:
+        copy.wait()
     for place in range(boxes):
         wide[place] = complex_columns(held[place, 0], held[place, 1])
 
@@ -295,7 +307,7 @@
         return carry
 
     lax.fori_loop(0, starts[boxes], landed, 0)
-    for copy in others[1:]:
+    for copy in before_copies:
         copy.wait()
 
     def group(box, index):
@@ -328,8 +340,10 @@
             return carry
 
         lax.fori_loop(1, (starts[box + 1] - starts[box] + GROUP - 1) // GROUP, more, 0)
-    if not kept:
-        pltpu.sync_copy(total_ref, out_ref)
+        if out_copies:
+            out_copies[box].start()
+    for copy in out_copies + kept_copies:
+        copy.wait()
 
 
 def near_field(ids, used, rank, blocks, source, first, before=None, keep=()):
@@ -346,7 +360,7 @@
         pltpu.VMEM((boxes, 2 * basis, 2 * rhs), BF16),
         pltpu.VMEM(shape, F32),
         pltpu.SMEM((boxes * slots,), jnp.int32),
-        pltpu.SemaphoreType.DMA((boxes * slots + 2 + kept,)),
+        pltpu.SemaphoreType.DMA((boxes * slots + 3 * boxes + kept,)),
     ]
     kernel = functools.partial(near_kernel, first, begun, kept)
     if kept:

time: 78.9 us -> 79 us (level)
  Pallas kernels: 33.3 us -> 32.3 us
    pallas_call x3, Pallas kernels: 20.2 us -> 19.3 us  [near_field(): pl.pallas_call(kernel, in_specs=[smem] * 3 + [hbm] * (2 + begun + kept),...]
  transfers between devices with their start and end apart: 8 -> 8, of which waited for: 3 -> 4; matrix products, arithmetic and copies ran while one was open for 3% -> 3% of each run, Pallas kernels for 40% -> 39%
where the time goes in v10:
time: 79 us; the launch traced here: 77.5 us
  Pallas kernels  32.3 us (41%)
  starting transfers between devices  25.6 us (32%)
  waiting for transfers between devices  14.5 us (18%)
  local copies, waits for them, and re-layouts  3.93 us (5%)
  other arithmetic  0.81 us (1%)
    pallas_call x3, Pallas kernels, near_field(): pl.pallas_call(kernel, in_specs=[smem] * 3 + [hbm] * (2 + begun + kept),...  19.3 us
    ppermute x3, starting transfers between devices, staged_bands(): received.append(lax.ppermute(piece, 'phi', ring))  8.15 us
    ppermute x2, starting transfers between devices, shift(): return lax.ppermute(block, axis, pairs)  6.41 us
    ppermute x2, waiting for transfers between devices, shift(): return lax.ppermute(block, axis, pairs)  6.36 us
    all_to_all x1, waiting for transfers between devices, parent_bands(): return lax.all_to_all(spread, axes, split_axis=0, concat_axis=0, tiled=True)  5.5 us
    pallas_call x1, Pallas kernels, upward(): pl.pallas_call(up_kernel, in_specs=[hbm] * 3, out_specs=hbm, out_shape=pl...  5.25 us
    all_to_all x1, starting transfers between devices, staged_bands(): bands = lax.all_to_all(bands, axes, split_axis=0, concat_axis=0, tiled=True)  4.83 us
    all_to_all x1, starting transfers between devices, parent_bands(): return lax.all_to_all(spread, axes, split_axis=0, concat_axis=0, tiled=True)  4.74 us
  transfers between devices with their start and end apart: 8, of which 4 were waited for; matrix products, arithmetic and copies ran while one was open for 3% of the time, Pallas kernels for 39%

profile of v10, /device:TPU:0, one launch (start us, length us, event | category | flops | bytes accessed | tf_op | source)
XLA Modules:
  0.0 77.5 jit_solution(18051908244110451488)
XLA Ops:
  0.0 5.1 %collective-permute-start = (bf16[8,2,128,256]{3,2,1,0:T(8,128)(2,1)}, bf16[8,2,128,256]{3,2,1,0:T(8,128)(2,1)S(1)}, u32[]{:S(2)}, u32[]{:S(2)}) collective-permute-start(bf16[8,2,128,256]{3,2,1,0:T(8,128)(2,1)} %refs_4_.1), channel_id=1, source_target_pairs={{0,1},{1,2},{2,3},{3,4},{4,5},{5,6},{6,7},{7,8},{8,9},{9,10},{10,1... | collective-permute-start | bytes 3145736 | tf_op jit(solution)/shard_map/ppermute | solution.py:488
  5.1 0.8 fusion
  5.9 0.1 stack.9
  6.0 0.8 %stack.10 = s32[256,1]{0,1:T(1,128)S(1)} reshape(s32[16,16]{1,0:T(8,128)} %param.17) | data formatting | bytes 2048 | tf_op jit(solution)/shard_map/stack | solution.py:494
  6.8 5.2 %upward.1 = bf16[32,16,512]{2,1,0:T(8,128)(2,1)} custom-call(bf16[8,2,128,256]{3,2,1,0:T(8,128)(2,1)} %refs_4_.1, bf16[8,2,128,128]{3,2,1,0:T(8,128)(2,1)} %rad_ref.1, bf16[1024,1024]{1,0:T(8,128)(2,1)} %constant.58.clone.w_hbm), custom_call_target="tpu_custom_call" | custom-call | flops 2000000000 | bytes 4194304 | tf_op jit(solution)/shard_map/upward/pallas_call | solution.py:127
  12.0 1.5 %collective-permute-start.2 = (s32[256,2]{0,1:T(2,128)S(1)}, s32[256,2]{0,1:T(2,128)S(1)}, u32[]{:S(2)}, u32[]{:S(2)}) collective-permute-start(s32[256,2]{0,1:T(2,128)S(1)} %pad_add_fusion.2), channel_id=1, source_target_pairs={{0,16},{16,0},{1,17},{17,1},{2,18},{18,2},{3,19},{19,3},{4,20},{20... | collective-permute-start | bytes 6152 | tf_op jit(solution)/shard_map/ppermute | solution.py:524
  13.5 0.1 copy.18.table_ref
  13.7 0.0 copy-start.2
  13.7 2.0 %adjoint.1.refs_7_ = bf16[8,128,256]{2,1,0:T(8,128)(2,1)} custom-call(bf16[8,2,128,128]{3,2,1,0:T(8,128)(2,1)} %rad_ref.1), custom_call_target="tpu_custom_call" | custom-call | flops 1000000 | bytes 2097152 | tf_op jit(solution)/shard_map/adjoint/pallas_call | solution.py:401
  15.7 0.0 collective-permute-done.2
  15.7 0.1 copy.16
  15.9 0.1 copy.17
  16.1 1.1 %coupling.1.lines_hbm = f32[2,32,512]{2,1,0:T(8,128)S(1)} custom-call(s32[512,2]{1,0:T(8,128)S(1)} %broadcast_select_fusion.lists_ref, s32[1]{0:T(128)} %constant.54.clone.1.base_ref, bf16[316,32]{1,0:T(8,128)(2,1)S(1)} %copy.18.table_ref), custom_call_target="tpu_custom_call" | custom-call | flops 200000000 | bytes 2097152 | tf_op jit(solution)/shard_map/coupling/pallas_call | solution.py:175
  17.2 0.7 copy-done.3
  17.8 4.7 %all-to-all-start = ((bf16[32,16,512]{2,1,0:T(8,128)(2,1)}), bf16[32,16,512]{2,1,0:T(8,128)(2,1)S(1)}, u32[]{:S(2)}, u32[]{:S(2)}) async-start(bf16[32,16,512]{2,1,0:T(8,128)(2,1)} %upward.1), calls=%async_computation | async-start | bytes 1048576 | tf_op jit(solution)/shard_map/all_to_all | solution.py:499
  22.6 6.4 %collective-permute-done.refs_4_ = bf16[8,2,128,256]{3,2,1,0:T(8,128)(2,1)S(1)} collective-permute-done((bf16[8,2,128,256]{3,2,1,0:T(8,128)(2,1)}, bf16[8,2,128,256]{3,2,1,0:T(8,128)(2,1)S(1)}, u32[]{:S(2)}, u32[]{:S(2)}) %collective-permute-start) | collective-permute-done | bytes 1048608 | tf_op jit(solution)/shard_map/ppermute | solution.py:488
  28.9 1.0 %copy-done.4 = bf16[8,2,128,256]{3,2,1,0:T(8,128)(2,1)} copy-done((bf16[8,2,128,256]{3,2,1,0:T(8,128)(2,1)}, bf16[8,2,128,256]{3,2,1,0:T(8,128)(2,1)S(1)}, u32[]{:S(2)}) %copy-start.4) | copy-done | bytes 1048600
  29.9 5.7 %near_low.1.refs_5_ = f32[8,2,128,256]{3,2,1,0:T(8,128)} custom-call(s32[8,12]{1,0:T(8,128)S(1)} %copy-done.1, s32[8]{0:T(128)S(1)} %copy-done.2, s32[1]{0:T(128)} %bitcast.1.refs_2_, bf16[8,12,2,128,128]{4,3,2,1,0:T(8,128)(2,1)} %refs_3_.5, bf16[8,2,128,256]{3,2,1,0:T(8,128)(2,1)} %copy-done.4), custom_call_target="tpu_custom_call" | custom-call | flops 2000000000 | bytes 8388608 | tf_op jit(solution)/shard_map/near_low/pallas_call | solution.py:374
  35.6 1.3 %collective-permute-start.1 = (bf16[8,2,128,256]{3,2,1,0:T(8,128)(2,1)S(1)}, bf16[8,2,128,256]{3,2,1,0:T(8,128)(2,1)S(1)}, u32[]{:S(2)}, u32[]{:S(2)}) collective-permute-start(bf16[8,2,128,256]{3,2,1,0:T(8,128)(2,1)S(1)} %copy-done.5), channel_id=1, source_target_pairs={{1,0},{2,1},{3,2},{4,3},{5,4},{6,5},{7,6},{8,7},{9,8},{10,9},{11,1... | collective-permute-start | bytes 3145736 | tf_op jit(solution)/shard_map/ppermute | solution.py:488
  36.9 5.5 %all-to-all-done.refs_0_ = bf16[32,16,512]{2,1,0:T(8,128)(2,1)S(1)} async-done(((bf16[32,16,512]{2,1,0:T(8,128)(2,1)}), bf16[32,16,512]{2,1,0:T(8,128)(2,1)S(1)}, u32[]{:S(2)}, u32[]{:S(2)}) %all-to-all-start) | async-done | bytes 524320 | tf_op jit(solution)/shard_map/all_to_all | solution.py:499
  42.4 2.5 %translate.1 = bf16[32,16,512]{2,1,0:T(8,128)(2,1)} custom-call(f32[2,32,512]{2,1,0:T(8,128)} %copy-done.3, bf16[32,16,512]{2,1,0:T(8,128)(2,1)S(1)} %all-to-all-done.refs_0_), custom_call_target="tpu_custom_call" | custom-call | flops 1000000000 | bytes 2097152 | tf_op jit(solution)/shard_map/translate/pallas_call | solution.py:230
  44.9 4.8 %all-to-all-start.1 = ((bf16[8,4,16,512]{3,2,1,0:T(8,128)(2,1)}), bf16[8,4,16,512]{3,2,1,0:T(8,128)(2,1)S(1)}, u32[]{:S(2)}, u32[]{:S(2)}) async-start(bf16[8,4,16,512]{3,2,1,0:T(8,128)(2,1)} %bitcast.10), calls=%async_computation.1 | async-start | bytes 1048576 | tf_op jit(solution)/shard_map/all_to_all | solution.py:507
  49.7 8.2 %near_own.1.refs_5_ = f32[8,2,128,256]{3,2,1,0:T(8,128)} custom-call(s32[8,12]{1,0:T(8,128)S(1)} %copy-done.1, s32[8]{0:T(128)S(1)} %copy-done.2, s32[1]{0:T(128)} %bitcast.1.refs_2_, bf16[8,12,2,128,128]{4,3,2,1,0:T(8,128)(2,1)} %refs_3_.5, bf16[8,2,128,256]{3,2,1,0:T(8,128)(2,1)} %refs_4_.1, f32[8,2,128,256]{3,2,1,0:T(8,128)} %near_low.1.refs_5_), custom_call_target="tpu_custom_call" | custom-call | flops 2000000000 | bytes 8388608 | tf_op jit(solution)/shard_map/near_own/pallas_call | solution.py:374
  57.9 0.6 all-to-all-done.1.refs_0_
  58.6 0.2 collective-permute-start.3
  58.8 7.9 %collective-permute-start.4 = (bf16[8,16,512]{2,1,0:T(8,128)(2,1)S(1)}, bf16[8,16,512]{2,1,0:T(8,128)(2,1)S(1)}, u32[]{:S(2)}, u32[]{:S(2)}) collective-permute-start(bf16[8,16,512]{2,1,0:T(8,128)(2,1)S(1)} %get-tuple-element.34), channel_id=1, source_target_pairs={{0,2},{1,3},{2,0},{3,1},{4,6},{5,7},{6,4},{7,5},{8,10},{9,11},{10,... | collective-permute-start | bytes 393224 | tf_op jit(solution)/shard_map/ppermute | solution.py:512
  66.7 0.0 collective-permute-done.1.refs_4_
  66.8 1.0 %copy-done.6 = bf16[8,2,128,256]{3,2,1,0:T(8,128)(2,1)} copy-done((bf16[8,2,128,256]{3,2,1,0:T(8,128)(2,1)}, bf16[8,2,128,256]{3,2,1,0:T(8,128)(2,1)S(1)}, u32[]{:S(2)}) %copy-start.6) | copy-done | bytes 1048600
  67.7 5.4 %near_high.1 = (f32[8,2,128,256]{3,2,1,0:T(8,128)S(1)}, bf16[1024,512]{1,0:T(8,128)(2,1)S(1)}, bf16[8,128,256]{2,1,0:T(8,128)(2,1)S(1)}) custom-call(s32[8,12]{1,0:T(8,128)S(1)} %copy-done.1, s32[8]{0:T(128)S(1)} %copy-done.2, s32[1]{0:T(128)} %bitcast.1.refs_2_, bf16[8,12,2,128,128]{4,3,2,1,0:T(8,128)(2,1)} %refs_3_.5, bf16[8,2,128,256]{3,2,1,0:T(8,128)(2,1)} %copy-done.6, ...), custom_call_target="tpu_custom_call" | custom-call | flops 99999997952 | bytes 8388608 | tf_op jit(solution)/shard_map/near_high/pallas_call | solution.py:374
  73.1 0.0 collective-permute-done.3.refs_1_
  73.1 2.0 %collective-permute-done.4.refs_2_ = bf16[8,16,512]{2,1,0:T(8,128)(2,1)S(1)} collective-permute-done((bf16[8,16,512]{2,1,0:T(8,128)(2,1)S(1)}, bf16[8,16,512]{2,1,0:T(8,128)(2,1)S(1)}, u32[]{:S(2)}, u32[]{:S(2)}) %collective-permute-start.4) | collective-permute-done | bytes 131104 | tf_op jit(solution)/shard_map/ppermute | solution.py:512
  75.1 2.2 %downward.1 = f32[8,2,128,256]{3,2,1,0:T(8,128)} custom-call(s32[1]{0:T(128)} %bitcast.phi_ref, f32[8,2,128,256]{3,2,1,0:T(8,128)S(1)} %get-tuple-element.29.near_ref, bf16[1024,512]{1,0:T(8,128)(2,1)S(1)} %get-tuple-element.30.w_ref, bf16[8,128,256]{2,1,0:T(8,128)(2,1)S(1)} %get-tuple-element.31.adjoint_ref, ...), custom_call_target="tpu_custom_call" | custom-call | flops 2000000000 | bytes 7340032 | tf_op jit(solution)/shard_map/downward/pallas_call | solution.py:465
  (17 shorter events, 0.1 us)
Async XLA Ops:
  0.0 13.5 %copy-start = (bf16[316,2,4,8]{0,3,2,1:T(8,128)(2,1)S(1)}, bf16[316,2,4,8]{0,3,2,1:T(8,128)(2,1)}, u32[]{:S(2)}) copy-start(bf16[316,2,4,8]{0,3,2,1:T(8,128)(2,1)} %param.19) | copy-start | bytes 121348
  0.0 28.9 %collective-permute-start = (bf16[8,2,128,256]{3,2,1,0:T(8,128)(2,1)}, bf16[8,2,128,256]{3,2,1,0:T(8,128)(2,1)S(1)}, u32[]{:S(2)}, u32[]{:S(2)}) collective-permute-start(bf16[8,2,128,256]{3,2,1,0:T(8,128)(2,1)} %refs_4_.1), channel_id=1, source_target_pairs={{0,1},{1,2},{2,3},{3,4},{4,5},{5,6},{6,7},{7,8},{8,9},{9,10},{10,1... | collective-permute-start | bytes 3145736 | tf_op jit(solution)/shard_map/ppermute | solution.py:488
  12.0 3.7 %collective-permute-start.2 = (s32[256,2]{0,1:T(2,128)S(1)}, s32[256,2]{0,1:T(2,128)S(1)}, u32[]{:S(2)}, u32[]{:S(2)}) collective-permute-start(s32[256,2]{0,1:T(2,128)S(1)} %pad_add_fusion.2), channel_id=1, source_target_pairs={{0,16},{16,0},{1,17},{17,1},{2,18},{18,2},{3,19},{19,3},{4,20},{20... | collective-permute-start | bytes 6152 | tf_op jit(solution)/shard_map/ppermute | solution.py:524
  13.7 16.2 %copy-start.1 = (s32[8,12]{1,0:T(8,128)S(1)}, s32[8,12]{1,0:T(8,128)}, u32[]{:S(2)}) copy-start(s32[8,12]{1,0:T(8,128)} %refs_0_.5) | copy-start | bytes 1156
  13.7 16.2 %copy-start.2 = (s32[8]{0:T(128)S(1)}, s32[8]{0:T(128)}, u32[]{:S(2)}) copy-start(s32[8]{0:T(128)} %refs_1_.5) | copy-start | bytes 100
  17.2 0.7 copy-start.3
  17.8 24.6 %all-to-all-start = ((bf16[32,16,512]{2,1,0:T(8,128)(2,1)}), bf16[32,16,512]{2,1,0:T(8,128)(2,1)S(1)}, u32[]{:S(2)}, u32[]{:S(2)}) async-start(bf16[32,16,512]{2,1,0:T(8,128)(2,1)} %upward.1), calls=%async_computation | async-start | bytes 1048576 | tf_op jit(solution)/shard_map/all_to_all | solution.py:499
  28.9 1.0 %copy-start.4 = (bf16[8,2,128,256]{3,2,1,0:T(8,128)(2,1)}, bf16[8,2,128,256]{3,2,1,0:T(8,128)(2,1)S(1)}, u32[]{:S(2)}) copy-start(bf16[8,2,128,256]{3,2,1,0:T(8,128)(2,1)S(1)} %collective-permute-done.refs_4_) | copy-start | bytes 3145732
  29.9 5.7 %copy-start.5 = (bf16[8,2,128,256]{3,2,1,0:T(8,128)(2,1)S(1)}, bf16[8,2,128,256]{3,2,1,0:T(8,128)(2,1)}, u32[]{:S(2)}) copy-start(bf16[8,2,128,256]{3,2,1,0:T(8,128)(2,1)} %refs_4_.1) | copy-start | bytes 3145732
  35.6 31.2 %collective-permute-start.1 = (bf16[8,2,128,256]{3,2,1,0:T(8,128)(2,1)S(1)}, bf16[8,2,128,256]{3,2,1,0:T(8,128)(2,1)S(1)}, u32[]{:S(2)}, u32[]{:S(2)}) collective-permute-start(bf16[8,2,128,256]{3,2,1,0:T(8,128)(2,1)S(1)} %copy-done.5), channel_id=1, source_target_pairs={{1,0},{2,1},{3,2},{4,3},{5,4},{6,5},{7,6},{8,7},{9,8},{10,9},{11,1... | collective-permute-start | bytes 3145736 | tf_op jit(solution)/shard_map/ppermute | solution.py:488
  44.9 13.7 %all-to-all-start.1 = ((bf16[8,4,16,512]{3,2,1,0:T(8,128)(2,1)}), bf16[8,4,16,512]{3,2,1,0:T(8,128)(2,1)S(1)}, u32[]{:S(2)}, u32[]{:S(2)}) async-start(bf16[8,4,16,512]{3,2,1,0:T(8,128)(2,1)} %bitcast.10), calls=%async_computation.1 | async-start | bytes 1048576 | tf_op jit(solution)/shard_map/all_to_all | solution.py:507
  58.6 14.5 %collective-permute-start.3 = (bf16[8,16,512]{2,1,0:T(8,128)(2,1)S(1)}, bf16[8,16,512]{2,1,0:T(8,128)(2,1)S(1)}, u32[]{:S(2)}, u32[]{:S(2)}) collective-permute-start(bf16[8,16,512]{2,1,0:T(8,128)(2,1)S(1)} %get-tuple-element.35), channel_id=1, source_target_pairs={{0,1},{1,2},{2,3},{3,0},{4,5},{5,6},{6,7},{7,4},{8,9},{9,10},{10,1... | collective-permute-start | bytes 393224 | tf_op jit(solution)/shard_map/ppermute | solution.py:512
  58.8 16.3 %collective-permute-start.4 = (bf16[8,16,512]{2,1,0:T(8,128)(2,1)S(1)}, bf16[8,16,512]{2,1,0:T(8,128)(2,1)S(1)}, u32[]{:S(2)}, u32[]{:S(2)}) collective-permute-start(bf16[8,16,512]{2,1,0:T(8,128)(2,1)S(1)} %get-tuple-element.34), channel_id=1, source_target_pairs={{0,2},{1,3},{2,0},{3,1},{4,6},{5,7},{6,4},{7,5},{8,10},{9,11},{10,... | collective-permute-start | bytes 393224 | tf_op jit(solution)/shard_map/ppermute | solution.py:512
  66.7 8.4 %collective-permute-start.5 = (bf16[8,16,512]{2,1,0:T(8,128)(2,1)S(1)}, bf16[8,16,512]{2,1,0:T(8,128)(2,1)S(1)}, u32[]{:S(2)}, u32[]{:S(2)}) collective-permute-start(bf16[8,16,512]{2,1,0:T(8,128)(2,1)S(1)} %get-tuple-element.33), channel_id=1, source_target_pairs={{0,3},{1,0},{2,1},{3,2},{4,7},{5,4},{6,5},{7,6},{8,11},{9,8},{10,9... | collective-permute-start | bytes 393224 | tf_op jit(solution)/shard_map/ppermute | solution.py:512
  66.8 1.0 %copy-start.6 = (bf16[8,2,128,256]{3,2,1,0:T(8,128)(2,1)}, bf16[8,2,128,256]{3,2,1,0:T(8,128)(2,1)S(1)}, u32[]{:S(2)}) copy-start(bf16[8,2,128,256]{3,2,1,0:T(8,128)(2,1)S(1)} %collective-permute-done.1.refs_4_) | copy-start | bytes 3145732

commit v11 on v10

--- a/solution.py
+++ b/solution.py
@@ -22,7 +22,7 @@
 F32 = jnp.float32
 BF16 = jnp.bfloat16
 MIB = 2**20
-GROUP = 4
+GROUP = 2
 NOWHERE = -(2**20)
 
 
@@ -85,7 +85,8 @@
     return jnp.concatenate([side_by_side(real, imag), side_by_side(-imag, real)], axis=0)
 
 
-def up_kernel(x_hbm, rad_hbm, w_hbm, out_hbm, x_ref, rad_ref, w_ref, right, result, sems):
+def up_kernel(phi_ref, x_hbm, rad_hbm, w_hbm, *refs):
+    pieces_hbm, (x_ref, rad_ref, w_ref, right, result, sems) = refs[:-6], refs[-6:]
     boxes, _, _, rhs = x_ref.shape
     points = rad_ref.shape[2]
     copies = [
@@ -116,33 +117,42 @@
     samples = total.shape[0] // 2
     total = total[:samples] + total[samples:]
     result[...] = total.astype(BF16).reshape(result.shape)
-    pltpu.sync_copy(result, out_hbm)
-
-
-def upward(coeffs, radiation, weights, groups):
+    phi_size = len(pieces_hbm)
+    copies = []
+    for distance, piece in enumerate(pieces_hbm):
+        place = lax.rem(phi_ref[0] + distance, phi_size)
+        copies.append(pltpu.make_async_copy(result.at[:, place], piece, sems.at[3 + distance]))
+        copies[-1].start()
+    for copy in copies:
+        copy.wait()
+
+
+def upward(phi, coeffs, radiation, weights, shape):
     boxes, _, basis, rhs = coeffs.shape
     rows, columns = weights.shape
     samples = rows // 2
+    shape = (*shape, samples // math.prod(shape), 2 * rhs)
+    piece = (shape[0], *shape[2:])
     hbm = pl.BlockSpec(memory_space=pltpu.HBM)
     return pl.pallas_call(
         up_kernel,
-        in_specs=[hbm] * 3,
-        out_specs=hbm,
-        out_shape=pltpu.HBM((groups, samples // groups, 2 * rhs), BF16),
+        in_specs=[pl.BlockSpec(memory_space=pltpu.SMEM)] + [hbm] * 3,
+        out_specs=[hbm] * shape[1],
+        out_shape=[pltpu.HBM(piece, BF16)] * shape[1],
         scratch_shapes=[
             pltpu.VMEM(coeffs.shape, BF16),
             pltpu.VMEM(radiation.shape, BF16),
             pltpu.VMEM(weights.shape, BF16),
             pltpu.VMEM((2, columns, 2 * rhs), BF16),
-            pltpu.VMEM((groups, samples // groups, 2 * rhs), BF16),
-            pltpu.SemaphoreType.DMA((3,)),
+            pltpu.VMEM(shape, BF16),
+            pltpu.SemaphoreType.DMA((3 + shape[1],)),
         ],
         compiler_params=pltpu.CompilerParams(vmem_limit_bytes=32 * MIB),
         cost_estimate=pl.CostEstimate(
             flops=2 * 10**9, bytes_accessed=4 * MIB, transcendentals=0
         ),
         name="upward",
-    )(*in_hbm(coeffs, radiation, weights))
+    )(phi, *in_hbm(coeffs, radiation, weights))
 
 
 def coupling_kernel(lists_ref, base_ref, table_ref, out_ref):
@@ -185,15 +195,22 @@
     )(lists, base, table)
 
 
-def translate_kernel(lines_hbm, *refs):
+def translate_kernel(phi_ref, lines_hbm, *refs):
     count = (len(refs) - 5) // 2
     sources, out_hbm = refs[:count], refs[count]
+    phi = phi_ref[0]
+    phi_size = sources[0].shape[1]
     held, lines, matrix, result, sems = refs[count + 1 :][:count], *refs[2 * count + 1 :]
     targets, samples, width = result.shape
     rhs = width // 2
+    pairs = [(lines_hbm, lines)]
+    for source, target in zip(sources, held):
+        for distance in range(phi_size):
+            place = lax.rem(phi + phi_size - distance, phi_size)
+            pairs.append((source.at[:, distance], target.at[:, place]))
     copies = [
         pltpu.make_async_copy(source, target, sems.at[place])
-        for place, (source, target) in enumerate(zip((lines_hbm, *sources), (lines, *held)))
+        for place, (source, target) in enumerate(pairs)
     ]
     for copy in copies:
         copy.start()
@@ -209,8 +226,9 @@
     total = None
     start = 0
     for place, source in enumerate(held):
-        copies[1 + place].wait()
-        stop = start + source.shape[0] * samples
+        for copy in copies[1 + place * phi_size : 1 + (place + 1) * phi_size]:
+            copy.wait()
+        stop = start + source.shape[0] * phi_size * samples
         part = dot(matrix[:, start:stop], source[...].reshape(stop - start, width))
         total = part if total is None else total + part
         start = stop
@@ -221,15 +239,15 @@
     pltpu.sync_copy(result, out_hbm)
 
 
-def translate(lines, sources):
-    _, samples, width = sources[0].shape
+def translate(phi, lines, sources):
+    _, phi_size, samples, width = sources[0].shape
     _, targets, columns = lines.shape
     shape = (targets, samples, width)
     hbm = pl.BlockSpec(memory_space=pltpu.HBM)
     anywhere = pl.BlockSpec(memory_space=pl.ANY)
     return pl.pallas_call(
         translate_kernel,
-        in_specs=[hbm] + [anywhere] * len(sources),
+        in_specs=[pl.BlockSpec(memory_space=pltpu.SMEM), hbm] + [anywhere] * len(sources),
         out_specs=hbm,
         out_shape=pltpu.HBM(shape, BF16),
         scratch_shapes=[
@@ -237,28 +255,27 @@
             pltpu.VMEM(lines.shape, F32),
             pltpu.VMEM((2 * targets * samples, columns), BF16),
             pltpu.VMEM(shape, BF16),
-            pltpu.SemaphoreType.DMA((1 + len(sources),)),
+            pltpu.SemaphoreType.DMA((1 + phi_size * len(sources),)),
         ],
         compiler_params=pltpu.CompilerParams(vmem_limit_bytes=24 * MIB),
         cost_estimate=pl.CostEstimate(
             flops=10**9, bytes_accessed=2 * MIB, transcendentals=0
         ),
         name="translate",
-    )(*in_hbm(lines), *sources)
+    )(phi, *in_hbm(lines), *sources)
 
 
 def near_kernel(first, begun, kept, *refs):
     refs = list(refs)
-    ids_ref, used_ref, rank_ref, blocks_hbm, source_hbm = refs[:5]
-    before_hbm = refs[5] if begun else None
-    kept_hbm = refs[5 + begun : 5 + begun + kept]
-    out_ref = refs[5 + begun + kept]
-    kept_refs = refs[6 + begun + kept : 6 + begun + 2 * kept]
-    blocks, held, wide, total_ref, listed, sems = refs[6 + begun + 2 * kept :]
+    listed, starts_ref, blocks_hbm, source_hbm = refs[:4]
+    before_hbm = refs[4] if begun else None
+    kept_hbm = refs[4 + begun : 4 + begun + kept]
+    out_ref = refs[4 + begun + kept]
+    kept_refs = refs[5 + begun + kept : 5 + begun + 2 * kept]
+    blocks, held, wide, total_ref, sems = refs[5 + begun + 2 * kept :]
     boxes, _, basis, rhs = held.shape
-    slots = blocks_hbm.shape[1]
-    most = boxes * slots
-    base = (rank_ref[0] - 1 + first) * boxes
+    most = blocks_hbm.shape[0]
+    starts = [starts_ref[first, box] for box in range(boxes + 1)]
 
     def by_box(source, target, turn):
         return [
@@ -278,23 +295,15 @@
     for copy in source_copies:
         copy.start()
 
-    def block_copy(box, slot, place):
-        return pltpu.make_async_copy(blocks_hbm.at[box, slot], blocks.at[place], sems.at[place])
-
-    starts = [jnp.int32(0)]
-    for box in range(boxes):
-        place = starts[box]
-        for slot in range(slots):
-            source = ids_ref[box, slot] - base
-            wanted = (slot < used_ref[box]) & (source >= 0) & (source < boxes)
-
-            @pl.when(wanted)
-            def _(box=box, slot=slot, place=place, source=source):
-                listed[place] = source
-                block_copy(box, slot, place).start()
-
-            place += wanted.astype(jnp.int32)
-        starts.append(place)
+    def block_copy(place):
+        block = listed[first, place] // boxes
+        return pltpu.make_async_copy(blocks_hbm.at[block], blocks.at[place], sems.at[place])
+
+    def fetch(place, carry):
+        block_copy(place).start()
+        return carry
+
+    lax.fori_loop(0, starts[boxes], fetch, 0)
     for copy in before_copies + kept_copies:
         copy.start()
     for copy in source_copies:
@@ -303,28 +312,30 @@
         wide[place] = complex_columns(held[place, 0], held[place, 1])
 
     def landed(place, carry):
-        block_copy(0, 0, place).wait()
+        block_copy(place).wait()
         return carry
 
     lax.fori_loop(0, starts[boxes], landed, 0)
     for copy in before_copies:
         copy.wait()
 
-    def group(box, index):
+    def group(box, begin, size):
         left, right = [], []
-        for step in range(GROUP):
-            place = starts[box] + index * GROUP + step
+        for step in range(size):
+            place = starts[box] + begin + step
             valid = place < starts[box + 1]
             place = jnp.where(valid, place, 0)
             real, imag = blocks[place, 0], blocks[place, 1]
             real = jnp.where(valid, real, jnp.zeros_like(real))
             imag = jnp.where(valid, imag, jnp.zeros_like(imag))
             left.append(side_by_side(real, imag))
-            right.append(wide[jnp.where(valid, listed[place], 0)])
+            right.append(wide[jnp.where(valid, listed[first, place] % boxes, 0)])
         return dot(jnp.concatenate(left, axis=1), jnp.concatenate(right, axis=0))
 
+    possible = [(boxes - box, boxes, box + 1)[first] for box in range(boxes)]
+    sizes = [min(count, 3 if count < 7 else 4) for count in possible]
     for box in range(boxes):
-        part = group(box, 0)
+        part = group(box, 0, sizes[box])
         if begun:
             total_ref[box, 0] += part[:, :rhs]
             total_ref[box, 1] += part[:, rhs:]
@@ -334,20 +345,38 @@
     for box in range(boxes):
 
         def more(index, carry, box=box):
-            part = group(box, index)
+            part = group(box, sizes[box] + GROUP * index, GROUP)
             total_ref[box, 0] += part[:, :rhs]
             total_ref[box, 1] += part[:, rhs:]
             return carry
 
-        lax.fori_loop(1, (starts[box + 1] - starts[box] + GROUP - 1) // GROUP, more, 0)
+        rest = starts[box + 1] - starts[box] - sizes[box]
+        lax.fori_loop(0, (jnp.maximum(rest, 0) + GROUP - 1) // GROUP, more, 0)
         if out_copies:
             out_copies[box].start()
     for copy in out_copies + kept_copies:
         copy.wait()
 
 
-def near_field(ids, used, rank, blocks, source, first, before=None, keep=()):
+def near_slots(ids, used, rank):
+    boxes, slots = ids.shape
+    total = boxes * slots
+    source = ids - (rank - 1) * boxes
+    source = jnp.where(jnp.arange(slots) < used[:, None], source, -1).reshape(-1)
+    wanted = (source >= 0) & (source // boxes == jnp.arange(3)[:, None])
+    earlier = jnp.arange(total)[None, :] < jnp.arange(total)[:, None]
+    place = jnp.sum((wanted[:, None, :] & earlier).astype(jnp.int32), axis=2)
+    code = jnp.arange(total) * boxes + source % boxes
+    chosen = wanted[:, None, :] & (place[:, None, :] == jnp.arange(total)[:, None])
+    listed = jnp.sum(jnp.where(chosen, code, 0), axis=2)
+    before = jnp.arange(total) // slots < jnp.arange(boxes + 1)[:, None]
+    starts = jnp.sum((wanted[:, None, :] & before).astype(jnp.int32), axis=2)
+    return listed.astype(jnp.int32), starts.astype(jnp.int32)
+
+
+def near_field(listed, starts, blocks, source, first, before=None, keep=()):
     boxes, slots, _, basis, _ = blocks.shape
+    blocks = blocks.reshape(boxes * slots, *blocks.shape[2:])
     rhs = source.shape[3]
     begun, kept = before is not None, len(keep)
     hbm = pl.BlockSpec(memory_space=pltpu.HBM)
@@ -355,11 +384,10 @@
     vmem = pl.BlockSpec(memory_space=pltpu.VMEM)
     shape = (boxes, 2, basis, rhs)
     scratch = [
-        pltpu.VMEM((boxes * slots, *blocks.shape[2:]), BF16),
+        pltpu.VMEM(blocks.shape, BF16),
         pltpu.VMEM(source.shape, BF16),
         pltpu.VMEM((boxes, 2 * basis, 2 * rhs), BF16),
         pltpu.VMEM(shape, F32),
-        pltpu.SMEM((boxes * slots,), jnp.int32),
         pltpu.SemaphoreType.DMA((boxes * slots + 3 * boxes + kept,)),
     ]
     kernel = functools.partial(near_kernel, first, begun, kept)
@@ -368,12 +396,12 @@
         inner = kernel
 
         def kernel(*refs):
-            place = 5 + begun + kept
-            inner(*refs[:-2], refs[place], *refs[-2:])
+            place = 4 + begun + kept
+            inner(*refs[:-1], refs[place], refs[-1])
 
     return pl.pallas_call(
         kernel,
-        in_specs=[smem] * 3 + [hbm] * (2 + begun + kept),
+        in_specs=[smem] * 2 + [hbm] * (2 + begun + kept),
         out_specs=[vmem] * (1 + kept) if kept else hbm,
         out_shape=[
             pltpu.VMEM(shape, F32),
@@ -387,7 +415,7 @@
             flops=10**11 if first == 2 else 2 * 10**9, bytes_accessed=8 * MIB, transcendentals=0
         ),
         name=("near_low", "near_own", "near_high")[first],
-    )(ids, used, rank, *in_hbm(blocks, source, *([before] if begun else []), *keep))
+    )(listed, starts, *in_hbm(blocks, source, *([before] if begun else []), *keep))
 
 
 def adjoint_kernel(rad_ref, out_hbm, held):
@@ -494,23 +522,18 @@
     return jnp.stack([names, vector_ids], axis=2).reshape(-1, 2)
 
 
-def parent_bands(spread, shares):
-    axes = ("box", "theta", "phi") if shares == lax.axis_size("box") else ("theta", "phi")
-    return lax.all_to_all(spread, axes, split_axis=0, concat_axis=0, tiled=True)
-
-
-def staged_bands(incoming, shares):
+def along_phi(pieces):
+    size = len(pieces)
+    received = [pieces[0]]
+    for distance in range(1, size):
+        ring = [(place, (place + distance) % size) for place in range(size)]
+        received.append(lax.ppermute(pieces[distance], "phi", ring))
+    return received
+
+
+def across(bands, shares):
     axes = ("box", "theta") if shares == lax.axis_size("box") else ("theta",)
-    phi_size = lax.axis_size("phi")
-    phi = lax.axis_index("phi")
-    bands = incoming.reshape(-1, phi_size, *incoming.shape[1:])
-    bands = lax.all_to_all(bands, axes, split_axis=0, concat_axis=0, tiled=True)
-    received = []
-    for distance in range(1, phi_size):
-        piece = lax.dynamic_index_in_dim(bands, (phi + distance) % phi_size, 1, keepdims=False)
-        ring = [(place, (place + distance) % phi_size) for place in range(phi_size)]
-        received.append(lax.ppermute(piece, "phi", ring))
-    return phi.astype(jnp.int32).reshape(1), bands, received
+    return lax.all_to_all(bands, axes, split_axis=0, concat_axis=0, tiled=True)
 
 
 def translation_lines(lists, translation, shares, per_group):
@@ -547,30 +570,39 @@
     translation,
 ):
     every = ("box", "theta", "phi")
-    per_group = lax.axis_size("theta") * lax.axis_size("phi")
-    rank = lax.axis_index(every).astype(jnp.int32).reshape(1)
+    phi_size = lax.axis_size("phi")
+    per_group = lax.axis_size("theta") * phi_size
+    groups = shares * per_group
+    phi = lax.axis_index("phi")
+    phi_ref = phi.astype(jnp.int32).reshape(1)
     low = shift(coeffs, every, 1)
-    spread = upward(coeffs, radiation, up_weights, shares * per_group)
+    pieces = upward(phi_ref, coeffs, radiation, up_weights, (groups // phi_size, phi_size))
+    lists = lists_of(partners, vector_ids, pair_count)
+    pieces, lists = lax.optimization_barrier((pieces, lists))
+    received = along_phi(pieces)
     radiation_adjoint = adjoint(radiation)
-    lists = lists_of(partners, vector_ids, pair_count)
-    spread, lists = lax.optimization_barrier((spread, lists))
     lines = translation_lines(lists, translation, shares, per_group)
-    spread, lines, radiation_adjoint = lax.optimization_barrier((spread, lines, radiation_adjoint))
-    parents = parent_bands(spread, shares)
-    slots = (near_ids, near_count, rank, near_blocks)
-    near = near_field(*slots, low, 0)
-    near, late = lax.optimization_barrier((near, coeffs))
+    slots = (*near_slots(near_ids, near_count, lax.axis_index(every)), near_blocks)
+    near = near_field(*slots, coeffs, 1)
+    received, lines, radiation_adjoint, near, late = lax.optimization_barrier(
+        (received, lines, radiation_adjoint, near, coeffs)
+    )
     high = shift(late, every, -1)
-    parents, near = lax.optimization_barrier((parents, near))
+    parents = across(jnp.stack(received, axis=1), shares)
     sources = [parents]
     if shares < lax.axis_size("box"):
         sources = [shift(parents, "box", 1), parents, shift(parents, "box", -1)]
-    incoming = translate(lines, sources)
-    incoming, near = lax.optimization_barrier((incoming, near))
-    phi, bands, received = staged_bands(incoming, shares)
-    near = near_field(*slots, coeffs, 1, near)
+    incoming = translate(phi_ref, lines, sources)
+    incoming, low = lax.optimization_barrier((incoming, low))
+    bands = across(incoming.reshape(-1, phi_size, *incoming.shape[1:]), shares)
+    pieces = [
+        lax.dynamic_index_in_dim(bands, (phi + distance) % phi_size, 1, keepdims=False)
+        for distance in range(phi_size)
+    ]
+    received = along_phi(pieces)[1:]
+    near = near_field(*slots, low, 0, near)
     ready = near_field(*slots, high, 2, near, keep=(down_weights, radiation_adjoint))
-    return downward(phi, bands, received, *ready)
+    return downward(phi_ref, bands, received, *ready)
 
 
 def solution(mesh):

time: 79 us -> 90 us (1.14)
  waiting for transfers between devices: 14.5 us -> 22.4 us
  starting transfers between devices: 25.6 us -> 30.9 us
  local copies, waits for them, and re-layouts: 3.93 us -> 1.52 us
  other arithmetic: 0.81 us -> 2.35 us
    ppermute x3 -> x6, waiting for transfers between devices: 1.98 us -> 12.1 us  [along_phi(): received.append(lax.ppermute(pieces[distance], 'phi', ring))]
    ppermute x3 -> x6, starting transfers between devices: 8.15 us -> 16 us  [along_phi(): received.append(lax.ppermute(pieces[distance], 'phi', ring))]
    ppermute x2, waiting for transfers between devices: 6.36 us -> 0.01 us  [shift(): return lax.ppermute(block, axis, pairs)]
    all_to_all x2, waiting for transfers between devices: 6.14 us -> 10.3 us  [across(): return lax.all_to_all(bands, axes, split_axis=0, concat_axis=0, tiled=True)]
    unnamed x14, local copies, waits for them, and re-layouts: 2.62 us -> 0.03 us
    all_to_all x2, starting transfers between devices: 9.57 us -> 7 us  [across(): return lax.all_to_all(bands, axes, split_axis=0, concat_axis=0, tiled=True)]
  transfers between devices with their start and end apart: 8 -> 11, of which waited for: 4 -> 5; matrix products, arithmetic and copies ran while one was open for 3% -> 4% of each run, Pallas kernels for 39% -> 33%
where the time goes in v11:
time: 90 us; the launch traced here: 89 us
  Pallas kernels  31.5 us (35%)
  starting transfers between devices  30.9 us (34%)
  waiting for transfers between devices  22.4 us (25%)
  other arithmetic  2.35 us (3%)
  local copies, waits for them, and re-layouts  1.52 us (2%)
    pallas_call x3, Pallas kernels, near_field(): pl.pallas_call(kernel, in_specs=[smem] * 2 + [hbm] * (2 + begun + kept),...  18.3 us
    ppermute x6, starting transfers between devices, along_phi(): received.append(lax.ppermute(pieces[distance], 'phi', ring))  16 us
    ppermute x6, waiting for transfers between devices, along_phi(): received.append(lax.ppermute(pieces[distance], 'phi', ring))  12.1 us
    all_to_all x2, waiting for transfers between devices, across(): return lax.all_to_all(bands, axes, split_axis=0, concat_axis=0, tiled=True)  10.3 us
    all_to_all x2, starting transfers between devices, across(): return lax.all_to_all(bands, axes, split_axis=0, concat_axis=0, tiled=True)  7 us
    ppermute x2, starting transfers between devices, shift(): return lax.ppermute(block, axis, pairs)  6.41 us
    pallas_call x1, Pallas kernels, upward(): pl.pallas_call(up_kernel, in_specs=[pl.BlockSpec(memory_space=pltpu.SMEM)...  5.29 us
    pallas_call x1, Pallas kernels, translate(): pl.pallas_call(translate_kernel, in_specs=[pl.BlockSpec(memory_space=pltp...  2.53 us
  transfers between devices with their start and end apart: 11, of which 5 were waited for; matrix products, arithmetic and copies ran while one was open for 4% of the time, Pallas kernels for 33%

profile of v11, /device:TPU:0, one launch (start us, length us, event | category | flops | bytes accessed | tf_op | source)
XLA Modules:
  0.0 89.0 jit_solution(15727763414503694114)
XLA Ops:
  0.0 5.1 %collective-permute-start.5 = (bf16[8,2,128,256]{3,2,1,0:T(8,128)(2,1)}, bf16[8,2,128,256]{3,2,1,0:T(8,128)(2,1)S(1)}, u32[]{:S(2)}, u32[]{:S(2)}) collective-permute-start(bf16[8,2,128,256]{3,2,1,0:T(8,128)(2,1)} %refs_3_.1), channel_id=1, source_target_pairs={{0,1},{1,2},{2,3},{3,4},{4,5},{5,6},{6,7},{7,8},{8,9},{9,10},{10,1... | collective-permute-start | bytes 3145736 | tf_op jit(solution)/shard_map/ppermute | solution.py:516
  5.1 0.8 fusion.1
  6.0 0.8 stack.25
  6.8 5.3 %upward.1 = (bf16[8,16,512]{2,1,0:T(8,128)(2,1)}, bf16[8,16,512]{2,1,0:T(8,128)(2,1)}, bf16[8,16,512]{2,1,0:T(8,128)(2,1)}, bf16[8,16,512]{2,1,0:T(8,128)(2,1)}) custom-call(s32[1]{0:T(128)} %bitcast.phi_ref, bf16[8,2,128,256]{3,2,1,0:T(8,128)(2,1)} %refs_3_.1, bf16[8,2,128,128]{3,2,1,0:T(8,128)(2,1)} %rad_ref.1, bf16[1024,1024]{1,0:T(8,128)(2,1)} %constant.93.clone.w_hbm), custom_call_target="tpu_custom_call" | custom-call | flops 2000000000 | bytes 4194304 | tf_op jit(solution)/shard_map/upward/pallas_call | solution.py:137
  12.1 1.5 %collective-permute-start.3 = (s32[256,2]{0,1:T(2,128)S(1)}, s32[256,2]{0,1:T(2,128)S(1)}, u32[]{:S(2)}, u32[]{:S(2)}) collective-permute-start(s32[256,2]{0,1:T(2,128)S(1)} %pad_add_fusion.2), channel_id=1, source_target_pairs={{0,16},{16,0},{1,17},{17,1},{2,18},{18,2},{3,19},{19,3},{4,20},{20... | collective-permute-start | bytes 6152 | tf_op jit(solution)/shard_map/ppermute | solution.py:547
  13.6 1.6 %collective-permute-start = (bf16[8,16,512]{2,1,0:T(8,128)(2,1)}, bf16[8,16,512]{2,1,0:T(8,128)(2,1)S(1)}, u32[]{:S(2)}, u32[]{:S(2)}) collective-permute-start(bf16[8,16,512]{2,1,0:T(8,128)(2,1)} %get-tuple-element.32), channel_id=1, source_target_pairs={{0,1},{1,2},{2,3},{3,0},{4,5},{5,6},{6,7},{7,4},{8,9},{9,10},{10,1... | collective-permute-start | bytes 393224 | tf_op jit(solution)/shard_map/ppermute | solution.py:530
  15.2 1.0 %collective-permute-start.1 = (bf16[8,16,512]{2,1,0:T(8,128)(2,1)}, bf16[8,16,512]{2,1,0:T(8,128)(2,1)S(1)}, u32[]{:S(2)}, u32[]{:S(2)}) collective-permute-start(bf16[8,16,512]{2,1,0:T(8,128)(2,1)} %get-tuple-element.33), channel_id=1, source_target_pairs={{0,2},{1,3},{2,0},{3,1},{4,6},{5,7},{6,4},{7,5},{8,10},{9,11},{10,... | collective-permute-start | bytes 393224 | tf_op jit(solution)/shard_map/ppermute | solution.py:530
  16.2 2.9 %collective-permute-start.2 = (bf16[8,16,512]{2,1,0:T(8,128)(2,1)}, bf16[8,16,512]{2,1,0:T(8,128)(2,1)S(1)}, u32[]{:S(2)}, u32[]{:S(2)}) collective-permute-start(bf16[8,16,512]{2,1,0:T(8,128)(2,1)} %get-tuple-element.34), channel_id=1, source_target_pairs={{0,3},{1,0},{2,1},{3,2},{4,7},{5,4},{6,5},{7,6},{8,11},{9,8},{10,9... | collective-permute-start | bytes 393224 | tf_op jit(solution)/shard_map/ppermute | solution.py:530
  19.3 0.1 convert_reduce_fusion
  19.5 0.3 convert_reduce_fusion.1
  19.8 0.2 select_reduce_fusion.refs_0_
  20.0 7.3 %near_own.1.refs_4_ = f32[8,2,128,256]{3,2,1,0:T(8,128)} custom-call(s32[3,96]{1,0:T(4,128)S(1)} %select_reduce_fusion.refs_0_, s32[3,9]{1,0:T(4,128)S(1)} %copy.24.refs_1_, bf16[96,2,128,128]{3,2,1,0:T(8,128)(2,1)} %bitcast.14, bf16[8,2,128,256]{3,2,1,0:T(8,128)(2,1)} %refs_3_.1), custom_call_target="tpu_custom_call" | custom-call | flops 2000000000 | bytes 8388608 | tf_op jit(solution)/shard_map/near_own/pallas_call | solution.py:402
  27.4 0.1 copy.21.table_ref
  27.5 2.0 %adjoint.1.refs_6_ = bf16[8,128,256]{2,1,0:T(8,128)(2,1)} custom-call(bf16[8,2,128,128]{3,2,1,0:T(8,128)(2,1)} %rad_ref.1), custom_call_target="tpu_custom_call" | custom-call | flops 1000000 | bytes 2097152 | tf_op jit(solution)/shard_map/adjoint/pallas_call | solution.py:429
  29.6 0.1 copy.19
  29.7 0.1 copy.20
  29.9 1.1 %coupling.1.lines_hbm = f32[2,32,512]{2,1,0:T(8,128)S(1)} custom-call(s32[512,2]{1,0:T(8,128)S(1)} %broadcast_select_fusion.lists_ref, s32[1]{0:T(128)} %constant.91.clone.1.base_ref, bf16[316,32]{1,0:T(8,128)(2,1)S(1)} %copy.21.table_ref), custom_call_target="tpu_custom_call" | custom-call | flops 200000000 | bytes 2097152 | tf_op jit(solution)/shard_map/coupling/pallas_call | solution.py:185
  31.0 2.8 %collective-permute-done = bf16[8,16,512]{2,1,0:T(8,128)(2,1)S(1)} collective-permute-done((bf16[8,16,512]{2,1,0:T(8,128)(2,1)}, bf16[8,16,512]{2,1,0:T(8,128)(2,1)S(1)}, u32[]{:S(2)}, u32[]{:S(2)}) %collective-permute-start) | collective-permute-done | bytes 131104 | tf_op jit(solution)/shard_map/ppermute | solution.py:530
  33.8 6.1 %collective-permute-done.1 = bf16[8,16,512]{2,1,0:T(8,128)(2,1)S(1)} collective-permute-done((bf16[8,16,512]{2,1,0:T(8,128)(2,1)}, bf16[8,16,512]{2,1,0:T(8,128)(2,1)S(1)}, u32[]{:S(2)}, u32[]{:S(2)}) %collective-permute-start.1) | collective-permute-done | bytes 131104 | tf_op jit(solution)/shard_map/ppermute | solution.py:530
  39.9 0.9 pad_maximum_fusion
  40.7 3.5 %all-to-all-start = ((bf16[8,4,16,512]{3,2,1,0:T(8,128)(2,1)}), bf16[8,4,16,512]{3,2,1,0:T(8,128)(2,1)S(1)}, u32[]{:S(2)}, u32[]{:S(2)}) async-start(bf16[8,4,16,512]{3,2,1,0:T(8,128)(2,1)} %pad_maximum_fusion), calls=%async_computation | async-start | bytes 1048576 | tf_op jit(solution)/shard_map/all_to_all | solution.py:536
  44.2 1.3 %collective-permute-start.4 = (bf16[8,2,128,256]{3,2,1,0:T(8,128)(2,1)S(1)}, bf16[8,2,128,256]{3,2,1,0:T(8,128)(2,1)}, u32[]{:S(2)}, u32[]{:S(2)}) collective-permute-start(bf16[8,2,128,256]{3,2,1,0:T(8,128)(2,1)S(1)} %copy-done.2), channel_id=1, source_target_pairs={{1,0},{2,1},{3,2},{4,3},{5,4},{6,5},{7,6},{8,7},{9,8},{10,9},{11,1... | collective-permute-start | bytes 3145736 | tf_op jit(solution)/shard_map/ppermute | solution.py:516
  45.5 7.5 %all-to-all-done.refs_0_ = bf16[8,4,16,512]{3,2,1,0:T(8,128)(2,1)S(1)} async-done(((bf16[8,4,16,512]{3,2,1,0:T(8,128)(2,1)}), bf16[8,4,16,512]{3,2,1,0:T(8,128)(2,1)S(1)}, u32[]{:S(2)}, u32[]{:S(2)}) %all-to-all-start) | async-done | bytes 524320 | tf_op jit(solution)/shard_map/all_to_all | solution.py:536
  53.0 2.5 %translate.1 = bf16[32,16,512]{2,1,0:T(8,128)(2,1)} custom-call(s32[1]{0:T(128)} %bitcast.phi_ref, f32[2,32,512]{2,1,0:T(8,128)} %copy-done.1, bf16[8,4,16,512]{3,2,1,0:T(8,128)(2,1)S(1)} %all-to-all-done.refs_0_), custom_call_target="tpu_custom_call" | custom-call | flops 1000000000 | bytes 2097152 | tf_op jit(solution)/shard_map/translate/pallas_call | solution.py:248
  55.6 3.5 %all-to-all-start.1 = ((bf16[8,4,16,512]{3,2,1,0:T(8,128)(2,1)}), bf16[8,4,16,512]{3,2,1,0:T(8,128)(2,1)S(1)}, u32[]{:S(2)}, u32[]{:S(2)}) async-start(bf16[8,4,16,512]{3,2,1,0:T(8,128)(2,1)} %bitcast.17), calls=%async_computation.1 | async-start | bytes 1048576 | tf_op jit(solution)/shard_map/all_to_all | solution.py:536
  59.1 5.9 %near_low.1.refs_4_ = f32[8,2,128,256]{3,2,1,0:T(8,128)} custom-call(s32[3,96]{1,0:T(4,128)S(1)} %select_reduce_fusion.refs_0_, s32[3,9]{1,0:T(4,128)S(1)} %copy.24.refs_1_, bf16[96,2,128,128]{3,2,1,0:T(8,128)(2,1)} %bitcast.15, bf16[8,2,128,256]{3,2,1,0:T(8,128)(2,1)} %copy-done.3, f32[8,2,128,256]{3,2,1,0:T(8,128)} %near_own.1.refs_4_), custom_call_target="tpu_custom_call" | custom-call | flops 2000000000 | bytes 8388608 | tf_op jit(solution)/shard_map/near_low/pallas_call | solution.py:402
  65.0 2.8 %all-to-all-done.1.refs_0_ = bf16[8,4,16,512]{3,2,1,0:T(8,128)(2,1)S(1)} async-done(((bf16[8,4,16,512]{3,2,1,0:T(8,128)(2,1)}), bf16[8,4,16,512]{3,2,1,0:T(8,128)(2,1)S(1)}, u32[]{:S(2)}, u32[]{:S(2)}) %all-to-all-start.1) | async-done | bytes 524320 | tf_op jit(solution)/shard_map/all_to_all | solution.py:536
  67.9 3.3 %collective-permute-start.6 = (bf16[8,16,512]{2,1,0:T(8,128)(2,1)S(1)}, bf16[8,16,512]{2,1,0:T(8,128)(2,1)S(1)}, u32[]{:S(2)}, u32[]{:S(2)}) collective-permute-start(bf16[8,16,512]{2,1,0:T(8,128)(2,1)S(1)} %get-tuple-element.51), channel_id=1, source_target_pairs={{0,1},{1,2},{2,3},{3,0},{4,5},{5,6},{6,7},{7,4},{8,9},{9,10},{10,1... | collective-permute-start | bytes 393224 | tf_op jit(solution)/shard_map/ppermute | solution.py:530
  71.2 7.2 %collective-permute-start.7 = (bf16[8,16,512]{2,1,0:T(8,128)(2,1)S(1)}, bf16[8,16,512]{2,1,0:T(8,128)(2,1)S(1)}, u32[]{:S(2)}, u32[]{:S(2)}) collective-permute-start(bf16[8,16,512]{2,1,0:T(8,128)(2,1)S(1)} %get-tuple-element.50), channel_id=1, source_target_pairs={{0,2},{1,3},{2,0},{3,1},{4,6},{5,7},{6,4},{7,5},{8,10},{9,11},{10,... | collective-permute-start | bytes 393224 | tf_op jit(solution)/shard_map/ppermute | solution.py:530
  78.4 5.1 %near_high.1 = (f32[8,2,128,256]{3,2,1,0:T(8,128)S(1)}, bf16[1024,512]{1,0:T(8,128)(2,1)S(1)}, bf16[8,128,256]{2,1,0:T(8,128)(2,1)S(1)}) custom-call(s32[3,96]{1,0:T(4,128)S(1)} %select_reduce_fusion.refs_0_, s32[3,9]{1,0:T(4,128)S(1)} %copy.24.refs_1_, bf16[96,2,128,128]{3,2,1,0:T(8,128)(2,1)} %bitcast.16, ...), custom_call_target="tpu_custom_call" | custom-call | flops 99999997952 | bytes 8388608 | tf_op jit(solution)/shard_map/near_high/pallas_call | solution.py:402
  83.5 3.2 %collective-permute-done.7.refs_2_ = bf16[8,16,512]{2,1,0:T(8,128)(2,1)S(1)} collective-permute-done((bf16[8,16,512]{2,1,0:T(8,128)(2,1)S(1)}, bf16[8,16,512]{2,1,0:T(8,128)(2,1)S(1)}, u32[]{:S(2)}, u32[]{:S(2)}) %collective-permute-start.7) | collective-permute-done | bytes 131104 | tf_op jit(solution)/shard_map/ppermute | solution.py:530
  86.7 2.3 %downward.1 = f32[8,2,128,256]{3,2,1,0:T(8,128)} custom-call(s32[1]{0:T(128)} %bitcast.phi_ref, f32[8,2,128,256]{3,2,1,0:T(8,128)S(1)} %get-tuple-element.45.near_ref, bf16[1024,512]{1,0:T(8,128)(2,1)S(1)} %get-tuple-element.46.w_ref, bf16[8,128,256]{2,1,0:T(8,128)(2,1)S(1)} %get-tuple-element.47.adjoint_ref, ...), custom_call_target="tpu_custom_call" | custom-call | flops 2000000000 | bytes 7340032 | tf_op jit(solution)/shard_map/downward/pallas_call | solution.py:493
  (35 shorter events, 0.5 us)
Async XLA Ops:
  0.0 27.3 %copy-start = (bf16[316,2,4,8]{0,3,2,1:T(8,128)(2,1)S(1)}, bf16[316,2,4,8]{0,3,2,1:T(8,128)(2,1)}, u32[]{:S(2)}) copy-start(bf16[316,2,4,8]{0,3,2,1:T(8,128)(2,1)} %param.19) | copy-start | bytes 121348
  0.0 55.5 %collective-permute-start.5 = (bf16[8,2,128,256]{3,2,1,0:T(8,128)(2,1)}, bf16[8,2,128,256]{3,2,1,0:T(8,128)(2,1)S(1)}, u32[]{:S(2)}, u32[]{:S(2)}) collective-permute-start(bf16[8,2,128,256]{3,2,1,0:T(8,128)(2,1)} %refs_3_.1), channel_id=1, source_target_pairs={{0,1},{1,2},{2,3},{3,4},{4,5},{5,6},{6,7},{7,8},{8,9},{9,10},{10,1... | collective-permute-start | bytes 3145736 | tf_op jit(solution)/shard_map/ppermute | solution.py:516
  6.8 12.3 %copy-start.5 = (s32[8,12]{1,0:T(8,128)S(1)}, s32[8,12]{1,0:T(8,128)}, u32[]{:S(2)}) copy-start(s32[8,12]{1,0:T(8,128)} %param.13) | copy-start | bytes 1156
  6.8 12.3 %copy-start.6 = (s32[8]{0:T(128)S(1)}, s32[8]{0:T(128)}, u32[]{:S(2)}) copy-start(s32[8]{0:T(128)} %param.14) | copy-start | bytes 100
  12.1 17.5 %collective-permute-start.3 = (s32[256,2]{0,1:T(2,128)S(1)}, s32[256,2]{0,1:T(2,128)S(1)}, u32[]{:S(2)}, u32[]{:S(2)}) collective-permute-start(s32[256,2]{0,1:T(2,128)S(1)} %pad_add_fusion.2), channel_id=1, source_target_pairs={{0,16},{16,0},{1,17},{17,1},{2,18},{18,2},{3,19},{19,3},{4,20},{20... | collective-permute-start | bytes 6152 | tf_op jit(solution)/shard_map/ppermute | solution.py:547
  13.6 20.2 %collective-permute-start = (bf16[8,16,512]{2,1,0:T(8,128)(2,1)}, bf16[8,16,512]{2,1,0:T(8,128)(2,1)S(1)}, u32[]{:S(2)}, u32[]{:S(2)}) collective-permute-start(bf16[8,16,512]{2,1,0:T(8,128)(2,1)} %get-tuple-element.32), channel_id=1, source_target_pairs={{0,1},{1,2},{2,3},{3,0},{4,5},{5,6},{6,7},{7,4},{8,9},{9,10},{10,1... | collective-permute-start | bytes 393224 | tf_op jit(solution)/shard_map/ppermute | solution.py:530
  15.2 24.7 %collective-permute-start.1 = (bf16[8,16,512]{2,1,0:T(8,128)(2,1)}, bf16[8,16,512]{2,1,0:T(8,128)(2,1)S(1)}, u32[]{:S(2)}, u32[]{:S(2)}) collective-permute-start(bf16[8,16,512]{2,1,0:T(8,128)(2,1)} %get-tuple-element.33), channel_id=1, source_target_pairs={{0,2},{1,3},{2,0},{3,1},{4,6},{5,7},{6,4},{7,5},{8,10},{9,11},{10,... | collective-permute-start | bytes 393224 | tf_op jit(solution)/shard_map/ppermute | solution.py:530
  16.2 23.7 %collective-permute-start.2 = (bf16[8,16,512]{2,1,0:T(8,128)(2,1)}, bf16[8,16,512]{2,1,0:T(8,128)(2,1)S(1)}, u32[]{:S(2)}, u32[]{:S(2)}) collective-permute-start(bf16[8,16,512]{2,1,0:T(8,128)(2,1)} %get-tuple-element.34), channel_id=1, source_target_pairs={{0,3},{1,0},{2,1},{3,2},{4,7},{5,4},{6,5},{7,6},{8,11},{9,8},{10,9... | collective-permute-start | bytes 393224 | tf_op jit(solution)/shard_map/ppermute | solution.py:530
  27.3 12.5 %copy-start.4 = (bf16[8,16,512]{2,1,0:T(8,128)(2,1)S(1)}, bf16[8,16,512]{2,1,0:T(8,128)(2,1)}, u32[]{:S(2)}) copy-start(bf16[8,16,512]{2,1,0:T(8,128)(2,1)} %get-tuple-element.38) | copy-start | bytes 393220
  29.5 14.7 %copy-start.2 = (bf16[8,2,128,256]{3,2,1,0:T(8,128)(2,1)S(1)}, bf16[8,2,128,256]{3,2,1,0:T(8,128)(2,1)}, u32[]{:S(2)}) copy-start(bf16[8,2,128,256]{3,2,1,0:T(8,128)(2,1)} %refs_3_.1) | copy-start | bytes 3145732
  31.0 9.8 %copy-start.1 = (f32[2,32,512]{2,1,0:T(8,128)}, f32[2,32,512]{2,1,0:T(8,128)S(1)}, u32[]{:S(2)}) copy-start(f32[2,32,512]{2,1,0:T(8,128)S(1)} %coupling.1.lines_hbm) | copy-start | bytes 393220
  40.7 12.3 %all-to-all-start = ((bf16[8,4,16,512]{3,2,1,0:T(8,128)(2,1)}), bf16[8,4,16,512]{3,2,1,0:T(8,128)(2,1)S(1)}, u32[]{:S(2)}, u32[]{:S(2)}) async-start(bf16[8,4,16,512]{3,2,1,0:T(8,128)(2,1)} %pad_maximum_fusion), calls=%async_computation | async-start | bytes 1048576 | tf_op jit(solution)/shard_map/all_to_all | solution.py:536
  44.2 34.1 %collective-permute-start.4 = (bf16[8,2,128,256]{3,2,1,0:T(8,128)(2,1)S(1)}, bf16[8,2,128,256]{3,2,1,0:T(8,128)(2,1)}, u32[]{:S(2)}, u32[]{:S(2)}) collective-permute-start(bf16[8,2,128,256]{3,2,1,0:T(8,128)(2,1)S(1)} %copy-done.2), channel_id=1, source_target_pairs={{1,0},{2,1},{3,2},{4,3},{5,4},{6,5},{7,6},{8,7},{9,8},{10,9},{11,1... | collective-permute-start | bytes 3145736 | tf_op jit(solution)/shard_map/ppermute | solution.py:516
  55.5 3.6 %copy-start.3 = (bf16[8,2,128,256]{3,2,1,0:T(8,128)(2,1)}, bf16[8,2,128,256]{3,2,1,0:T(8,128)(2,1)S(1)}, u32[]{:S(2)}) copy-start(bf16[8,2,128,256]{3,2,1,0:T(8,128)(2,1)S(1)} %collective-permute-done.5.refs_3_) | copy-start | bytes 3145732
  55.6 12.3 %all-to-all-start.1 = ((bf16[8,4,16,512]{3,2,1,0:T(8,128)(2,1)}), bf16[8,4,16,512]{3,2,1,0:T(8,128)(2,1)S(1)}, u32[]{:S(2)}, u32[]{:S(2)}) async-start(bf16[8,4,16,512]{3,2,1,0:T(8,128)(2,1)} %bitcast.17), calls=%async_computation.1 | async-start | bytes 1048576 | tf_op jit(solution)/shard_map/all_to_all | solution.py:536
  67.9 15.6 %collective-permute-start.6 = (bf16[8,16,512]{2,1,0:T(8,128)(2,1)S(1)}, bf16[8,16,512]{2,1,0:T(8,128)(2,1)S(1)}, u32[]{:S(2)}, u32[]{:S(2)}) collective-permute-start(bf16[8,16,512]{2,1,0:T(8,128)(2,1)S(1)} %get-tuple-element.51), channel_id=1, source_target_pairs={{0,1},{1,2},{2,3},{3,0},{4,5},{5,6},{6,7},{7,4},{8,9},{9,10},{10,1... | collective-permute-start | bytes 393224 | tf_op jit(solution)/shard_map/ppermute | solution.py:530
  71.2 15.5 %collective-permute-start.7 = (bf16[8,16,512]{2,1,0:T(8,128)(2,1)S(1)}, bf16[8,16,512]{2,1,0:T(8,128)(2,1)S(1)}, u32[]{:S(2)}, u32[]{:S(2)}) collective-permute-start(bf16[8,16,512]{2,1,0:T(8,128)(2,1)S(1)} %get-tuple-element.50), channel_id=1, source_target_pairs={{0,2},{1,3},{2,0},{3,1},{4,6},{5,7},{6,4},{7,5},{8,10},{9,11},{10,... | collective-permute-start | bytes 393224 | tf_op jit(solution)/shard_map/ppermute | solution.py:530
  78.4 8.3 %collective-permute-start.8 = (bf16[8,16,512]{2,1,0:T(8,128)(2,1)S(1)}, bf16[8,16,512]{2,1,0:T(8,128)(2,1)S(1)}, u32[]{:S(2)}, u32[]{:S(2)}) collective-permute-start(bf16[8,16,512]{2,1,0:T(8,128)(2,1)S(1)} %get-tuple-element.49), channel_id=1, source_target_pairs={{0,3},{1,0},{2,1},{3,2},{4,7},{5,4},{6,5},{7,6},{8,11},{9,8},{10,9... | collective-permute-start | bytes 393224 | tf_op jit(solution)/shard_map/ppermute | solution.py:530

commit v12 on v10

--- a/solution.py
+++ b/solution.py
@@ -22,7 +22,7 @@
 F32 = jnp.float32
 BF16 = jnp.bfloat16
 MIB = 2**20
-GROUP = 4
+GROUP = 2
 NOWHERE = -(2**20)
 
 
@@ -249,16 +249,15 @@
 
 def near_kernel(first, begun, kept, *refs):
     refs = list(refs)
-    ids_ref, used_ref, rank_ref, blocks_hbm, source_hbm = refs[:5]
-    before_hbm = refs[5] if begun else None
-    kept_hbm = refs[5 + begun : 5 + begun + kept]
-    out_ref = refs[5 + begun + kept]
-    kept_refs = refs[6 + begun + kept : 6 + begun + 2 * kept]
-    blocks, held, wide, total_ref, listed, sems = refs[6 + begun + 2 * kept :]
+    listed, starts_ref, blocks_hbm, source_hbm = refs[:4]
+    before_hbm = refs[4] if begun else None
+    kept_hbm = refs[4 + begun : 4 + begun + kept]
+    out_ref = refs[4 + begun + kept]
+    kept_refs = refs[5 + begun + kept : 5 + begun + 2 * kept]
+    blocks, held, wide, total_ref, sems = refs[5 + begun + 2 * kept :]
     boxes, _, basis, rhs = held.shape
-    slots = blocks_hbm.shape[1]
-    most = boxes * slots
-    base = (rank_ref[0] - 1 + first) * boxes
+    most = blocks_hbm.shape[0]
+    starts = [starts_ref[first, box] for box in range(boxes + 1)]
 
     def by_box(source, target, turn):
         return [
@@ -278,23 +277,15 @@
     for copy in source_copies:
         copy.start()
 
-    def block_copy(box, slot, place):
-        return pltpu.make_async_copy(blocks_hbm.at[box, slot], blocks.at[place], sems.at[place])
-
-    starts = [jnp.int32(0)]
-    for box in range(boxes):
-        place = starts[box]
-        for slot in range(slots):
-            source = ids_ref[box, slot] - base
-            wanted = (slot < used_ref[box]) & (source >= 0) & (source < boxes)
-
-            @pl.when(wanted)
-            def _(box=box, slot=slot, place=place, source=source):
-                listed[place] = source
-                block_copy(box, slot, place).start()
-
-            place += wanted.astype(jnp.int32)
-        starts.append(place)
+    def block_copy(place):
+        block = listed[first, place] // boxes
+        return pltpu.make_async_copy(blocks_hbm.at[block], blocks.at[place], sems.at[place])
+
+    def fetch(place, carry):
+        block_copy(place).start()
+        return carry
+
+    lax.fori_loop(0, starts[boxes], fetch, 0)
     for copy in before_copies + kept_copies:
         copy.start()
     for copy in source_copies:
@@ -303,28 +294,30 @@
         wide[place] = complex_columns(held[place, 0], held[place, 1])
 
     def landed(place, carry):
-        block_copy(0, 0, place).wait()
+        block_copy(place).wait()
         return carry
 
     lax.fori_loop(0, starts[boxes], landed, 0)
     for copy in before_copies:
         copy.wait()
 
-    def group(box, index):
+    def group(box, begin, size):
         left, right = [], []
-        for step in range(GROUP):
-            place = starts[box] + index * GROUP + step
+        for step in range(size):
+            place = starts[box] + begin + step
             valid = place < starts[box + 1]
             place = jnp.where(valid, place, 0)
             real, imag = blocks[place, 0], blocks[place, 1]
             real = jnp.where(valid, real, jnp.zeros_like(real))
             imag = jnp.where(valid, imag, jnp.zeros_like(imag))
             left.append(side_by_side(real, imag))
-            right.append(wide[jnp.where(valid, listed[place], 0)])
+            right.append(wide[jnp.where(valid, listed[first, place] % boxes, 0)])
         return dot(jnp.concatenate(left, axis=1), jnp.concatenate(right, axis=0))
 
+    possible = [(boxes - box, boxes, box + 1)[first] for box in range(boxes)]
+    sizes = [min(count, 3 if count < 7 else 4) for count in possible]
     for box in range(boxes):
-        part = group(box, 0)
+        part = group(box, 0, sizes[box])
         if begun:
             total_ref[box, 0] += part[:, :rhs]
             total_ref[box, 1] += part[:, rhs:]
@@ -334,20 +327,38 @@
     for box in range(boxes):
 
         def more(index, carry, box=box):
-            part = group(box, index)
+            part = group(box, sizes[box] + GROUP * index, GROUP)
             total_ref[box, 0] += part[:, :rhs]
             total_ref[box, 1] += part[:, rhs:]
             return carry
 
-        lax.fori_loop(1, (starts[box + 1] - starts[box] + GROUP - 1) // GROUP, more, 0)
+        rest = starts[box + 1] - starts[box] - sizes[box]
+        lax.fori_loop(0, (jnp.maximum(rest, 0) + GROUP - 1) // GROUP, more, 0)
         if out_copies:
             out_copies[box].start()
     for copy in out_copies + kept_copies:
         copy.wait()
 
 
-def near_field(ids, used, rank, blocks, source, first, before=None, keep=()):
+def near_slots(ids, used, rank):
+    boxes, slots = ids.shape
+    total = boxes * slots
+    source = ids - (rank - 1) * boxes
+    source = jnp.where(jnp.arange(slots) < used[:, None], source, -1).reshape(-1)
+    wanted = (source >= 0) & (source // boxes == jnp.arange(3)[:, None])
+    earlier = jnp.arange(total)[None, :] < jnp.arange(total)[:, None]
+    place = jnp.sum((wanted[:, None, :] & earlier).astype(jnp.int32), axis=2)
+    code = jnp.arange(total) * boxes + source % boxes
+    chosen = wanted[:, None, :] & (place[:, None, :] == jnp.arange(total)[:, None])
+    listed = jnp.sum(jnp.where(chosen, code, 0), axis=2)
+    before = jnp.arange(total) // slots < jnp.arange(boxes + 1)[:, None]
+    starts = jnp.sum((wanted[:, None, :] & before).astype(jnp.int32), axis=2)
+    return listed.astype(jnp.int32), starts.astype(jnp.int32)
+
+
+def near_field(listed, starts, blocks, source, first, before=None, keep=()):
     boxes, slots, _, basis, _ = blocks.shape
+    blocks = blocks.reshape(boxes * slots, *blocks.shape[2:])
     rhs = source.shape[3]
     begun, kept = before is not None, len(keep)
     hbm = pl.BlockSpec(memory_space=pltpu.HBM)
@@ -355,11 +366,10 @@
     vmem = pl.BlockSpec(memory_space=pltpu.VMEM)
     shape = (boxes, 2, basis, rhs)
     scratch = [
-        pltpu.VMEM((boxes * slots, *blocks.shape[2:]), BF16),
+        pltpu.VMEM(blocks.shape, BF16),
         pltpu.VMEM(source.shape, BF16),
         pltpu.VMEM((boxes, 2 * basis, 2 * rhs), BF16),
         pltpu.VMEM(shape, F32),
-        pltpu.SMEM((boxes * slots,), jnp.int32),
         pltpu.SemaphoreType.DMA((boxes * slots + 3 * boxes + kept,)),
     ]
     kernel = functools.partial(near_kernel, first, begun, kept)
@@ -368,12 +378,14 @@
         inner = kernel
 
         def kernel(*refs):
-            place = 5 + begun + kept
-            inner(*refs[:-2], refs[place], *refs[-2:])
+            place = 4 + begun + kept
+            inner(*refs[:-1], refs[place], refs[-1])
 
     return pl.pallas_call(
         kernel,
-        in_specs=[smem] * 3 + [hbm] * (2 + begun + kept),
+        in_specs=[smem] * 2
+        + [hbm, pl.BlockSpec(memory_space=pl.ANY)]
+        + [hbm] * (begun + kept),
         out_specs=[vmem] * (1 + kept) if kept else hbm,
         out_shape=[
             pltpu.VMEM(shape, F32),
@@ -387,7 +399,13 @@
             flops=10**11 if first == 2 else 2 * 10**9, bytes_accessed=8 * MIB, transcendentals=0
         ),
         name=("near_low", "near_own", "near_high")[first],
-    )(ids, used, rank, *in_hbm(blocks, source, *([before] if begun else []), *keep))
+    )(
+        listed,
+        starts,
+        *in_hbm(blocks),
+        source if first != 1 else in_hbm(source)[0],
+        *in_hbm(*([before] if begun else []), *keep),
+    )
 
 
 def adjoint_kernel(rad_ref, out_hbm, held):
@@ -548,17 +566,18 @@
 ):
     every = ("box", "theta", "phi")
     per_group = lax.axis_size("theta") * lax.axis_size("phi")
-    rank = lax.axis_index(every).astype(jnp.int32).reshape(1)
     low = shift(coeffs, every, 1)
     spread = upward(coeffs, radiation, up_weights, shares * per_group)
     radiation_adjoint = adjoint(radiation)
     lists = lists_of(partners, vector_ids, pair_count)
     spread, lists = lax.optimization_barrier((spread, lists))
     lines = translation_lines(lists, translation, shares, per_group)
-    spread, lines, radiation_adjoint = lax.optimization_barrier((spread, lines, radiation_adjoint))
+    listed, starts = near_slots(near_ids, near_count, lax.axis_index(every))
+    spread, lines, radiation_adjoint, listed, starts = lax.optimization_barrier(
+        (spread, lines, radiation_adjoint, listed, starts)
+    )
     parents = parent_bands(spread, shares)
-    slots = (near_ids, near_count, rank, near_blocks)
-    near = near_field(*slots, low, 0)
+    near = near_field(listed, starts, near_blocks, low, 0)
     near, late = lax.optimization_barrier((near, coeffs))
     high = shift(late, every, -1)
     parents, near = lax.optimization_barrier((parents, near))
@@ -568,8 +587,10 @@
     incoming = translate(lines, sources)
     incoming, near = lax.optimization_barrier((incoming, near))
     phi, bands, received = staged_bands(incoming, shares)
-    near = near_field(*slots, coeffs, 1, near)
-    ready = near_field(*slots, high, 2, near, keep=(down_weights, radiation_adjoint))
+    near = near_field(listed, starts, near_blocks, coeffs, 1, near)
+    ready = near_field(
+        listed, starts, near_blocks, high, 2, near, keep=(down_weights, radiation_adjoint)
+    )
     return downward(phi, bands, received, *ready)
 
 

time: 79 us -> 79 us (level)
  the two profiles are of different devices: /device:TPU:0 before, /device:TPU:12 now
where the time goes in v12:
time: 79 us; the launch traced here: 78.6 us
  Pallas kernels  34.2 us (43%)
  starting transfers between devices  26.4 us (33%)
  waiting for transfers between devices  14.2 us (18%)
  local copies, waits for them, and re-layouts  2.16 us (3%)
  other arithmetic  1.49 us (2%)
    pallas_call x3, Pallas kernels, near_field(): pl.pallas_call(kernel, in_specs=[smem] * 2 + [hbm, pl.BlockSpec(memory_sp...  21.1 us
    ppermute x2, waiting for transfers between devices, shift(): return lax.ppermute(block, axis, pairs)  13.2 us
    ppermute x3, starting transfers between devices, staged_bands(): received.append(lax.ppermute(piece, 'phi', ring))  8.86 us
    ppermute x2, starting transfers between devices, shift(): return lax.ppermute(block, axis, pairs)  7.59 us
    pallas_call x1, Pallas kernels, upward(): pl.pallas_call(up_kernel, in_specs=[hbm] * 3, out_specs=hbm, out_shape=pl...  5.25 us
    all_to_all x1, starting transfers between devices, staged_bands(): bands = lax.all_to_all(bands, axes, split_axis=0, concat_axis=0, tiled=True)  4.27 us
    all_to_all x1, starting transfers between devices, parent_bands(): return lax.all_to_all(spread, axes, split_axis=0, concat_axis=0, tiled=True)  4.08 us
    pallas_call x1, Pallas kernels, translate(): pl.pallas_call(translate_kernel, in_specs=[hbm] + [anywhere] * len(source...  2.49 us
  transfers between devices with their start and end apart: 8, of which 4 were waited for; matrix products, arithmetic and copies ran while one was open for 4% of the time, Pallas kernels for 41%

profile of v12, /device:TPU:12, one launch (start us, length us, event | category | flops | bytes accessed | tf_op | source)
XLA Modules:
  0.0 78.6 jit_solution(8446810706988273817)
XLA Ops:
  0.0 3.6 %collective-permute-start.1 = (bf16[8,2,128,256]{3,2,1,0:T(8,128)(2,1)}, bf16[8,2,128,256]{3,2,1,0:T(8,128)(2,1)S(1)}, u32[]{:S(2)}, u32[]{:S(2)}) collective-permute-start(bf16[8,2,128,256]{3,2,1,0:T(8,128)(2,1)} %refs_3_.1), channel_id=1, source_target_pairs={{0,1},{1,2},{2,3},{3,4},{4,5},{5,6},{6,7},{7,8},{8,9},{9,10},{10,1... | collective-permute-start | bytes 3145736 | tf_op jit(solution)/shard_map/ppermute | solution.py:506
  3.6 0.8 fusion.1
  4.4 0.1 stack.9
  4.5 0.8 stack.10
  5.3 5.3 %upward.1 = bf16[32,16,512]{2,1,0:T(8,128)(2,1)} custom-call(bf16[8,2,128,256]{3,2,1,0:T(8,128)(2,1)} %refs_3_.1, bf16[8,2,128,128]{3,2,1,0:T(8,128)(2,1)} %rad_ref.1, bf16[1024,1024]{1,0:T(8,128)(2,1)} %constant.93.clone.w_hbm), custom_call_target="tpu_custom_call" | custom-call | flops 2000000000 | bytes 4194304 | tf_op jit(solution)/shard_map/upward/pallas_call | solution.py:127
  10.5 1.6 %collective-permute-start = (s32[256,2]{0,1:T(2,128)S(1)}, s32[256,2]{0,1:T(2,128)S(1)}, u32[]{:S(2)}, u32[]{:S(2)}) collective-permute-start(s32[256,2]{0,1:T(2,128)S(1)} %pad_add_fusion.2), channel_id=1, source_target_pairs={{0,16},{16,0},{1,17},{17,1},{2,18},{18,2},{3,19},{19,3},{4,20},{20... | collective-permute-start | bytes 6152 | tf_op jit(solution)/shard_map/ppermute | solution.py:542
  12.2 0.1 reshape.134
  12.3 0.1 convert_reduce_fusion
  12.5 0.2 select_reduce_fusion.refs_0_
  12.7 0.2 convert_reduce_fusion.1
  12.9 0.1 copy.21.table_ref
  13.0 2.0 %adjoint.1.refs_6_ = bf16[8,128,256]{2,1,0:T(8,128)(2,1)} custom-call(bf16[8,2,128,128]{3,2,1,0:T(8,128)(2,1)} %rad_ref.1), custom_call_target="tpu_custom_call" | custom-call | flops 1000000 | bytes 2097152 | tf_op jit(solution)/shard_map/adjoint/pallas_call | solution.py:419
  15.1 0.1 copy.19
  15.2 0.1 copy.20
  15.4 1.1 %coupling.1.lines_hbm = f32[2,32,512]{2,1,0:T(8,128)S(1)} custom-call(s32[512,2]{1,0:T(8,128)S(1)} %broadcast_select_fusion.lists_ref, s32[1]{0:T(128)} %constant.82.clone.1.base_ref, bf16[316,32]{1,0:T(8,128)(2,1)S(1)} %copy.21.table_ref), custom_call_target="tpu_custom_call" | custom-call | flops 200000000 | bytes 2097152 | tf_op jit(solution)/shard_map/coupling/pallas_call | solution.py:175
  16.5 0.6 copy-done.1
  17.2 4.1 %all-to-all-start = ((bf16[32,16,512]{2,1,0:T(8,128)(2,1)}), bf16[32,16,512]{2,1,0:T(8,128)(2,1)S(1)}, u32[]{:S(2)}, u32[]{:S(2)}) async-start(bf16[32,16,512]{2,1,0:T(8,128)(2,1)} %upward.1), calls=%async_computation | async-start | bytes 1048576 | tf_op jit(solution)/shard_map/all_to_all | solution.py:517
  21.2 0.1 copy.24.refs_1_
  21.3 7.7 %collective-permute-done.1.refs_3_ = bf16[8,2,128,256]{3,2,1,0:T(8,128)(2,1)S(1)} collective-permute-done((bf16[8,2,128,256]{3,2,1,0:T(8,128)(2,1)}, bf16[8,2,128,256]{3,2,1,0:T(8,128)(2,1)S(1)}, u32[]{:S(2)}, u32[]{:S(2)}) %collective-permute-start.1) | collective-permute-done | bytes 1048608 | tf_op jit(solution)/shard_map/ppermute | solution.py:506
  29.0 6.5 %near_low.1.refs_4_ = f32[8,2,128,256]{3,2,1,0:T(8,128)} custom-call(s32[3,96]{1,0:T(4,128)S(1)} %select_reduce_fusion.refs_0_, s32[3,9]{1,0:T(4,128)S(1)} %copy.24.refs_1_, bf16[96,2,128,128]{3,2,1,0:T(8,128)(2,1)} %bitcast.10, bf16[8,2,128,256]{3,2,1,0:T(8,128)(2,1)S(1)} %collective-permute-done.1.refs_3_), custom_call_target="tpu_custom_call" | custom-call | flops 2000000000 | bytes 8388608 | tf_op jit(solution)/shard_map/near_low/pallas_call | solution.py:384
  35.5 4.0 %collective-permute-start.2 = (bf16[8,2,128,256]{3,2,1,0:T(8,128)(2,1)}, bf16[8,2,128,256]{3,2,1,0:T(8,128)(2,1)S(1)}, u32[]{:S(2)}, u32[]{:S(2)}) collective-permute-start(bf16[8,2,128,256]{3,2,1,0:T(8,128)(2,1)} %refs_3_.1), channel_id=1, source_target_pairs={{1,0},{2,1},{3,2},{4,3},{5,4},{6,5},{7,6},{8,7},{9,8},{10,9},{11,1... | collective-permute-start | bytes 3145736 | tf_op jit(solution)/shard_map/ppermute | solution.py:506
  39.5 0.5 all-to-all-done.refs_0_
  40.0 2.5 %translate.1 = bf16[32,16,512]{2,1,0:T(8,128)(2,1)} custom-call(f32[2,32,512]{2,1,0:T(8,128)} %copy-done.1, bf16[32,16,512]{2,1,0:T(8,128)(2,1)S(1)} %all-to-all-done.refs_0_), custom_call_target="tpu_custom_call" | custom-call | flops 1000000000 | bytes 2097152 | tf_op jit(solution)/shard_map/translate/pallas_call | solution.py:230
  42.5 4.3 %all-to-all-start.1 = ((bf16[8,4,16,512]{3,2,1,0:T(8,128)(2,1)}), bf16[8,4,16,512]{3,2,1,0:T(8,128)(2,1)S(1)}, u32[]{:S(2)}, u32[]{:S(2)}) async-start(bf16[8,4,16,512]{3,2,1,0:T(8,128)(2,1)} %bitcast.13), calls=%async_computation.1 | async-start | bytes 1048576 | tf_op jit(solution)/shard_map/all_to_all | solution.py:525
  46.7 7.8 %near_own.1.refs_4_ = f32[8,2,128,256]{3,2,1,0:T(8,128)} custom-call(s32[3,96]{1,0:T(4,128)S(1)} %select_reduce_fusion.refs_0_, s32[3,9]{1,0:T(4,128)S(1)} %copy.24.refs_1_, bf16[96,2,128,128]{3,2,1,0:T(8,128)(2,1)} %bitcast.11, bf16[8,2,128,256]{3,2,1,0:T(8,128)(2,1)} %refs_3_.1, f32[8,2,128,256]{3,2,1,0:T(8,128)} %near_low.1.refs_4_), custom_call_target="tpu_custom_call" | custom-call | flops 2000000000 | bytes 8388608 | tf_op jit(solution)/shard_map/near_own/pallas_call | solution.py:384
  54.5 0.5 all-to-all-done.1.refs_0_
  55.1 1.0 %collective-permute-start.3 = (bf16[8,16,512]{2,1,0:T(8,128)(2,1)S(1)}, bf16[8,16,512]{2,1,0:T(8,128)(2,1)S(1)}, u32[]{:S(2)}, u32[]{:S(2)}) collective-permute-start(bf16[8,16,512]{2,1,0:T(8,128)(2,1)S(1)} %get-tuple-element.39), channel_id=1, source_target_pairs={{0,1},{1,2},{2,3},{3,0},{4,5},{5,6},{6,7},{7,4},{8,9},{9,10},{10,1... | collective-permute-start | bytes 393224 | tf_op jit(solution)/shard_map/ppermute | solution.py:530
  56.0 5.9 %collective-permute-start.4 = (bf16[8,16,512]{2,1,0:T(8,128)(2,1)S(1)}, bf16[8,16,512]{2,1,0:T(8,128)(2,1)S(1)}, u32[]{:S(2)}, u32[]{:S(2)}) collective-permute-start(bf16[8,16,512]{2,1,0:T(8,128)(2,1)S(1)} %get-tuple-element.38), channel_id=1, source_target_pairs={{0,2},{1,3},{2,0},{3,1},{4,6},{5,7},{6,4},{7,5},{8,10},{9,11},{10,... | collective-permute-start | bytes 393224 | tf_op jit(solution)/shard_map/ppermute | solution.py:530
  62.0 1.9 %collective-permute-start.5 = (bf16[8,16,512]{2,1,0:T(8,128)(2,1)S(1)}, bf16[8,16,512]{2,1,0:T(8,128)(2,1)S(1)}, u32[]{:S(2)}, u32[]{:S(2)}) collective-permute-start(bf16[8,16,512]{2,1,0:T(8,128)(2,1)S(1)} %get-tuple-element.37), channel_id=1, source_target_pairs={{0,3},{1,0},{2,1},{3,2},{4,7},{5,4},{6,5},{7,6},{8,11},{9,8},{10,9... | collective-permute-start | bytes 393224 | tf_op jit(solution)/shard_map/ppermute | solution.py:530
  63.9 5.5 %collective-permute-done.2.refs_3_ = bf16[8,2,128,256]{3,2,1,0:T(8,128)(2,1)S(1)} collective-permute-done((bf16[8,2,128,256]{3,2,1,0:T(8,128)(2,1)}, bf16[8,2,128,256]{3,2,1,0:T(8,128)(2,1)S(1)}, u32[]{:S(2)}, u32[]{:S(2)}) %collective-permute-start.2) | collective-permute-done | bytes 1048608 | tf_op jit(solution)/shard_map/ppermute | solution.py:506
  69.4 6.9 %near_high.1 = (f32[8,2,128,256]{3,2,1,0:T(8,128)S(1)}, bf16[1024,512]{1,0:T(8,128)(2,1)S(1)}, bf16[8,128,256]{2,1,0:T(8,128)(2,1)S(1)}) custom-call(s32[3,96]{1,0:T(4,128)S(1)} %select_reduce_fusion.refs_0_, s32[3,9]{1,0:T(4,128)S(1)} %copy.24.refs_1_, bf16[96,2,128,128]{3,2,1,0:T(8,128)(2,1)} %bitcast.12, ...), custom_call_target="tpu_custom_call" | custom-call | flops 99999997952 | bytes 8388608 | tf_op jit(solution)/shard_map/near_high/pallas_call | solution.py:384
  76.3 2.3 %downward.1 = f32[8,2,128,256]{3,2,1,0:T(8,128)} custom-call(s32[1]{0:T(128)} %bitcast.phi_ref, f32[8,2,128,256]{3,2,1,0:T(8,128)S(1)} %get-tuple-element.33.near_ref, bf16[1024,512]{1,0:T(8,128)(2,1)S(1)} %get-tuple-element.34.w_ref, bf16[8,128,256]{2,1,0:T(8,128)(2,1)S(1)} %get-tuple-element.35.adjoint_ref, ...), custom_call_target="tpu_custom_call" | custom-call | flops 2000000000 | bytes 7340032 | tf_op jit(solution)/shard_map/downward/pallas_call | solution.py:483
  (22 shorter events, 0.2 us)
Async XLA Ops:
  0.0 12.6 %copy-start = (bf16[316,2,4,8]{0,3,2,1:T(8,128)(2,1)S(1)}, bf16[316,2,4,8]{0,3,2,1:T(8,128)(2,1)}, u32[]{:S(2)}) copy-start(bf16[316,2,4,8]{0,3,2,1:T(8,128)(2,1)} %param.19) | copy-start | bytes 121348
  0.0 29.0 %collective-permute-start.1 = (bf16[8,2,128,256]{3,2,1,0:T(8,128)(2,1)}, bf16[8,2,128,256]{3,2,1,0:T(8,128)(2,1)S(1)}, u32[]{:S(2)}, u32[]{:S(2)}) collective-permute-start(bf16[8,2,128,256]{3,2,1,0:T(8,128)(2,1)} %refs_3_.1), channel_id=1, source_target_pairs={{0,1},{1,2},{2,3},{3,4},{4,5},{5,6},{6,7},{7,8},{8,9},{9,10},{10,1... | collective-permute-start | bytes 3145736 | tf_op jit(solution)/shard_map/ppermute | solution.py:506
  5.2 6.8 %copy-start.2 = (s32[8,12]{1,0:T(8,128)S(1)}, s32[8,12]{1,0:T(8,128)}, u32[]{:S(2)}) copy-start(s32[8,12]{1,0:T(8,128)} %param.13) | copy-start | bytes 1156
  5.3 6.8 %copy-start.3 = (s32[8]{0:T(128)S(1)}, s32[8]{0:T(128)}, u32[]{:S(2)}) copy-start(s32[8]{0:T(128)} %param.14) | copy-start | bytes 100
  10.5 4.5 %collective-permute-start = (s32[256,2]{0,1:T(2,128)S(1)}, s32[256,2]{0,1:T(2,128)S(1)}, u32[]{:S(2)}, u32[]{:S(2)}) collective-permute-start(s32[256,2]{0,1:T(2,128)S(1)} %pad_add_fusion.2), channel_id=1, source_target_pairs={{0,16},{16,0},{1,17},{17,1},{2,18},{18,2},{3,19},{19,3},{4,20},{20... | collective-permute-start | bytes 6152 | tf_op jit(solution)/shard_map/ppermute | solution.py:542
  16.5 0.6 copy-start.1
  17.2 22.8 %all-to-all-start = ((bf16[32,16,512]{2,1,0:T(8,128)(2,1)}), bf16[32,16,512]{2,1,0:T(8,128)(2,1)S(1)}, u32[]{:S(2)}, u32[]{:S(2)}) async-start(bf16[32,16,512]{2,1,0:T(8,128)(2,1)} %upward.1), calls=%async_computation | async-start | bytes 1048576 | tf_op jit(solution)/shard_map/all_to_all | solution.py:517
  35.5 33.9 %collective-permute-start.2 = (bf16[8,2,128,256]{3,2,1,0:T(8,128)(2,1)}, bf16[8,2,128,256]{3,2,1,0:T(8,128)(2,1)S(1)}, u32[]{:S(2)}, u32[]{:S(2)}) collective-permute-start(bf16[8,2,128,256]{3,2,1,0:T(8,128)(2,1)} %refs_3_.1), channel_id=1, source_target_pairs={{1,0},{2,1},{3,2},{4,3},{5,4},{6,5},{7,6},{8,7},{9,8},{10,9},{11,1... | collective-permute-start | bytes 3145736 | tf_op jit(solution)/shard_map/ppermute | solution.py:506
  42.5 12.6 %all-to-all-start.1 = ((bf16[8,4,16,512]{3,2,1,0:T(8,128)(2,1)}), bf16[8,4,16,512]{3,2,1,0:T(8,128)(2,1)S(1)}, u32[]{:S(2)}, u32[]{:S(2)}) async-start(bf16[8,4,16,512]{3,2,1,0:T(8,128)(2,1)} %bitcast.13), calls=%async_computation.1 | async-start | bytes 1048576 | tf_op jit(solution)/shard_map/all_to_all | solution.py:525
  55.1 21.2 %collective-permute-start.3 = (bf16[8,16,512]{2,1,0:T(8,128)(2,1)S(1)}, bf16[8,16,512]{2,1,0:T(8,128)(2,1)S(1)}, u32[]{:S(2)}, u32[]{:S(2)}) collective-permute-start(bf16[8,16,512]{2,1,0:T(8,128)(2,1)S(1)} %get-tuple-element.39), channel_id=1, source_target_pairs={{0,1},{1,2},{2,3},{3,0},{4,5},{5,6},{6,7},{7,4},{8,9},{9,10},{10,1... | collective-permute-start | bytes 393224 | tf_op jit(solution)/shard_map/ppermute | solution.py:530
  56.0 20.3 %collective-permute-start.4 = (bf16[8,16,512]{2,1,0:T(8,128)(2,1)S(1)}, bf16[8,16,512]{2,1,0:T(8,128)(2,1)S(1)}, u32[]{:S(2)}, u32[]{:S(2)}) collective-permute-start(bf16[8,16,512]{2,1,0:T(8,128)(2,1)S(1)} %get-tuple-element.38), channel_id=1, source_target_pairs={{0,2},{1,3},{2,0},{3,1},{4,6},{5,7},{6,4},{7,5},{8,10},{9,11},{10,... | collective-permute-start | bytes 393224 | tf_op jit(solution)/shard_map/ppermute | solution.py:530
  62.0 14.3 %collective-permute-start.5 = (bf16[8,16,512]{2,1,0:T(8,128)(2,1)S(1)}, bf16[8,16,512]{2,1,0:T(8,128)(2,1)S(1)}, u32[]{:S(2)}, u32[]{:S(2)}) collective-permute-start(bf16[8,16,512]{2,1,0:T(8,128)(2,1)S(1)} %get-tuple-element.37), channel_id=1, source_target_pairs={{0,3},{1,0},{2,1},{3,2},{4,7},{5,4},{6,5},{7,6},{8,11},{9,8},{10,9... | collective-permute-start | bytes 393224 | tf_op jit(solution)/shard_map/ppermute | solution.py:530

commit v13 on v12

--- a/solution.py
+++ b/solution.py
@@ -512,6 +512,15 @@
     return jnp.stack([names, vector_ids], axis=2).reshape(-1, 2)
 
 
+def cross_lines(block):
+    every = ("box", "theta", "phi")
+    size = lax.axis_size("phi")
+    lines = lax.axis_size("box") * lax.axis_size("theta")
+    pairs = [(line * size, (line - 1) * size) for line in range(1, lines)]
+    crossed = lax.ppermute(block, every, pairs)
+    return jnp.where(lax.axis_index("phi") == 0, crossed, block)
+
+
 def parent_bands(spread, shares):
     axes = ("box", "theta", "phi") if shares == lax.axis_size("box") else ("theta", "phi")
     return lax.all_to_all(spread, axes, split_axis=0, concat_axis=0, tiled=True)
@@ -567,19 +576,21 @@
     every = ("box", "theta", "phi")
     per_group = lax.axis_size("theta") * lax.axis_size("phi")
     low = shift(coeffs, every, 1)
+    ahead = cross_lines(coeffs)
     spread = upward(coeffs, radiation, up_weights, shares * per_group)
     radiation_adjoint = adjoint(radiation)
     lists = lists_of(partners, vector_ids, pair_count)
     spread, lists = lax.optimization_barrier((spread, lists))
     lines = translation_lines(lists, translation, shares, per_group)
     listed, starts = near_slots(near_ids, near_count, lax.axis_index(every))
-    spread, lines, radiation_adjoint, listed, starts = lax.optimization_barrier(
-        (spread, lines, radiation_adjoint, listed, starts)
+    spread, lines, radiation_adjoint, listed, starts, ahead = lax.optimization_barrier(
+        (spread, lines, radiation_adjoint, listed, starts, ahead)
     )
     parents = parent_bands(spread, shares)
     near = near_field(listed, starts, near_blocks, low, 0)
-    near, late = lax.optimization_barrier((near, coeffs))
-    high = shift(late, every, -1)
+    near, ahead = lax.optimization_barrier((near, ahead))
+    phi_size = lax.axis_size("phi")
+    high = lax.ppermute(ahead, "phi", [(i, (i - 1) % phi_size) for i in range(phi_size)])
     parents, near = lax.optimization_barrier((parents, near))
     sources = [parents]
     if shares < lax.axis_size("box"):

time: 79 us -> 98.3 us (1.24)
  the two profiles are of different devices: /device:TPU:12 before, /device:TPU:0 now
where the time goes in v13:
time: 98.3 us; the launch traced here: 96.7 us
  starting transfers between devices  46.3 us (47%)
  Pallas kernels  33.7 us (34%)
  waiting for transfers between devices  11.1 us (11%)
  other arithmetic  3.96 us (4%)
  local copies, waits for them, and re-layouts  1.52 us (2%)
    ppermute x3, starting transfers between devices, staged_bands(): received.append(lax.ppermute(piece, 'phi', ring))  26.4 us
    pallas_call x3, Pallas kernels, near_field(): pl.pallas_call(kernel, in_specs=[smem] * 2 + [hbm, pl.BlockSpec(memory_sp...  20.5 us
    ppermute x1, waiting for transfers between devices, translation_lines(): other = lax.ppermute(lists, 'box', [(0, 1), (1, 0)])  6.22 us
    ppermute x1, starting transfers between devices, shift(): return lax.ppermute(block, axis, pairs)  5.32 us
    pallas_call x1, Pallas kernels, upward(): pl.pallas_call(up_kernel, in_specs=[hbm] * 3, out_specs=hbm, out_shape=pl...  5.26 us
    ppermute x1, starting transfers between devices, per_device(): lax.ppermute(ahead, 'phi', [(i, (i - 1) % phi_size) for i in range(phi_si...  5.15 us
    all_to_all x1, starting transfers between devices, staged_bands(): bands = lax.all_to_all(bands, axes, split_axis=0, concat_axis=0, tiled=True)  3.84 us
    all_to_all x1, waiting for transfers between devices, parent_bands(): return lax.all_to_all(spread, axes, split_axis=0, concat_axis=0, tiled=True)  3.71 us
  transfers between devices with their start and end apart: 9, of which 4 were waited for; matrix products, arithmetic and copies ran while one was open for 6% of the time, Pallas kernels for 32%

profile of v13, /device:TPU:0, one launch (start us, length us, event | category | flops | bytes accessed | tf_op | source)
XLA Modules:
  0.0 96.7 jit_solution(16059553203005425588)
XLA Ops:
  0.0 1.4 %collective-permute-start.1 = (bf16[8,2,128,256]{3,2,1,0:T(8,128)(2,1)}, bf16[8,2,128,256]{3,2,1,0:T(8,128)(2,1)}, u32[]{:S(2)}, u32[]{:S(2)}) collective-permute-start(bf16[8,2,128,256]{3,2,1,0:T(8,128)(2,1)} %refs_3_.1), channel_id=1, source_target_pairs={{4,0},{8,4},{12,8},{16,12},{20,16},{24,20},{28,24}} | collective-permute-start | bytes 3145736 | tf_op jit(solution)/shard_map/ppermute | solution.py:520
  1.4 5.3 %collective-permute-start.2 = (bf16[8,2,128,256]{3,2,1,0:T(8,128)(2,1)}, bf16[8,2,128,256]{3,2,1,0:T(8,128)(2,1)S(1)}, u32[]{:S(2)}, u32[]{:S(2)}) collective-permute-start(bf16[8,2,128,256]{3,2,1,0:T(8,128)(2,1)} %refs_3_.1), channel_id=1, source_target_pairs={{0,1},{1,2},{2,3},{3,4},{4,5},{5,6},{6,7},{7,8},{8,9},{9,10},{10,1... | collective-permute-start | bytes 3145736 | tf_op jit(solution)/shard_map/ppermute | solution.py:506
  6.8 0.8 fusion.1
  7.6 0.8 stack.10
  8.4 5.3 %upward.1 = bf16[32,16,512]{2,1,0:T(8,128)(2,1)} custom-call(bf16[8,2,128,256]{3,2,1,0:T(8,128)(2,1)} %refs_3_.1, bf16[8,2,128,128]{3,2,1,0:T(8,128)(2,1)} %rad_ref.1, bf16[1024,1024]{1,0:T(8,128)(2,1)} %constant.93.clone.w_hbm), custom_call_target="tpu_custom_call" | custom-call | flops 2000000000 | bytes 4194304 | tf_op jit(solution)/shard_map/upward/pallas_call | solution.py:127
  13.7 1.5 %collective-permute-start = (s32[256,2]{0,1:T(2,128)S(1)}, s32[256,2]{0,1:T(2,128)S(1)}, u32[]{:S(2)}, u32[]{:S(2)}) collective-permute-start(s32[256,2]{0,1:T(2,128)S(1)} %pad_add_fusion.2), channel_id=1, source_target_pairs={{0,16},{16,0},{1,17},{17,1},{2,18},{18,2},{3,19},{19,3},{4,20},{20... | collective-permute-start | bytes 6152 | tf_op jit(solution)/shard_map/ppermute | solution.py:551
  15.3 0.1 reshape.134
  15.4 0.1 convert_reduce_fusion
  15.6 0.2 select_reduce_fusion.refs_0_
  15.8 0.3 convert_reduce_fusion.1
  16.0 0.1 copy.21.table_ref
  16.1 2.1 %adjoint.1.refs_6_ = bf16[8,128,256]{2,1,0:T(8,128)(2,1)} custom-call(bf16[8,2,128,128]{3,2,1,0:T(8,128)(2,1)} %rad_ref.1), custom_call_target="tpu_custom_call" | custom-call | flops 1000000 | bytes 2097152 | tf_op jit(solution)/shard_map/adjoint/pallas_call | solution.py:419
  18.2 6.2 %collective-permute-done = s32[256,2]{0,1:T(2,128)S(1)} collective-permute-done((s32[256,2]{0,1:T(2,128)S(1)}, s32[256,2]{0,1:T(2,128)S(1)}, u32[]{:S(2)}, u32[]{:S(2)}) %collective-permute-start) | collective-permute-done | bytes 2080 | tf_op jit(solution)/shard_map/ppermute | solution.py:551
  24.4 0.1 copy.19
  24.6 0.1 copy.20
  24.8 1.1 %coupling.1.lines_hbm = f32[2,32,512]{2,1,0:T(8,128)S(1)} custom-call(s32[512,2]{1,0:T(8,128)S(1)} %broadcast_select_fusion.1.lists_ref, s32[1]{0:T(128)} %constant.82.clone.1.base_ref, bf16[316,32]{1,0:T(8,128)(2,1)S(1)} %copy.21.table_ref), custom_call_target="tpu_custom_call" | custom-call | flops 200000000 | bytes 2097152 | tf_op jit(solution)/shard_map/coupling/pallas_call | solution.py:175
  25.9 2.5 %broadcast_select_fusion = bf16[8,2,128,256]{3,2,1,0:T(8,128)(2,1)} fusion(bf16[8,2,128,256]{3,2,1,0:T(8,128)(2,1)} %collective-permute-done.1, bf16[8,2,128,256]{3,2,1,0:T(8,128)(2,1)S(1)} %copy-done.2, pred[]{:T(512)S(6)} %eq.49), kind=kLoop, calls=%fused_computation | loop fusion | flops 524288 | bytes 3145729 | tf_op jit(solution)/shard_map/jit(_where)/select_n | solution.py:521
  28.3 2.6 %all-to-all-start = ((bf16[32,16,512]{2,1,0:T(8,128)(2,1)}), bf16[32,16,512]{2,1,0:T(8,128)(2,1)S(1)}, u32[]{:S(2)}, u32[]{:S(2)}) async-start(bf16[32,16,512]{2,1,0:T(8,128)(2,1)} %upward.1), calls=%async_computation | async-start | bytes 1048576 | tf_op jit(solution)/shard_map/all_to_all | solution.py:526
  31.0 0.1 copy.24.refs_1_
  31.1 5.4 %near_low.1.refs_4_ = f32[8,2,128,256]{3,2,1,0:T(8,128)} custom-call(s32[3,96]{1,0:T(4,128)S(1)} %select_reduce_fusion.refs_0_, s32[3,9]{1,0:T(4,128)S(1)} %copy.24.refs_1_, bf16[96,2,128,128]{3,2,1,0:T(8,128)(2,1)} %bitcast.10, bf16[8,2,128,256]{3,2,1,0:T(8,128)(2,1)S(1)} %collective-permute-done.2.refs_3_), custom_call_target="tpu_custom_call" | custom-call | flops 2000000000 | bytes 8388608 | tf_op jit(solution)/shard_map/near_low/pallas_call | solution.py:384
  36.5 5.1 %collective-permute-start.3 = (bf16[8,2,128,256]{3,2,1,0:T(8,128)(2,1)}, bf16[8,2,128,256]{3,2,1,0:T(8,128)(2,1)S(1)}, u32[]{:S(2)}, u32[]{:S(2)}) collective-permute-start(bf16[8,2,128,256]{3,2,1,0:T(8,128)(2,1)} %broadcast_select_fusion), channel_id=1, source_target_pairs={{0,3},{1,0},{2,1},{3,2},{4,7},{5,4},{6,5},{7,6},{8,11},{9,8},{10,9... | collective-permute-start | bytes 3145736 | tf_op jit(solution)/shard_map/ppermute | solution.py:593
  41.6 3.7 %all-to-all-done.refs_0_ = bf16[32,16,512]{2,1,0:T(8,128)(2,1)S(1)} async-done(((bf16[32,16,512]{2,1,0:T(8,128)(2,1)}), bf16[32,16,512]{2,1,0:T(8,128)(2,1)S(1)}, u32[]{:S(2)}, u32[]{:S(2)}) %all-to-all-start) | async-done | bytes 524320 | tf_op jit(solution)/shard_map/all_to_all | solution.py:526
  45.4 2.5 %translate.1 = bf16[32,16,512]{2,1,0:T(8,128)(2,1)} custom-call(f32[2,32,512]{2,1,0:T(8,128)} %copy-done.1, bf16[32,16,512]{2,1,0:T(8,128)(2,1)S(1)} %all-to-all-done.refs_0_), custom_call_target="tpu_custom_call" | custom-call | flops 1000000000 | bytes 2097152 | tf_op jit(solution)/shard_map/translate/pallas_call | solution.py:230
  47.9 3.8 %all-to-all-start.1 = ((bf16[8,4,16,512]{3,2,1,0:T(8,128)(2,1)}), bf16[8,4,16,512]{3,2,1,0:T(8,128)(2,1)S(1)}, u32[]{:S(2)}, u32[]{:S(2)}) async-start(bf16[8,4,16,512]{3,2,1,0:T(8,128)(2,1)} %bitcast.13), calls=%async_computation.1 | async-start | bytes 1048576 | tf_op jit(solution)/shard_map/all_to_all | solution.py:534
  51.7 8.7 %near_own.1.refs_4_ = f32[8,2,128,256]{3,2,1,0:T(8,128)} custom-call(s32[3,96]{1,0:T(4,128)S(1)} %select_reduce_fusion.refs_0_, s32[3,9]{1,0:T(4,128)S(1)} %copy.24.refs_1_, bf16[96,2,128,128]{3,2,1,0:T(8,128)(2,1)} %bitcast.11, bf16[8,2,128,256]{3,2,1,0:T(8,128)(2,1)} %refs_3_.1, f32[8,2,128,256]{3,2,1,0:T(8,128)} %near_low.1.refs_4_), custom_call_target="tpu_custom_call" | custom-call | flops 2000000000 | bytes 8388608 | tf_op jit(solution)/shard_map/near_own/pallas_call | solution.py:384
  60.4 0.5 all-to-all-done.1.refs_0_
  61.0 21.2 %collective-permute-start.4 = (bf16[8,16,512]{2,1,0:T(8,128)(2,1)S(1)}, bf16[8,16,512]{2,1,0:T(8,128)(2,1)S(1)}, u32[]{:S(2)}, u32[]{:S(2)}) collective-permute-start(bf16[8,16,512]{2,1,0:T(8,128)(2,1)S(1)} %get-tuple-element.41), channel_id=1, source_target_pairs={{0,1},{1,2},{2,3},{3,0},{4,5},{5,6},{6,7},{7,4},{8,9},{9,10},{10,1... | collective-permute-start | bytes 393224 | tf_op jit(solution)/shard_map/ppermute | solution.py:539
  82.1 3.9 %collective-permute-start.5 = (bf16[8,16,512]{2,1,0:T(8,128)(2,1)S(1)}, bf16[8,16,512]{2,1,0:T(8,128)(2,1)S(1)}, u32[]{:S(2)}, u32[]{:S(2)}) collective-permute-start(bf16[8,16,512]{2,1,0:T(8,128)(2,1)S(1)} %get-tuple-element.40), channel_id=1, source_target_pairs={{0,2},{1,3},{2,0},{3,1},{4,6},{5,7},{6,4},{7,5},{8,10},{9,11},{10,... | collective-permute-start | bytes 393224 | tf_op jit(solution)/shard_map/ppermute | solution.py:539
  86.0 1.4 %collective-permute-start.6 = (bf16[8,16,512]{2,1,0:T(8,128)(2,1)S(1)}, bf16[8,16,512]{2,1,0:T(8,128)(2,1)S(1)}, u32[]{:S(2)}, u32[]{:S(2)}) collective-permute-start(bf16[8,16,512]{2,1,0:T(8,128)(2,1)S(1)} %get-tuple-element.39), channel_id=1, source_target_pairs={{0,3},{1,0},{2,1},{3,2},{4,7},{5,4},{6,5},{7,6},{8,11},{9,8},{10,9... | collective-permute-start | bytes 393224 | tf_op jit(solution)/shard_map/ppermute | solution.py:539
  87.4 6.4 %near_high.1 = (f32[8,2,128,256]{3,2,1,0:T(8,128)S(1)}, bf16[1024,512]{1,0:T(8,128)(2,1)S(1)}, bf16[8,128,256]{2,1,0:T(8,128)(2,1)S(1)}) custom-call(s32[3,96]{1,0:T(4,128)S(1)} %select_reduce_fusion.refs_0_, s32[3,9]{1,0:T(4,128)S(1)} %copy.24.refs_1_, bf16[96,2,128,128]{3,2,1,0:T(8,128)(2,1)} %bitcast.12, ...), custom_call_target="tpu_custom_call" | custom-call | flops 99999997952 | bytes 8388608 | tf_op jit(solution)/shard_map/near_high/pallas_call | solution.py:384
  93.8 0.6 collective-permute-done.5.refs_2_
  94.4 2.3 %downward.1 = f32[8,2,128,256]{3,2,1,0:T(8,128)} custom-call(s32[1]{0:T(128)} %bitcast.phi_ref, f32[8,2,128,256]{3,2,1,0:T(8,128)S(1)} %get-tuple-element.35.near_ref, bf16[1024,512]{1,0:T(8,128)(2,1)S(1)} %get-tuple-element.36.w_ref, bf16[8,128,256]{2,1,0:T(8,128)(2,1)S(1)} %get-tuple-element.37.adjoint_ref, ...), custom_call_target="tpu_custom_call" | custom-call | flops 2000000000 | bytes 7340032 | tf_op jit(solution)/shard_map/downward/pallas_call | solution.py:483
  (27 shorter events, 0.3 us)
Async XLA Ops:
  0.0 15.4 %copy-start = (bf16[316,2,4,8]{0,3,2,1:T(8,128)(2,1)S(1)}, bf16[316,2,4,8]{0,3,2,1:T(8,128)(2,1)}, u32[]{:S(2)}) copy-start(bf16[316,2,4,8]{0,3,2,1:T(8,128)(2,1)} %param.19) | copy-start | bytes 121348
  0.0 25.9 %collective-permute-start.1 = (bf16[8,2,128,256]{3,2,1,0:T(8,128)(2,1)}, bf16[8,2,128,256]{3,2,1,0:T(8,128)(2,1)}, u32[]{:S(2)}, u32[]{:S(2)}) collective-permute-start(bf16[8,2,128,256]{3,2,1,0:T(8,128)(2,1)} %refs_3_.1), channel_id=1, source_target_pairs={{4,0},{8,4},{12,8},{16,12},{20,16},{24,20},{28,24}} | collective-permute-start | bytes 3145736 | tf_op jit(solution)/shard_map/ppermute | solution.py:520
  1.4 29.6 %collective-permute-start.2 = (bf16[8,2,128,256]{3,2,1,0:T(8,128)(2,1)}, bf16[8,2,128,256]{3,2,1,0:T(8,128)(2,1)S(1)}, u32[]{:S(2)}, u32[]{:S(2)}) collective-permute-start(bf16[8,2,128,256]{3,2,1,0:T(8,128)(2,1)} %refs_3_.1), channel_id=1, source_target_pairs={{0,1},{1,2},{2,3},{3,4},{4,5},{5,6},{6,7},{7,8},{8,9},{9,10},{10,1... | collective-permute-start | bytes 3145736 | tf_op jit(solution)/shard_map/ppermute | solution.py:506
  8.4 6.8 %copy-start.3 = (s32[8,12]{1,0:T(8,128)S(1)}, s32[8,12]{1,0:T(8,128)}, u32[]{:S(2)}) copy-start(s32[8,12]{1,0:T(8,128)} %param.13) | copy-start | bytes 1156
  8.4 6.8 %copy-start.4 = (s32[8]{0:T(128)S(1)}, s32[8]{0:T(128)}, u32[]{:S(2)}) copy-start(s32[8]{0:T(128)} %param.14) | copy-start | bytes 100
  13.7 12.2 %copy-start.2 = (bf16[8,2,128,256]{3,2,1,0:T(8,128)(2,1)S(1)}, bf16[8,2,128,256]{3,2,1,0:T(8,128)(2,1)}, u32[]{:S(2)}) copy-start(bf16[8,2,128,256]{3,2,1,0:T(8,128)(2,1)} %refs_3_.1) | copy-start | bytes 3145732
  13.7 10.7 %collective-permute-start = (s32[256,2]{0,1:T(2,128)S(1)}, s32[256,2]{0,1:T(2,128)S(1)}, u32[]{:S(2)}, u32[]{:S(2)}) collective-permute-start(s32[256,2]{0,1:T(2,128)S(1)} %pad_add_fusion.2), channel_id=1, source_target_pairs={{0,16},{16,0},{1,17},{17,1},{2,18},{18,2},{3,19},{19,3},{4,20},{20... | collective-permute-start | bytes 6152 | tf_op jit(solution)/shard_map/ppermute | solution.py:551
  25.9 2.5 %copy-start.1 = (f32[2,32,512]{2,1,0:T(8,128)}, f32[2,32,512]{2,1,0:T(8,128)S(1)}, u32[]{:S(2)}) copy-start(f32[2,32,512]{2,1,0:T(8,128)S(1)} %coupling.1.lines_hbm) | copy-start | bytes 393220
  28.3 17.0 %all-to-all-start = ((bf16[32,16,512]{2,1,0:T(8,128)(2,1)}), bf16[32,16,512]{2,1,0:T(8,128)(2,1)S(1)}, u32[]{:S(2)}, u32[]{:S(2)}) async-start(bf16[32,16,512]{2,1,0:T(8,128)(2,1)} %upward.1), calls=%async_computation | async-start | bytes 1048576 | tf_op jit(solution)/shard_map/all_to_all | solution.py:526
  36.5 50.9 %collective-permute-start.3 = (bf16[8,2,128,256]{3,2,1,0:T(8,128)(2,1)}, bf16[8,2,128,256]{3,2,1,0:T(8,128)(2,1)S(1)}, u32[]{:S(2)}, u32[]{:S(2)}) collective-permute-start(bf16[8,2,128,256]{3,2,1,0:T(8,128)(2,1)} %broadcast_select_fusion), channel_id=1, source_target_pairs={{0,3},{1,0},{2,1},{3,2},{4,7},{5,4},{6,5},{7,6},{8,11},{9,8},{10,9... | collective-permute-start | bytes 3145736 | tf_op jit(solution)/shard_map/ppermute | solution.py:593
  47.9 13.1 %all-to-all-start.1 = ((bf16[8,4,16,512]{3,2,1,0:T(8,128)(2,1)}), bf16[8,4,16,512]{3,2,1,0:T(8,128)(2,1)S(1)}, u32[]{:S(2)}, u32[]{:S(2)}) async-start(bf16[8,4,16,512]{3,2,1,0:T(8,128)(2,1)} %bitcast.13), calls=%async_computation.1 | async-start | bytes 1048576 | tf_op jit(solution)/shard_map/all_to_all | solution.py:534
  61.0 32.9 %collective-permute-start.4 = (bf16[8,16,512]{2,1,0:T(8,128)(2,1)S(1)}, bf16[8,16,512]{2,1,0:T(8,128)(2,1)S(1)}, u32[]{:S(2)}, u32[]{:S(2)}) collective-permute-start(bf16[8,16,512]{2,1,0:T(8,128)(2,1)S(1)} %get-tuple-element.41), channel_id=1, source_target_pairs={{0,1},{1,2},{2,3},{3,0},{4,5},{5,6},{6,7},{7,4},{8,9},{9,10},{10,1... | collective-permute-start | bytes 393224 | tf_op jit(solution)/shard_map/ppermute | solution.py:539
  82.1 12.3 %collective-permute-start.5 = (bf16[8,16,512]{2,1,0:T(8,128)(2,1)S(1)}, bf16[8,16,512]{2,1,0:T(8,128)(2,1)S(1)}, u32[]{:S(2)}, u32[]{:S(2)}) collective-permute-start(bf16[8,16,512]{2,1,0:T(8,128)(2,1)S(1)} %get-tuple-element.40), channel_id=1, source_target_pairs={{0,2},{1,3},{2,0},{3,1},{4,6},{5,7},{6,4},{7,5},{8,10},{9,11},{10,... | collective-permute-start | bytes 393224 | tf_op jit(solution)/shard_map/ppermute | solution.py:539
  86.0 8.4 %collective-permute-start.6 = (bf16[8,16,512]{2,1,0:T(8,128)(2,1)S(1)}, bf16[8,16,512]{2,1,0:T(8,128)(2,1)S(1)}, u32[]{:S(2)}, u32[]{:S(2)}) collective-permute-start(bf16[8,16,512]{2,1,0:T(8,128)(2,1)S(1)} %get-tuple-element.39), channel_id=1, source_target_pairs={{0,3},{1,0},{2,1},{3,2},{4,7},{5,4},{6,5},{7,6},{8,11},{9,8},{10,9... | collective-permute-start | bytes 393224 | tf_op jit(solution)/shard_map/ppermute | solution.py:539

commit v14 on v13

--- a/solution.py
+++ b/solution.py
@@ -580,13 +580,11 @@
     spread = upward(coeffs, radiation, up_weights, shares * per_group)
     radiation_adjoint = adjoint(radiation)
     lists = lists_of(partners, vector_ids, pair_count)
-    spread, lists = lax.optimization_barrier((spread, lists))
     lines = translation_lines(lists, translation, shares, per_group)
     listed, starts = near_slots(near_ids, near_count, lax.axis_index(every))
-    spread, lines, radiation_adjoint, listed, starts, ahead = lax.optimization_barrier(
-        (spread, lines, radiation_adjoint, listed, starts, ahead)
-    )
+    spread, radiation_adjoint = lax.optimization_barrier((spread, radiation_adjoint))
     parents = parent_bands(spread, shares)
+    lines, listed, starts, ahead = lax.optimization_barrier((lines, listed, starts, ahead))
     near = near_field(listed, starts, near_blocks, low, 0)
     near, ahead = lax.optimization_barrier((near, ahead))
     phi_size = lax.axis_size("phi")

time: 98.3 us -> 95.4 us (0.970)
  waiting for transfers between devices: 11.1 us -> 6.06 us
  starting transfers between devices: 46.3 us -> 48.7 us
    ppermute x1, waiting for transfers between devices: 6.22 us -> 1.16 us  [translation_lines(): other = lax.ppermute(lists, 'box', [(0, 1), (1, 0)])]
    all_to_all x1, starting transfers between devices: 2.6 us -> 5.08 us  [parent_bands(): return lax.all_to_all(spread, axes, split_axis=0, concat_axis=0, tiled=True)]
    all_to_all x1, waiting for transfers between devices: 3.71 us -> 1.67 us  [parent_bands(): return lax.all_to_all(spread, axes, split_axis=0, concat_axis=0, tiled=True)]
    ppermute x1, starting transfers between devices: 5.15 us -> 6.99 us  [per_device(): lax.ppermute(ahead, 'phi', [(i, (i - 1) % phi_size) for i in range(phi_si...]
    ppermute x3, starting transfers between devices: 26.4 us -> 24.9 us  [staged_bands(): received.append(lax.ppermute(piece, 'phi', ring))]
    ppermute x1, waiting for transfers between devices: 0.01 us -> 1.47 us  [shift(): return lax.ppermute(block, axis, pairs)]
  transfers between devices with their start and end apart: 9 -> 9, of which waited for: 4 -> 5; matrix products, arithmetic and copies ran while one was open for 6% -> 6% of each run, Pallas kernels for 32% -> 33%
where the time goes in v14:
time: 95.4 us; the launch traced here: 94.5 us
  starting transfers between devices  48.7 us (51%)
  Pallas kernels  33.4 us (35%)
  waiting for transfers between devices  6.06 us (6%)
  other arithmetic  3.91 us (4%)
  local copies, waits for them, and re-layouts  2.18 us (2%)
    ppermute x3, starting transfers between devices, staged_bands(): received.append(lax.ppermute(piece, 'phi', ring))  24.9 us
    pallas_call x3, Pallas kernels, near_field(): pl.pallas_call(kernel, in_specs=[smem] * 2 + [hbm, pl.BlockSpec(memory_sp...  20.3 us
    ppermute x1, starting transfers between devices, per_device(): lax.ppermute(ahead, 'phi', [(i, (i - 1) % phi_size) for i in range(phi_si...  6.99 us
    ppermute x1, starting transfers between devices, shift(): return lax.ppermute(block, axis, pairs)  5.32 us
    pallas_call x1, Pallas kernels, upward(): pl.pallas_call(up_kernel, in_specs=[hbm] * 3, out_specs=hbm, out_shape=pl...  5.27 us
    all_to_all x1, starting transfers between devices, parent_bands(): return lax.all_to_all(spread, axes, split_axis=0, concat_axis=0, tiled=True)  5.08 us
    all_to_all x1, starting transfers between devices, staged_bands(): bands = lax.all_to_all(bands, axes, split_axis=0, concat_axis=0, tiled=True)  3.5 us
    pallas_call x1, Pallas kernels, translate(): pl.pallas_call(translate_kernel, in_specs=[hbm] + [anywhere] * len(source...  2.49 us
  transfers between devices with their start and end apart: 9, of which 5 were waited for; matrix products, arithmetic and copies ran while one was open for 6% of the time, Pallas kernels for 33%

profile of v14, /device:TPU:0, one launch (start us, length us, event | category | flops | bytes accessed | tf_op | source)
XLA Modules:
  0.0 94.5 jit_solution(4132299023730040417)
XLA Ops:
  0.0 1.4 %collective-permute-start.1 = (bf16[8,2,128,256]{3,2,1,0:T(8,128)(2,1)}, bf16[8,2,128,256]{3,2,1,0:T(8,128)(2,1)}, u32[]{:S(2)}, u32[]{:S(2)}) collective-permute-start(bf16[8,2,128,256]{3,2,1,0:T(8,128)(2,1)} %refs_3_.1), channel_id=1, source_target_pairs={{4,0},{8,4},{12,8},{16,12},{20,16},{24,20},{28,24}} | collective-permute-start | bytes 3145736 | tf_op jit(solution)/shard_map/ppermute | solution.py:520
  1.4 5.3 %collective-permute-start.2 = (bf16[8,2,128,256]{3,2,1,0:T(8,128)(2,1)}, bf16[8,2,128,256]{3,2,1,0:T(8,128)(2,1)S(1)}, u32[]{:S(2)}, u32[]{:S(2)}) collective-permute-start(bf16[8,2,128,256]{3,2,1,0:T(8,128)(2,1)} %refs_3_.1), channel_id=1, source_target_pairs={{0,1},{1,2},{2,3},{3,4},{4,5},{5,6},{6,7},{7,8},{8,9},{9,10},{10,1... | collective-permute-start | bytes 3145736 | tf_op jit(solution)/shard_map/ppermute | solution.py:506
  6.8 0.8 fusion.1
  7.6 0.8 stack.10
  8.4 1.5 %collective-permute-start = (s32[256,2]{0,1:T(2,128)S(1)}, s32[256,2]{0,1:T(2,128)S(1)}, u32[]{:S(2)}, u32[]{:S(2)}) collective-permute-start(s32[256,2]{0,1:T(2,128)S(1)} %pad_add_fusion.1), channel_id=1, source_target_pairs={{0,16},{16,0},{1,17},{17,1},{2,18},{18,2},{3,19},{19,3},{4,20},{20... | collective-permute-start | bytes 6152 | tf_op jit(solution)/shard_map/ppermute | solution.py:551
  9.9 2.0 %adjoint.1.refs_6_ = bf16[8,128,256]{2,1,0:T(8,128)(2,1)} custom-call(bf16[8,2,128,128]{3,2,1,0:T(8,128)(2,1)} %rad_ref.1), custom_call_target="tpu_custom_call" | custom-call | flops 1000000 | bytes 2097152 | tf_op jit(solution)/shard_map/adjoint/pallas_call | solution.py:419
  11.9 5.3 %upward.1 = bf16[32,16,512]{2,1,0:T(8,128)(2,1)} custom-call(bf16[8,2,128,256]{3,2,1,0:T(8,128)(2,1)} %refs_3_.1, bf16[8,2,128,128]{3,2,1,0:T(8,128)(2,1)} %rad_ref.1, bf16[1024,1024]{1,0:T(8,128)(2,1)} %constant.93.clone.w_hbm), custom_call_target="tpu_custom_call" | custom-call | flops 2000000000 | bytes 4194304 | tf_op jit(solution)/shard_map/upward/pallas_call | solution.py:127
  17.2 5.1 %all-to-all-start = ((bf16[32,16,512]{2,1,0:T(8,128)(2,1)}), bf16[32,16,512]{2,1,0:T(8,128)(2,1)S(1)}, u32[]{:S(2)}, u32[]{:S(2)}) async-start(bf16[32,16,512]{2,1,0:T(8,128)(2,1)} %upward.1), calls=%async_computation | async-start | bytes 1048576 | tf_op jit(solution)/shard_map/all_to_all | solution.py:526
  22.6 0.1 convert_reduce_fusion
  22.7 0.2 select_reduce_fusion.refs_0_
  22.9 0.2 convert_reduce_fusion.1
  23.2 0.1 copy.21.table_ref
  23.3 1.2 %collective-permute-done = s32[256,2]{0,1:T(2,128)S(1)} collective-permute-done((s32[256,2]{0,1:T(2,128)S(1)}, s32[256,2]{0,1:T(2,128)S(1)}, u32[]{:S(2)}, u32[]{:S(2)}) %collective-permute-start) | collective-permute-done | bytes 2080 | tf_op jit(solution)/shard_map/ppermute | solution.py:551
  24.5 0.1 copy.19
  24.6 0.1 copy.20
  24.8 1.1 %coupling.1.lines_hbm = f32[2,32,512]{2,1,0:T(8,128)S(1)} custom-call(s32[512,2]{1,0:T(8,128)S(1)} %broadcast_select_fusion.1.lists_ref, s32[1]{0:T(128)} %constant.82.clone.1.base_ref, bf16[316,32]{1,0:T(8,128)(2,1)S(1)} %copy.21.table_ref), custom_call_target="tpu_custom_call" | custom-call | flops 200000000 | bytes 2097152 | tf_op jit(solution)/shard_map/coupling/pallas_call | solution.py:175
  25.9 0.7 copy-done.1
  26.6 2.4 %broadcast_select_fusion = bf16[8,2,128,256]{3,2,1,0:T(8,128)(2,1)} fusion(bf16[8,2,128,256]{3,2,1,0:T(8,128)(2,1)} %collective-permute-done.1, bf16[8,2,128,256]{3,2,1,0:T(8,128)(2,1)S(1)} %copy-done.2, pred[]{:T(512)S(6)} %eq.49), kind=kLoop, calls=%fused_computation | loop fusion | flops 524288 | bytes 3145729 | tf_op jit(solution)/shard_map/jit(_where)/select_n | solution.py:521
  29.1 1.5 %collective-permute-done.2.refs_3_ = bf16[8,2,128,256]{3,2,1,0:T(8,128)(2,1)S(1)} collective-permute-done((bf16[8,2,128,256]{3,2,1,0:T(8,128)(2,1)}, bf16[8,2,128,256]{3,2,1,0:T(8,128)(2,1)S(1)}, u32[]{:S(2)}, u32[]{:S(2)}) %collective-permute-start.2) | collective-permute-done | bytes 1048608 | tf_op jit(solution)/shard_map/ppermute | solution.py:506
  30.6 5.4 %near_low.1.refs_4_ = f32[8,2,128,256]{3,2,1,0:T(8,128)} custom-call(s32[3,96]{1,0:T(4,128)S(1)} %select_reduce_fusion.refs_0_, s32[3,9]{1,0:T(4,128)S(1)} %copy.24.refs_1_, bf16[96,2,128,128]{3,2,1,0:T(8,128)(2,1)} %bitcast.10, bf16[8,2,128,256]{3,2,1,0:T(8,128)(2,1)S(1)} %collective-permute-done.2.refs_3_), custom_call_target="tpu_custom_call" | custom-call | flops 2000000000 | bytes 8388608 | tf_op jit(solution)/shard_map/near_low/pallas_call | solution.py:384
  36.0 7.0 %collective-permute-start.3 = (bf16[8,2,128,256]{3,2,1,0:T(8,128)(2,1)}, bf16[8,2,128,256]{3,2,1,0:T(8,128)(2,1)S(1)}, u32[]{:S(2)}, u32[]{:S(2)}) collective-permute-start(bf16[8,2,128,256]{3,2,1,0:T(8,128)(2,1)} %broadcast_select_fusion), channel_id=1, source_target_pairs={{0,3},{1,0},{2,1},{3,2},{4,7},{5,4},{6,5},{7,6},{8,11},{9,8},{10,9... | collective-permute-start | bytes 3145736 | tf_op jit(solution)/shard_map/ppermute | solution.py:591
  43.0 1.7 %all-to-all-done.refs_0_ = bf16[32,16,512]{2,1,0:T(8,128)(2,1)S(1)} async-done(((bf16[32,16,512]{2,1,0:T(8,128)(2,1)}), bf16[32,16,512]{2,1,0:T(8,128)(2,1)S(1)}, u32[]{:S(2)}, u32[]{:S(2)}) %all-to-all-start) | async-done | bytes 524320 | tf_op jit(solution)/shard_map/all_to_all | solution.py:526
  44.7 2.5 %translate.1 = bf16[32,16,512]{2,1,0:T(8,128)(2,1)} custom-call(f32[2,32,512]{2,1,0:T(8,128)} %copy-done.1, bf16[32,16,512]{2,1,0:T(8,128)(2,1)S(1)} %all-to-all-done.refs_0_), custom_call_target="tpu_custom_call" | custom-call | flops 1000000000 | bytes 2097152 | tf_op jit(solution)/shard_map/translate/pallas_call | solution.py:230
  47.2 3.5 %all-to-all-start.1 = ((bf16[8,4,16,512]{3,2,1,0:T(8,128)(2,1)}), bf16[8,4,16,512]{3,2,1,0:T(8,128)(2,1)S(1)}, u32[]{:S(2)}, u32[]{:S(2)}) async-start(bf16[8,4,16,512]{3,2,1,0:T(8,128)(2,1)} %bitcast.13), calls=%async_computation.1 | async-start | bytes 1048576 | tf_op jit(solution)/shard_map/all_to_all | solution.py:534
  50.7 8.2 %near_own.1.refs_4_ = f32[8,2,128,256]{3,2,1,0:T(8,128)} custom-call(s32[3,96]{1,0:T(4,128)S(1)} %select_reduce_fusion.refs_0_, s32[3,9]{1,0:T(4,128)S(1)} %copy.24.refs_1_, bf16[96,2,128,128]{3,2,1,0:T(8,128)(2,1)} %bitcast.11, bf16[8,2,128,256]{3,2,1,0:T(8,128)(2,1)} %refs_3_.1, f32[8,2,128,256]{3,2,1,0:T(8,128)} %near_low.1.refs_4_), custom_call_target="tpu_custom_call" | custom-call | flops 2000000000 | bytes 8388608 | tf_op jit(solution)/shard_map/near_own/pallas_call | solution.py:384
  58.9 0.6 all-to-all-done.1.refs_0_
  59.5 20.3 %collective-permute-start.4 = (bf16[8,16,512]{2,1,0:T(8,128)(2,1)S(1)}, bf16[8,16,512]{2,1,0:T(8,128)(2,1)S(1)}, u32[]{:S(2)}, u32[]{:S(2)}) collective-permute-start(bf16[8,16,512]{2,1,0:T(8,128)(2,1)S(1)} %get-tuple-element.37), channel_id=1, source_target_pairs={{0,1},{1,2},{2,3},{3,0},{4,5},{5,6},{6,7},{7,4},{8,9},{9,10},{10,1... | collective-permute-start | bytes 393224 | tf_op jit(solution)/shard_map/ppermute | solution.py:539
  79.7 4.1 %collective-permute-start.5 = (bf16[8,16,512]{2,1,0:T(8,128)(2,1)S(1)}, bf16[8,16,512]{2,1,0:T(8,128)(2,1)S(1)}, u32[]{:S(2)}, u32[]{:S(2)}) collective-permute-start(bf16[8,16,512]{2,1,0:T(8,128)(2,1)S(1)} %get-tuple-element.36), channel_id=1, source_target_pairs={{0,2},{1,3},{2,0},{3,1},{4,6},{5,7},{6,4},{7,5},{8,10},{9,11},{10,... | collective-permute-start | bytes 393224 | tf_op jit(solution)/shard_map/ppermute | solution.py:539
  83.8 0.6 collective-permute-start.6
  84.4 6.7 %near_high.1 = (f32[8,2,128,256]{3,2,1,0:T(8,128)S(1)}, bf16[1024,512]{1,0:T(8,128)(2,1)S(1)}, bf16[8,128,256]{2,1,0:T(8,128)(2,1)S(1)}) custom-call(s32[3,96]{1,0:T(4,128)S(1)} %select_reduce_fusion.refs_0_, s32[3,9]{1,0:T(4,128)S(1)} %copy.24.refs_1_, bf16[96,2,128,128]{3,2,1,0:T(8,128)(2,1)} %bitcast.12, ...), custom_call_target="tpu_custom_call" | custom-call | flops 99999997952 | bytes 8388608 | tf_op jit(solution)/shard_map/near_high/pallas_call | solution.py:384
  91.1 1.2 %collective-permute-done.5.refs_2_ = bf16[8,16,512]{2,1,0:T(8,128)(2,1)S(1)} collective-permute-done((bf16[8,16,512]{2,1,0:T(8,128)(2,1)S(1)}, bf16[8,16,512]{2,1,0:T(8,128)(2,1)S(1)}, u32[]{:S(2)}, u32[]{:S(2)}) %collective-permute-start.5) | collective-permute-done | bytes 131104 | tf_op jit(solution)/shard_map/ppermute | solution.py:539
  92.3 2.3 %downward.1 = f32[8,2,128,256]{3,2,1,0:T(8,128)} custom-call(s32[1]{0:T(128)} %bitcast.phi_ref, f32[8,2,128,256]{3,2,1,0:T(8,128)S(1)} %get-tuple-element.31.near_ref, bf16[1024,512]{1,0:T(8,128)(2,1)S(1)} %get-tuple-element.32.w_ref, bf16[8,128,256]{2,1,0:T(8,128)(2,1)S(1)} %get-tuple-element.33.adjoint_ref, ...), custom_call_target="tpu_custom_call" | custom-call | flops 2000000000 | bytes 7340032 | tf_op jit(solution)/shard_map/downward/pallas_call | solution.py:483
  (27 shorter events, 0.5 us)
Async XLA Ops:
  0.0 22.9 %copy-start = (bf16[316,2,4,8]{0,3,2,1:T(8,128)(2,1)S(1)}, bf16[316,2,4,8]{0,3,2,1:T(8,128)(2,1)}, u32[]{:S(2)}) copy-start(bf16[316,2,4,8]{0,3,2,1:T(8,128)(2,1)} %param.19) | copy-start | bytes 121348
  0.0 26.6 %collective-permute-start.1 = (bf16[8,2,128,256]{3,2,1,0:T(8,128)(2,1)}, bf16[8,2,128,256]{3,2,1,0:T(8,128)(2,1)}, u32[]{:S(2)}, u32[]{:S(2)}) collective-permute-start(bf16[8,2,128,256]{3,2,1,0:T(8,128)(2,1)} %refs_3_.1), channel_id=1, source_target_pairs={{4,0},{8,4},{12,8},{16,12},{20,16},{24,20},{28,24}} | collective-permute-start | bytes 3145736 | tf_op jit(solution)/shard_map/ppermute | solution.py:520
  1.4 29.1 %collective-permute-start.2 = (bf16[8,2,128,256]{3,2,1,0:T(8,128)(2,1)}, bf16[8,2,128,256]{3,2,1,0:T(8,128)(2,1)S(1)}, u32[]{:S(2)}, u32[]{:S(2)}) collective-permute-start(bf16[8,2,128,256]{3,2,1,0:T(8,128)(2,1)} %refs_3_.1), channel_id=1, source_target_pairs={{0,1},{1,2},{2,3},{3,4},{4,5},{5,6},{6,7},{7,8},{8,9},{9,10},{10,1... | collective-permute-start | bytes 3145736 | tf_op jit(solution)/shard_map/ppermute | solution.py:506
  8.4 16.1 %collective-permute-start = (s32[256,2]{0,1:T(2,128)S(1)}, s32[256,2]{0,1:T(2,128)S(1)}, u32[]{:S(2)}, u32[]{:S(2)}) collective-permute-start(s32[256,2]{0,1:T(2,128)S(1)} %pad_add_fusion.1), channel_id=1, source_target_pairs={{0,16},{16,0},{1,17},{17,1},{2,18},{18,2},{3,19},{19,3},{4,20},{20... | collective-permute-start | bytes 6152 | tf_op jit(solution)/shard_map/ppermute | solution.py:551
  11.9 10.4 %copy-start.3 = (s32[8,12]{1,0:T(8,128)S(1)}, s32[8,12]{1,0:T(8,128)}, u32[]{:S(2)}) copy-start(s32[8,12]{1,0:T(8,128)} %param.13) | copy-start | bytes 1156
  11.9 10.4 %copy-start.4 = (s32[8]{0:T(128)S(1)}, s32[8]{0:T(128)}, u32[]{:S(2)}) copy-start(s32[8]{0:T(128)} %param.14) | copy-start | bytes 100
  17.2 9.4 %copy-start.2 = (bf16[8,2,128,256]{3,2,1,0:T(8,128)(2,1)S(1)}, bf16[8,2,128,256]{3,2,1,0:T(8,128)(2,1)}, u32[]{:S(2)}) copy-start(bf16[8,2,128,256]{3,2,1,0:T(8,128)(2,1)} %refs_3_.1) | copy-start | bytes 3145732
  17.2 27.4 %all-to-all-start = ((bf16[32,16,512]{2,1,0:T(8,128)(2,1)}), bf16[32,16,512]{2,1,0:T(8,128)(2,1)S(1)}, u32[]{:S(2)}, u32[]{:S(2)}) async-start(bf16[32,16,512]{2,1,0:T(8,128)(2,1)} %upward.1), calls=%async_computation | async-start | bytes 1048576 | tf_op jit(solution)/shard_map/all_to_all | solution.py:526
  25.9 0.7 copy-start.1
  36.0 48.4 %collective-permute-start.3 = (bf16[8,2,128,256]{3,2,1,0:T(8,128)(2,1)}, bf16[8,2,128,256]{3,2,1,0:T(8,128)(2,1)S(1)}, u32[]{:S(2)}, u32[]{:S(2)}) collective-permute-start(bf16[8,2,128,256]{3,2,1,0:T(8,128)(2,1)} %broadcast_select_fusion), channel_id=1, source_target_pairs={{0,3},{1,0},{2,1},{3,2},{4,7},{5,4},{6,5},{7,6},{8,11},{9,8},{10,9... | collective-permute-start | bytes 3145736 | tf_op jit(solution)/shard_map/ppermute | solution.py:591
  47.2 12.3 %all-to-all-start.1 = ((bf16[8,4,16,512]{3,2,1,0:T(8,128)(2,1)}), bf16[8,4,16,512]{3,2,1,0:T(8,128)(2,1)S(1)}, u32[]{:S(2)}, u32[]{:S(2)}) async-start(bf16[8,4,16,512]{3,2,1,0:T(8,128)(2,1)} %bitcast.13), calls=%async_computation.1 | async-start | bytes 1048576 | tf_op jit(solution)/shard_map/all_to_all | solution.py:534
  59.5 31.6 %collective-permute-start.4 = (bf16[8,16,512]{2,1,0:T(8,128)(2,1)S(1)}, bf16[8,16,512]{2,1,0:T(8,128)(2,1)S(1)}, u32[]{:S(2)}, u32[]{:S(2)}) collective-permute-start(bf16[8,16,512]{2,1,0:T(8,128)(2,1)S(1)} %get-tuple-element.37), channel_id=1, source_target_pairs={{0,1},{1,2},{2,3},{3,0},{4,5},{5,6},{6,7},{7,4},{8,9},{9,10},{10,1... | collective-permute-start | bytes 393224 | tf_op jit(solution)/shard_map/ppermute | solution.py:539
  79.7 12.5 %collective-permute-start.5 = (bf16[8,16,512]{2,1,0:T(8,128)(2,1)S(1)}, bf16[8,16,512]{2,1,0:T(8,128)(2,1)S(1)}, u32[]{:S(2)}, u32[]{:S(2)}) collective-permute-start(bf16[8,16,512]{2,1,0:T(8,128)(2,1)S(1)} %get-tuple-element.36), channel_id=1, source_target_pairs={{0,2},{1,3},{2,0},{3,1},{4,6},{5,7},{6,4},{7,5},{8,10},{9,11},{10,... | collective-permute-start | bytes 393224 | tf_op jit(solution)/shard_map/ppermute | solution.py:539
  83.8 8.4 %collective-permute-start.6 = (bf16[8,16,512]{2,1,0:T(8,128)(2,1)S(1)}, bf16[8,16,512]{2,1,0:T(8,128)(2,1)S(1)}, u32[]{:S(2)}, u32[]{:S(2)}) collective-permute-start(bf16[8,16,512]{2,1,0:T(8,128)(2,1)S(1)} %get-tuple-element.35), channel_id=1, source_target_pairs={{0,3},{1,0},{2,1},{3,2},{4,7},{5,4},{6,5},{7,6},{8,11},{9,8},{10,9... | collective-permute-start | bytes 393224 | tf_op jit(solution)/shard_map/ppermute | solution.py:539

commit v15 on v14

--- a/solution.py
+++ b/solution.py
@@ -586,10 +586,9 @@
     parents = parent_bands(spread, shares)
     lines, listed, starts, ahead = lax.optimization_barrier((lines, listed, starts, ahead))
     near = near_field(listed, starts, near_blocks, low, 0)
-    near, ahead = lax.optimization_barrier((near, ahead))
+    parents, near, ahead = lax.optimization_barrier((parents, near, ahead))
     phi_size = lax.axis_size("phi")
     high = lax.ppermute(ahead, "phi", [(i, (i - 1) % phi_size) for i in range(phi_size)])
-    parents, near = lax.optimization_barrier((parents, near))
     sources = [parents]
     if shares < lax.axis_size("box"):
         sources = [shift(parents, "box", 1), parents, shift(parents, "box", -1)]

time: 95.4 us -> 83.9 us (0.88)
  starting transfers between devices: 48.7 us -> 22.2 us
  waiting for transfers between devices: 6.06 us -> 20.9 us
    ppermute x3, starting transfers between devices: 24.9 us -> 4.07 us  [staged_bands(): received.append(lax.ppermute(piece, 'phi', ring))]
    ppermute x1, waiting for transfers between devices: 0.01 us -> 9.28 us  [per_device(): lax.ppermute(ahead, 'phi', [(i, (i - 1) % phi_size) for i in range(phi_si...]
    all_to_all x1, waiting for transfers between devices: 1.67 us -> 8.63 us  [parent_bands(): return lax.all_to_all(spread, axes, split_axis=0, concat_axis=0, tiled=True)]
    ppermute x1, starting transfers between devices: 6.99 us -> 1.31 us  [per_device(): lax.ppermute(ahead, 'phi', [(i, (i - 1) % phi_size) for i in range(phi_si...]
    ppermute x3, waiting for transfers between devices: 1.2 us -> 0.01 us  [staged_bands(): received.append(lax.ppermute(piece, 'phi', ring))]
  transfers between devices with their start and end apart: 9 -> 9, of which waited for: 5 -> 5; matrix products, arithmetic and copies ran while one was open for 6% -> 7% of each run, Pallas kernels for 33% -> 38%
where the time goes in v15:
time: 83.9 us; the launch traced here: 83.3 us
  Pallas kernels  33.9 us (40%)
  starting transfers between devices  22.2 us (26%)
  waiting for transfers between devices  20.9 us (25%)
  other arithmetic  3.93 us (5%)
  local copies, waits for them, and re-layouts  2.17 us (3%)
    pallas_call x3, Pallas kernels, near_field(): pl.pallas_call(kernel, in_specs=[smem] * 2 + [hbm, pl.BlockSpec(memory_sp...  20.7 us
    ppermute x1, waiting for transfers between devices, per_device(): lax.ppermute(ahead, 'phi', [(i, (i - 1) % phi_size) for i in range(phi_si...  9.28 us
    all_to_all x1, waiting for transfers between devices, parent_bands(): return lax.all_to_all(spread, axes, split_axis=0, concat_axis=0, tiled=True)  8.63 us
    ppermute x1, starting transfers between devices, shift(): return lax.ppermute(block, axis, pairs)  5.33 us
    pallas_call x1, Pallas kernels, upward(): pl.pallas_call(up_kernel, in_specs=[hbm] * 3, out_specs=hbm, out_shape=pl...  5.26 us
    all_to_all x1, starting transfers between devices, parent_bands(): return lax.all_to_all(spread, axes, split_axis=0, concat_axis=0, tiled=True)  5.07 us
    ppermute x3, starting transfers between devices, staged_bands(): received.append(lax.ppermute(piece, 'phi', ring))  4.07 us
    all_to_all x1, starting transfers between devices, staged_bands(): bands = lax.all_to_all(bands, axes, split_axis=0, concat_axis=0, tiled=True)  3.5 us
  transfers between devices with their start and end apart: 9, of which 5 were waited for; matrix products, arithmetic and copies ran while one was open for 7% of the time, Pallas kernels for 38%

profile of v15, /device:TPU:0, one launch (start us, length us, event | category | flops | bytes accessed | tf_op | source)
XLA Modules:
  0.0 83.3 jit_solution(4120143078494272814)
XLA Ops:
  0.0 1.4 %collective-permute-start.1 = (bf16[8,2,128,256]{3,2,1,0:T(8,128)(2,1)}, bf16[8,2,128,256]{3,2,1,0:T(8,128)(2,1)}, u32[]{:S(2)}, u32[]{:S(2)}) collective-permute-start(bf16[8,2,128,256]{3,2,1,0:T(8,128)(2,1)} %refs_3_.1), channel_id=1, source_target_pairs={{4,0},{8,4},{12,8},{16,12},{20,16},{24,20},{28,24}} | collective-permute-start | bytes 3145736 | tf_op jit(solution)/shard_map/ppermute | solution.py:520
  1.4 5.3 %collective-permute-start.2 = (bf16[8,2,128,256]{3,2,1,0:T(8,128)(2,1)}, bf16[8,2,128,256]{3,2,1,0:T(8,128)(2,1)S(1)}, u32[]{:S(2)}, u32[]{:S(2)}) collective-permute-start(bf16[8,2,128,256]{3,2,1,0:T(8,128)(2,1)} %refs_3_.1), channel_id=1, source_target_pairs={{0,1},{1,2},{2,3},{3,4},{4,5},{5,6},{6,7},{7,8},{8,9},{9,10},{10,1... | collective-permute-start | bytes 3145736 | tf_op jit(solution)/shard_map/ppermute | solution.py:506
  6.8 0.8 fusion.1
  7.6 0.8 stack.10
  8.4 1.5 %collective-permute-start = (s32[256,2]{0,1:T(2,128)S(1)}, s32[256,2]{0,1:T(2,128)S(1)}, u32[]{:S(2)}, u32[]{:S(2)}) collective-permute-start(s32[256,2]{0,1:T(2,128)S(1)} %pad_add_fusion.1), channel_id=1, source_target_pairs={{0,16},{16,0},{1,17},{17,1},{2,18},{18,2},{3,19},{19,3},{4,20},{20... | collective-permute-start | bytes 6152 | tf_op jit(solution)/shard_map/ppermute | solution.py:551
  9.9 2.0 %adjoint.1.refs_6_ = bf16[8,128,256]{2,1,0:T(8,128)(2,1)} custom-call(bf16[8,2,128,128]{3,2,1,0:T(8,128)(2,1)} %rad_ref.1), custom_call_target="tpu_custom_call" | custom-call | flops 1000000 | bytes 2097152 | tf_op jit(solution)/shard_map/adjoint/pallas_call | solution.py:419
  11.9 5.3 %upward.1 = bf16[32,16,512]{2,1,0:T(8,128)(2,1)} custom-call(bf16[8,2,128,256]{3,2,1,0:T(8,128)(2,1)} %refs_3_.1, bf16[8,2,128,128]{3,2,1,0:T(8,128)(2,1)} %rad_ref.1, bf16[1024,1024]{1,0:T(8,128)(2,1)} %constant.93.clone.w_hbm), custom_call_target="tpu_custom_call" | custom-call | flops 2000000000 | bytes 4194304 | tf_op jit(solution)/shard_map/upward/pallas_call | solution.py:127
  17.2 5.1 %all-to-all-start = ((bf16[32,16,512]{2,1,0:T(8,128)(2,1)}), bf16[32,16,512]{2,1,0:T(8,128)(2,1)S(1)}, u32[]{:S(2)}, u32[]{:S(2)}) async-start(bf16[32,16,512]{2,1,0:T(8,128)(2,1)} %upward.1), calls=%async_computation | async-start | bytes 1048576 | tf_op jit(solution)/shard_map/all_to_all | solution.py:526
  22.6 0.1 convert_reduce_fusion
  22.7 0.2 select_reduce_fusion.refs_0_
  22.9 0.2 convert_reduce_fusion.1
  23.1 0.1 copy.21.table_ref
  23.3 1.2 %collective-permute-done = s32[256,2]{0,1:T(2,128)S(1)} collective-permute-done((s32[256,2]{0,1:T(2,128)S(1)}, s32[256,2]{0,1:T(2,128)S(1)}, u32[]{:S(2)}, u32[]{:S(2)}) %collective-permute-start) | collective-permute-done | bytes 2080 | tf_op jit(solution)/shard_map/ppermute | solution.py:551
  24.5 0.1 copy.19
  24.6 0.1 copy.20
  24.8 1.1 %coupling.1.lines_hbm = f32[2,32,512]{2,1,0:T(8,128)S(1)} custom-call(s32[512,2]{1,0:T(8,128)S(1)} %broadcast_select_fusion.1.lists_ref, s32[1]{0:T(128)} %constant.82.clone.1.base_ref, bf16[316,32]{1,0:T(8,128)(2,1)S(1)} %copy.21.table_ref), custom_call_target="tpu_custom_call" | custom-call | flops 200000000 | bytes 2097152 | tf_op jit(solution)/shard_map/coupling/pallas_call | solution.py:175
  25.9 0.7 copy-done.1
  26.6 2.4 %broadcast_select_fusion = bf16[8,2,128,256]{3,2,1,0:T(8,128)(2,1)} fusion(bf16[8,2,128,256]{3,2,1,0:T(8,128)(2,1)} %collective-permute-done.1, bf16[8,2,128,256]{3,2,1,0:T(8,128)(2,1)S(1)} %copy-done.2, pred[]{:T(512)S(6)} %eq.49), kind=kLoop, calls=%fused_computation | loop fusion | flops 524288 | bytes 3145729 | tf_op jit(solution)/shard_map/jit(_where)/select_n | solution.py:521
  29.1 1.5 %collective-permute-done.2.refs_3_ = bf16[8,2,128,256]{3,2,1,0:T(8,128)(2,1)S(1)} collective-permute-done((bf16[8,2,128,256]{3,2,1,0:T(8,128)(2,1)}, bf16[8,2,128,256]{3,2,1,0:T(8,128)(2,1)S(1)}, u32[]{:S(2)}, u32[]{:S(2)}) %collective-permute-start.2) | collective-permute-done | bytes 1048608 | tf_op jit(solution)/shard_map/ppermute | solution.py:506
  30.6 5.4 %near_low.1.refs_4_ = f32[8,2,128,256]{3,2,1,0:T(8,128)} custom-call(s32[3,96]{1,0:T(4,128)S(1)} %select_reduce_fusion.refs_0_, s32[3,9]{1,0:T(4,128)S(1)} %copy.24.refs_1_, bf16[96,2,128,128]{3,2,1,0:T(8,128)(2,1)} %bitcast.10, bf16[8,2,128,256]{3,2,1,0:T(8,128)(2,1)S(1)} %collective-permute-done.2.refs_3_), custom_call_target="tpu_custom_call" | custom-call | flops 2000000000 | bytes 8388608 | tf_op jit(solution)/shard_map/near_low/pallas_call | solution.py:384
  36.0 8.6 %all-to-all-done.refs_0_ = bf16[32,16,512]{2,1,0:T(8,128)(2,1)S(1)} async-done(((bf16[32,16,512]{2,1,0:T(8,128)(2,1)}), bf16[32,16,512]{2,1,0:T(8,128)(2,1)S(1)}, u32[]{:S(2)}, u32[]{:S(2)}) %all-to-all-start) | async-done | bytes 524320 | tf_op jit(solution)/shard_map/all_to_all | solution.py:526
  44.6 1.3 %collective-permute-start.3 = (bf16[8,2,128,256]{3,2,1,0:T(8,128)(2,1)S(1)}, bf16[8,2,128,256]{3,2,1,0:T(8,128)(2,1)S(1)}, u32[]{:S(2)}, u32[]{:S(2)}) collective-permute-start(bf16[8,2,128,256]{3,2,1,0:T(8,128)(2,1)S(1)} %copy-done.3), channel_id=1, source_target_pairs={{0,3},{1,0},{2,1},{3,2},{4,7},{5,4},{6,5},{7,6},{8,11},{9,8},{10,9... | collective-permute-start | bytes 3145736 | tf_op jit(solution)/shard_map/ppermute | solution.py:591
  45.9 2.5 %translate.1 = bf16[32,16,512]{2,1,0:T(8,128)(2,1)} custom-call(f32[2,32,512]{2,1,0:T(8,128)} %copy-done.1, bf16[32,16,512]{2,1,0:T(8,128)(2,1)S(1)} %all-to-all-done.refs_0_), custom_call_target="tpu_custom_call" | custom-call | flops 1000000000 | bytes 2097152 | tf_op jit(solution)/shard_map/translate/pallas_call | solution.py:230
  48.5 3.5 %all-to-all-start.1 = ((bf16[8,4,16,512]{3,2,1,0:T(8,128)(2,1)}), bf16[8,4,16,512]{3,2,1,0:T(8,128)(2,1)S(1)}, u32[]{:S(2)}, u32[]{:S(2)}) async-start(bf16[8,4,16,512]{3,2,1,0:T(8,128)(2,1)} %bitcast.13), calls=%async_computation.1 | async-start | bytes 1048576 | tf_op jit(solution)/shard_map/all_to_all | solution.py:534
  52.0 8.4 %near_own.1.refs_4_ = f32[8,2,128,256]{3,2,1,0:T(8,128)} custom-call(s32[3,96]{1,0:T(4,128)S(1)} %select_reduce_fusion.refs_0_, s32[3,9]{1,0:T(4,128)S(1)} %copy.24.refs_1_, bf16[96,2,128,128]{3,2,1,0:T(8,128)(2,1)} %bitcast.11, bf16[8,2,128,256]{3,2,1,0:T(8,128)(2,1)} %refs_3_.1, f32[8,2,128,256]{3,2,1,0:T(8,128)} %near_low.1.refs_4_), custom_call_target="tpu_custom_call" | custom-call | flops 2000000000 | bytes 8388608 | tf_op jit(solution)/shard_map/near_own/pallas_call | solution.py:384
  60.4 0.3 all-to-all-done.1.refs_0_
  60.8 0.8 collective-permute-start.4
  61.5 0.5 collective-permute-start.5
  62.0 2.8 %collective-permute-start.6 = (bf16[8,16,512]{2,1,0:T(8,128)(2,1)S(1)}, bf16[8,16,512]{2,1,0:T(8,128)(2,1)S(1)}, u32[]{:S(2)}, u32[]{:S(2)}) collective-permute-start(bf16[8,16,512]{2,1,0:T(8,128)(2,1)S(1)} %get-tuple-element.33), channel_id=1, source_target_pairs={{0,3},{1,0},{2,1},{3,2},{4,7},{5,4},{6,5},{7,6},{8,11},{9,8},{10,9... | collective-permute-start | bytes 393224 | tf_op jit(solution)/shard_map/ppermute | solution.py:539
  64.8 9.3 %collective-permute-done.3.refs_3_ = bf16[8,2,128,256]{3,2,1,0:T(8,128)(2,1)S(1)} collective-permute-done((bf16[8,2,128,256]{3,2,1,0:T(8,128)(2,1)S(1)}, bf16[8,2,128,256]{3,2,1,0:T(8,128)(2,1)S(1)}, u32[]{:S(2)}, u32[]{:S(2)}) %collective-permute-start.3) | collective-permute-done | bytes 1048608 | tf_op jit(solution)/shard_map/ppermute | solution.py:591
  74.1 6.9 %near_high.1 = (f32[8,2,128,256]{3,2,1,0:T(8,128)S(1)}, bf16[1024,512]{1,0:T(8,128)(2,1)S(1)}, bf16[8,128,256]{2,1,0:T(8,128)(2,1)S(1)}) custom-call(s32[3,96]{1,0:T(4,128)S(1)} %select_reduce_fusion.refs_0_, s32[3,9]{1,0:T(4,128)S(1)} %copy.24.refs_1_, bf16[96,2,128,128]{3,2,1,0:T(8,128)(2,1)} %bitcast.12, ...), custom_call_target="tpu_custom_call" | custom-call | flops 99999997952 | bytes 8388608 | tf_op jit(solution)/shard_map/near_high/pallas_call | solution.py:384
  81.1 2.3 %downward.1 = f32[8,2,128,256]{3,2,1,0:T(8,128)} custom-call(s32[1]{0:T(128)} %bitcast.phi_ref, f32[8,2,128,256]{3,2,1,0:T(8,128)S(1)} %get-tuple-element.29.near_ref, bf16[1024,512]{1,0:T(8,128)(2,1)S(1)} %get-tuple-element.30.w_ref, bf16[8,128,256]{2,1,0:T(8,128)(2,1)S(1)} %get-tuple-element.31.adjoint_ref, ...), custom_call_target="tpu_custom_call" | custom-call | flops 2000000000 | bytes 7340032 | tf_op jit(solution)/shard_map/downward/pallas_call | solution.py:483
  (29 shorter events, 0.5 us)
Async XLA Ops:
  0.0 22.9 %copy-start = (bf16[316,2,4,8]{0,3,2,1:T(8,128)(2,1)S(1)}, bf16[316,2,4,8]{0,3,2,1:T(8,128)(2,1)}, u32[]{:S(2)}) copy-start(bf16[316,2,4,8]{0,3,2,1:T(8,128)(2,1)} %param.19) | copy-start | bytes 121348
  0.0 26.6 %collective-permute-start.1 = (bf16[8,2,128,256]{3,2,1,0:T(8,128)(2,1)}, bf16[8,2,128,256]{3,2,1,0:T(8,128)(2,1)}, u32[]{:S(2)}, u32[]{:S(2)}) collective-permute-start(bf16[8,2,128,256]{3,2,1,0:T(8,128)(2,1)} %refs_3_.1), channel_id=1, source_target_pairs={{4,0},{8,4},{12,8},{16,12},{20,16},{24,20},{28,24}} | collective-permute-start | bytes 3145736 | tf_op jit(solution)/shard_map/ppermute | solution.py:520
  1.4 29.1 %collective-permute-start.2 = (bf16[8,2,128,256]{3,2,1,0:T(8,128)(2,1)}, bf16[8,2,128,256]{3,2,1,0:T(8,128)(2,1)S(1)}, u32[]{:S(2)}, u32[]{:S(2)}) collective-permute-start(bf16[8,2,128,256]{3,2,1,0:T(8,128)(2,1)} %refs_3_.1), channel_id=1, source_target_pairs={{0,1},{1,2},{2,3},{3,4},{4,5},{5,6},{6,7},{7,8},{8,9},{9,10},{10,1... | collective-permute-start | bytes 3145736 | tf_op jit(solution)/shard_map/ppermute | solution.py:506
  8.4 16.1 %collective-permute-start = (s32[256,2]{0,1:T(2,128)S(1)}, s32[256,2]{0,1:T(2,128)S(1)}, u32[]{:S(2)}, u32[]{:S(2)}) collective-permute-start(s32[256,2]{0,1:T(2,128)S(1)} %pad_add_fusion.1), channel_id=1, source_target_pairs={{0,16},{16,0},{1,17},{17,1},{2,18},{18,2},{3,19},{19,3},{4,20},{20... | collective-permute-start | bytes 6152 | tf_op jit(solution)/shard_map/ppermute | solution.py:551
  11.9 10.4 %copy-start.4 = (s32[8,12]{1,0:T(8,128)S(1)}, s32[8,12]{1,0:T(8,128)}, u32[]{:S(2)}) copy-start(s32[8,12]{1,0:T(8,128)} %param.13) | copy-start | bytes 1156
  11.9 10.4 %copy-start.5 = (s32[8]{0:T(128)S(1)}, s32[8]{0:T(128)}, u32[]{:S(2)}) copy-start(s32[8]{0:T(128)} %param.14) | copy-start | bytes 100
  17.2 9.4 %copy-start.2 = (bf16[8,2,128,256]{3,2,1,0:T(8,128)(2,1)S(1)}, bf16[8,2,128,256]{3,2,1,0:T(8,128)(2,1)}, u32[]{:S(2)}) copy-start(bf16[8,2,128,256]{3,2,1,0:T(8,128)(2,1)} %refs_3_.1) | copy-start | bytes 3145732
  17.2 27.4 %all-to-all-start = ((bf16[32,16,512]{2,1,0:T(8,128)(2,1)}), bf16[32,16,512]{2,1,0:T(8,128)(2,1)S(1)}, u32[]{:S(2)}, u32[]{:S(2)}) async-start(bf16[32,16,512]{2,1,0:T(8,128)(2,1)} %upward.1), calls=%async_computation | async-start | bytes 1048576 | tf_op jit(solution)/shard_map/all_to_all | solution.py:526
  25.9 0.7 copy-start.1
  30.6 14.1 %copy-start.3 = (bf16[8,2,128,256]{3,2,1,0:T(8,128)(2,1)S(1)}, bf16[8,2,128,256]{3,2,1,0:T(8,128)(2,1)}, u32[]{:S(2)}) copy-start(bf16[8,2,128,256]{3,2,1,0:T(8,128)(2,1)} %broadcast_select_fusion) | copy-start | bytes 3145732
  44.6 29.5 %collective-permute-start.3 = (bf16[8,2,128,256]{3,2,1,0:T(8,128)(2,1)S(1)}, bf16[8,2,128,256]{3,2,1,0:T(8,128)(2,1)S(1)}, u32[]{:S(2)}, u32[]{:S(2)}) collective-permute-start(bf16[8,2,128,256]{3,2,1,0:T(8,128)(2,1)S(1)} %copy-done.3), channel_id=1, source_target_pairs={{0,3},{1,0},{2,1},{3,2},{4,7},{5,4},{6,5},{7,6},{8,11},{9,8},{10,9... | collective-permute-start | bytes 3145736 | tf_op jit(solution)/shard_map/ppermute | solution.py:591
  48.5 12.3 %all-to-all-start.1 = ((bf16[8,4,16,512]{3,2,1,0:T(8,128)(2,1)}), bf16[8,4,16,512]{3,2,1,0:T(8,128)(2,1)S(1)}, u32[]{:S(2)}, u32[]{:S(2)}) async-start(bf16[8,4,16,512]{3,2,1,0:T(8,128)(2,1)} %bitcast.13), calls=%async_computation.1 | async-start | bytes 1048576 | tf_op jit(solution)/shard_map/all_to_all | solution.py:534
  60.8 20.3 %collective-permute-start.4 = (bf16[8,16,512]{2,1,0:T(8,128)(2,1)S(1)}, bf16[8,16,512]{2,1,0:T(8,128)(2,1)S(1)}, u32[]{:S(2)}, u32[]{:S(2)}) collective-permute-start(bf16[8,16,512]{2,1,0:T(8,128)(2,1)S(1)} %get-tuple-element.35), channel_id=1, source_target_pairs={{0,1},{1,2},{2,3},{3,0},{4,5},{5,6},{6,7},{7,4},{8,9},{9,10},{10,1... | collective-permute-start | bytes 393224 | tf_op jit(solution)/shard_map/ppermute | solution.py:539
  61.5 19.5 %collective-permute-start.5 = (bf16[8,16,512]{2,1,0:T(8,128)(2,1)S(1)}, bf16[8,16,512]{2,1,0:T(8,128)(2,1)S(1)}, u32[]{:S(2)}, u32[]{:S(2)}) collective-permute-start(bf16[8,16,512]{2,1,0:T(8,128)(2,1)S(1)} %get-tuple-element.34), channel_id=1, source_target_pairs={{0,2},{1,3},{2,0},{3,1},{4,6},{5,7},{6,4},{7,5},{8,10},{9,11},{10,... | collective-permute-start | bytes 393224 | tf_op jit(solution)/shard_map/ppermute | solution.py:539
  62.0 19.1 %collective-permute-start.6 = (bf16[8,16,512]{2,1,0:T(8,128)(2,1)S(1)}, bf16[8,16,512]{2,1,0:T(8,128)(2,1)S(1)}, u32[]{:S(2)}, u32[]{:S(2)}) collective-permute-start(bf16[8,16,512]{2,1,0:T(8,128)(2,1)S(1)} %get-tuple-element.33), channel_id=1, source_target_pairs={{0,3},{1,0},{2,1},{3,2},{4,7},{5,4},{6,5},{7,6},{8,11},{9,8},{10,9... | collective-permute-start | bytes 393224 | tf_op jit(solution)/shard_map/ppermute | solution.py:539

commit v16 on v12

--- a/solution.py
+++ b/solution.py
@@ -249,15 +249,15 @@
 
 def near_kernel(first, begun, kept, *refs):
     refs = list(refs)
-    listed, starts_ref, blocks_hbm, source_hbm = refs[:4]
-    before_hbm = refs[4] if begun else None
-    kept_hbm = refs[4 + begun : 4 + begun + kept]
-    out_ref = refs[4 + begun + kept]
-    kept_refs = refs[5 + begun + kept : 5 + begun + 2 * kept]
-    blocks, held, wide, total_ref, sems = refs[5 + begun + 2 * kept :]
+    listed, blocks_hbm, held = refs[:3]
+    before_hbm = refs[3] if begun else None
+    kept_hbm = refs[3 + begun : 3 + begun + kept]
+    out_ref = refs[3 + begun + kept]
+    kept_refs = refs[4 + begun + kept : 4 + begun + 2 * kept]
+    blocks, wide, total_ref, sems = refs[4 + begun + 2 * kept :]
     boxes, _, basis, rhs = held.shape
     most = blocks_hbm.shape[0]
-    starts = [starts_ref[first, box] for box in range(boxes + 1)]
+    starts = [listed[first, most + box] for box in range(boxes + 1)]
 
     def by_box(source, target, turn):
         return [
@@ -267,15 +267,12 @@
             for box in range(boxes)
         ]
 
-    source_copies = by_box(source_hbm, held, 0)
-    before_copies = by_box(before_hbm, total_ref, 1) if begun else []
-    out_copies = [] if kept else by_box(total_ref, out_ref, 2)
+    before_copies = by_box(before_hbm, total_ref, 0) if begun else []
+    out_copies = [] if kept else by_box(total_ref, out_ref, 1)
     kept_copies = [
-        pltpu.make_async_copy(kept_hbm[place], kept_refs[place], sems.at[most + 3 * boxes + place])
+        pltpu.make_async_copy(kept_hbm[place], kept_refs[place], sems.at[most + 2 * boxes + place])
         for place in range(kept)
     ]
-    for copy in source_copies:
-        copy.start()
 
     def block_copy(place):
         block = listed[first, place] // boxes
@@ -288,8 +285,6 @@
     lax.fori_loop(0, starts[boxes], fetch, 0)
     for copy in before_copies + kept_copies:
         copy.start()
-    for copy in source_copies:
-        copy.wait()
     for place in range(boxes):
         wide[place] = complex_columns(held[place, 0], held[place, 1])
 
@@ -353,10 +348,10 @@
     listed = jnp.sum(jnp.where(chosen, code, 0), axis=2)
     before = jnp.arange(total) // slots < jnp.arange(boxes + 1)[:, None]
     starts = jnp.sum((wanted[:, None, :] & before).astype(jnp.int32), axis=2)
-    return listed.astype(jnp.int32), starts.astype(jnp.int32)
-
-
-def near_field(listed, starts, blocks, source, first, before=None, keep=()):
+    return jnp.concatenate([listed, starts], axis=1).astype(jnp.int32)
+
+
+def near_field(listed, blocks, source, first, before=None, keep=()):
     boxes, slots, _, basis, _ = blocks.shape
     blocks = blocks.reshape(boxes * slots, *blocks.shape[2:])
     rhs = source.shape[3]
@@ -367,25 +362,22 @@
     shape = (boxes, 2, basis, rhs)
     scratch = [
         pltpu.VMEM(blocks.shape, BF16),
-        pltpu.VMEM(source.shape, BF16),
         pltpu.VMEM((boxes, 2 * basis, 2 * rhs), BF16),
         pltpu.VMEM(shape, F32),
-        pltpu.SemaphoreType.DMA((boxes * slots + 3 * boxes + kept,)),
+        pltpu.SemaphoreType.DMA((boxes * slots + 2 * boxes + kept,)),
     ]
     kernel = functools.partial(near_kernel, first, begun, kept)
     if kept:
-        del scratch[3]
+        del scratch[2]
         inner = kernel
 
         def kernel(*refs):
-            place = 4 + begun + kept
+            place = 3 + begun + kept
             inner(*refs[:-1], refs[place], refs[-1])
 
     return pl.pallas_call(
         kernel,
-        in_specs=[smem] * 2
-        + [hbm, pl.BlockSpec(memory_space=pl.ANY)]
-        + [hbm] * (begun + kept),
+        in_specs=[smem, hbm, vmem] + [hbm] * (begun + kept),
         out_specs=[vmem] * (1 + kept) if kept else hbm,
         out_shape=[
             pltpu.VMEM(shape, F32),
@@ -401,9 +393,8 @@
         name=("near_low", "near_own", "near_high")[first],
     )(
         listed,
-        starts,
         *in_hbm(blocks),
-        source if first != 1 else in_hbm(source)[0],
+        source,
         *in_hbm(*([before] if begun else []), *keep),
     )
 
@@ -429,7 +420,7 @@
     )(radiation)
 
 
-def down_kernel(phi_ref, near_ref, w_ref, adjoint_ref, *refs):
+def down_kernel(phi_ref, near_ref, before_ref, w_ref, adjoint_ref, *refs):
     bands_ref, received = refs[0], refs[1:-4]
     out_hbm, field, held, sems = refs[-4:]
     boxes, _, width = adjoint_ref.shape
@@ -466,24 +457,24 @@
             real, imag = real.astype(BF16), imag.astype(BF16)
             right = jnp.concatenate([side_by_side(real, imag), side_by_side(imag, -real)], axis=0)
             far = dot(adjoint_ref[box], right)
-            held[box, 0] = near_ref[box, 0] + far[:, :rhs]
-            held[box, 1] = near_ref[box, 1] + far[:, rhs:]
+            held[box, 0] = near_ref[box, 0] + before_ref[box, 0] + far[:, :rhs]
+            held[box, 1] = near_ref[box, 1] + before_ref[box, 1] + far[:, rhs:]
             out_copies[box].start()
     for copy in out_copies:
         copy.wait()
 
 
-def downward(phi, bands, received, near, weights, radiation_adjoint):
+def downward(phi, bands, received, near, before, weights, radiation_adjoint):
     boxes = near.shape[0]
     anywhere = pl.BlockSpec(memory_space=pl.ANY)
     ready = [
         pltpu.with_memory_space_constraint(array, pltpu.VMEM)
-        for array in (near, weights, radiation_adjoint)
+        for array in (near, before, weights, radiation_adjoint)
     ]
     return pl.pallas_call(
         down_kernel,
         in_specs=[pl.BlockSpec(memory_space=pltpu.SMEM)]
-        + [pl.BlockSpec(memory_space=pltpu.VMEM)] * 3
+        + [pl.BlockSpec(memory_space=pltpu.VMEM)] * 4
         + [anywhere] * (1 + len(received)),
         out_specs=pl.BlockSpec(memory_space=pltpu.HBM),
         out_shape=jax.ShapeDtypeStruct(near.shape, F32),
@@ -572,12 +563,12 @@
     lists = lists_of(partners, vector_ids, pair_count)
     spread, lists = lax.optimization_barrier((spread, lists))
     lines = translation_lines(lists, translation, shares, per_group)
-    listed, starts = near_slots(near_ids, near_count, lax.axis_index(every))
-    spread, lines, radiation_adjoint, listed, starts = lax.optimization_barrier(
-        (spread, lines, radiation_adjoint, listed, starts)
+    listed = near_slots(near_ids, near_count, lax.axis_index(every))
+    spread, lines, radiation_adjoint, listed = lax.optimization_barrier(
+        (spread, lines, radiation_adjoint, listed)
     )
     parents = parent_bands(spread, shares)
-    near = near_field(listed, starts, near_blocks, low, 0)
+    near = near_field(listed, near_blocks, low, 0)
     near, late = lax.optimization_barrier((near, coeffs))
     high = shift(late, every, -1)
     parents, near = lax.optimization_barrier((parents, near))
@@ -587,9 +578,9 @@
     incoming = translate(lines, sources)
     incoming, near = lax.optimization_barrier((incoming, near))
     phi, bands, received = staged_bands(incoming, shares)
-    near = near_field(listed, starts, near_blocks, coeffs, 1, near)
+    near = near_field(listed, near_blocks, coeffs, 1, near)
     ready = near_field(
-        listed, starts, near_blocks, high, 2, near, keep=(down_weights, radiation_adjoint)
+        listed, near_blocks, high, 2, keep=(near, down_weights, radiation_adjoint)
     )
     return downward(phi, bands, received, *ready)
 

time: 79 us -> 77.4 us (0.980)
  the two profiles are of different devices: /device:TPU:12 before, /device:TPU:0 now
where the time goes in v16:
time: 77.4 us; the launch traced here: 75.9 us
  Pallas kernels  28.7 us (37%)
  starting transfers between devices  23.3 us (30%)
  waiting for transfers between devices  19.9 us (26%)
  local copies, waits for them, and re-layouts  2.16 us (3%)
  other arithmetic  1.56 us (2%)
    pallas_call x3, Pallas kernels, near_field(): pl.pallas_call(kernel, in_specs=[smem, hbm, vmem] + [hbm] * (begun + kept...  15.6 us
    all_to_all x1, waiting for transfers between devices, parent_bands(): return lax.all_to_all(spread, axes, split_axis=0, concat_axis=0, tiled=True)  8.26 us
    ppermute x3, starting transfers between devices, staged_bands(): received.append(lax.ppermute(piece, 'phi', ring))  7.95 us
    ppermute x2, starting transfers between devices, shift(): return lax.ppermute(block, axis, pairs)  6.41 us
    ppermute x2, waiting for transfers between devices, shift(): return lax.ppermute(block, axis, pairs)  6.24 us
    pallas_call x1, Pallas kernels, upward(): pl.pallas_call(up_kernel, in_specs=[hbm] * 3, out_specs=hbm, out_shape=pl...  5.24 us
    ppermute x3, waiting for transfers between devices, staged_bands(): received.append(lax.ppermute(piece, 'phi', ring))  4.35 us
    all_to_all x1, starting transfers between devices, parent_bands(): return lax.all_to_all(spread, axes, split_axis=0, concat_axis=0, tiled=True)  3.91 us
  transfers between devices with their start and end apart: 8, of which 4 were waited for; matrix products, arithmetic and copies ran while one was open for 4% of the time, Pallas kernels for 35%

profile of v16, /device:TPU:0, one launch (start us, length us, event | category | flops | bytes accessed | tf_op | source)
XLA Modules:
  0.0 75.9 jit_solution(17223376182942872380)
XLA Ops:
  0.0 5.1 %collective-permute-start.1 = (bf16[8,2,128,256]{3,2,1,0:T(8,128)(2,1)}, bf16[8,2,128,256]{3,2,1,0:T(8,128)(2,1)S(1)}, u32[]{:S(2)}, u32[]{:S(2)}) collective-permute-start(bf16[8,2,128,256]{3,2,1,0:T(8,128)(2,1)} %refs_2_.1), channel_id=1, source_target_pairs={{0,1},{1,2},{2,3},{3,4},{4,5},{5,6},{6,7},{7,8},{8,9},{9,10},{10,1... | collective-permute-start | bytes 3145736 | tf_op jit(solution)/shard_map/ppermute | solution.py:497
  5.1 0.8 %fusion.1 = s32[16,16]{1,0:T(8,128)S(1)} fusion(s32[16,16]{1,0:T(8,128)} %param.16, s32[16]{0:T(128)} %param.18), kind=kLoop, calls=%fused_computation.12 | loop fusion | flops 512 | bytes 2112 | tf_op jit(solution)/shard_map/jit(_where)/select_n | solution.py:502
  5.9 0.1 stack.9
  6.0 0.8 %stack.10 = s32[256,1]{0,1:T(1,128)S(1)} reshape(s32[16,16]{1,0:T(8,128)} %param.17) | data formatting | bytes 2048 | tf_op jit(solution)/shard_map/stack | solution.py:503
  6.8 5.2 %upward.1 = bf16[32,16,512]{2,1,0:T(8,128)(2,1)} custom-call(bf16[8,2,128,256]{3,2,1,0:T(8,128)(2,1)} %refs_2_.1, bf16[8,2,128,128]{3,2,1,0:T(8,128)(2,1)} %rad_ref.1, bf16[1024,1024]{1,0:T(8,128)(2,1)} %constant.93.clone.w_hbm), custom_call_target="tpu_custom_call" | custom-call | flops 2000000000 | bytes 4194304 | tf_op jit(solution)/shard_map/upward/pallas_call | solution.py:127
  12.0 1.5 %collective-permute-start = (s32[256,2]{0,1:T(2,128)S(1)}, s32[256,2]{0,1:T(2,128)S(1)}, u32[]{:S(2)}, u32[]{:S(2)}) collective-permute-start(s32[256,2]{0,1:T(2,128)S(1)} %pad_add_fusion.2), channel_id=1, source_target_pairs={{0,16},{16,0},{1,17},{17,1},{2,18},{18,2},{3,19},{19,3},{4,20},{20... | collective-permute-start | bytes 6152 | tf_op jit(solution)/shard_map/ppermute | solution.py:533
  13.6 0.1 reshape.134
  13.8 0.1 convert_reduce_fusion
  13.9 0.3 convert_reduce_fusion.1
  14.2 0.1 copy.22
  14.3 0.2 select_reduce_fusion
  14.4 0.1 pad_add_fusion.3.refs_0_
  14.5 0.1 copy.21.table_ref
  14.6 2.0 %adjoint.1.refs_5_ = bf16[8,128,256]{2,1,0:T(8,128)(2,1)} custom-call(bf16[8,2,128,128]{3,2,1,0:T(8,128)(2,1)} %rad_ref.1), custom_call_target="tpu_custom_call" | custom-call | flops 1000000 | bytes 2097152 | tf_op jit(solution)/shard_map/adjoint/pallas_call | solution.py:410
  16.7 0.1 copy.19
  16.8 0.1 copy.20
  17.0 1.1 %coupling.1.lines_hbm = f32[2,32,512]{2,1,0:T(8,128)S(1)} custom-call(s32[512,2]{1,0:T(8,128)S(1)} %broadcast_select_fusion.lists_ref, s32[1]{0:T(128)} %constant.82.clone.1.base_ref, bf16[316,32]{1,0:T(8,128)(2,1)S(1)} %copy.21.table_ref), custom_call_target="tpu_custom_call" | custom-call | flops 200000000 | bytes 2097152 | tf_op jit(solution)/shard_map/coupling/pallas_call | solution.py:175
  18.1 0.6 copy-done.2
  18.8 3.9 %all-to-all-start = ((bf16[32,16,512]{2,1,0:T(8,128)(2,1)}), bf16[32,16,512]{2,1,0:T(8,128)(2,1)S(1)}, u32[]{:S(2)}, u32[]{:S(2)}) async-start(bf16[32,16,512]{2,1,0:T(8,128)(2,1)} %upward.1), calls=%async_computation | async-start | bytes 1048576 | tf_op jit(solution)/shard_map/all_to_all | solution.py:508
  22.7 6.2 %collective-permute-done.1.refs_2_ = bf16[8,2,128,256]{3,2,1,0:T(8,128)(2,1)S(1)} collective-permute-done((bf16[8,2,128,256]{3,2,1,0:T(8,128)(2,1)}, bf16[8,2,128,256]{3,2,1,0:T(8,128)(2,1)S(1)}, u32[]{:S(2)}, u32[]{:S(2)}) %collective-permute-start.1) | collective-permute-done | bytes 1048608 | tf_op jit(solution)/shard_map/ppermute | solution.py:497
  28.9 4.0 %near_low.1.refs_3_ = f32[8,2,128,256]{3,2,1,0:T(8,128)} custom-call(s32[3,105]{1,0:T(4,128)S(1)} %pad_add_fusion.3.refs_0_, bf16[96,2,128,128]{3,2,1,0:T(8,128)(2,1)} %bitcast.10, bf16[8,2,128,256]{3,2,1,0:T(8,128)(2,1)S(1)} %collective-permute-done.1.refs_2_), custom_call_target="tpu_custom_call" | custom-call | flops 2000000000 | bytes 8388608 | tf_op jit(solution)/shard_map/near_low/pallas_call | solution.py:378
  32.9 1.3 %collective-permute-start.2 = (bf16[8,2,128,256]{3,2,1,0:T(8,128)(2,1)S(1)}, bf16[8,2,128,256]{3,2,1,0:T(8,128)(2,1)S(1)}, u32[]{:S(2)}, u32[]{:S(2)}) collective-permute-start(bf16[8,2,128,256]{3,2,1,0:T(8,128)(2,1)S(1)} %copy-done.1), channel_id=1, source_target_pairs={{1,0},{2,1},{3,2},{4,3},{5,4},{6,5},{7,6},{8,7},{9,8},{10,9},{11,1... | collective-permute-start | bytes 3145736 | tf_op jit(solution)/shard_map/ppermute | solution.py:497
  34.2 8.3 %all-to-all-done.refs_0_ = bf16[32,16,512]{2,1,0:T(8,128)(2,1)S(1)} async-done(((bf16[32,16,512]{2,1,0:T(8,128)(2,1)}), bf16[32,16,512]{2,1,0:T(8,128)(2,1)S(1)}, u32[]{:S(2)}, u32[]{:S(2)}) %all-to-all-start) | async-done | bytes 524320 | tf_op jit(solution)/shard_map/all_to_all | solution.py:508
  42.5 2.5 %translate.1 = bf16[32,16,512]{2,1,0:T(8,128)(2,1)} custom-call(f32[2,32,512]{2,1,0:T(8,128)} %copy-done.2, bf16[32,16,512]{2,1,0:T(8,128)(2,1)S(1)} %all-to-all-done.refs_0_), custom_call_target="tpu_custom_call" | custom-call | flops 1000000000 | bytes 2097152 | tf_op jit(solution)/shard_map/translate/pallas_call | solution.py:230
  45.0 3.5 %all-to-all-start.1 = ((bf16[8,4,16,512]{3,2,1,0:T(8,128)(2,1)}), bf16[8,4,16,512]{3,2,1,0:T(8,128)(2,1)S(1)}, u32[]{:S(2)}, u32[]{:S(2)}) async-start(bf16[8,4,16,512]{3,2,1,0:T(8,128)(2,1)} %bitcast.13), calls=%async_computation.1 | async-start | bytes 1048576 | tf_op jit(solution)/shard_map/all_to_all | solution.py:516
  48.5 7.6 %near_own.1.refs_3_ = f32[8,2,128,256]{3,2,1,0:T(8,128)} custom-call(s32[3,105]{1,0:T(4,128)S(1)} %pad_add_fusion.3.refs_0_, bf16[96,2,128,128]{3,2,1,0:T(8,128)(2,1)} %bitcast.11, bf16[8,2,128,256]{3,2,1,0:T(8,128)(2,1)S(1)} %copy-done.1, f32[8,2,128,256]{3,2,1,0:T(8,128)} %near_low.1.refs_3_), custom_call_target="tpu_custom_call" | custom-call | flops 2000000000 | bytes 8388608 | tf_op jit(solution)/shard_map/near_own/pallas_call | solution.py:378
  56.2 1.1 %all-to-all-done.1.refs_0_ = bf16[8,4,16,512]{3,2,1,0:T(8,128)(2,1)S(1)} async-done(((bf16[8,4,16,512]{3,2,1,0:T(8,128)(2,1)}), bf16[8,4,16,512]{3,2,1,0:T(8,128)(2,1)S(1)}, u32[]{:S(2)}, u32[]{:S(2)}) %all-to-all-start.1) | async-done | bytes 524320 | tf_op jit(solution)/shard_map/all_to_all | solution.py:516
  57.3 0.9 %collective-permute-start.3 = (bf16[8,16,512]{2,1,0:T(8,128)(2,1)S(1)}, bf16[8,16,512]{2,1,0:T(8,128)(2,1)S(1)}, u32[]{:S(2)}, u32[]{:S(2)}) collective-permute-start(bf16[8,16,512]{2,1,0:T(8,128)(2,1)S(1)} %get-tuple-element.39), channel_id=1, source_target_pairs={{0,1},{1,2},{2,3},{3,0},{4,5},{5,6},{6,7},{7,4},{8,9},{9,10},{10,1... | collective-permute-start | bytes 393224 | tf_op jit(solution)/shard_map/ppermute | solution.py:521
  58.2 7.1 %collective-permute-start.4 = (bf16[8,16,512]{2,1,0:T(8,128)(2,1)S(1)}, bf16[8,16,512]{2,1,0:T(8,128)(2,1)S(1)}, u32[]{:S(2)}, u32[]{:S(2)}) collective-permute-start(bf16[8,16,512]{2,1,0:T(8,128)(2,1)S(1)} %get-tuple-element.38), channel_id=1, source_target_pairs={{0,2},{1,3},{2,0},{3,1},{4,6},{5,7},{6,4},{7,5},{8,10},{9,11},{10,... | collective-permute-start | bytes 393224 | tf_op jit(solution)/shard_map/ppermute | solution.py:521
  65.2 4.0 %near_high.1 = (f32[8,2,128,256]{3,2,1,0:T(8,128)S(1)}, f32[8,2,128,256]{3,2,1,0:T(8,128)S(1)}, bf16[1024,512]{1,0:T(8,128)(2,1)S(1)}, bf16[8,128,256]{2,1,0:T(8,128)(2,1)S(1)}) custom-call(s32[3,105]{1,0:T(4,128)S(1)} %pad_add_fusion.3.refs_0_, bf16[96,2,128,128]{3,2,1,0:T(8,128)(2,1)} %bitcast.12, ...), custom_call_target="tpu_custom_call" | custom-call | flops 99999997952 | bytes 8388608 | tf_op jit(solution)/shard_map/near_high/pallas_call | solution.py:378
  69.3 4.3 %collective-permute-done.4.refs_2_ = bf16[8,16,512]{2,1,0:T(8,128)(2,1)S(1)} collective-permute-done((bf16[8,16,512]{2,1,0:T(8,128)(2,1)S(1)}, bf16[8,16,512]{2,1,0:T(8,128)(2,1)S(1)}, u32[]{:S(2)}, u32[]{:S(2)}) %collective-permute-start.4) | collective-permute-done | bytes 131104 | tf_op jit(solution)/shard_map/ppermute | solution.py:521
  73.6 2.3 %downward.1 = f32[8,2,128,256]{3,2,1,0:T(8,128)} custom-call(s32[1]{0:T(128)} %bitcast.phi_ref, f32[8,2,128,256]{3,2,1,0:T(8,128)S(1)} %get-tuple-element.32.near_ref, f32[8,2,128,256]{3,2,1,0:T(8,128)S(1)} %get-tuple-element.33.before_ref, bf16[1024,512]{1,0:T(8,128)(2,1)S(1)} %get-tuple-element.34.w_ref, ...), custom_call_target="tpu_custom_call" | custom-call | flops 2000000000 | bytes 7340032 | tf_op jit(solution)/shard_map/downward/pallas_call | solution.py:474
  (25 shorter events, 0.2 us)
Async XLA Ops:
  0.0 14.4 %copy-start = (bf16[316,2,4,8]{0,3,2,1:T(8,128)(2,1)S(1)}, bf16[316,2,4,8]{0,3,2,1:T(8,128)(2,1)}, u32[]{:S(2)}) copy-start(bf16[316,2,4,8]{0,3,2,1:T(8,128)(2,1)} %param.19) | copy-start | bytes 121348
  0.0 28.9 %collective-permute-start.1 = (bf16[8,2,128,256]{3,2,1,0:T(8,128)(2,1)}, bf16[8,2,128,256]{3,2,1,0:T(8,128)(2,1)S(1)}, u32[]{:S(2)}, u32[]{:S(2)}) collective-permute-start(bf16[8,2,128,256]{3,2,1,0:T(8,128)(2,1)} %refs_2_.1), channel_id=1, source_target_pairs={{0,1},{1,2},{2,3},{3,4},{4,5},{5,6},{6,7},{7,8},{8,9},{9,10},{10,1... | collective-permute-start | bytes 3145736 | tf_op jit(solution)/shard_map/ppermute | solution.py:497
  6.8 6.8 %copy-start.3 = (s32[8,12]{1,0:T(8,128)S(1)}, s32[8,12]{1,0:T(8,128)}, u32[]{:S(2)}) copy-start(s32[8,12]{1,0:T(8,128)} %param.13) | copy-start | bytes 1156
  6.8 6.8 %copy-start.4 = (s32[8]{0:T(128)S(1)}, s32[8]{0:T(128)}, u32[]{:S(2)}) copy-start(s32[8]{0:T(128)} %param.14) | copy-start | bytes 100
  12.0 4.7 %collective-permute-start = (s32[256,2]{0,1:T(2,128)S(1)}, s32[256,2]{0,1:T(2,128)S(1)}, u32[]{:S(2)}, u32[]{:S(2)}) collective-permute-start(s32[256,2]{0,1:T(2,128)S(1)} %pad_add_fusion.2), channel_id=1, source_target_pairs={{0,16},{16,0},{1,17},{17,1},{2,18},{18,2},{3,19},{19,3},{4,20},{20... | collective-permute-start | bytes 6152 | tf_op jit(solution)/shard_map/ppermute | solution.py:533
  18.1 0.6 copy-start.2
  18.8 23.7 %all-to-all-start = ((bf16[32,16,512]{2,1,0:T(8,128)(2,1)}), bf16[32,16,512]{2,1,0:T(8,128)(2,1)S(1)}, u32[]{:S(2)}, u32[]{:S(2)}) async-start(bf16[32,16,512]{2,1,0:T(8,128)(2,1)} %upward.1), calls=%async_computation | async-start | bytes 1048576 | tf_op jit(solution)/shard_map/all_to_all | solution.py:508
  28.9 4.0 %copy-start.1 = (bf16[8,2,128,256]{3,2,1,0:T(8,128)(2,1)S(1)}, bf16[8,2,128,256]{3,2,1,0:T(8,128)(2,1)}, u32[]{:S(2)}) copy-start(bf16[8,2,128,256]{3,2,1,0:T(8,128)(2,1)} %refs_2_.1) | copy-start | bytes 3145732
  32.9 32.3 %collective-permute-start.2 = (bf16[8,2,128,256]{3,2,1,0:T(8,128)(2,1)S(1)}, bf16[8,2,128,256]{3,2,1,0:T(8,128)(2,1)S(1)}, u32[]{:S(2)}, u32[]{:S(2)}) collective-permute-start(bf16[8,2,128,256]{3,2,1,0:T(8,128)(2,1)S(1)} %copy-done.1), channel_id=1, source_target_pairs={{1,0},{2,1},{3,2},{4,3},{5,4},{6,5},{7,6},{8,7},{9,8},{10,9},{11,1... | collective-permute-start | bytes 3145736 | tf_op jit(solution)/shard_map/ppermute | solution.py:497
  45.0 12.3 %all-to-all-start.1 = ((bf16[8,4,16,512]{3,2,1,0:T(8,128)(2,1)}), bf16[8,4,16,512]{3,2,1,0:T(8,128)(2,1)S(1)}, u32[]{:S(2)}, u32[]{:S(2)}) async-start(bf16[8,4,16,512]{3,2,1,0:T(8,128)(2,1)} %bitcast.13), calls=%async_computation.1 | async-start | bytes 1048576 | tf_op jit(solution)/shard_map/all_to_all | solution.py:516
  57.3 12.0 %collective-permute-start.3 = (bf16[8,16,512]{2,1,0:T(8,128)(2,1)S(1)}, bf16[8,16,512]{2,1,0:T(8,128)(2,1)S(1)}, u32[]{:S(2)}, u32[]{:S(2)}) collective-permute-start(bf16[8,16,512]{2,1,0:T(8,128)(2,1)S(1)} %get-tuple-element.39), channel_id=1, source_target_pairs={{0,1},{1,2},{2,3},{3,0},{4,5},{5,6},{6,7},{7,4},{8,9},{9,10},{10,1... | collective-permute-start | bytes 393224 | tf_op jit(solution)/shard_map/ppermute | solution.py:521
  58.2 15.4 %collective-permute-start.4 = (bf16[8,16,512]{2,1,0:T(8,128)(2,1)S(1)}, bf16[8,16,512]{2,1,0:T(8,128)(2,1)S(1)}, u32[]{:S(2)}, u32[]{:S(2)}) collective-permute-start(bf16[8,16,512]{2,1,0:T(8,128)(2,1)S(1)} %get-tuple-element.38), channel_id=1, source_target_pairs={{0,2},{1,3},{2,0},{3,1},{4,6},{5,7},{6,4},{7,5},{8,10},{9,11},{10,... | collective-permute-start | bytes 393224 | tf_op jit(solution)/shard_map/ppermute | solution.py:521
  65.2 8.4 %collective-permute-start.5 = (bf16[8,16,512]{2,1,0:T(8,128)(2,1)S(1)}, bf16[8,16,512]{2,1,0:T(8,128)(2,1)S(1)}, u32[]{:S(2)}, u32[]{:S(2)}) collective-permute-start(bf16[8,16,512]{2,1,0:T(8,128)(2,1)S(1)} %get-tuple-element.37), channel_id=1, source_target_pairs={{0,3},{1,0},{2,1},{3,2},{4,7},{5,4},{6,5},{7,6},{8,11},{9,8},{10,9... | collective-permute-start | bytes 393224 | tf_op jit(solution)/shard_map/ppermute | solution.py:521

commit v17 on v16

--- a/solution.py
+++ b/solution.py
@@ -66,7 +66,9 @@
         low = np.concatenate([cos_low, sin_low], axis=1)
         up.append(np.concatenate([high, low], axis=0))
         down += [cos_high.T, sin_high.T]
-    return np.concatenate(up, axis=1), np.concatenate(down, axis=0)
+    down = np.concatenate(down, axis=0)
+    down = down.reshape(down.shape[0], shares * theta_size, phi_size, -1).transpose(2, 0, 1, 3)
+    return np.concatenate(up, axis=1), down.reshape(phi_size, down.shape[1], -1)
 
 
 def in_hbm(*arrays):
@@ -254,7 +256,8 @@
     kept_hbm = refs[3 + begun : 3 + begun + kept]
     out_ref = refs[3 + begun + kept]
     kept_refs = refs[4 + begun + kept : 4 + begun + 2 * kept]
-    blocks, wide, total_ref, sems = refs[4 + begun + 2 * kept :]
+    blocks, wide, total_ref, *earlier, sems = refs[4 + begun + 2 * kept :]
+    held_back = begun and kept
     boxes, _, basis, rhs = held.shape
     most = blocks_hbm.shape[0]
     starts = [listed[first, most + box] for box in range(boxes + 1)]
@@ -267,7 +270,7 @@
             for box in range(boxes)
         ]
 
-    before_copies = by_box(before_hbm, total_ref, 0) if begun else []
+    before_copies = by_box(before_hbm, earlier[0] if held_back else total_ref, 0) if begun else []
     out_copies = [] if kept else by_box(total_ref, out_ref, 1)
     kept_copies = [
         pltpu.make_async_copy(kept_hbm[place], kept_refs[place], sems.at[most + 2 * boxes + place])
@@ -293,8 +296,9 @@
         return carry
 
     lax.fori_loop(0, starts[boxes], landed, 0)
-    for copy in before_copies:
-        copy.wait()
+    if not held_back:
+        for copy in before_copies:
+            copy.wait()
 
     def group(box, begin, size):
         left, right = [], []
@@ -313,7 +317,7 @@
     sizes = [min(count, 3 if count < 7 else 4) for count in possible]
     for box in range(boxes):
         part = group(box, 0, sizes[box])
-        if begun:
+        if begun and not held_back:
             total_ref[box, 0] += part[:, :rhs]
             total_ref[box, 1] += part[:, rhs:]
         else:
@@ -333,6 +337,10 @@
             out_copies[box].start()
     for copy in out_copies + kept_copies:
         copy.wait()
+    if held_back:
+        for box in range(boxes):
+            before_copies[box].wait()
+            total_ref[box] += earlier[0][box]
 
 
 def near_slots(ids, used, rank):
@@ -369,11 +377,13 @@
     kernel = functools.partial(near_kernel, first, begun, kept)
     if kept:
         del scratch[2]
+        if begun:
+            scratch.insert(2, pltpu.VMEM(shape, F32))
         inner = kernel
 
         def kernel(*refs):
-            place = 3 + begun + kept
-            inner(*refs[:-1], refs[place], refs[-1])
+            place, tail = 3 + begun + kept, 1 + begun
+            inner(*refs[:-tail], refs[place], *refs[-tail:])
 
     return pl.pallas_call(
         kernel,
@@ -420,29 +430,20 @@
     )(radiation)
 
 
-def down_kernel(phi_ref, near_ref, before_ref, w_ref, adjoint_ref, *refs):
-    bands_ref, received = refs[0], refs[1:-4]
-    out_hbm, field, held, sems = refs[-4:]
+def down_kernel(phi_ref, near_ref, w_ref, adjoint_ref, *refs):
+    pieces, (out_hbm, held, sems) = refs[:-3], refs[-3:]
     boxes, _, width = adjoint_ref.shape
     points = width // 2
     rhs = held.shape[3]
     phi = phi_ref[0]
-    phi_size = field.shape[1]
-    pairs = [(bands_ref.at[:, phi], field.at[:, phi])]
-    for distance, piece in enumerate(received, 1):
-        pairs.append((piece, field.at[:, lax.rem(phi + phi_size - distance, phi_size)]))
-    copies = [
-        pltpu.make_async_copy(source, target, sems.at[boxes + place])
-        for place, (source, target) in enumerate(pairs)
-    ]
+    phi_size = len(pieces)
     out_copies = [
         pltpu.make_async_copy(held.at[box], out_hbm.at[box], sems.at[box]) for box in range(boxes)
     ]
-    for copy in copies:
-        copy.start()
-    for copy in copies:
-        copy.wait()
-    mixed = dot(w_ref[...], field[...].reshape(w_ref.shape[1], 2 * rhs))
+    places = [lax.rem(phi + phi_size - distance, phi_size) for distance in range(phi_size)]
+    left = jnp.concatenate([w_ref[place] for place in places], axis=1)
+    right = jnp.concatenate([piece[...].reshape(-1, 2 * rhs) for piece in pieces], axis=0)
+    mixed = dot(left, right)
     for octant in range(boxes // 2):
         start = 2 * octant * points
         cos_part = mixed[start : start + points]
@@ -457,38 +458,35 @@
             real, imag = real.astype(BF16), imag.astype(BF16)
             right = jnp.concatenate([side_by_side(real, imag), side_by_side(imag, -real)], axis=0)
             far = dot(adjoint_ref[box], right)
-            held[box, 0] = near_ref[box, 0] + before_ref[box, 0] + far[:, :rhs]
-            held[box, 1] = near_ref[box, 1] + before_ref[box, 1] + far[:, rhs:]
+            held[box, 0] = near_ref[box, 0] + far[:, :rhs]
+            held[box, 1] = near_ref[box, 1] + far[:, rhs:]
             out_copies[box].start()
     for copy in out_copies:
         copy.wait()
 
 
-def downward(phi, bands, received, near, before, weights, radiation_adjoint):
+def downward(phi, pieces, near, weights, radiation_adjoint):
     boxes = near.shape[0]
-    anywhere = pl.BlockSpec(memory_space=pl.ANY)
+    vmem = pl.BlockSpec(memory_space=pltpu.VMEM)
     ready = [
         pltpu.with_memory_space_constraint(array, pltpu.VMEM)
-        for array in (near, before, weights, radiation_adjoint)
+        for array in (near, weights, radiation_adjoint)
     ]
     return pl.pallas_call(
         down_kernel,
-        in_specs=[pl.BlockSpec(memory_space=pltpu.SMEM)]
-        + [pl.BlockSpec(memory_space=pltpu.VMEM)] * 4
-        + [anywhere] * (1 + len(received)),
+        in_specs=[pl.BlockSpec(memory_space=pltpu.SMEM)] + [vmem] * (3 + len(pieces)),
         out_specs=pl.BlockSpec(memory_space=pltpu.HBM),
         out_shape=jax.ShapeDtypeStruct(near.shape, F32),
         scratch_shapes=[
-            pltpu.VMEM(bands.shape, BF16),
             pltpu.VMEM(near.shape, F32),
-            pltpu.SemaphoreType.DMA((boxes + 1 + len(received),)),
+            pltpu.SemaphoreType.DMA((boxes,)),
         ],
         compiler_params=pltpu.CompilerParams(vmem_limit_bytes=32 * MIB),
         cost_estimate=pl.CostEstimate(
             flops=2 * 10**9, bytes_accessed=7 * MIB, transcendentals=0
         ),
         name="downward",
-    )(phi, *ready, bands, *received)
+    )(phi, *ready, *pieces)
 
 
 def shift(block, axis, step):
@@ -515,11 +513,13 @@
     bands = incoming.reshape(-1, phi_size, *incoming.shape[1:])
     bands = lax.all_to_all(bands, axes, split_axis=0, concat_axis=0, tiled=True)
     received = []
-    for distance in range(1, phi_size):
+    for distance in range(phi_size):
         piece = lax.dynamic_index_in_dim(bands, (phi + distance) % phi_size, 1, keepdims=False)
-        ring = [(place, (place + distance) % phi_size) for place in range(phi_size)]
-        received.append(lax.ppermute(piece, "phi", ring))
-    return phi.astype(jnp.int32).reshape(1), bands, received
+        if distance:
+            ring = [(place, (place + distance) % phi_size) for place in range(phi_size)]
+            piece = lax.ppermute(piece, "phi", ring)
+        received.append(piece)
+    return phi.astype(jnp.int32).reshape(1), received
 
 
 def translation_lines(lists, translation, shares, per_group):
@@ -577,12 +577,12 @@
         sources = [shift(parents, "box", 1), parents, shift(parents, "box", -1)]
     incoming = translate(lines, sources)
     incoming, near = lax.optimization_barrier((incoming, near))
-    phi, bands, received = staged_bands(incoming, shares)
+    phi, pieces = staged_bands(incoming, shares)
     near = near_field(listed, near_blocks, coeffs, 1, near)
     ready = near_field(
-        listed, near_blocks, high, 2, keep=(near, down_weights, radiation_adjoint)
+        listed, near_blocks, high, 2, near, keep=(down_weights, radiation_adjoint)
     )
-    return downward(phi, bands, received, *ready)
+    return downward(phi, pieces, *ready)
 
 
 def solution(mesh):

time: 77.4 us -> 79 us (1.021); the launches traced: 75.9 us -> 78.4 us
  waiting for transfers between devices: 19.9 us -> 21.8 us
    ppermute x3, waiting for transfers between devices: 4.35 us -> 6.27 us  [staged_bands(): piece = lax.ppermute(piece, 'phi', ring)]
  transfers between devices with their start and end apart: 8 -> 8, of which waited for: 4 -> 4; matrix products, arithmetic and copies ran while one was open for 4% -> 4% of each run, Pallas kernels for 35% -> 34%
where the time goes in v17:
time: 79 us; the launch traced here: 78.4 us
  Pallas kernels  29.1 us (37%)
  starting transfers between devices  23.4 us (30%)
  waiting for transfers between devices  21.8 us (28%)
  local copies, waits for them, and re-layouts  2.17 us (3%)
  other arithmetic  1.57 us (2%)
    pallas_call x3, Pallas kernels, near_field(): pl.pallas_call(kernel, in_specs=[smem, hbm, vmem] + [hbm] * (begun + kept...  16.1 us
    all_to_all x1, waiting for transfers between devices, parent_bands(): return lax.all_to_all(spread, axes, split_axis=0, concat_axis=0, tiled=True)  8.26 us
    ppermute x3, starting transfers between devices, staged_bands(): piece = lax.ppermute(piece, 'phi', ring)  8.12 us
    ppermute x2, starting transfers between devices, shift(): return lax.ppermute(block, axis, pairs)  6.41 us
    ppermute x3, waiting for transfers between devices, staged_bands(): piece = lax.ppermute(piece, 'phi', ring)  6.27 us
    ppermute x2, waiting for transfers between devices, shift(): return lax.ppermute(block, axis, pairs)  6.25 us
    pallas_call x1, Pallas kernels, upward(): pl.pallas_call(up_kernel, in_specs=[hbm] * 3, out_specs=hbm, out_shape=pl...  5.24 us
    all_to_all x1, starting transfers between devices, parent_bands(): return lax.all_to_all(spread, axes, split_axis=0, concat_axis=0, tiled=True)  3.9 us
  transfers between devices with their start and end apart: 8, of which 4 were waited for; matrix products, arithmetic and copies ran while one was open for 4% of the time, Pallas kernels for 34%

profile of v17, /device:TPU:0, one launch (start us, length us, event | category | flops | bytes accessed | tf_op | source)
XLA Modules:
  0.0 78.4 jit_solution(13371220033898011138)
XLA Ops:
  0.0 5.1 %collective-permute-start.1 = (bf16[8,2,128,256]{3,2,1,0:T(8,128)(2,1)}, bf16[8,2,128,256]{3,2,1,0:T(8,128)(2,1)S(1)}, u32[]{:S(2)}, u32[]{:S(2)}) collective-permute-start(bf16[8,2,128,256]{3,2,1,0:T(8,128)(2,1)} %refs_2_.1), channel_id=1, source_target_pairs={{0,1},{1,2},{2,3},{3,4},{4,5},{5,6},{6,7},{7,8},{8,9},{9,10},{10,1... | collective-permute-start | bytes 3145736 | tf_op jit(solution)/shard_map/ppermute | solution.py:495
  5.1 0.8 stack.10
  5.9 0.8 fusion.1
  6.7 0.1 stack.9
  6.8 5.2 %upward.1 = bf16[32,16,512]{2,1,0:T(8,128)(2,1)} custom-call(bf16[8,2,128,256]{3,2,1,0:T(8,128)(2,1)} %refs_2_.1, bf16[8,2,128,128]{3,2,1,0:T(8,128)(2,1)} %rad_ref.1, bf16[1024,1024]{1,0:T(8,128)(2,1)} %constant.99.clone.w_hbm), custom_call_target="tpu_custom_call" | custom-call | flops 2000000000 | bytes 4194304 | tf_op jit(solution)/shard_map/upward/pallas_call | solution.py:129
  12.0 1.5 %collective-permute-start = (s32[256,2]{0,1:T(2,128)S(1)}, s32[256,2]{0,1:T(2,128)S(1)}, u32[]{:S(2)}, u32[]{:S(2)}) collective-permute-start(s32[256,2]{0,1:T(2,128)S(1)} %pad_add_fusion.2), channel_id=1, source_target_pairs={{0,16},{16,0},{1,17},{17,1},{2,18},{18,2},{3,19},{19,3},{4,20},{20... | collective-permute-start | bytes 6152 | tf_op jit(solution)/shard_map/ppermute | solution.py:533
  13.6 0.1 reshape.134
  13.8 0.2 convert_reduce_fusion.1
  14.0 0.1 copy.24
  14.1 0.2 convert_reduce_fusion
  14.3 0.2 select_reduce_fusion
  14.4 0.1 pad_add_fusion.3.refs_0_
  14.5 0.1 copy.23.table_ref
  14.6 2.0 %adjoint.1.refs_5_ = bf16[8,128,256]{2,1,0:T(8,128)(2,1)} custom-call(bf16[8,2,128,128]{3,2,1,0:T(8,128)(2,1)} %rad_ref.1), custom_call_target="tpu_custom_call" | custom-call | flops 1000000 | bytes 2097152 | tf_op jit(solution)/shard_map/adjoint/pallas_call | solution.py:420
  16.7 0.1 copy.22
  16.8 0.1 copy.21
  17.0 1.1 %coupling.1.lines_hbm = f32[2,32,512]{2,1,0:T(8,128)S(1)} custom-call(s32[512,2]{1,0:T(8,128)S(1)} %broadcast_select_fusion.lists_ref, s32[1]{0:T(128)} %constant.88.clone.1.base_ref, bf16[316,32]{1,0:T(8,128)(2,1)S(1)} %copy.23.table_ref), custom_call_target="tpu_custom_call" | custom-call | flops 200000000 | bytes 2097152 | tf_op jit(solution)/shard_map/coupling/pallas_call | solution.py:177
  18.1 0.6 copy-done.2
  18.8 3.9 %all-to-all-start = ((bf16[32,16,512]{2,1,0:T(8,128)(2,1)}), bf16[32,16,512]{2,1,0:T(8,128)(2,1)S(1)}, u32[]{:S(2)}, u32[]{:S(2)}) async-start(bf16[32,16,512]{2,1,0:T(8,128)(2,1)} %upward.1), calls=%async_computation | async-start | bytes 1048576 | tf_op jit(solution)/shard_map/all_to_all | solution.py:506
  22.7 6.2 %collective-permute-done.1.refs_2_ = bf16[8,2,128,256]{3,2,1,0:T(8,128)(2,1)S(1)} collective-permute-done((bf16[8,2,128,256]{3,2,1,0:T(8,128)(2,1)}, bf16[8,2,128,256]{3,2,1,0:T(8,128)(2,1)S(1)}, u32[]{:S(2)}, u32[]{:S(2)}) %collective-permute-start.1) | collective-permute-done | bytes 1048608 | tf_op jit(solution)/shard_map/ppermute | solution.py:495
  28.9 4.0 %near_low.1.refs_3_ = f32[8,2,128,256]{3,2,1,0:T(8,128)} custom-call(s32[3,105]{1,0:T(4,128)S(1)} %pad_add_fusion.3.refs_0_, bf16[96,2,128,128]{3,2,1,0:T(8,128)(2,1)} %bitcast.12, bf16[8,2,128,256]{3,2,1,0:T(8,128)(2,1)S(1)} %collective-permute-done.1.refs_2_), custom_call_target="tpu_custom_call" | custom-call | flops 2000000000 | bytes 8388608 | tf_op jit(solution)/shard_map/near_low/pallas_call | solution.py:388
  32.9 1.3 %collective-permute-start.2 = (bf16[8,2,128,256]{3,2,1,0:T(8,128)(2,1)S(1)}, bf16[8,2,128,256]{3,2,1,0:T(8,128)(2,1)S(1)}, u32[]{:S(2)}, u32[]{:S(2)}) collective-permute-start(bf16[8,2,128,256]{3,2,1,0:T(8,128)(2,1)S(1)} %copy-done.1), channel_id=1, source_target_pairs={{1,0},{2,1},{3,2},{4,3},{5,4},{6,5},{7,6},{8,7},{9,8},{10,9},{11,1... | collective-permute-start | bytes 3145736 | tf_op jit(solution)/shard_map/ppermute | solution.py:495
  34.2 8.3 %all-to-all-done.refs_0_ = bf16[32,16,512]{2,1,0:T(8,128)(2,1)S(1)} async-done(((bf16[32,16,512]{2,1,0:T(8,128)(2,1)}), bf16[32,16,512]{2,1,0:T(8,128)(2,1)S(1)}, u32[]{:S(2)}, u32[]{:S(2)}) %all-to-all-start) | async-done | bytes 524320 | tf_op jit(solution)/shard_map/all_to_all | solution.py:506
  42.5 2.5 %translate.1 = bf16[32,16,512]{2,1,0:T(8,128)(2,1)} custom-call(f32[2,32,512]{2,1,0:T(8,128)} %copy-done.2, bf16[32,16,512]{2,1,0:T(8,128)(2,1)S(1)} %all-to-all-done.refs_0_), custom_call_target="tpu_custom_call" | custom-call | flops 1000000000 | bytes 2097152 | tf_op jit(solution)/shard_map/translate/pallas_call | solution.py:232
  45.0 3.5 %all-to-all-start.1 = ((bf16[8,4,16,512]{3,2,1,0:T(8,128)(2,1)}), bf16[8,4,16,512]{3,2,1,0:T(8,128)(2,1)S(1)}, u32[]{:S(2)}, u32[]{:S(2)}) async-start(bf16[8,4,16,512]{3,2,1,0:T(8,128)(2,1)} %bitcast.15), calls=%async_computation.1 | async-start | bytes 1048576 | tf_op jit(solution)/shard_map/all_to_all | solution.py:514
  48.6 7.6 %near_own.1.refs_3_ = f32[8,2,128,256]{3,2,1,0:T(8,128)} custom-call(s32[3,105]{1,0:T(4,128)S(1)} %pad_add_fusion.3.refs_0_, bf16[96,2,128,128]{3,2,1,0:T(8,128)(2,1)} %bitcast.13, bf16[8,2,128,256]{3,2,1,0:T(8,128)(2,1)S(1)} %copy-done.1, f32[8,2,128,256]{3,2,1,0:T(8,128)} %near_low.1.refs_3_), custom_call_target="tpu_custom_call" | custom-call | flops 2000000000 | bytes 8388608 | tf_op jit(solution)/shard_map/near_own/pallas_call | solution.py:388
  56.2 1.1 %all-to-all-done.1 = bf16[8,4,16,512]{3,2,1,0:T(8,128)(2,1)S(1)} async-done(((bf16[8,4,16,512]{3,2,1,0:T(8,128)(2,1)}), bf16[8,4,16,512]{3,2,1,0:T(8,128)(2,1)S(1)}, u32[]{:S(2)}, u32[]{:S(2)}) %all-to-all-start.1) | async-done | bytes 524320 | tf_op jit(solution)/shard_map/all_to_all | solution.py:514
  57.3 7.5 %collective-permute-start.5 = (bf16[8,16,512]{2,1,0:T(8,128)(2,1)S(1)}, bf16[8,16,512]{2,1,0:T(8,128)(2,1)S(1)}, u32[]{:S(2)}, u32[]{:S(2)}) collective-permute-start(bf16[8,16,512]{2,1,0:T(8,128)(2,1)S(1)} %get-tuple-element.35), channel_id=1, source_target_pairs={{0,3},{1,0},{2,1},{3,2},{4,7},{5,4},{6,5},{7,6},{8,11},{9,8},{10,9... | collective-permute-start | bytes 393224 | tf_op jit(solution)/shard_map/ppermute | solution.py:520
  64.8 0.6 collective-permute-start.3
  65.4 4.5 %near_high.1 = (f32[8,2,128,256]{3,2,1,0:T(8,128)S(1)}, bf16[4,1024,128]{2,1,0:T(8,128)(2,1)S(1)}, bf16[8,128,256]{2,1,0:T(8,128)(2,1)S(1)}) custom-call(s32[3,105]{1,0:T(4,128)S(1)} %pad_add_fusion.3.refs_0_, bf16[96,2,128,128]{3,2,1,0:T(8,128)(2,1)} %bitcast.14, bf16[8,2,128,256]{3,2,1,0:T(8,128)(2,1)S(1)} %collective-permute-done.2.refs_2_, ...), custom_call_target="tpu_custom_call" | custom-call | flops 99999997952 | bytes 8388608 | tf_op jit(solution)/shard_map/near_high/pallas_call | solution.py:388
  70.0 6.3 %collective-permute-done.4.refs_2_ = bf16[8,16,512]{2,1,0:T(8,128)(2,1)S(1)} collective-permute-done((bf16[8,16,512]{2,1,0:T(8,128)(2,1)S(1)}, bf16[8,16,512]{2,1,0:T(8,128)(2,1)S(1)}, u32[]{:S(2)}, u32[]{:S(2)}) %collective-permute-start.4) | collective-permute-done | bytes 131104 | tf_op jit(solution)/shard_map/ppermute | solution.py:520
  76.2 2.1 %downward.1 = f32[8,2,128,256]{3,2,1,0:T(8,128)} custom-call(s32[1]{0:T(128)} %bitcast.phi_ref, f32[8,2,128,256]{3,2,1,0:T(8,128)S(1)} %get-tuple-element.31.near_ref, bf16[4,1024,128]{2,1,0:T(8,128)(2,1)S(1)} %get-tuple-element.32.w_ref, bf16[8,128,256]{2,1,0:T(8,128)(2,1)S(1)} %get-tuple-element.33.adjoint_ref, ...), custom_call_target="tpu_custom_call" | custom-call | flops 2000000000 | bytes 7340032 | tf_op jit(solution)/shard_map/downward/pallas_call | solution.py:475
  (25 shorter events, 0.2 us)
Async XLA Ops:
  0.0 14.4 %copy-start = (bf16[316,2,4,8]{0,3,2,1:T(8,128)(2,1)S(1)}, bf16[316,2,4,8]{0,3,2,1:T(8,128)(2,1)}, u32[]{:S(2)}) copy-start(bf16[316,2,4,8]{0,3,2,1:T(8,128)(2,1)} %param.19) | copy-start | bytes 121348
  0.0 28.9 %collective-permute-start.1 = (bf16[8,2,128,256]{3,2,1,0:T(8,128)(2,1)}, bf16[8,2,128,256]{3,2,1,0:T(8,128)(2,1)S(1)}, u32[]{:S(2)}, u32[]{:S(2)}) collective-permute-start(bf16[8,2,128,256]{3,2,1,0:T(8,128)(2,1)} %refs_2_.1), channel_id=1, source_target_pairs={{0,1},{1,2},{2,3},{3,4},{4,5},{5,6},{6,7},{7,8},{8,9},{9,10},{10,1... | collective-permute-start | bytes 3145736 | tf_op jit(solution)/shard_map/ppermute | solution.py:495
  6.8 6.8 %copy-start.3 = (s32[8,12]{1,0:T(8,128)S(1)}, s32[8,12]{1,0:T(8,128)}, u32[]{:S(2)}) copy-start(s32[8,12]{1,0:T(8,128)} %param.13) | copy-start | bytes 1156
  6.8 6.8 %copy-start.4 = (s32[8]{0:T(128)S(1)}, s32[8]{0:T(128)}, u32[]{:S(2)}) copy-start(s32[8]{0:T(128)} %param.14) | copy-start | bytes 100
  12.0 4.6 %collective-permute-start = (s32[256,2]{0,1:T(2,128)S(1)}, s32[256,2]{0,1:T(2,128)S(1)}, u32[]{:S(2)}, u32[]{:S(2)}) collective-permute-start(s32[256,2]{0,1:T(2,128)S(1)} %pad_add_fusion.2), channel_id=1, source_target_pairs={{0,16},{16,0},{1,17},{17,1},{2,18},{18,2},{3,19},{19,3},{4,20},{20... | collective-permute-start | bytes 6152 | tf_op jit(solution)/shard_map/ppermute | solution.py:533
  18.1 0.6 copy-start.2
  18.8 23.7 %all-to-all-start = ((bf16[32,16,512]{2,1,0:T(8,128)(2,1)}), bf16[32,16,512]{2,1,0:T(8,128)(2,1)S(1)}, u32[]{:S(2)}, u32[]{:S(2)}) async-start(bf16[32,16,512]{2,1,0:T(8,128)(2,1)} %upward.1), calls=%async_computation | async-start | bytes 1048576 | tf_op jit(solution)/shard_map/all_to_all | solution.py:506
  28.9 4.0 %copy-start.1 = (bf16[8,2,128,256]{3,2,1,0:T(8,128)(2,1)S(1)}, bf16[8,2,128,256]{3,2,1,0:T(8,128)(2,1)}, u32[]{:S(2)}) copy-start(bf16[8,2,128,256]{3,2,1,0:T(8,128)(2,1)} %refs_2_.1) | copy-start | bytes 3145732
  32.9 32.5 %collective-permute-start.2 = (bf16[8,2,128,256]{3,2,1,0:T(8,128)(2,1)S(1)}, bf16[8,2,128,256]{3,2,1,0:T(8,128)(2,1)S(1)}, u32[]{:S(2)}, u32[]{:S(2)}) collective-permute-start(bf16[8,2,128,256]{3,2,1,0:T(8,128)(2,1)S(1)} %copy-done.1), channel_id=1, source_target_pairs={{1,0},{2,1},{3,2},{4,3},{5,4},{6,5},{7,6},{8,7},{9,8},{10,9},{11,1... | collective-permute-start | bytes 3145736 | tf_op jit(solution)/shard_map/ppermute | solution.py:495
  45.0 12.3 %all-to-all-start.1 = ((bf16[8,4,16,512]{3,2,1,0:T(8,128)(2,1)}), bf16[8,4,16,512]{3,2,1,0:T(8,128)(2,1)S(1)}, u32[]{:S(2)}, u32[]{:S(2)}) async-start(bf16[8,4,16,512]{3,2,1,0:T(8,128)(2,1)} %bitcast.15), calls=%async_computation.1 | async-start | bytes 1048576 | tf_op jit(solution)/shard_map/all_to_all | solution.py:514
  57.3 12.7 %collective-permute-start.5 = (bf16[8,16,512]{2,1,0:T(8,128)(2,1)S(1)}, bf16[8,16,512]{2,1,0:T(8,128)(2,1)S(1)}, u32[]{:S(2)}, u32[]{:S(2)}) collective-permute-start(bf16[8,16,512]{2,1,0:T(8,128)(2,1)S(1)} %get-tuple-element.35), channel_id=1, source_target_pairs={{0,3},{1,0},{2,1},{3,2},{4,7},{5,4},{6,5},{7,6},{8,11},{9,8},{10,9... | collective-permute-start | bytes 393224 | tf_op jit(solution)/shard_map/ppermute | solution.py:520
  64.8 11.5 %collective-permute-start.4 = (bf16[8,16,512]{2,1,0:T(8,128)(2,1)S(1)}, bf16[8,16,512]{2,1,0:T(8,128)(2,1)S(1)}, u32[]{:S(2)}, u32[]{:S(2)}) collective-permute-start(bf16[8,16,512]{2,1,0:T(8,128)(2,1)S(1)} %get-tuple-element.36), channel_id=1, source_target_pairs={{0,2},{1,3},{2,0},{3,1},{4,6},{5,7},{6,4},{7,5},{8,10},{9,11},{10,... | collective-permute-start | bytes 393224 | tf_op jit(solution)/shard_map/ppermute | solution.py:520
  64.8 11.5 %collective-permute-start.3 = (bf16[8,16,512]{2,1,0:T(8,128)(2,1)S(1)}, bf16[8,16,512]{2,1,0:T(8,128)(2,1)S(1)}, u32[]{:S(2)}, u32[]{:S(2)}) collective-permute-start(bf16[8,16,512]{2,1,0:T(8,128)(2,1)S(1)} %get-tuple-element.37), channel_id=1, source_target_pairs={{0,1},{1,2},{2,3},{3,0},{4,5},{5,6},{6,7},{7,4},{8,9},{9,10},{10,1... | collective-permute-start | bytes 393224 | tf_op jit(solution)/shard_map/ppermute | solution.py:520

commit v18 on v16

--- a/solution.py
+++ b/solution.py
@@ -429,7 +429,7 @@
     phi = phi_ref[0]
     phi_size = field.shape[1]
     pairs = [(bands_ref.at[:, phi], field.at[:, phi])]
-    for distance, piece in enumerate(received, 1):
+    for distance, piece in zip(phi_distances(phi_size), received):
         pairs.append((piece, field.at[:, lax.rem(phi + phi_size - distance, phi_size)]))
     copies = [
         pltpu.make_async_copy(source, target, sems.at[boxes + place])
@@ -508,6 +508,10 @@
     return lax.all_to_all(spread, axes, split_axis=0, concat_axis=0, tiled=True)
 
 
+def phi_distances(size):
+    return sorted(range(1, size), key=lambda distance: min(distance, size - distance))
+
+
 def staged_bands(incoming, shares):
     axes = ("box", "theta") if shares == lax.axis_size("box") else ("theta",)
     phi_size = lax.axis_size("phi")
@@ -515,7 +519,7 @@
     bands = incoming.reshape(-1, phi_size, *incoming.shape[1:])
     bands = lax.all_to_all(bands, axes, split_axis=0, concat_axis=0, tiled=True)
     received = []
-    for distance in range(1, phi_size):
+    for distance in phi_distances(phi_size):
         piece = lax.dynamic_index_in_dim(bands, (phi + distance) % phi_size, 1, keepdims=False)
         ring = [(place, (place + distance) % phi_size) for place in range(phi_size)]
         received.append(lax.ppermute(piece, "phi", ring))

time: 77.4 us -> 79.2 us (1.023); the launches traced: 75.9 us -> 78.6 us
  waiting for transfers between devices: 19.9 us -> 23.2 us
    ppermute x3, waiting for transfers between devices: 4.35 us -> 6.94 us  [staged_bands(): received.append(lax.ppermute(piece, 'phi', ring))]
  transfers between devices with their start and end apart: 8 -> 8, of which waited for: 4 -> 5; matrix products, arithmetic and copies ran while one was open for 4% -> 4% of each run, Pallas kernels for 35% -> 33%
where the time goes in v18:
time: 79.2 us; the launch traced here: 78.6 us
  Pallas kernels  28.2 us (36%)
  starting transfers between devices  23.3 us (29%)
  waiting for transfers between devices  23.2 us (29%)
  local copies, waits for them, and re-layouts  2.16 us (3%)
  other arithmetic  1.56 us (2%)
    pallas_call x3, Pallas kernels, near_field(): pl.pallas_call(kernel, in_specs=[smem, hbm, vmem] + [hbm] * (begun + kept...  15.1 us
    all_to_all x1, waiting for transfers between devices, parent_bands(): return lax.all_to_all(spread, axes, split_axis=0, concat_axis=0, tiled=True)  8.26 us
    ppermute x3, starting transfers between devices, staged_bands(): received.append(lax.ppermute(piece, 'phi', ring))  7.95 us
    ppermute x3, waiting for transfers between devices, staged_bands(): received.append(lax.ppermute(piece, 'phi', ring))  6.94 us
    ppermute x2, starting transfers between devices, shift(): return lax.ppermute(block, axis, pairs)  6.41 us
    ppermute x2, waiting for transfers between devices, shift(): return lax.ppermute(block, axis, pairs)  6.24 us
    pallas_call x1, Pallas kernels, upward(): pl.pallas_call(up_kernel, in_specs=[hbm] * 3, out_specs=hbm, out_shape=pl...  5.24 us
    all_to_all x1, starting transfers between devices, parent_bands(): return lax.all_to_all(spread, axes, split_axis=0, concat_axis=0, tiled=True)  3.91 us
  transfers between devices with their start and end apart: 8, of which 5 were waited for; matrix products, arithmetic and copies ran while one was open for 4% of the time, Pallas kernels for 33%

profile of v18, /device:TPU:0, one launch (start us, length us, event | category | flops | bytes accessed | tf_op | source)
XLA Modules:
  0.0 78.6 jit_solution(5911435020103400428)
XLA Ops:
  0.0 5.1 %collective-permute-start.1 = (bf16[8,2,128,256]{3,2,1,0:T(8,128)(2,1)}, bf16[8,2,128,256]{3,2,1,0:T(8,128)(2,1)S(1)}, u32[]{:S(2)}, u32[]{:S(2)}) collective-permute-start(bf16[8,2,128,256]{3,2,1,0:T(8,128)(2,1)} %refs_2_.1), channel_id=1, source_target_pairs={{0,1},{1,2},{2,3},{3,4},{4,5},{5,6},{6,7},{7,8},{8,9},{9,10},{10,1... | collective-permute-start | bytes 3145736 | tf_op jit(solution)/shard_map/ppermute | solution.py:497
  5.1 0.8 fusion.1
  6.0 0.8 stack.10
  6.8 5.2 %upward.1 = bf16[32,16,512]{2,1,0:T(8,128)(2,1)} custom-call(bf16[8,2,128,256]{3,2,1,0:T(8,128)(2,1)} %refs_2_.1, bf16[8,2,128,128]{3,2,1,0:T(8,128)(2,1)} %rad_ref.1, bf16[1024,1024]{1,0:T(8,128)(2,1)} %constant.93.clone.w_hbm), custom_call_target="tpu_custom_call" | custom-call | flops 2000000000 | bytes 4194304 | tf_op jit(solution)/shard_map/upward/pallas_call | solution.py:127
  12.0 1.5 %collective-permute-start = (s32[256,2]{0,1:T(2,128)S(1)}, s32[256,2]{0,1:T(2,128)S(1)}, u32[]{:S(2)}, u32[]{:S(2)}) collective-permute-start(s32[256,2]{0,1:T(2,128)S(1)} %pad_add_fusion.2), channel_id=1, source_target_pairs={{0,16},{16,0},{1,17},{17,1},{2,18},{18,2},{3,19},{19,3},{4,20},{20... | collective-permute-start | bytes 6152 | tf_op jit(solution)/shard_map/ppermute | solution.py:537
  13.6 0.1 reshape.134
  13.8 0.1 convert_reduce_fusion
  13.9 0.3 convert_reduce_fusion.1
  14.2 0.1 copy.22
  14.3 0.2 select_reduce_fusion
  14.5 0.1 copy.21.table_ref
  14.6 2.0 %adjoint.1.refs_5_ = bf16[8,128,256]{2,1,0:T(8,128)(2,1)} custom-call(bf16[8,2,128,128]{3,2,1,0:T(8,128)(2,1)} %rad_ref.1), custom_call_target="tpu_custom_call" | custom-call | flops 1000000 | bytes 2097152 | tf_op jit(solution)/shard_map/adjoint/pallas_call | solution.py:410
  16.7 0.1 copy.19
  16.8 0.1 copy.20
  17.0 1.1 %coupling.1.lines_hbm = f32[2,32,512]{2,1,0:T(8,128)S(1)} custom-call(s32[512,2]{1,0:T(8,128)S(1)} %broadcast_select_fusion.lists_ref, s32[1]{0:T(128)} %constant.82.clone.1.base_ref, bf16[316,32]{1,0:T(8,128)(2,1)S(1)} %copy.21.table_ref), custom_call_target="tpu_custom_call" | custom-call | flops 200000000 | bytes 2097152 | tf_op jit(solution)/shard_map/coupling/pallas_call | solution.py:175
  18.1 0.6 copy-done.2
  18.8 3.9 %all-to-all-start = ((bf16[32,16,512]{2,1,0:T(8,128)(2,1)}), bf16[32,16,512]{2,1,0:T(8,128)(2,1)S(1)}, u32[]{:S(2)}, u32[]{:S(2)}) async-start(bf16[32,16,512]{2,1,0:T(8,128)(2,1)} %upward.1), calls=%async_computation | async-start | bytes 1048576 | tf_op jit(solution)/shard_map/all_to_all | solution.py:508
  22.7 6.2 %collective-permute-done.1.refs_2_ = bf16[8,2,128,256]{3,2,1,0:T(8,128)(2,1)S(1)} collective-permute-done((bf16[8,2,128,256]{3,2,1,0:T(8,128)(2,1)}, bf16[8,2,128,256]{3,2,1,0:T(8,128)(2,1)S(1)}, u32[]{:S(2)}, u32[]{:S(2)}) %collective-permute-start.1) | collective-permute-done | bytes 1048608 | tf_op jit(solution)/shard_map/ppermute | solution.py:497
  28.9 4.0 %near_low.1.refs_3_ = f32[8,2,128,256]{3,2,1,0:T(8,128)} custom-call(s32[3,105]{1,0:T(4,128)S(1)} %pad_add_fusion.3.refs_0_, bf16[96,2,128,128]{3,2,1,0:T(8,128)(2,1)} %bitcast.10, bf16[8,2,128,256]{3,2,1,0:T(8,128)(2,1)S(1)} %collective-permute-done.1.refs_2_), custom_call_target="tpu_custom_call" | custom-call | flops 2000000000 | bytes 8388608 | tf_op jit(solution)/shard_map/near_low/pallas_call | solution.py:378
  32.9 1.3 %collective-permute-start.2 = (bf16[8,2,128,256]{3,2,1,0:T(8,128)(2,1)S(1)}, bf16[8,2,128,256]{3,2,1,0:T(8,128)(2,1)S(1)}, u32[]{:S(2)}, u32[]{:S(2)}) collective-permute-start(bf16[8,2,128,256]{3,2,1,0:T(8,128)(2,1)S(1)} %copy-done.1), channel_id=1, source_target_pairs={{1,0},{2,1},{3,2},{4,3},{5,4},{6,5},{7,6},{8,7},{9,8},{10,9},{11,1... | collective-permute-start | bytes 3145736 | tf_op jit(solution)/shard_map/ppermute | solution.py:497
  34.2 8.3 %all-to-all-done.refs_0_ = bf16[32,16,512]{2,1,0:T(8,128)(2,1)S(1)} async-done(((bf16[32,16,512]{2,1,0:T(8,128)(2,1)}), bf16[32,16,512]{2,1,0:T(8,128)(2,1)S(1)}, u32[]{:S(2)}, u32[]{:S(2)}) %all-to-all-start) | async-done | bytes 524320 | tf_op jit(solution)/shard_map/all_to_all | solution.py:508
  42.5 2.5 %translate.1 = bf16[32,16,512]{2,1,0:T(8,128)(2,1)} custom-call(f32[2,32,512]{2,1,0:T(8,128)} %copy-done.2, bf16[32,16,512]{2,1,0:T(8,128)(2,1)S(1)} %all-to-all-done.refs_0_), custom_call_target="tpu_custom_call" | custom-call | flops 1000000000 | bytes 2097152 | tf_op jit(solution)/shard_map/translate/pallas_call | solution.py:230
  45.0 3.5 %all-to-all-start.1 = ((bf16[8,4,16,512]{3,2,1,0:T(8,128)(2,1)}), bf16[8,4,16,512]{3,2,1,0:T(8,128)(2,1)S(1)}, u32[]{:S(2)}, u32[]{:S(2)}) async-start(bf16[8,4,16,512]{3,2,1,0:T(8,128)(2,1)} %bitcast.13), calls=%async_computation.1 | async-start | bytes 1048576 | tf_op jit(solution)/shard_map/all_to_all | solution.py:520
  48.5 7.0 %near_own.1.refs_3_ = f32[8,2,128,256]{3,2,1,0:T(8,128)} custom-call(s32[3,105]{1,0:T(4,128)S(1)} %pad_add_fusion.3.refs_0_, bf16[96,2,128,128]{3,2,1,0:T(8,128)(2,1)} %bitcast.11, bf16[8,2,128,256]{3,2,1,0:T(8,128)(2,1)S(1)} %copy-done.1, f32[8,2,128,256]{3,2,1,0:T(8,128)} %near_low.1.refs_3_), custom_call_target="tpu_custom_call" | custom-call | flops 2000000000 | bytes 8388608 | tf_op jit(solution)/shard_map/near_own/pallas_call | solution.py:378
  55.5 1.7 %all-to-all-done.1.refs_0_ = bf16[8,4,16,512]{3,2,1,0:T(8,128)(2,1)S(1)} async-done(((bf16[8,4,16,512]{3,2,1,0:T(8,128)(2,1)}), bf16[8,4,16,512]{3,2,1,0:T(8,128)(2,1)S(1)}, u32[]{:S(2)}, u32[]{:S(2)}) %all-to-all-start.1) | async-done | bytes 524320 | tf_op jit(solution)/shard_map/all_to_all | solution.py:520
  57.3 0.9 %collective-permute-start.3 = (bf16[8,16,512]{2,1,0:T(8,128)(2,1)S(1)}, bf16[8,16,512]{2,1,0:T(8,128)(2,1)S(1)}, u32[]{:S(2)}, u32[]{:S(2)}) collective-permute-start(bf16[8,16,512]{2,1,0:T(8,128)(2,1)S(1)} %get-tuple-element.39), channel_id=1, source_target_pairs={{0,1},{1,2},{2,3},{3,0},{4,5},{5,6},{6,7},{7,4},{8,9},{9,10},{10,1... | collective-permute-start | bytes 393224 | tf_op jit(solution)/shard_map/ppermute | solution.py:525
  58.2 6.6 %collective-permute-start.4 = (bf16[8,16,512]{2,1,0:T(8,128)(2,1)S(1)}, bf16[8,16,512]{2,1,0:T(8,128)(2,1)S(1)}, u32[]{:S(2)}, u32[]{:S(2)}) collective-permute-start(bf16[8,16,512]{2,1,0:T(8,128)(2,1)S(1)} %get-tuple-element.38), channel_id=1, source_target_pairs={{0,3},{1,0},{2,1},{3,2},{4,7},{5,4},{6,5},{7,6},{8,11},{9,8},{10,9... | collective-permute-start | bytes 393224 | tf_op jit(solution)/shard_map/ppermute | solution.py:525
  64.7 0.5 collective-permute-start.5
  65.3 4.1 %near_high.1 = (f32[8,2,128,256]{3,2,1,0:T(8,128)S(1)}, f32[8,2,128,256]{3,2,1,0:T(8,128)S(1)}, bf16[1024,512]{1,0:T(8,128)(2,1)S(1)}, bf16[8,128,256]{2,1,0:T(8,128)(2,1)S(1)}) custom-call(s32[3,105]{1,0:T(4,128)S(1)} %pad_add_fusion.3.refs_0_, bf16[96,2,128,128]{3,2,1,0:T(8,128)(2,1)} %bitcast.12, ...), custom_call_target="tpu_custom_call" | custom-call | flops 99999997952 | bytes 8388608 | tf_op jit(solution)/shard_map/near_high/pallas_call | solution.py:378
  69.4 0.2 collective-permute-done.4.refs_2_
  69.6 6.8 %collective-permute-done.5.refs_3_ = bf16[8,16,512]{2,1,0:T(8,128)(2,1)S(1)} collective-permute-done((bf16[8,16,512]{2,1,0:T(8,128)(2,1)S(1)}, bf16[8,16,512]{2,1,0:T(8,128)(2,1)S(1)}, u32[]{:S(2)}, u32[]{:S(2)}) %collective-permute-start.5) | collective-permute-done | bytes 131104 | tf_op jit(solution)/shard_map/ppermute | solution.py:525
  76.3 2.3 %downward.1 = f32[8,2,128,256]{3,2,1,0:T(8,128)} custom-call(s32[1]{0:T(128)} %bitcast.phi_ref, f32[8,2,128,256]{3,2,1,0:T(8,128)S(1)} %get-tuple-element.32.near_ref, f32[8,2,128,256]{3,2,1,0:T(8,128)S(1)} %get-tuple-element.33.before_ref, bf16[1024,512]{1,0:T(8,128)(2,1)S(1)} %get-tuple-element.34.w_ref, ...), custom_call_target="tpu_custom_call" | custom-call | flops 2000000000 | bytes 7340032 | tf_op jit(solution)/shard_map/downward/pallas_call | solution.py:474
  (25 shorter events, 0.4 us)
Async XLA Ops:
  0.0 14.4 %copy-start = (bf16[316,2,4,8]{0,3,2,1:T(8,128)(2,1)S(1)}, bf16[316,2,4,8]{0,3,2,1:T(8,128)(2,1)}, u32[]{:S(2)}) copy-start(bf16[316,2,4,8]{0,3,2,1:T(8,128)(2,1)} %param.19) | copy-start | bytes 121348
  0.0 28.9 %collective-permute-start.1 = (bf16[8,2,128,256]{3,2,1,0:T(8,128)(2,1)}, bf16[8,2,128,256]{3,2,1,0:T(8,128)(2,1)S(1)}, u32[]{:S(2)}, u32[]{:S(2)}) collective-permute-start(bf16[8,2,128,256]{3,2,1,0:T(8,128)(2,1)} %refs_2_.1), channel_id=1, source_target_pairs={{0,1},{1,2},{2,3},{3,4},{4,5},{5,6},{6,7},{7,8},{8,9},{9,10},{10,1... | collective-permute-start | bytes 3145736 | tf_op jit(solution)/shard_map/ppermute | solution.py:497
  6.8 6.8 %copy-start.3 = (s32[8,12]{1,0:T(8,128)S(1)}, s32[8,12]{1,0:T(8,128)}, u32[]{:S(2)}) copy-start(s32[8,12]{1,0:T(8,128)} %param.13) | copy-start | bytes 1156
  6.8 6.8 %copy-start.4 = (s32[8]{0:T(128)S(1)}, s32[8]{0:T(128)}, u32[]{:S(2)}) copy-start(s32[8]{0:T(128)} %param.14) | copy-start | bytes 100
  12.0 4.7 %collective-permute-start = (s32[256,2]{0,1:T(2,128)S(1)}, s32[256,2]{0,1:T(2,128)S(1)}, u32[]{:S(2)}, u32[]{:S(2)}) collective-permute-start(s32[256,2]{0,1:T(2,128)S(1)} %pad_add_fusion.2), channel_id=1, source_target_pairs={{0,16},{16,0},{1,17},{17,1},{2,18},{18,2},{3,19},{19,3},{4,20},{20... | collective-permute-start | bytes 6152 | tf_op jit(solution)/shard_map/ppermute | solution.py:537
  18.1 0.6 copy-start.2
  18.8 23.7 %all-to-all-start = ((bf16[32,16,512]{2,1,0:T(8,128)(2,1)}), bf16[32,16,512]{2,1,0:T(8,128)(2,1)S(1)}, u32[]{:S(2)}, u32[]{:S(2)}) async-start(bf16[32,16,512]{2,1,0:T(8,128)(2,1)} %upward.1), calls=%async_computation | async-start | bytes 1048576 | tf_op jit(solution)/shard_map/all_to_all | solution.py:508
  28.9 4.0 %copy-start.1 = (bf16[8,2,128,256]{3,2,1,0:T(8,128)(2,1)S(1)}, bf16[8,2,128,256]{3,2,1,0:T(8,128)(2,1)}, u32[]{:S(2)}) copy-start(bf16[8,2,128,256]{3,2,1,0:T(8,128)(2,1)} %refs_2_.1) | copy-start | bytes 3145732
  32.9 32.3 %collective-permute-start.2 = (bf16[8,2,128,256]{3,2,1,0:T(8,128)(2,1)S(1)}, bf16[8,2,128,256]{3,2,1,0:T(8,128)(2,1)S(1)}, u32[]{:S(2)}, u32[]{:S(2)}) collective-permute-start(bf16[8,2,128,256]{3,2,1,0:T(8,128)(2,1)S(1)} %copy-done.1), channel_id=1, source_target_pairs={{1,0},{2,1},{3,2},{4,3},{5,4},{6,5},{7,6},{8,7},{9,8},{10,9},{11,1... | collective-permute-start | bytes 3145736 | tf_op jit(solution)/shard_map/ppermute | solution.py:497
  45.0 12.3 %all-to-all-start.1 = ((bf16[8,4,16,512]{3,2,1,0:T(8,128)(2,1)}), bf16[8,4,16,512]{3,2,1,0:T(8,128)(2,1)S(1)}, u32[]{:S(2)}, u32[]{:S(2)}) async-start(bf16[8,4,16,512]{3,2,1,0:T(8,128)(2,1)} %bitcast.13), calls=%async_computation.1 | async-start | bytes 1048576 | tf_op jit(solution)/shard_map/all_to_all | solution.py:520
  57.3 12.1 %collective-permute-start.3 = (bf16[8,16,512]{2,1,0:T(8,128)(2,1)S(1)}, bf16[8,16,512]{2,1,0:T(8,128)(2,1)S(1)}, u32[]{:S(2)}, u32[]{:S(2)}) collective-permute-start(bf16[8,16,512]{2,1,0:T(8,128)(2,1)S(1)} %get-tuple-element.39), channel_id=1, source_target_pairs={{0,1},{1,2},{2,3},{3,0},{4,5},{5,6},{6,7},{7,4},{8,9},{9,10},{10,1... | collective-permute-start | bytes 393224 | tf_op jit(solution)/shard_map/ppermute | solution.py:525
  58.2 11.4 %collective-permute-start.4 = (bf16[8,16,512]{2,1,0:T(8,128)(2,1)S(1)}, bf16[8,16,512]{2,1,0:T(8,128)(2,1)S(1)}, u32[]{:S(2)}, u32[]{:S(2)}) collective-permute-start(bf16[8,16,512]{2,1,0:T(8,128)(2,1)S(1)} %get-tuple-element.38), channel_id=1, source_target_pairs={{0,3},{1,0},{2,1},{3,2},{4,7},{5,4},{6,5},{7,6},{8,11},{9,8},{10,9... | collective-permute-start | bytes 393224 | tf_op jit(solution)/shard_map/ppermute | solution.py:525
  64.7 11.6 %collective-permute-start.5 = (bf16[8,16,512]{2,1,0:T(8,128)(2,1)S(1)}, bf16[8,16,512]{2,1,0:T(8,128)(2,1)S(1)}, u32[]{:S(2)}, u32[]{:S(2)}) collective-permute-start(bf16[8,16,512]{2,1,0:T(8,128)(2,1)S(1)} %get-tuple-element.37), channel_id=1, source_target_pairs={{0,2},{1,3},{2,0},{3,1},{4,6},{5,7},{6,4},{7,5},{8,10},{9,11},{10,... | collective-permute-start | bytes 393224 | tf_op jit(solution)/shard_map/ppermute | solution.py:525

commit v19 on v18

--- a/solution.py
+++ b/solution.py
@@ -509,7 +509,7 @@
 
 
 def phi_distances(size):
-    return sorted(range(1, size), key=lambda distance: min(distance, size - distance))
+    return sorted(range(1, size), key=lambda distance: -min(distance, size - distance))
 
 
 def staged_bands(incoming, shares):

time: 79.2 us -> 77.6 us (0.980)
  waiting for transfers between devices: 23.2 us -> 19.8 us
  Pallas kernels: 28.2 us -> 29.8 us
    ppermute x3, waiting for transfers between devices: 6.94 us -> 5.08 us  [staged_bands(): received.append(lax.ppermute(piece, 'phi', ring))]
    pallas_call x3, Pallas kernels: 15.1 us -> 16.7 us  [near_field(): pl.pallas_call(kernel, in_specs=[smem, hbm, vmem] + [hbm] * (begun + kept...]
    all_to_all x1, waiting for transfers between devices: 1.74 us -> 0.28 us  [staged_bands(): bands = lax.all_to_all(bands, axes, split_axis=0, concat_axis=0, tiled=True)]
  transfers between devices with their start and end apart: 8 -> 8, of which waited for: 5 -> 5; matrix products, arithmetic and copies ran while one was open for 4% -> 4% of each run, Pallas kernels for 33% -> 36%
where the time goes in v19:
time: 77.6 us; the launch traced here: 77 us
  Pallas kernels  29.8 us (38%)
  starting transfers between devices  23.5 us (30%)
  waiting for transfers between devices  19.8 us (26%)
  local copies, waits for them, and re-layouts  2.16 us (3%)
  other arithmetic  1.56 us (2%)
    pallas_call x3, Pallas kernels, near_field(): pl.pallas_call(kernel, in_specs=[smem, hbm, vmem] + [hbm] * (begun + kept...  16.7 us
    all_to_all x1, waiting for transfers between devices, parent_bands(): return lax.all_to_all(spread, axes, split_axis=0, concat_axis=0, tiled=True)  8.19 us
    ppermute x3, starting transfers between devices, staged_bands(): received.append(lax.ppermute(piece, 'phi', ring))  8.13 us
    ppermute x2, starting transfers between devices, shift(): return lax.ppermute(block, axis, pairs)  6.41 us
    ppermute x2, waiting for transfers between devices, shift(): return lax.ppermute(block, axis, pairs)  6.24 us
    pallas_call x1, Pallas kernels, upward(): pl.pallas_call(up_kernel, in_specs=[hbm] * 3, out_specs=hbm, out_shape=pl...  5.24 us
    ppermute x3, waiting for transfers between devices, staged_bands(): received.append(lax.ppermute(piece, 'phi', ring))  5.08 us
    all_to_all x1, starting transfers between devices, parent_bands(): return lax.all_to_all(spread, axes, split_axis=0, concat_axis=0, tiled=True)  3.91 us
  transfers between devices with their start and end apart: 8, of which 5 were waited for; matrix products, arithmetic and copies ran while one was open for 4% of the time, Pallas kernels for 36%

profile of v19, /device:TPU:0, one launch (start us, length us, event | category | flops | bytes accessed | tf_op | source)
XLA Modules:
  0.0 77.0 jit_solution(3781955920560841287)
XLA Ops:
  0.0 5.1 %collective-permute-start.1 = (bf16[8,2,128,256]{3,2,1,0:T(8,128)(2,1)}, bf16[8,2,128,256]{3,2,1,0:T(8,128)(2,1)S(1)}, u32[]{:S(2)}, u32[]{:S(2)}) collective-permute-start(bf16[8,2,128,256]{3,2,1,0:T(8,128)(2,1)} %refs_2_.1), channel_id=1, source_target_pairs={{0,1},{1,2},{2,3},{3,4},{4,5},{5,6},{6,7},{7,8},{8,9},{9,10},{10,1... | collective-permute-start | bytes 3145736 | tf_op jit(solution)/shard_map/ppermute | solution.py:497
  5.1 0.8 %fusion.1 = s32[16,16]{1,0:T(8,128)S(1)} fusion(s32[16,16]{1,0:T(8,128)} %param.16, s32[16]{0:T(128)} %param.18), kind=kLoop, calls=%fused_computation.12 | loop fusion | flops 512 | bytes 2112 | tf_op jit(solution)/shard_map/jit(_where)/select_n | solution.py:502
  5.9 0.1 stack.9
  6.0 0.8 %stack.10 = s32[256,1]{0,1:T(1,128)S(1)} reshape(s32[16,16]{1,0:T(8,128)} %param.17) | data formatting | bytes 2048 | tf_op jit(solution)/shard_map/stack | solution.py:503
  6.8 5.2 %upward.1 = bf16[32,16,512]{2,1,0:T(8,128)(2,1)} custom-call(bf16[8,2,128,256]{3,2,1,0:T(8,128)(2,1)} %refs_2_.1, bf16[8,2,128,128]{3,2,1,0:T(8,128)(2,1)} %rad_ref.1, bf16[1024,1024]{1,0:T(8,128)(2,1)} %constant.93.clone.w_hbm), custom_call_target="tpu_custom_call" | custom-call | flops 2000000000 | bytes 4194304 | tf_op jit(solution)/shard_map/upward/pallas_call | solution.py:127
  12.0 1.5 %collective-permute-start = (s32[256,2]{0,1:T(2,128)S(1)}, s32[256,2]{0,1:T(2,128)S(1)}, u32[]{:S(2)}, u32[]{:S(2)}) collective-permute-start(s32[256,2]{0,1:T(2,128)S(1)} %pad_add_fusion.2), channel_id=1, source_target_pairs={{0,16},{16,0},{1,17},{17,1},{2,18},{18,2},{3,19},{19,3},{4,20},{20... | collective-permute-start | bytes 6152 | tf_op jit(solution)/shard_map/ppermute | solution.py:537
  13.6 0.1 reshape.134
  13.8 0.1 convert_reduce_fusion
  13.9 0.3 convert_reduce_fusion.1
  14.2 0.1 copy.22
  14.3 0.2 select_reduce_fusion
  14.5 0.1 copy.21.table_ref
  14.6 2.0 %adjoint.1.refs_5_ = bf16[8,128,256]{2,1,0:T(8,128)(2,1)} custom-call(bf16[8,2,128,128]{3,2,1,0:T(8,128)(2,1)} %rad_ref.1), custom_call_target="tpu_custom_call" | custom-call | flops 1000000 | bytes 2097152 | tf_op jit(solution)/shard_map/adjoint/pallas_call | solution.py:410
  16.7 0.1 copy.19
  16.8 0.1 copy.20
  17.0 1.1 %coupling.1.lines_hbm = f32[2,32,512]{2,1,0:T(8,128)S(1)} custom-call(s32[512,2]{1,0:T(8,128)S(1)} %broadcast_select_fusion.lists_ref, s32[1]{0:T(128)} %constant.82.clone.1.base_ref, bf16[316,32]{1,0:T(8,128)(2,1)S(1)} %copy.21.table_ref), custom_call_target="tpu_custom_call" | custom-call | flops 200000000 | bytes 2097152 | tf_op jit(solution)/shard_map/coupling/pallas_call | solution.py:175
  18.1 0.6 copy-done.2
  18.8 3.9 %all-to-all-start = ((bf16[32,16,512]{2,1,0:T(8,128)(2,1)}), bf16[32,16,512]{2,1,0:T(8,128)(2,1)S(1)}, u32[]{:S(2)}, u32[]{:S(2)}) async-start(bf16[32,16,512]{2,1,0:T(8,128)(2,1)} %upward.1), calls=%async_computation | async-start | bytes 1048576 | tf_op jit(solution)/shard_map/all_to_all | solution.py:508
  22.7 6.2 %collective-permute-done.1.refs_2_ = bf16[8,2,128,256]{3,2,1,0:T(8,128)(2,1)S(1)} collective-permute-done((bf16[8,2,128,256]{3,2,1,0:T(8,128)(2,1)}, bf16[8,2,128,256]{3,2,1,0:T(8,128)(2,1)S(1)}, u32[]{:S(2)}, u32[]{:S(2)}) %collective-permute-start.1) | collective-permute-done | bytes 1048608 | tf_op jit(solution)/shard_map/ppermute | solution.py:497
  28.9 4.0 %near_low.1.refs_3_ = f32[8,2,128,256]{3,2,1,0:T(8,128)} custom-call(s32[3,105]{1,0:T(4,128)S(1)} %pad_add_fusion.3.refs_0_, bf16[96,2,128,128]{3,2,1,0:T(8,128)(2,1)} %bitcast.10, bf16[8,2,128,256]{3,2,1,0:T(8,128)(2,1)S(1)} %collective-permute-done.1.refs_2_), custom_call_target="tpu_custom_call" | custom-call | flops 2000000000 | bytes 8388608 | tf_op jit(solution)/shard_map/near_low/pallas_call | solution.py:378
  32.9 1.3 %collective-permute-start.2 = (bf16[8,2,128,256]{3,2,1,0:T(8,128)(2,1)S(1)}, bf16[8,2,128,256]{3,2,1,0:T(8,128)(2,1)S(1)}, u32[]{:S(2)}, u32[]{:S(2)}) collective-permute-start(bf16[8,2,128,256]{3,2,1,0:T(8,128)(2,1)S(1)} %copy-done.1), channel_id=1, source_target_pairs={{1,0},{2,1},{3,2},{4,3},{5,4},{6,5},{7,6},{8,7},{9,8},{10,9},{11,1... | collective-permute-start | bytes 3145736 | tf_op jit(solution)/shard_map/ppermute | solution.py:497
  34.2 8.2 %all-to-all-done.refs_0_ = bf16[32,16,512]{2,1,0:T(8,128)(2,1)S(1)} async-done(((bf16[32,16,512]{2,1,0:T(8,128)(2,1)}), bf16[32,16,512]{2,1,0:T(8,128)(2,1)S(1)}, u32[]{:S(2)}, u32[]{:S(2)}) %all-to-all-start) | async-done | bytes 524320 | tf_op jit(solution)/shard_map/all_to_all | solution.py:508
  42.4 2.5 %translate.1 = bf16[32,16,512]{2,1,0:T(8,128)(2,1)} custom-call(f32[2,32,512]{2,1,0:T(8,128)} %copy-done.2, bf16[32,16,512]{2,1,0:T(8,128)(2,1)S(1)} %all-to-all-done.refs_0_), custom_call_target="tpu_custom_call" | custom-call | flops 1000000000 | bytes 2097152 | tf_op jit(solution)/shard_map/translate/pallas_call | solution.py:230
  44.9 3.5 %all-to-all-start.1 = ((bf16[8,4,16,512]{3,2,1,0:T(8,128)(2,1)}), bf16[8,4,16,512]{3,2,1,0:T(8,128)(2,1)S(1)}, u32[]{:S(2)}, u32[]{:S(2)}) async-start(bf16[8,4,16,512]{3,2,1,0:T(8,128)(2,1)} %bitcast.13), calls=%async_computation.1 | async-start | bytes 1048576 | tf_op jit(solution)/shard_map/all_to_all | solution.py:520
  48.5 8.4 %near_own.1.refs_3_ = f32[8,2,128,256]{3,2,1,0:T(8,128)} custom-call(s32[3,105]{1,0:T(4,128)S(1)} %pad_add_fusion.3.refs_0_, bf16[96,2,128,128]{3,2,1,0:T(8,128)(2,1)} %bitcast.11, bf16[8,2,128,256]{3,2,1,0:T(8,128)(2,1)S(1)} %copy-done.1, f32[8,2,128,256]{3,2,1,0:T(8,128)} %near_low.1.refs_3_), custom_call_target="tpu_custom_call" | custom-call | flops 2000000000 | bytes 8388608 | tf_op jit(solution)/shard_map/near_own/pallas_call | solution.py:378
  56.9 0.3 all-to-all-done.1.refs_0_
  57.2 0.1 collective-permute-start.3
  57.4 8.0 %collective-permute-start.4 = (bf16[8,16,512]{2,1,0:T(8,128)(2,1)S(1)}, bf16[8,16,512]{2,1,0:T(8,128)(2,1)S(1)}, u32[]{:S(2)}, u32[]{:S(2)}) collective-permute-start(bf16[8,16,512]{2,1,0:T(8,128)(2,1)S(1)} %get-tuple-element.38), channel_id=1, source_target_pairs={{0,1},{1,2},{2,3},{3,0},{4,5},{5,6},{6,7},{7,4},{8,9},{9,10},{10,1... | collective-permute-start | bytes 393224 | tf_op jit(solution)/shard_map/ppermute | solution.py:525
  65.4 4.3 %near_high.1 = (f32[8,2,128,256]{3,2,1,0:T(8,128)S(1)}, f32[8,2,128,256]{3,2,1,0:T(8,128)S(1)}, bf16[1024,512]{1,0:T(8,128)(2,1)S(1)}, bf16[8,128,256]{2,1,0:T(8,128)(2,1)S(1)}) custom-call(s32[3,105]{1,0:T(4,128)S(1)} %pad_add_fusion.3.refs_0_, bf16[96,2,128,128]{3,2,1,0:T(8,128)(2,1)} %bitcast.12, ...), custom_call_target="tpu_custom_call" | custom-call | flops 99999997952 | bytes 8388608 | tf_op jit(solution)/shard_map/near_high/pallas_call | solution.py:378
  69.7 4.7 %collective-permute-done.3.refs_1_ = bf16[8,16,512]{2,1,0:T(8,128)(2,1)S(1)} collective-permute-done((bf16[8,16,512]{2,1,0:T(8,128)(2,1)S(1)}, bf16[8,16,512]{2,1,0:T(8,128)(2,1)S(1)}, u32[]{:S(2)}, u32[]{:S(2)}) %collective-permute-start.3) | collective-permute-done | bytes 131104 | tf_op jit(solution)/shard_map/ppermute | solution.py:525
  74.4 0.3 collective-permute-done.5.refs_3_
  74.7 2.3 %downward.1 = f32[8,2,128,256]{3,2,1,0:T(8,128)} custom-call(s32[1]{0:T(128)} %bitcast.phi_ref, f32[8,2,128,256]{3,2,1,0:T(8,128)S(1)} %get-tuple-element.32.near_ref, f32[8,2,128,256]{3,2,1,0:T(8,128)S(1)} %get-tuple-element.33.before_ref, bf16[1024,512]{1,0:T(8,128)(2,1)S(1)} %get-tuple-element.34.w_ref, ...), custom_call_target="tpu_custom_call" | custom-call | flops 2000000000 | bytes 7340032 | tf_op jit(solution)/shard_map/downward/pallas_call | solution.py:474
  (25 shorter events, 0.3 us)
Async XLA Ops:
  0.0 14.4 %copy-start = (bf16[316,2,4,8]{0,3,2,1:T(8,128)(2,1)S(1)}, bf16[316,2,4,8]{0,3,2,1:T(8,128)(2,1)}, u32[]{:S(2)}) copy-start(bf16[316,2,4,8]{0,3,2,1:T(8,128)(2,1)} %param.19) | copy-start | bytes 121348
  0.0 28.9 %collective-permute-start.1 = (bf16[8,2,128,256]{3,2,1,0:T(8,128)(2,1)}, bf16[8,2,128,256]{3,2,1,0:T(8,128)(2,1)S(1)}, u32[]{:S(2)}, u32[]{:S(2)}) collective-permute-start(bf16[8,2,128,256]{3,2,1,0:T(8,128)(2,1)} %refs_2_.1), channel_id=1, source_target_pairs={{0,1},{1,2},{2,3},{3,4},{4,5},{5,6},{6,7},{7,8},{8,9},{9,10},{10,1... | collective-permute-start | bytes 3145736 | tf_op jit(solution)/shard_map/ppermute | solution.py:497
  6.8 6.8 %copy-start.3 = (s32[8,12]{1,0:T(8,128)S(1)}, s32[8,12]{1,0:T(8,128)}, u32[]{:S(2)}) copy-start(s32[8,12]{1,0:T(8,128)} %param.13) | copy-start | bytes 1156
  6.8 6.8 %copy-start.4 = (s32[8]{0:T(128)S(1)}, s32[8]{0:T(128)}, u32[]{:S(2)}) copy-start(s32[8]{0:T(128)} %param.14) | copy-start | bytes 100
  12.0 4.7 %collective-permute-start = (s32[256,2]{0,1:T(2,128)S(1)}, s32[256,2]{0,1:T(2,128)S(1)}, u32[]{:S(2)}, u32[]{:S(2)}) collective-permute-start(s32[256,2]{0,1:T(2,128)S(1)} %pad_add_fusion.2), channel_id=1, source_target_pairs={{0,16},{16,0},{1,17},{17,1},{2,18},{18,2},{3,19},{19,3},{4,20},{20... | collective-permute-start | bytes 6152 | tf_op jit(solution)/shard_map/ppermute | solution.py:537
  18.1 0.6 copy-start.2
  18.8 23.6 %all-to-all-start = ((bf16[32,16,512]{2,1,0:T(8,128)(2,1)}), bf16[32,16,512]{2,1,0:T(8,128)(2,1)S(1)}, u32[]{:S(2)}, u32[]{:S(2)}) async-start(bf16[32,16,512]{2,1,0:T(8,128)(2,1)} %upward.1), calls=%async_computation | async-start | bytes 1048576 | tf_op jit(solution)/shard_map/all_to_all | solution.py:508
  28.9 4.0 %copy-start.1 = (bf16[8,2,128,256]{3,2,1,0:T(8,128)(2,1)S(1)}, bf16[8,2,128,256]{3,2,1,0:T(8,128)(2,1)}, u32[]{:S(2)}) copy-start(bf16[8,2,128,256]{3,2,1,0:T(8,128)(2,1)} %refs_2_.1) | copy-start | bytes 3145732
  32.9 32.4 %collective-permute-start.2 = (bf16[8,2,128,256]{3,2,1,0:T(8,128)(2,1)S(1)}, bf16[8,2,128,256]{3,2,1,0:T(8,128)(2,1)S(1)}, u32[]{:S(2)}, u32[]{:S(2)}) collective-permute-start(bf16[8,2,128,256]{3,2,1,0:T(8,128)(2,1)S(1)} %copy-done.1), channel_id=1, source_target_pairs={{1,0},{2,1},{3,2},{4,3},{5,4},{6,5},{7,6},{8,7},{9,8},{10,9},{11,1... | collective-permute-start | bytes 3145736 | tf_op jit(solution)/shard_map/ppermute | solution.py:497
  44.9 12.3 %all-to-all-start.1 = ((bf16[8,4,16,512]{3,2,1,0:T(8,128)(2,1)}), bf16[8,4,16,512]{3,2,1,0:T(8,128)(2,1)S(1)}, u32[]{:S(2)}, u32[]{:S(2)}) async-start(bf16[8,4,16,512]{3,2,1,0:T(8,128)(2,1)} %bitcast.13), calls=%async_computation.1 | async-start | bytes 1048576 | tf_op jit(solution)/shard_map/all_to_all | solution.py:520
  57.2 17.2 %collective-permute-start.3 = (bf16[8,16,512]{2,1,0:T(8,128)(2,1)S(1)}, bf16[8,16,512]{2,1,0:T(8,128)(2,1)S(1)}, u32[]{:S(2)}, u32[]{:S(2)}) collective-permute-start(bf16[8,16,512]{2,1,0:T(8,128)(2,1)S(1)} %get-tuple-element.39), channel_id=1, source_target_pairs={{0,2},{1,3},{2,0},{3,1},{4,6},{5,7},{6,4},{7,5},{8,10},{9,11},{10,... | collective-permute-start | bytes 393224 | tf_op jit(solution)/shard_map/ppermute | solution.py:525
  57.4 17.0 %collective-permute-start.4 = (bf16[8,16,512]{2,1,0:T(8,128)(2,1)S(1)}, bf16[8,16,512]{2,1,0:T(8,128)(2,1)S(1)}, u32[]{:S(2)}, u32[]{:S(2)}) collective-permute-start(bf16[8,16,512]{2,1,0:T(8,128)(2,1)S(1)} %get-tuple-element.38), channel_id=1, source_target_pairs={{0,1},{1,2},{2,3},{3,0},{4,5},{5,6},{6,7},{7,4},{8,9},{9,10},{10,1... | collective-permute-start | bytes 393224 | tf_op jit(solution)/shard_map/ppermute | solution.py:525
  65.4 9.4 %collective-permute-start.5 = (bf16[8,16,512]{2,1,0:T(8,128)(2,1)S(1)}, bf16[8,16,512]{2,1,0:T(8,128)(2,1)S(1)}, u32[]{:S(2)}, u32[]{:S(2)}) collective-permute-start(bf16[8,16,512]{2,1,0:T(8,128)(2,1)S(1)} %get-tuple-element.37), channel_id=1, source_target_pairs={{0,3},{1,0},{2,1},{3,2},{4,7},{5,4},{6,5},{7,6},{8,11},{9,8},{10,9... | collective-permute-start | bytes 393224 | tf_op jit(solution)/shard_map/ppermute | solution.py:525

commit v20 on v16

--- a/solution.py
+++ b/solution.py
@@ -401,7 +401,8 @@
 
 def adjoint_kernel(rad_ref, out_hbm, held):
     for box in range(rad_ref.shape[0]):
-        held[box] = side_by_side(rad_ref[box, 0].T, rad_ref[box, 1].T)
+        real, imag = rad_ref[box, 0].T, rad_ref[box, 1].T
+        held[box] = jnp.concatenate([side_by_side(real, imag), side_by_side(-imag, real)], axis=0)
     pltpu.sync_copy(held, out_hbm)
 
 
@@ -411,8 +412,8 @@
         adjoint_kernel,
         in_specs=[pl.BlockSpec(memory_space=pltpu.VMEM)],
         out_specs=pl.BlockSpec(memory_space=pltpu.HBM),
-        scratch_shapes=[pltpu.VMEM((boxes, basis, 2 * points), BF16)],
-        out_shape=pltpu.HBM((boxes, basis, 2 * points), BF16),
+        scratch_shapes=[pltpu.VMEM((boxes, 2 * basis, 2 * points), BF16)],
+        out_shape=pltpu.HBM((boxes, 2 * basis, 2 * points), BF16),
         cost_estimate=pl.CostEstimate(
             flops=10**6, bytes_accessed=2 * MIB, transcendentals=0
         ),
@@ -454,11 +455,9 @@
             (boxes - 1 - octant, cos_re - sin_im, cos_im + sin_re),
         )
         for box, real, imag in leaves:
-            real, imag = real.astype(BF16), imag.astype(BF16)
-            right = jnp.concatenate([side_by_side(real, imag), side_by_side(imag, -real)], axis=0)
-            far = dot(adjoint_ref[box], right)
-            held[box, 0] = near_ref[box, 0] + before_ref[box, 0] + far[:, :rhs]
-            held[box, 1] = near_ref[box, 1] + before_ref[box, 1] + far[:, rhs:]
+            leaf = jnp.concatenate([real, imag], axis=0).astype(BF16)
+            far = dot(adjoint_ref[box], leaf)
+            held[box] = near_ref[box] + before_ref[box] + far.reshape(held.shape[1:])
             out_copies[box].start()
     for copy in out_copies:
         copy.wait()

time: 77.4 us -> 77.2 us (level)
  Pallas kernels: 28.7 us -> 30.3 us
  waiting for transfers between devices: 19.9 us -> 18.3 us
    pallas_call x3, Pallas kernels: 15.6 us -> 17 us  [near_field(): pl.pallas_call(kernel, in_specs=[smem, hbm, vmem] + [hbm] * (begun + kept...]
    all_to_all x1, waiting for transfers between devices: 1.08 us -> 0.11 us  [staged_bands(): bands = lax.all_to_all(bands, axes, split_axis=0, concat_axis=0, tiled=True)]
  transfers between devices with their start and end apart: 8 -> 8, of which waited for: 4 -> 4; matrix products, arithmetic and copies ran while one was open for 4% -> 4% of each run, Pallas kernels for 35% -> 37%
where the time goes in v20:
time: 77.2 us; the launch traced here: 76 us
  Pallas kernels  30.3 us (39%)
  starting transfers between devices  23.3 us (30%)
  waiting for transfers between devices  18.3 us (24%)
  local copies, waits for them, and re-layouts  2.16 us (3%)
  other arithmetic  1.56 us (2%)
    pallas_call x3, Pallas kernels, near_field(): pl.pallas_call(kernel, in_specs=[smem, hbm, vmem] + [hbm] * (begun + kept...  17 us
    all_to_all x1, waiting for transfers between devices, parent_bands(): return lax.all_to_all(spread, axes, split_axis=0, concat_axis=0, tiled=True)  8.19 us
    ppermute x3, starting transfers between devices, staged_bands(): received.append(lax.ppermute(piece, 'phi', ring))  8.02 us
    ppermute x2, starting transfers between devices, shift(): return lax.ppermute(block, axis, pairs)  6.41 us
    ppermute x2, waiting for transfers between devices, shift(): return lax.ppermute(block, axis, pairs)  6.06 us
    pallas_call x1, Pallas kernels, upward(): pl.pallas_call(up_kernel, in_specs=[hbm] * 3, out_specs=hbm, out_shape=pl...  5.24 us
    ppermute x3, waiting for transfers between devices, staged_bands(): received.append(lax.ppermute(piece, 'phi', ring))  3.96 us
    all_to_all x1, starting transfers between devices, parent_bands(): return lax.all_to_all(spread, axes, split_axis=0, concat_axis=0, tiled=True)  3.91 us
  transfers between devices with their start and end apart: 8, of which 4 were waited for; matrix products, arithmetic and copies ran while one was open for 4% of the time, Pallas kernels for 37%

profile of v20, /device:TPU:0, one launch (start us, length us, event | category | flops | bytes accessed | tf_op | source)
XLA Modules:
  0.0 76.0 jit_solution(5126580950774219923)
XLA Ops:
  0.0 5.1 %collective-permute-start.1 = (bf16[8,2,128,256]{3,2,1,0:T(8,128)(2,1)}, bf16[8,2,128,256]{3,2,1,0:T(8,128)(2,1)S(1)}, u32[]{:S(2)}, u32[]{:S(2)}) collective-permute-start(bf16[8,2,128,256]{3,2,1,0:T(8,128)(2,1)} %refs_2_.1), channel_id=1, source_target_pairs={{0,1},{1,2},{2,3},{3,4},{4,5},{5,6},{6,7},{7,8},{8,9},{9,10},{10,1... | collective-permute-start | bytes 3145736 | tf_op jit(solution)/shard_map/ppermute | solution.py:496
  5.1 0.8 %fusion.1 = s32[16,16]{1,0:T(8,128)S(1)} fusion(s32[16,16]{1,0:T(8,128)} %param.16, s32[16]{0:T(128)} %param.18), kind=kLoop, calls=%fused_computation.12 | loop fusion | flops 512 | bytes 2112 | tf_op jit(solution)/shard_map/jit(_where)/select_n | solution.py:501
  5.9 0.1 stack.9
  6.0 0.8 %stack.10 = s32[256,1]{0,1:T(1,128)S(1)} reshape(s32[16,16]{1,0:T(8,128)} %param.17) | data formatting | bytes 2048 | tf_op jit(solution)/shard_map/stack | solution.py:502
  6.8 5.2 %upward.1 = bf16[32,16,512]{2,1,0:T(8,128)(2,1)} custom-call(bf16[8,2,128,256]{3,2,1,0:T(8,128)(2,1)} %refs_2_.1, bf16[8,2,128,128]{3,2,1,0:T(8,128)(2,1)} %rad_ref.1, bf16[1024,1024]{1,0:T(8,128)(2,1)} %constant.93.clone.w_hbm), custom_call_target="tpu_custom_call" | custom-call | flops 2000000000 | bytes 4194304 | tf_op jit(solution)/shard_map/upward/pallas_call | solution.py:127
  12.0 1.5 %collective-permute-start = (s32[256,2]{0,1:T(2,128)S(1)}, s32[256,2]{0,1:T(2,128)S(1)}, u32[]{:S(2)}, u32[]{:S(2)}) collective-permute-start(s32[256,2]{0,1:T(2,128)S(1)} %pad_add_fusion.2), channel_id=1, source_target_pairs={{0,16},{16,0},{1,17},{17,1},{2,18},{18,2},{3,19},{19,3},{4,20},{20... | collective-permute-start | bytes 6152 | tf_op jit(solution)/shard_map/ppermute | solution.py:532
  13.6 0.1 reshape.134
  13.8 0.1 convert_reduce_fusion
  13.9 0.3 convert_reduce_fusion.1
  14.2 0.1 copy.22
  14.3 0.2 select_reduce_fusion
  14.4 0.1 pad_add_fusion.3.refs_0_
  14.5 0.1 copy.21.table_ref
  14.6 2.2 %adjoint.1.refs_5_ = bf16[8,256,256]{2,1,0:T(8,128)(2,1)} custom-call(bf16[8,2,128,128]{3,2,1,0:T(8,128)(2,1)} %rad_ref.1), custom_call_target="tpu_custom_call" | custom-call | flops 1000000 | bytes 2097152 | tf_op jit(solution)/shard_map/adjoint/pallas_call | solution.py:411
  16.9 0.1 copy.19
  17.0 0.1 copy.20
  17.2 1.1 %coupling.1.lines_hbm = f32[2,32,512]{2,1,0:T(8,128)S(1)} custom-call(s32[512,2]{1,0:T(8,128)S(1)} %broadcast_select_fusion.lists_ref, s32[1]{0:T(128)} %constant.82.clone.1.base_ref, bf16[316,32]{1,0:T(8,128)(2,1)S(1)} %copy.21.table_ref), custom_call_target="tpu_custom_call" | custom-call | flops 200000000 | bytes 2097152 | tf_op jit(solution)/shard_map/coupling/pallas_call | solution.py:175
  18.3 0.6 copy-done.2
  19.0 3.9 %all-to-all-start = ((bf16[32,16,512]{2,1,0:T(8,128)(2,1)}), bf16[32,16,512]{2,1,0:T(8,128)(2,1)S(1)}, u32[]{:S(2)}, u32[]{:S(2)}) async-start(bf16[32,16,512]{2,1,0:T(8,128)(2,1)} %upward.1), calls=%async_computation | async-start | bytes 1048576 | tf_op jit(solution)/shard_map/all_to_all | solution.py:507
  22.9 6.1 %collective-permute-done.1.refs_2_ = bf16[8,2,128,256]{3,2,1,0:T(8,128)(2,1)S(1)} collective-permute-done((bf16[8,2,128,256]{3,2,1,0:T(8,128)(2,1)}, bf16[8,2,128,256]{3,2,1,0:T(8,128)(2,1)S(1)}, u32[]{:S(2)}, u32[]{:S(2)}) %collective-permute-start.1) | collective-permute-done | bytes 1048608 | tf_op jit(solution)/shard_map/ppermute | solution.py:496
  28.9 4.0 %near_low.1.refs_3_ = f32[8,2,128,256]{3,2,1,0:T(8,128)} custom-call(s32[3,105]{1,0:T(4,128)S(1)} %pad_add_fusion.3.refs_0_, bf16[96,2,128,128]{3,2,1,0:T(8,128)(2,1)} %bitcast.10, bf16[8,2,128,256]{3,2,1,0:T(8,128)(2,1)S(1)} %collective-permute-done.1.refs_2_), custom_call_target="tpu_custom_call" | custom-call | flops 2000000000 | bytes 8388608 | tf_op jit(solution)/shard_map/near_low/pallas_call | solution.py:378
  32.9 1.3 %collective-permute-start.2 = (bf16[8,2,128,256]{3,2,1,0:T(8,128)(2,1)S(1)}, bf16[8,2,128,256]{3,2,1,0:T(8,128)(2,1)S(1)}, u32[]{:S(2)}, u32[]{:S(2)}) collective-permute-start(bf16[8,2,128,256]{3,2,1,0:T(8,128)(2,1)S(1)} %copy-done.1), channel_id=1, source_target_pairs={{1,0},{2,1},{3,2},{4,3},{5,4},{6,5},{7,6},{8,7},{9,8},{10,9},{11,1... | collective-permute-start | bytes 3145736 | tf_op jit(solution)/shard_map/ppermute | solution.py:496
  34.2 8.2 %all-to-all-done.refs_0_ = bf16[32,16,512]{2,1,0:T(8,128)(2,1)S(1)} async-done(((bf16[32,16,512]{2,1,0:T(8,128)(2,1)}), bf16[32,16,512]{2,1,0:T(8,128)(2,1)S(1)}, u32[]{:S(2)}, u32[]{:S(2)}) %all-to-all-start) | async-done | bytes 524320 | tf_op jit(solution)/shard_map/all_to_all | solution.py:507
  42.4 2.5 %translate.1 = bf16[32,16,512]{2,1,0:T(8,128)(2,1)} custom-call(f32[2,32,512]{2,1,0:T(8,128)} %copy-done.2, bf16[32,16,512]{2,1,0:T(8,128)(2,1)S(1)} %all-to-all-done.refs_0_), custom_call_target="tpu_custom_call" | custom-call | flops 1000000000 | bytes 2097152 | tf_op jit(solution)/shard_map/translate/pallas_call | solution.py:230
  44.9 3.5 %all-to-all-start.1 = ((bf16[8,4,16,512]{3,2,1,0:T(8,128)(2,1)}), bf16[8,4,16,512]{3,2,1,0:T(8,128)(2,1)S(1)}, u32[]{:S(2)}, u32[]{:S(2)}) async-start(bf16[8,4,16,512]{3,2,1,0:T(8,128)(2,1)} %bitcast.13), calls=%async_computation.1 | async-start | bytes 1048576 | tf_op jit(solution)/shard_map/all_to_all | solution.py:515
  48.5 8.6 %near_own.1.refs_3_ = f32[8,2,128,256]{3,2,1,0:T(8,128)} custom-call(s32[3,105]{1,0:T(4,128)S(1)} %pad_add_fusion.3.refs_0_, bf16[96,2,128,128]{3,2,1,0:T(8,128)(2,1)} %bitcast.11, bf16[8,2,128,256]{3,2,1,0:T(8,128)(2,1)S(1)} %copy-done.1, f32[8,2,128,256]{3,2,1,0:T(8,128)} %near_low.1.refs_3_), custom_call_target="tpu_custom_call" | custom-call | flops 2000000000 | bytes 8388608 | tf_op jit(solution)/shard_map/near_own/pallas_call | solution.py:378
  57.1 0.1 all-to-all-done.1.refs_0_
  57.2 1.0 %collective-permute-start.3 = (bf16[8,16,512]{2,1,0:T(8,128)(2,1)S(1)}, bf16[8,16,512]{2,1,0:T(8,128)(2,1)S(1)}, u32[]{:S(2)}, u32[]{:S(2)}) collective-permute-start(bf16[8,16,512]{2,1,0:T(8,128)(2,1)S(1)} %get-tuple-element.39), channel_id=1, source_target_pairs={{0,1},{1,2},{2,3},{3,0},{4,5},{5,6},{6,7},{7,4},{8,9},{9,10},{10,1... | collective-permute-start | bytes 393224 | tf_op jit(solution)/shard_map/ppermute | solution.py:520
  58.2 7.1 %collective-permute-start.4 = (bf16[8,16,512]{2,1,0:T(8,128)(2,1)S(1)}, bf16[8,16,512]{2,1,0:T(8,128)(2,1)S(1)}, u32[]{:S(2)}, u32[]{:S(2)}) collective-permute-start(bf16[8,16,512]{2,1,0:T(8,128)(2,1)S(1)} %get-tuple-element.38), channel_id=1, source_target_pairs={{0,2},{1,3},{2,0},{3,1},{4,6},{5,7},{6,4},{7,5},{8,10},{9,11},{10,... | collective-permute-start | bytes 393224 | tf_op jit(solution)/shard_map/ppermute | solution.py:520
  65.3 4.4 %near_high.1 = (f32[8,2,128,256]{3,2,1,0:T(8,128)S(1)}, f32[8,2,128,256]{3,2,1,0:T(8,128)S(1)}, bf16[1024,512]{1,0:T(8,128)(2,1)S(1)}, bf16[8,256,256]{2,1,0:T(8,128)(2,1)S(1)}) custom-call(s32[3,105]{1,0:T(4,128)S(1)} %pad_add_fusion.3.refs_0_, bf16[96,2,128,128]{3,2,1,0:T(8,128)(2,1)} %bitcast.12, ...), custom_call_target="tpu_custom_call" | custom-call | flops 99999997952 | bytes 8388608 | tf_op jit(solution)/shard_map/near_high/pallas_call | solution.py:378
  69.7 4.0 %collective-permute-done.4.refs_2_ = bf16[8,16,512]{2,1,0:T(8,128)(2,1)S(1)} collective-permute-done((bf16[8,16,512]{2,1,0:T(8,128)(2,1)S(1)}, bf16[8,16,512]{2,1,0:T(8,128)(2,1)S(1)}, u32[]{:S(2)}, u32[]{:S(2)}) %collective-permute-start.4) | collective-permute-done | bytes 131104 | tf_op jit(solution)/shard_map/ppermute | solution.py:520
  73.6 2.3 %downward.1 = f32[8,2,128,256]{3,2,1,0:T(8,128)} custom-call(s32[1]{0:T(128)} %bitcast.phi_ref, f32[8,2,128,256]{3,2,1,0:T(8,128)S(1)} %get-tuple-element.32.near_ref, f32[8,2,128,256]{3,2,1,0:T(8,128)S(1)} %get-tuple-element.33.before_ref, bf16[1024,512]{1,0:T(8,128)(2,1)S(1)} %get-tuple-element.34.w_ref, ...), custom_call_target="tpu_custom_call" | custom-call | flops 2000000000 | bytes 7340032 | tf_op jit(solution)/shard_map/downward/pallas_call | solution.py:473
  (25 shorter events, 0.2 us)
Async XLA Ops:
  0.0 14.4 %copy-start = (bf16[316,2,4,8]{0,3,2,1:T(8,128)(2,1)S(1)}, bf16[316,2,4,8]{0,3,2,1:T(8,128)(2,1)}, u32[]{:S(2)}) copy-start(bf16[316,2,4,8]{0,3,2,1:T(8,128)(2,1)} %param.19) | copy-start | bytes 121348
  0.0 28.9 %collective-permute-start.1 = (bf16[8,2,128,256]{3,2,1,0:T(8,128)(2,1)}, bf16[8,2,128,256]{3,2,1,0:T(8,128)(2,1)S(1)}, u32[]{:S(2)}, u32[]{:S(2)}) collective-permute-start(bf16[8,2,128,256]{3,2,1,0:T(8,128)(2,1)} %refs_2_.1), channel_id=1, source_target_pairs={{0,1},{1,2},{2,3},{3,4},{4,5},{5,6},{6,7},{7,8},{8,9},{9,10},{10,1... | collective-permute-start | bytes 3145736 | tf_op jit(solution)/shard_map/ppermute | solution.py:496
  6.8 6.8 %copy-start.3 = (s32[8,12]{1,0:T(8,128)S(1)}, s32[8,12]{1,0:T(8,128)}, u32[]{:S(2)}) copy-start(s32[8,12]{1,0:T(8,128)} %param.13) | copy-start | bytes 1156
  6.8 6.8 %copy-start.4 = (s32[8]{0:T(128)S(1)}, s32[8]{0:T(128)}, u32[]{:S(2)}) copy-start(s32[8]{0:T(128)} %param.14) | copy-start | bytes 100
  12.0 4.8 %collective-permute-start = (s32[256,2]{0,1:T(2,128)S(1)}, s32[256,2]{0,1:T(2,128)S(1)}, u32[]{:S(2)}, u32[]{:S(2)}) collective-permute-start(s32[256,2]{0,1:T(2,128)S(1)} %pad_add_fusion.2), channel_id=1, source_target_pairs={{0,16},{16,0},{1,17},{17,1},{2,18},{18,2},{3,19},{19,3},{4,20},{20... | collective-permute-start | bytes 6152 | tf_op jit(solution)/shard_map/ppermute | solution.py:532
  18.3 0.6 copy-start.2
  19.0 23.5 %all-to-all-start = ((bf16[32,16,512]{2,1,0:T(8,128)(2,1)}), bf16[32,16,512]{2,1,0:T(8,128)(2,1)S(1)}, u32[]{:S(2)}, u32[]{:S(2)}) async-start(bf16[32,16,512]{2,1,0:T(8,128)(2,1)} %upward.1), calls=%async_computation | async-start | bytes 1048576 | tf_op jit(solution)/shard_map/all_to_all | solution.py:507
  28.9 4.0 %copy-start.1 = (bf16[8,2,128,256]{3,2,1,0:T(8,128)(2,1)S(1)}, bf16[8,2,128,256]{3,2,1,0:T(8,128)(2,1)}, u32[]{:S(2)}) copy-start(bf16[8,2,128,256]{3,2,1,0:T(8,128)(2,1)} %refs_2_.1) | copy-start | bytes 3145732
  32.9 32.3 %collective-permute-start.2 = (bf16[8,2,128,256]{3,2,1,0:T(8,128)(2,1)S(1)}, bf16[8,2,128,256]{3,2,1,0:T(8,128)(2,1)S(1)}, u32[]{:S(2)}, u32[]{:S(2)}) collective-permute-start(bf16[8,2,128,256]{3,2,1,0:T(8,128)(2,1)S(1)} %copy-done.1), channel_id=1, source_target_pairs={{1,0},{2,1},{3,2},{4,3},{5,4},{6,5},{7,6},{8,7},{9,8},{10,9},{11,1... | collective-permute-start | bytes 3145736 | tf_op jit(solution)/shard_map/ppermute | solution.py:496
  44.9 12.3 %all-to-all-start.1 = ((bf16[8,4,16,512]{3,2,1,0:T(8,128)(2,1)}), bf16[8,4,16,512]{3,2,1,0:T(8,128)(2,1)S(1)}, u32[]{:S(2)}, u32[]{:S(2)}) async-start(bf16[8,4,16,512]{3,2,1,0:T(8,128)(2,1)} %bitcast.13), calls=%async_computation.1 | async-start | bytes 1048576 | tf_op jit(solution)/shard_map/all_to_all | solution.py:515
  57.2 12.4 %collective-permute-start.3 = (bf16[8,16,512]{2,1,0:T(8,128)(2,1)S(1)}, bf16[8,16,512]{2,1,0:T(8,128)(2,1)S(1)}, u32[]{:S(2)}, u32[]{:S(2)}) collective-permute-start(bf16[8,16,512]{2,1,0:T(8,128)(2,1)S(1)} %get-tuple-element.39), channel_id=1, source_target_pairs={{0,1},{1,2},{2,3},{3,0},{4,5},{5,6},{6,7},{7,4},{8,9},{9,10},{10,1... | collective-permute-start | bytes 393224 | tf_op jit(solution)/shard_map/ppermute | solution.py:520
  58.2 15.4 %collective-permute-start.4 = (bf16[8,16,512]{2,1,0:T(8,128)(2,1)S(1)}, bf16[8,16,512]{2,1,0:T(8,128)(2,1)S(1)}, u32[]{:S(2)}, u32[]{:S(2)}) collective-permute-start(bf16[8,16,512]{2,1,0:T(8,128)(2,1)S(1)} %get-tuple-element.38), channel_id=1, source_target_pairs={{0,2},{1,3},{2,0},{3,1},{4,6},{5,7},{6,4},{7,5},{8,10},{9,11},{10,... | collective-permute-start | bytes 393224 | tf_op jit(solution)/shard_map/ppermute | solution.py:520
  65.2 8.4 %collective-permute-start.5 = (bf16[8,16,512]{2,1,0:T(8,128)(2,1)S(1)}, bf16[8,16,512]{2,1,0:T(8,128)(2,1)S(1)}, u32[]{:S(2)}, u32[]{:S(2)}) collective-permute-start(bf16[8,16,512]{2,1,0:T(8,128)(2,1)S(1)} %get-tuple-element.37), channel_id=1, source_target_pairs={{0,3},{1,0},{2,1},{3,2},{4,7},{5,4},{6,5},{7,6},{8,11},{9,8},{10,9... | collective-permute-start | bytes 393224 | tf_op jit(solution)/shard_map/ppermute | solution.py:520

commit v21 on v16

--- a/solution.py
+++ b/solution.py
@@ -561,13 +561,11 @@
     spread = upward(coeffs, radiation, up_weights, shares * per_group)
     radiation_adjoint = adjoint(radiation)
     lists = lists_of(partners, vector_ids, pair_count)
-    spread, lists = lax.optimization_barrier((spread, lists))
     lines = translation_lines(lists, translation, shares, per_group)
     listed = near_slots(near_ids, near_count, lax.axis_index(every))
-    spread, lines, radiation_adjoint, listed = lax.optimization_barrier(
-        (spread, lines, radiation_adjoint, listed)
-    )
+    spread, radiation_adjoint = lax.optimization_barrier((spread, radiation_adjoint))
     parents = parent_bands(spread, shares)
+    lines, listed = lax.optimization_barrier((lines, listed))
     near = near_field(listed, near_blocks, low, 0)
     near, late = lax.optimization_barrier((near, coeffs))
     high = shift(late, every, -1)

time: 77.4 us -> 79.9 us (1.032)
  waiting for transfers between devices: 19.9 us -> 22.1 us
  Pallas kernels: 28.7 us -> 29.5 us
    ppermute x2, waiting for transfers between devices: 6.24 us -> 9.43 us  [shift(): return lax.ppermute(block, axis, pairs)]
    ppermute x2, starting transfers between devices: 6.41 us -> 4.83 us  [shift(): return lax.ppermute(block, axis, pairs)]
    ppermute x1, starting transfers between devices: 1.5 us -> 3 us  [translation_lines(): other = lax.ppermute(lists, 'box', [(0, 1), (1, 0)])]
    pallas_call x3, Pallas kernels: 15.6 us -> 16.4 us  [near_field(): pl.pallas_call(kernel, in_specs=[smem, hbm, vmem] + [hbm] * (begun + kept...]
  transfers between devices with their start and end apart: 8 -> 8, of which waited for: 4 -> 4; matrix products, arithmetic and copies ran while one was open for 4% -> 2% of each run, Pallas kernels for 35% -> 35%
where the time goes in v21:
time: 79.9 us; the launch traced here: 78.8 us
  Pallas kernels  29.5 us (37%)
  starting transfers between devices  23.2 us (29%)
  waiting for transfers between devices  22.1 us (28%)
  local copies, waits for them, and re-layouts  2.16 us (3%)
  other arithmetic  1.58 us (2%)
    pallas_call x3, Pallas kernels, near_field(): pl.pallas_call(kernel, in_specs=[smem, hbm, vmem] + [hbm] * (begun + kept...  16.4 us
    ppermute x2, waiting for transfers between devices, shift(): return lax.ppermute(block, axis, pairs)  9.43 us
    ppermute x3, starting transfers between devices, staged_bands(): received.append(lax.ppermute(piece, 'phi', ring))  7.99 us
    all_to_all x1, waiting for transfers between devices, parent_bands(): return lax.all_to_all(spread, axes, split_axis=0, concat_axis=0, tiled=True)  7.9 us
    pallas_call x1, Pallas kernels, upward(): pl.pallas_call(up_kernel, in_specs=[hbm] * 3, out_specs=hbm, out_shape=pl...  5.24 us
    ppermute x2, starting transfers between devices, shift(): return lax.ppermute(block, axis, pairs)  4.83 us
    ppermute x3, waiting for transfers between devices, staged_bands(): received.append(lax.ppermute(piece, 'phi', ring))  4.33 us
    all_to_all x1, starting transfers between devices, parent_bands(): return lax.all_to_all(spread, axes, split_axis=0, concat_axis=0, tiled=True)  3.86 us
  transfers between devices with their start and end apart: 8, of which 4 were waited for; matrix products, arithmetic and copies ran while one was open for 2% of the time, Pallas kernels for 35%

profile of v21, /device:TPU:0, one launch (start us, length us, event | category | flops | bytes accessed | tf_op | source)
XLA Modules:
  0.0 78.8 jit_solution(17518458557233543446)
XLA Ops:
  0.0 0.8 fusion.1
  0.8 0.1 stack.9
  0.9 0.8 stack.10
  1.7 3.0 %collective-permute-start = (s32[256,2]{0,1:T(2,128)S(1)}, s32[256,2]{0,1:T(2,128)S(1)}, u32[]{:S(2)}, u32[]{:S(2)}) collective-permute-start(s32[256,2]{0,1:T(2,128)S(1)} %pad_add_fusion.1), channel_id=1, source_target_pairs={{0,16},{16,0},{1,17},{17,1},{2,18},{18,2},{3,19},{19,3},{4,20},{20... | collective-permute-start | bytes 6152 | tf_op jit(solution)/shard_map/ppermute | solution.py:533
  4.7 3.5 %collective-permute-start.1 = (bf16[8,2,128,256]{3,2,1,0:T(8,128)(2,1)}, bf16[8,2,128,256]{3,2,1,0:T(8,128)(2,1)S(1)}, u32[]{:S(2)}, u32[]{:S(2)}) collective-permute-start(bf16[8,2,128,256]{3,2,1,0:T(8,128)(2,1)} %refs_2_.1), channel_id=1, source_target_pairs={{0,1},{1,2},{2,3},{3,4},{4,5},{5,6},{6,7},{7,8},{8,9},{9,10},{10,1... | collective-permute-start | bytes 3145736 | tf_op jit(solution)/shard_map/ppermute | solution.py:497
  8.2 2.0 %adjoint.1.refs_5_ = bf16[8,128,256]{2,1,0:T(8,128)(2,1)} custom-call(bf16[8,2,128,128]{3,2,1,0:T(8,128)(2,1)} %rad_ref.1), custom_call_target="tpu_custom_call" | custom-call | flops 1000000 | bytes 2097152 | tf_op jit(solution)/shard_map/adjoint/pallas_call | solution.py:410
  10.2 5.2 %upward.1 = bf16[32,16,512]{2,1,0:T(8,128)(2,1)} custom-call(bf16[8,2,128,256]{3,2,1,0:T(8,128)(2,1)} %refs_2_.1, bf16[8,2,128,128]{3,2,1,0:T(8,128)(2,1)} %rad_ref.1, bf16[1024,1024]{1,0:T(8,128)(2,1)} %constant.93.clone.w_hbm), custom_call_target="tpu_custom_call" | custom-call | flops 2000000000 | bytes 4194304 | tf_op jit(solution)/shard_map/upward/pallas_call | solution.py:127
  15.5 3.9 %all-to-all-start = ((bf16[32,16,512]{2,1,0:T(8,128)(2,1)}), bf16[32,16,512]{2,1,0:T(8,128)(2,1)S(1)}, u32[]{:S(2)}, u32[]{:S(2)}) async-start(bf16[32,16,512]{2,1,0:T(8,128)(2,1)} %upward.1), calls=%async_computation | async-start | bytes 1048576 | tf_op jit(solution)/shard_map/all_to_all | solution.py:508
  19.5 0.1 reshape.134
  19.6 0.2 convert_reduce_fusion.1
  19.8 0.1 copy.22
  20.0 0.1 convert_reduce_fusion
  20.1 0.2 select_reduce_fusion
  20.3 0.1 pad_add_fusion.2.refs_0_
  20.4 0.1 copy.21.table_ref
  20.5 0.1 copy.19
  20.7 0.1 copy.20
  20.9 1.1 %coupling.1.lines_hbm = f32[2,32,512]{2,1,0:T(8,128)S(1)} custom-call(s32[512,2]{1,0:T(8,128)S(1)} %broadcast_select_fusion.lists_ref, s32[1]{0:T(128)} %constant.82.clone.1.base_ref, bf16[316,32]{1,0:T(8,128)(2,1)S(1)} %copy.21.table_ref), custom_call_target="tpu_custom_call" | custom-call | flops 200000000 | bytes 2097152 | tf_op jit(solution)/shard_map/coupling/pallas_call | solution.py:175
  22.0 0.6 copy-done.2
  22.6 9.4 %collective-permute-done.1.refs_2_ = bf16[8,2,128,256]{3,2,1,0:T(8,128)(2,1)S(1)} collective-permute-done((bf16[8,2,128,256]{3,2,1,0:T(8,128)(2,1)}, bf16[8,2,128,256]{3,2,1,0:T(8,128)(2,1)S(1)}, u32[]{:S(2)}, u32[]{:S(2)}) %collective-permute-start.1) | collective-permute-done | bytes 1048608 | tf_op jit(solution)/shard_map/ppermute | solution.py:497
  32.0 4.0 %near_low.1.refs_3_ = f32[8,2,128,256]{3,2,1,0:T(8,128)} custom-call(s32[3,105]{1,0:T(4,128)S(1)} %pad_add_fusion.2.refs_0_, bf16[96,2,128,128]{3,2,1,0:T(8,128)(2,1)} %bitcast.10, bf16[8,2,128,256]{3,2,1,0:T(8,128)(2,1)S(1)} %collective-permute-done.1.refs_2_), custom_call_target="tpu_custom_call" | custom-call | flops 2000000000 | bytes 8388608 | tf_op jit(solution)/shard_map/near_low/pallas_call | solution.py:378
  36.0 1.3 %collective-permute-start.2 = (bf16[8,2,128,256]{3,2,1,0:T(8,128)(2,1)S(1)}, bf16[8,2,128,256]{3,2,1,0:T(8,128)(2,1)S(1)}, u32[]{:S(2)}, u32[]{:S(2)}) collective-permute-start(bf16[8,2,128,256]{3,2,1,0:T(8,128)(2,1)S(1)} %copy-done.1), channel_id=1, source_target_pairs={{1,0},{2,1},{3,2},{4,3},{5,4},{6,5},{7,6},{8,7},{9,8},{10,9},{11,1... | collective-permute-start | bytes 3145736 | tf_op jit(solution)/shard_map/ppermute | solution.py:497
  37.3 7.9 %all-to-all-done.refs_0_ = bf16[32,16,512]{2,1,0:T(8,128)(2,1)S(1)} async-done(((bf16[32,16,512]{2,1,0:T(8,128)(2,1)}), bf16[32,16,512]{2,1,0:T(8,128)(2,1)S(1)}, u32[]{:S(2)}, u32[]{:S(2)}) %all-to-all-start) | async-done | bytes 524320 | tf_op jit(solution)/shard_map/all_to_all | solution.py:508
  45.2 2.5 %translate.1 = bf16[32,16,512]{2,1,0:T(8,128)(2,1)} custom-call(f32[2,32,512]{2,1,0:T(8,128)} %copy-done.2, bf16[32,16,512]{2,1,0:T(8,128)(2,1)S(1)} %all-to-all-done.refs_0_), custom_call_target="tpu_custom_call" | custom-call | flops 1000000000 | bytes 2097152 | tf_op jit(solution)/shard_map/translate/pallas_call | solution.py:230
  47.7 3.5 %all-to-all-start.1 = ((bf16[8,4,16,512]{3,2,1,0:T(8,128)(2,1)}), bf16[8,4,16,512]{3,2,1,0:T(8,128)(2,1)S(1)}, u32[]{:S(2)}, u32[]{:S(2)}) async-start(bf16[8,4,16,512]{3,2,1,0:T(8,128)(2,1)} %bitcast.13), calls=%async_computation.1 | async-start | bytes 1048576 | tf_op jit(solution)/shard_map/all_to_all | solution.py:516
  51.3 8.3 %near_own.1.refs_3_ = f32[8,2,128,256]{3,2,1,0:T(8,128)} custom-call(s32[3,105]{1,0:T(4,128)S(1)} %pad_add_fusion.2.refs_0_, bf16[96,2,128,128]{3,2,1,0:T(8,128)(2,1)} %bitcast.11, bf16[8,2,128,256]{3,2,1,0:T(8,128)(2,1)S(1)} %copy-done.1, f32[8,2,128,256]{3,2,1,0:T(8,128)} %near_low.1.refs_3_), custom_call_target="tpu_custom_call" | custom-call | flops 2000000000 | bytes 8388608 | tf_op jit(solution)/shard_map/near_own/pallas_call | solution.py:378
  59.6 0.4 all-to-all-done.1.refs_0_
  60.0 0.3 collective-permute-start.3
  60.4 7.7 %collective-permute-start.4 = (bf16[8,16,512]{2,1,0:T(8,128)(2,1)S(1)}, bf16[8,16,512]{2,1,0:T(8,128)(2,1)S(1)}, u32[]{:S(2)}, u32[]{:S(2)}) collective-permute-start(bf16[8,16,512]{2,1,0:T(8,128)(2,1)S(1)} %get-tuple-element.34), channel_id=1, source_target_pairs={{0,2},{1,3},{2,0},{3,1},{4,6},{5,7},{6,4},{7,5},{8,10},{9,11},{10,... | collective-permute-start | bytes 393224 | tf_op jit(solution)/shard_map/ppermute | solution.py:521
  68.0 4.2 %near_high.1 = (f32[8,2,128,256]{3,2,1,0:T(8,128)S(1)}, f32[8,2,128,256]{3,2,1,0:T(8,128)S(1)}, bf16[1024,512]{1,0:T(8,128)(2,1)S(1)}, bf16[8,128,256]{2,1,0:T(8,128)(2,1)S(1)}) custom-call(s32[3,105]{1,0:T(4,128)S(1)} %pad_add_fusion.2.refs_0_, bf16[96,2,128,128]{3,2,1,0:T(8,128)(2,1)} %bitcast.12, ...), custom_call_target="tpu_custom_call" | custom-call | flops 99999997952 | bytes 8388608 | tf_op jit(solution)/shard_map/near_high/pallas_call | solution.py:378
  72.2 4.3 %collective-permute-done.4.refs_2_ = bf16[8,16,512]{2,1,0:T(8,128)(2,1)S(1)} collective-permute-done((bf16[8,16,512]{2,1,0:T(8,128)(2,1)S(1)}, bf16[8,16,512]{2,1,0:T(8,128)(2,1)S(1)}, u32[]{:S(2)}, u32[]{:S(2)}) %collective-permute-start.4) | collective-permute-done | bytes 131104 | tf_op jit(solution)/shard_map/ppermute | solution.py:521
  76.5 2.2 %downward.1 = f32[8,2,128,256]{3,2,1,0:T(8,128)} custom-call(s32[1]{0:T(128)} %bitcast.phi_ref, f32[8,2,128,256]{3,2,1,0:T(8,128)S(1)} %get-tuple-element.28.near_ref, f32[8,2,128,256]{3,2,1,0:T(8,128)S(1)} %get-tuple-element.29.before_ref, bf16[1024,512]{1,0:T(8,128)(2,1)S(1)} %get-tuple-element.30.w_ref, ...), custom_call_target="tpu_custom_call" | custom-call | flops 2000000000 | bytes 7340032 | tf_op jit(solution)/shard_map/downward/pallas_call | solution.py:474
  (25 shorter events, 0.2 us)
Async XLA Ops:
  0.0 20.0 %copy-start = (bf16[316,2,4,8]{0,3,2,1:T(8,128)(2,1)S(1)}, bf16[316,2,4,8]{0,3,2,1:T(8,128)(2,1)}, u32[]{:S(2)}) copy-start(bf16[316,2,4,8]{0,3,2,1:T(8,128)(2,1)} %param.19) | copy-start | bytes 121348
  1.7 18.9 %collective-permute-start = (s32[256,2]{0,1:T(2,128)S(1)}, s32[256,2]{0,1:T(2,128)S(1)}, u32[]{:S(2)}, u32[]{:S(2)}) collective-permute-start(s32[256,2]{0,1:T(2,128)S(1)} %pad_add_fusion.1), channel_id=1, source_target_pairs={{0,16},{16,0},{1,17},{17,1},{2,18},{18,2},{3,19},{19,3},{4,20},{20... | collective-permute-start | bytes 6152 | tf_op jit(solution)/shard_map/ppermute | solution.py:533
  4.7 27.4 %collective-permute-start.1 = (bf16[8,2,128,256]{3,2,1,0:T(8,128)(2,1)}, bf16[8,2,128,256]{3,2,1,0:T(8,128)(2,1)S(1)}, u32[]{:S(2)}, u32[]{:S(2)}) collective-permute-start(bf16[8,2,128,256]{3,2,1,0:T(8,128)(2,1)} %refs_2_.1), channel_id=1, source_target_pairs={{0,1},{1,2},{2,3},{3,4},{4,5},{5,6},{6,7},{7,8},{8,9},{9,10},{10,1... | collective-permute-start | bytes 3145736 | tf_op jit(solution)/shard_map/ppermute | solution.py:497
  10.2 9.1 %copy-start.3 = (s32[8,12]{1,0:T(8,128)S(1)}, s32[8,12]{1,0:T(8,128)}, u32[]{:S(2)}) copy-start(s32[8,12]{1,0:T(8,128)} %param.13) | copy-start | bytes 1156
  10.2 9.1 %copy-start.4 = (s32[8]{0:T(128)S(1)}, s32[8]{0:T(128)}, u32[]{:S(2)}) copy-start(s32[8]{0:T(128)} %param.14) | copy-start | bytes 100
  15.5 29.7 %all-to-all-start = ((bf16[32,16,512]{2,1,0:T(8,128)(2,1)}), bf16[32,16,512]{2,1,0:T(8,128)(2,1)S(1)}, u32[]{:S(2)}, u32[]{:S(2)}) async-start(bf16[32,16,512]{2,1,0:T(8,128)(2,1)} %upward.1), calls=%async_computation | async-start | bytes 1048576 | tf_op jit(solution)/shard_map/all_to_all | solution.py:508
  22.0 0.6 copy-start.2
  32.0 4.0 %copy-start.1 = (bf16[8,2,128,256]{3,2,1,0:T(8,128)(2,1)S(1)}, bf16[8,2,128,256]{3,2,1,0:T(8,128)(2,1)}, u32[]{:S(2)}) copy-start(bf16[8,2,128,256]{3,2,1,0:T(8,128)(2,1)} %refs_2_.1) | copy-start | bytes 3145732
  36.0 32.0 %collective-permute-start.2 = (bf16[8,2,128,256]{3,2,1,0:T(8,128)(2,1)S(1)}, bf16[8,2,128,256]{3,2,1,0:T(8,128)(2,1)S(1)}, u32[]{:S(2)}, u32[]{:S(2)}) collective-permute-start(bf16[8,2,128,256]{3,2,1,0:T(8,128)(2,1)S(1)} %copy-done.1), channel_id=1, source_target_pairs={{1,0},{2,1},{3,2},{4,3},{5,4},{6,5},{7,6},{8,7},{9,8},{10,9},{11,1... | collective-permute-start | bytes 3145736 | tf_op jit(solution)/shard_map/ppermute | solution.py:497
  47.7 12.3 %all-to-all-start.1 = ((bf16[8,4,16,512]{3,2,1,0:T(8,128)(2,1)}), bf16[8,4,16,512]{3,2,1,0:T(8,128)(2,1)S(1)}, u32[]{:S(2)}, u32[]{:S(2)}) async-start(bf16[8,4,16,512]{3,2,1,0:T(8,128)(2,1)} %bitcast.13), calls=%async_computation.1 | async-start | bytes 1048576 | tf_op jit(solution)/shard_map/all_to_all | solution.py:516
  60.0 12.2 %collective-permute-start.3 = (bf16[8,16,512]{2,1,0:T(8,128)(2,1)S(1)}, bf16[8,16,512]{2,1,0:T(8,128)(2,1)S(1)}, u32[]{:S(2)}, u32[]{:S(2)}) collective-permute-start(bf16[8,16,512]{2,1,0:T(8,128)(2,1)S(1)} %get-tuple-element.35), channel_id=1, source_target_pairs={{0,1},{1,2},{2,3},{3,0},{4,5},{5,6},{6,7},{7,4},{8,9},{9,10},{10,1... | collective-permute-start | bytes 393224 | tf_op jit(solution)/shard_map/ppermute | solution.py:521
  60.4 16.2 %collective-permute-start.4 = (bf16[8,16,512]{2,1,0:T(8,128)(2,1)S(1)}, bf16[8,16,512]{2,1,0:T(8,128)(2,1)S(1)}, u32[]{:S(2)}, u32[]{:S(2)}) collective-permute-start(bf16[8,16,512]{2,1,0:T(8,128)(2,1)S(1)} %get-tuple-element.34), channel_id=1, source_target_pairs={{0,2},{1,3},{2,0},{3,1},{4,6},{5,7},{6,4},{7,5},{8,10},{9,11},{10,... | collective-permute-start | bytes 393224 | tf_op jit(solution)/shard_map/ppermute | solution.py:521
  68.0 8.5 %collective-permute-start.5 = (bf16[8,16,512]{2,1,0:T(8,128)(2,1)S(1)}, bf16[8,16,512]{2,1,0:T(8,128)(2,1)S(1)}, u32[]{:S(2)}, u32[]{:S(2)}) collective-permute-start(bf16[8,16,512]{2,1,0:T(8,128)(2,1)S(1)} %get-tuple-element.33), channel_id=1, source_target_pairs={{0,3},{1,0},{2,1},{3,2},{4,7},{5,4},{6,5},{7,6},{8,11},{9,8},{10,9... | collective-permute-start | bytes 393224 | tf_op jit(solution)/shard_map/ppermute | solution.py:521

commit v22 on v17

--- a/solution.py
+++ b/solution.py
@@ -440,7 +440,7 @@
     out_copies = [
         pltpu.make_async_copy(held.at[box], out_hbm.at[box], sems.at[box]) for box in range(boxes)
     ]
-    places = [lax.rem(phi + phi_size - distance, phi_size) for distance in range(phi_size)]
+    places = [lax.rem(phi + distance, phi_size) for distance in range(phi_size)]
     left = jnp.concatenate([w_ref[place] for place in places], axis=1)
     right = jnp.concatenate([piece[...].reshape(-1, 2 * rhs) for piece in pieces], axis=0)
     mixed = dot(left, right)
@@ -513,7 +513,7 @@
     bands = incoming.reshape(-1, phi_size, *incoming.shape[1:])
     bands = lax.all_to_all(bands, axes, split_axis=0, concat_axis=0, tiled=True)
     received = []
-    for distance in range(phi_size):
+    for distance in [0, *range(phi_size - 1, 0, -1)]:
         piece = lax.dynamic_index_in_dim(bands, (phi + distance) % phi_size, 1, keepdims=False)
         if distance:
             ring = [(place, (place + distance) % phi_size) for place in range(phi_size)]

time: 79 us -> 77.1 us (0.976)
  waiting for transfers between devices: 21.8 us -> 19.5 us
    ppermute x3, waiting for transfers between devices: 6.27 us -> 4.14 us  [staged_bands(): piece = lax.ppermute(piece, 'phi', ring)]
  transfers between devices with their start and end apart: 8 -> 8, of which waited for: 4 -> 4; matrix products, arithmetic and copies ran while one was open for 4% -> 4% of each run, Pallas kernels for 34% -> 35%
where the time goes in v22:
time: 77.1 us; the launch traced here: 75.8 us
  Pallas kernels  29 us (38%)
  starting transfers between devices  23.3 us (30%)
  waiting for transfers between devices  19.5 us (25%)
  local copies, waits for them, and re-layouts  2.17 us (3%)
  other arithmetic  1.57 us (2%)
    pallas_call x3, Pallas kernels, near_field(): pl.pallas_call(kernel, in_specs=[smem, hbm, vmem] + [hbm] * (begun + kept...  16 us
    all_to_all x1, waiting for transfers between devices, parent_bands(): return lax.all_to_all(spread, axes, split_axis=0, concat_axis=0, tiled=True)  8.19 us
    ppermute x3, starting transfers between devices, staged_bands(): piece = lax.ppermute(piece, 'phi', ring)  8.02 us
    ppermute x2, starting transfers between devices, shift(): return lax.ppermute(block, axis, pairs)  6.41 us
    ppermute x2, waiting for transfers between devices, shift(): return lax.ppermute(block, axis, pairs)  6.25 us
    pallas_call x1, Pallas kernels, upward(): pl.pallas_call(up_kernel, in_specs=[hbm] * 3, out_specs=hbm, out_shape=pl...  5.24 us
    ppermute x3, waiting for transfers between devices, staged_bands(): piece = lax.ppermute(piece, 'phi', ring)  4.14 us
    all_to_all x1, starting transfers between devices, parent_bands(): return lax.all_to_all(spread, axes, split_axis=0, concat_axis=0, tiled=True)  3.9 us
  transfers between devices with their start and end apart: 8, of which 4 were waited for; matrix products, arithmetic and copies ran while one was open for 4% of the time, Pallas kernels for 35%

profile of v22, /device:TPU:0, one launch (start us, length us, event | category | flops | bytes accessed | tf_op | source)
XLA Modules:
  0.0 75.8 jit_solution(12655193011326404552)
XLA Ops:
  0.0 5.1 %collective-permute-start.1 = (bf16[8,2,128,256]{3,2,1,0:T(8,128)(2,1)}, bf16[8,2,128,256]{3,2,1,0:T(8,128)(2,1)S(1)}, u32[]{:S(2)}, u32[]{:S(2)}) collective-permute-start(bf16[8,2,128,256]{3,2,1,0:T(8,128)(2,1)} %refs_2_.1), channel_id=1, source_target_pairs={{0,1},{1,2},{2,3},{3,4},{4,5},{5,6},{6,7},{7,8},{8,9},{9,10},{10,1... | collective-permute-start | bytes 3145736 | tf_op jit(solution)/shard_map/ppermute | solution.py:495
  5.1 0.8 %stack.10 = s32[256,1]{0,1:T(1,128)S(1)} reshape(s32[16,16]{1,0:T(8,128)} %param.17) | data formatting | bytes 2048 | tf_op jit(solution)/shard_map/stack | solution.py:501
  5.9 0.8 %fusion.1 = s32[16,16]{1,0:T(8,128)S(1)} fusion(s32[16,16]{1,0:T(8,128)} %param.16, s32[16]{0:T(128)} %param.18), kind=kLoop, calls=%fused_computation.13 | loop fusion | flops 512 | bytes 2112 | tf_op jit(solution)/shard_map/jit(_where)/select_n | solution.py:500
  6.7 0.1 stack.9
  6.8 5.2 %upward.1 = bf16[32,16,512]{2,1,0:T(8,128)(2,1)} custom-call(bf16[8,2,128,256]{3,2,1,0:T(8,128)(2,1)} %refs_2_.1, bf16[8,2,128,128]{3,2,1,0:T(8,128)(2,1)} %rad_ref.1, bf16[1024,1024]{1,0:T(8,128)(2,1)} %constant.99.clone.w_hbm), custom_call_target="tpu_custom_call" | custom-call | flops 2000000000 | bytes 4194304 | tf_op jit(solution)/shard_map/upward/pallas_call | solution.py:129
  12.0 1.5 %collective-permute-start = (s32[256,2]{0,1:T(2,128)S(1)}, s32[256,2]{0,1:T(2,128)S(1)}, u32[]{:S(2)}, u32[]{:S(2)}) collective-permute-start(s32[256,2]{0,1:T(2,128)S(1)} %pad_add_fusion.2), channel_id=1, source_target_pairs={{0,16},{16,0},{1,17},{17,1},{2,18},{18,2},{3,19},{19,3},{4,20},{20... | collective-permute-start | bytes 6152 | tf_op jit(solution)/shard_map/ppermute | solution.py:533
  13.6 0.1 reshape.134
  13.8 0.2 convert_reduce_fusion.1
  14.0 0.1 copy.24
  14.1 0.2 convert_reduce_fusion
  14.3 0.2 select_reduce_fusion
  14.4 0.1 pad_add_fusion.3.refs_0_
  14.5 0.1 copy.23.table_ref
  14.6 2.0 %adjoint.1.refs_5_ = bf16[8,128,256]{2,1,0:T(8,128)(2,1)} custom-call(bf16[8,2,128,128]{3,2,1,0:T(8,128)(2,1)} %rad_ref.1), custom_call_target="tpu_custom_call" | custom-call | flops 1000000 | bytes 2097152 | tf_op jit(solution)/shard_map/adjoint/pallas_call | solution.py:420
  16.7 0.1 copy.22
  16.8 0.1 copy.21
  17.0 1.1 %coupling.1.lines_hbm = f32[2,32,512]{2,1,0:T(8,128)S(1)} custom-call(s32[512,2]{1,0:T(8,128)S(1)} %broadcast_select_fusion.lists_ref, s32[1]{0:T(128)} %constant.88.clone.1.base_ref, bf16[316,32]{1,0:T(8,128)(2,1)S(1)} %copy.23.table_ref), custom_call_target="tpu_custom_call" | custom-call | flops 200000000 | bytes 2097152 | tf_op jit(solution)/shard_map/coupling/pallas_call | solution.py:177
  18.1 0.6 copy-done.2
  18.8 3.9 %all-to-all-start = ((bf16[32,16,512]{2,1,0:T(8,128)(2,1)}), bf16[32,16,512]{2,1,0:T(8,128)(2,1)S(1)}, u32[]{:S(2)}, u32[]{:S(2)}) async-start(bf16[32,16,512]{2,1,0:T(8,128)(2,1)} %upward.1), calls=%async_computation | async-start | bytes 1048576 | tf_op jit(solution)/shard_map/all_to_all | solution.py:506
  22.7 6.2 %collective-permute-done.1.refs_2_ = bf16[8,2,128,256]{3,2,1,0:T(8,128)(2,1)S(1)} collective-permute-done((bf16[8,2,128,256]{3,2,1,0:T(8,128)(2,1)}, bf16[8,2,128,256]{3,2,1,0:T(8,128)(2,1)S(1)}, u32[]{:S(2)}, u32[]{:S(2)}) %collective-permute-start.1) | collective-permute-done | bytes 1048608 | tf_op jit(solution)/shard_map/ppermute | solution.py:495
  28.9 4.0 %near_low.1.refs_3_ = f32[8,2,128,256]{3,2,1,0:T(8,128)} custom-call(s32[3,105]{1,0:T(4,128)S(1)} %pad_add_fusion.3.refs_0_, bf16[96,2,128,128]{3,2,1,0:T(8,128)(2,1)} %bitcast.12, bf16[8,2,128,256]{3,2,1,0:T(8,128)(2,1)S(1)} %collective-permute-done.1.refs_2_), custom_call_target="tpu_custom_call" | custom-call | flops 2000000000 | bytes 8388608 | tf_op jit(solution)/shard_map/near_low/pallas_call | solution.py:388
  32.9 1.3 %collective-permute-start.2 = (bf16[8,2,128,256]{3,2,1,0:T(8,128)(2,1)S(1)}, bf16[8,2,128,256]{3,2,1,0:T(8,128)(2,1)S(1)}, u32[]{:S(2)}, u32[]{:S(2)}) collective-permute-start(bf16[8,2,128,256]{3,2,1,0:T(8,128)(2,1)S(1)} %copy-done.1), channel_id=1, source_target_pairs={{1,0},{2,1},{3,2},{4,3},{5,4},{6,5},{7,6},{8,7},{9,8},{10,9},{11,1... | collective-permute-start | bytes 3145736 | tf_op jit(solution)/shard_map/ppermute | solution.py:495
  34.2 8.2 %all-to-all-done.refs_0_ = bf16[32,16,512]{2,1,0:T(8,128)(2,1)S(1)} async-done(((bf16[32,16,512]{2,1,0:T(8,128)(2,1)}), bf16[32,16,512]{2,1,0:T(8,128)(2,1)S(1)}, u32[]{:S(2)}, u32[]{:S(2)}) %all-to-all-start) | async-done | bytes 524320 | tf_op jit(solution)/shard_map/all_to_all | solution.py:506
  42.4 2.5 %translate.1 = bf16[32,16,512]{2,1,0:T(8,128)(2,1)} custom-call(f32[2,32,512]{2,1,0:T(8,128)} %copy-done.2, bf16[32,16,512]{2,1,0:T(8,128)(2,1)S(1)} %all-to-all-done.refs_0_), custom_call_target="tpu_custom_call" | custom-call | flops 1000000000 | bytes 2097152 | tf_op jit(solution)/shard_map/translate/pallas_call | solution.py:232
  44.9 3.5 %all-to-all-start.1 = ((bf16[8,4,16,512]{3,2,1,0:T(8,128)(2,1)}), bf16[8,4,16,512]{3,2,1,0:T(8,128)(2,1)S(1)}, u32[]{:S(2)}, u32[]{:S(2)}) async-start(bf16[8,4,16,512]{3,2,1,0:T(8,128)(2,1)} %bitcast.15), calls=%async_computation.1 | async-start | bytes 1048576 | tf_op jit(solution)/shard_map/all_to_all | solution.py:514
  48.5 7.8 %near_own.1.refs_3_ = f32[8,2,128,256]{3,2,1,0:T(8,128)} custom-call(s32[3,105]{1,0:T(4,128)S(1)} %pad_add_fusion.3.refs_0_, bf16[96,2,128,128]{3,2,1,0:T(8,128)(2,1)} %bitcast.13, bf16[8,2,128,256]{3,2,1,0:T(8,128)(2,1)S(1)} %copy-done.1, f32[8,2,128,256]{3,2,1,0:T(8,128)} %near_low.1.refs_3_), custom_call_target="tpu_custom_call" | custom-call | flops 2000000000 | bytes 8388608 | tf_op jit(solution)/shard_map/near_own/pallas_call | solution.py:388
  56.3 0.9 %all-to-all-done.1 = bf16[8,4,16,512]{3,2,1,0:T(8,128)(2,1)S(1)} async-done(((bf16[8,4,16,512]{3,2,1,0:T(8,128)(2,1)}), bf16[8,4,16,512]{3,2,1,0:T(8,128)(2,1)S(1)}, u32[]{:S(2)}, u32[]{:S(2)}) %all-to-all-start.1) | async-done | bytes 524320 | tf_op jit(solution)/shard_map/all_to_all | solution.py:514
  57.2 1.0 %collective-permute-start.5 = (bf16[8,16,512]{2,1,0:T(8,128)(2,1)S(1)}, bf16[8,16,512]{2,1,0:T(8,128)(2,1)S(1)}, u32[]{:S(2)}, u32[]{:S(2)}) collective-permute-start(bf16[8,16,512]{2,1,0:T(8,128)(2,1)S(1)} %get-tuple-element.35), channel_id=1, source_target_pairs={{0,1},{1,2},{2,3},{3,0},{4,5},{5,6},{6,7},{7,4},{8,9},{9,10},{10,1... | collective-permute-start | bytes 393224 | tf_op jit(solution)/shard_map/ppermute | solution.py:520
  58.2 7.1 %collective-permute-start.4 = (bf16[8,16,512]{2,1,0:T(8,128)(2,1)S(1)}, bf16[8,16,512]{2,1,0:T(8,128)(2,1)S(1)}, u32[]{:S(2)}, u32[]{:S(2)}) collective-permute-start(bf16[8,16,512]{2,1,0:T(8,128)(2,1)S(1)} %get-tuple-element.36), channel_id=1, source_target_pairs={{0,2},{1,3},{2,0},{3,1},{4,6},{5,7},{6,4},{7,5},{8,10},{9,11},{10,... | collective-permute-start | bytes 393224 | tf_op jit(solution)/shard_map/ppermute | solution.py:520
  65.3 4.2 %near_high.1 = (f32[8,2,128,256]{3,2,1,0:T(8,128)S(1)}, bf16[4,1024,128]{2,1,0:T(8,128)(2,1)S(1)}, bf16[8,128,256]{2,1,0:T(8,128)(2,1)S(1)}) custom-call(s32[3,105]{1,0:T(4,128)S(1)} %pad_add_fusion.3.refs_0_, bf16[96,2,128,128]{3,2,1,0:T(8,128)(2,1)} %bitcast.14, bf16[8,2,128,256]{3,2,1,0:T(8,128)(2,1)S(1)} %collective-permute-done.2.refs_2_, ...), custom_call_target="tpu_custom_call" | custom-call | flops 99999997952 | bytes 8388608 | tf_op jit(solution)/shard_map/near_high/pallas_call | solution.py:388
  69.5 4.1 %collective-permute-done.4.refs_2_ = bf16[8,16,512]{2,1,0:T(8,128)(2,1)S(1)} collective-permute-done((bf16[8,16,512]{2,1,0:T(8,128)(2,1)S(1)}, bf16[8,16,512]{2,1,0:T(8,128)(2,1)S(1)}, u32[]{:S(2)}, u32[]{:S(2)}) %collective-permute-start.4) | collective-permute-done | bytes 131104 | tf_op jit(solution)/shard_map/ppermute | solution.py:520
  73.6 2.1 %downward.1 = f32[8,2,128,256]{3,2,1,0:T(8,128)} custom-call(s32[1]{0:T(128)} %bitcast.phi_ref, f32[8,2,128,256]{3,2,1,0:T(8,128)S(1)} %get-tuple-element.31.near_ref, bf16[4,1024,128]{2,1,0:T(8,128)(2,1)S(1)} %get-tuple-element.32.w_ref, bf16[8,128,256]{2,1,0:T(8,128)(2,1)S(1)} %get-tuple-element.33.adjoint_ref, ...), custom_call_target="tpu_custom_call" | custom-call | flops 2000000000 | bytes 7340032 | tf_op jit(solution)/shard_map/downward/pallas_call | solution.py:475
  (25 shorter events, 0.2 us)
Async XLA Ops:
  0.0 14.4 %copy-start = (bf16[316,2,4,8]{0,3,2,1:T(8,128)(2,1)S(1)}, bf16[316,2,4,8]{0,3,2,1:T(8,128)(2,1)}, u32[]{:S(2)}) copy-start(bf16[316,2,4,8]{0,3,2,1:T(8,128)(2,1)} %param.19) | copy-start | bytes 121348
  0.0 28.9 %collective-permute-start.1 = (bf16[8,2,128,256]{3,2,1,0:T(8,128)(2,1)}, bf16[8,2,128,256]{3,2,1,0:T(8,128)(2,1)S(1)}, u32[]{:S(2)}, u32[]{:S(2)}) collective-permute-start(bf16[8,2,128,256]{3,2,1,0:T(8,128)(2,1)} %refs_2_.1), channel_id=1, source_target_pairs={{0,1},{1,2},{2,3},{3,4},{4,5},{5,6},{6,7},{7,8},{8,9},{9,10},{10,1... | collective-permute-start | bytes 3145736 | tf_op jit(solution)/shard_map/ppermute | solution.py:495
  6.8 6.8 %copy-start.3 = (s32[8,12]{1,0:T(8,128)S(1)}, s32[8,12]{1,0:T(8,128)}, u32[]{:S(2)}) copy-start(s32[8,12]{1,0:T(8,128)} %param.13) | copy-start | bytes 1156
  6.8 6.8 %copy-start.4 = (s32[8]{0:T(128)S(1)}, s32[8]{0:T(128)}, u32[]{:S(2)}) copy-start(s32[8]{0:T(128)} %param.14) | copy-start | bytes 100
  12.0 4.6 %collective-permute-start = (s32[256,2]{0,1:T(2,128)S(1)}, s32[256,2]{0,1:T(2,128)S(1)}, u32[]{:S(2)}, u32[]{:S(2)}) collective-permute-start(s32[256,2]{0,1:T(2,128)S(1)} %pad_add_fusion.2), channel_id=1, source_target_pairs={{0,16},{16,0},{1,17},{17,1},{2,18},{18,2},{3,19},{19,3},{4,20},{20... | collective-permute-start | bytes 6152 | tf_op jit(solution)/shard_map/ppermute | solution.py:533
  18.1 0.6 copy-start.2
  18.8 23.7 %all-to-all-start = ((bf16[32,16,512]{2,1,0:T(8,128)(2,1)}), bf16[32,16,512]{2,1,0:T(8,128)(2,1)S(1)}, u32[]{:S(2)}, u32[]{:S(2)}) async-start(bf16[32,16,512]{2,1,0:T(8,128)(2,1)} %upward.1), calls=%async_computation | async-start | bytes 1048576 | tf_op jit(solution)/shard_map/all_to_all | solution.py:506
  28.9 4.0 %copy-start.1 = (bf16[8,2,128,256]{3,2,1,0:T(8,128)(2,1)S(1)}, bf16[8,2,128,256]{3,2,1,0:T(8,128)(2,1)}, u32[]{:S(2)}) copy-start(bf16[8,2,128,256]{3,2,1,0:T(8,128)(2,1)} %refs_2_.1) | copy-start | bytes 3145732
  32.9 32.3 %collective-permute-start.2 = (bf16[8,2,128,256]{3,2,1,0:T(8,128)(2,1)S(1)}, bf16[8,2,128,256]{3,2,1,0:T(8,128)(2,1)S(1)}, u32[]{:S(2)}, u32[]{:S(2)}) collective-permute-start(bf16[8,2,128,256]{3,2,1,0:T(8,128)(2,1)S(1)} %copy-done.1), channel_id=1, source_target_pairs={{1,0},{2,1},{3,2},{4,3},{5,4},{6,5},{7,6},{8,7},{9,8},{10,9},{11,1... | collective-permute-start | bytes 3145736 | tf_op jit(solution)/shard_map/ppermute | solution.py:495
  44.9 12.3 %all-to-all-start.1 = ((bf16[8,4,16,512]{3,2,1,0:T(8,128)(2,1)}), bf16[8,4,16,512]{3,2,1,0:T(8,128)(2,1)S(1)}, u32[]{:S(2)}, u32[]{:S(2)}) async-start(bf16[8,4,16,512]{3,2,1,0:T(8,128)(2,1)} %bitcast.15), calls=%async_computation.1 | async-start | bytes 1048576 | tf_op jit(solution)/shard_map/all_to_all | solution.py:514
  57.2 12.3 %collective-permute-start.5 = (bf16[8,16,512]{2,1,0:T(8,128)(2,1)S(1)}, bf16[8,16,512]{2,1,0:T(8,128)(2,1)S(1)}, u32[]{:S(2)}, u32[]{:S(2)}) collective-permute-start(bf16[8,16,512]{2,1,0:T(8,128)(2,1)S(1)} %get-tuple-element.35), channel_id=1, source_target_pairs={{0,1},{1,2},{2,3},{3,0},{4,5},{5,6},{6,7},{7,4},{8,9},{9,10},{10,1... | collective-permute-start | bytes 393224 | tf_op jit(solution)/shard_map/ppermute | solution.py:520
  58.2 15.4 %collective-permute-start.4 = (bf16[8,16,512]{2,1,0:T(8,128)(2,1)S(1)}, bf16[8,16,512]{2,1,0:T(8,128)(2,1)S(1)}, u32[]{:S(2)}, u32[]{:S(2)}) collective-permute-start(bf16[8,16,512]{2,1,0:T(8,128)(2,1)S(1)} %get-tuple-element.36), channel_id=1, source_target_pairs={{0,2},{1,3},{2,0},{3,1},{4,6},{5,7},{6,4},{7,5},{8,10},{9,11},{10,... | collective-permute-start | bytes 393224 | tf_op jit(solution)/shard_map/ppermute | solution.py:520
  65.3 8.4 %collective-permute-start.3 = (bf16[8,16,512]{2,1,0:T(8,128)(2,1)S(1)}, bf16[8,16,512]{2,1,0:T(8,128)(2,1)S(1)}, u32[]{:S(2)}, u32[]{:S(2)}) collective-permute-start(bf16[8,16,512]{2,1,0:T(8,128)(2,1)S(1)} %get-tuple-element.37), channel_id=1, source_target_pairs={{0,3},{1,0},{2,1},{3,2},{4,7},{5,4},{6,5},{7,6},{8,11},{9,8},{10,9... | collective-permute-start | bytes 393224 | tf_op jit(solution)/shard_map/ppermute | solution.py:520
